TPU v7x, 32 devices: a whole 2x2x4 slice. The times are simulated.
32 devices in a mesh: seq: 4 (over y, x), shard: 8 (over z, core).
Axes of the slice: x: 2, y: 2, z: 4, core: 2. Of those that a mesh axis runs over, the one named last changes fastest.
Arguments:
- tokens: bfloat16 [8, 2048, 1024], P('shard', 'seq'), may hold values from -6 to 6
- order: int32 [8, 2048], P('shard'), may hold values from 0 to 2047, each once within a row
- seq_lengths: int32 [8, 3], P('shard'), may hold values from 1 to 1365, 2048 in all within a row
- attn_gain: bfloat16 [1024], P('shard'), may hold values from 0.5 to 1.5
- w_query: bfloat16 [1024, 1024], P('shard'), may hold values from -0.1875 to 0.1875
- w_key: bfloat16 [1024, 512], P('shard'), may hold values from -0.1875 to 0.1875
- w_value: bfloat16 [1024, 512], P('shard'), may hold values from -0.1875 to 0.1875
- query_gain: bfloat16 [64], replicated, may hold values from 1.1953125 to 1.796875
- key_gain: bfloat16 [64], replicated, may hold values from 1.1953125 to 1.796875
- w_out: bfloat16 [1024, 1024], P('shard'), may hold values from -1 to 1
- ffn_gain: bfloat16 [1024], P('shard'), may hold values from 0.5 to 1.5
- w_gate: bfloat16 [1024, 4608], P('shard'), may hold values from -0.1875 to 0.1875
- w_up: bfloat16 [1024, 4608], P('shard'), may hold values from -0.1875 to 0.1875
- w_down: bfloat16 [4608, 1024], P('shard'), may hold values from -0.09375 to 0.09375
- cotangent: bfloat16 [8, 2048, 1024], P('shard', 'seq'), may hold values from -6 to 6
Outputs:
- block_out: bfloat16 [8, 2048, 1024], P('shard', 'seq')
- d_tokens: bfloat16 [8, 2048, 1024], P('shard', 'seq')
- d_attn_gain: float32 [1024], P('shard')
- d_w_query: float32 [1024, 1024], P('shard')
- d_w_key: float32 [1024, 512], P('shard')
- d_w_value: float32 [1024, 512], P('shard')
- d_query_gain: float32 [64], replicated
- d_key_gain: float32 [64], replicated
- d_w_out: float32 [1024, 1024], P('shard')
- d_ffn_gain: float32 [1024], P('shard')
- d_w_gate: float32 [1024, 4608], P('shard')
- d_w_up: float32 [1024, 4608], P('shard')
- d_w_down: float32 [4608, 1024], P('shard')
Inputs may be any that keep to these rules, and one draw needn't show every extreme that they name: Each row is a permutation of the 2048 tokens of one group: order[j] is the given-order token at dealt position j. `seq_lengths`: each row sums to 2048; its longest sequence has exactly 1365 tokens.
All inputs are finite; a program needn't handle non-finite values.
Results may differ from a plain program's by a relative error of at most 0.02.
Values may be sent and summed in bfloat16 or wider, within the bound.
A program may use at most 256 MiB of HBM per device.

v0:
```python
import jax
import jax.numpy as jnp
from jax import lax
from jax.sharding import PartitionSpec as P

EPSILON = 1e-05
ROPE_BASE = 1000000.0
MASKED = -1e30


def product(left_arg, right_arg):
    return jnp.dot(left_arg, right_arg, preferred_element_type=jnp.float32)


def rows_product(left_arg, right_arg):
    return lax.dot_general(
        left_arg, right_arg, (((0,), (0,)), ((), ())), preferred_element_type=jnp.float32
    )


def transposed_product(left_arg, right_arg):
    return lax.dot_general(
        left_arg, right_arg, (((1,), (1,)), ((), ())), preferred_element_type=jnp.float32
    )


def rms_norm(values, scale_gain):
    return (
        values * lax.rsqrt(jnp.mean(values * values, axis=-1, keepdims=True) + EPSILON) * scale_gain
    )


def rotary(values, places):
    half_dim = values.shape[-1] // 2
    frequency = ROPE_BASE ** (-2.0 * jnp.arange(half_dim, dtype=jnp.float32) / values.shape[-1])
    angles = places.astype(jnp.float32)[:, None] * frequency[None, :]
    cosine_table = jnp.concatenate([jnp.cos(angles), jnp.cos(angles)], axis=-1)[:, None, :]
    sine_table = jnp.concatenate([jnp.sin(angles), jnp.sin(angles)], axis=-1)[:, None, :]
    turned = jnp.concatenate([-values[..., half_dim:], values[..., :half_dim]], axis=-1)
    return values * cosine_table + turned * sine_table


def layout(lengths_row, token_count):
    seq_ends = jnp.cumsum(lengths_row)
    dealt_index = jnp.arange(token_count, dtype=jnp.int32)
    segment = jnp.sum((dealt_index[:, None] >= seq_ends[None, :]).astype(jnp.int32), axis=1)
    starts = seq_ends - lengths_row
    match_table = segment[:, None] == jnp.arange(lengths_row.shape[0], dtype=jnp.int32)[None, :]
    seq_begin = jnp.sum(jnp.where(match_table, starts[None, :], 0), axis=1)
    return (segment, dealt_index, dealt_index - seq_begin)


def head_prep(raw_rows, head_gain, places):
    tok_rows = raw_rows.shape[0]
    shaped = raw_rows.reshape(tok_rows, -1, head_gain.shape[0])
    return rotary(rms_norm(shaped, head_gain), places).reshape(tok_rows, -1)


def masked_scores(query_block, key_block, seg_query, seg_key, index_query, index_key, score_scale):
    scores = (
        jnp.einsum("qgrd,kgd->grqk", query_block, key_block, preferred_element_type=jnp.float32)
        * score_scale
    )
    allowed = (seg_query[:, None] == seg_key[None, :]) & (
        index_query[:, None] >= index_key[None, :]
    )
    return jnp.where(allowed[None, None], scores, MASKED)


def body(
    tokens,
    order,
    seq_lengths,
    attn_gain,
    w_query,
    w_key,
    w_value,
    query_gain,
    key_gain,
    w_out,
    ffn_gain,
    w_gate,
    w_up,
    w_down,
    cotangent,
):
    tok_rows = tokens.shape[1]
    all_rows = tok_rows * lax.axis_size("seq")
    head_dim = query_gain.shape[0]
    dealt_order = order[0]
    segment, dealt_index, places = layout(seq_lengths[0], all_rows)
    inverse = jnp.zeros((all_rows,), jnp.int32).at[dealt_order].set(dealt_index)
    given_places = jnp.take(places, inverse)
    my_places = lax.dynamic_slice_in_dim(given_places, lax.axis_index("seq") * tok_rows, tok_rows)
    gathered = (
        lax.all_gather(attn_gain, "shard", axis=0, tiled=True),
        lax.all_gather(w_query, "shard", axis=0, tiled=True),
        lax.all_gather(w_key, "shard", axis=0, tiled=True),
        lax.all_gather(w_value, "shard", axis=0, tiled=True),
        lax.all_gather(w_out, "shard", axis=0, tiled=True),
        lax.all_gather(ffn_gain, "shard", axis=0, tiled=True),
        lax.all_gather(w_gate, "shard", axis=0, tiled=True),
        lax.all_gather(w_up, "shard", axis=0, tiled=True),
        lax.all_gather(w_down, "shard", axis=0, tiled=True),
    )
    q_gain = query_gain.astype(jnp.float32)
    k_gain = key_gain.astype(jnp.float32)
    x_in = tokens[0].astype(jnp.float32)
    normed = rms_norm(x_in, gathered[0].astype(jnp.float32)).astype(jnp.bfloat16)
    q_raw = product(normed, gathered[1])
    k_raw = product(normed, gathered[2])
    value_rows = product(normed, gathered[3]).astype(jnp.bfloat16)
    query_rows = head_prep(q_raw, q_gain, my_places).astype(jnp.bfloat16)
    key_rows = head_prep(k_raw, k_gain, my_places).astype(jnp.bfloat16)
    query_here, key_here, value_here = (
        lax.all_to_all(query_rows, "seq", split_axis=1, concat_axis=0, tiled=True),
        lax.all_to_all(key_rows, "seq", split_axis=1, concat_axis=0, tiled=True),
        lax.all_to_all(value_rows, "seq", split_axis=1, concat_axis=0, tiled=True),
    )
    kv_local = key_here.shape[1] // head_dim
    repeat = query_here.shape[1] // key_here.shape[1]
    query_dealt = jnp.take(query_here, dealt_order, axis=0).reshape(
        all_rows, kv_local, repeat, head_dim
    )
    key_dealt = jnp.take(key_here, dealt_order, axis=0).reshape(all_rows, kv_local, head_dim)
    value_dealt = jnp.take(value_here, dealt_order, axis=0).reshape(all_rows, kv_local, head_dim)
    block_rows = min(512, all_rows)
    block_count = all_rows // block_rows
    score_scale = head_dim ** (-0.5)
    first_block = (dealt_index - places).reshape(block_count, block_rows)[:, 0] // block_rows

    def take_block(array_in, block_at, axis_at):
        return lax.dynamic_slice_in_dim(array_in, block_at * block_rows, block_rows, axis_at)

    def forward_block(q_block):
        query_block = take_block(query_dealt, q_block, 0)
        seg_query = take_block(segment, q_block, 0)
        index_query = take_block(dealt_index, q_block, 0)

        def block_scores(k_block):
            return masked_scores(
                query_block,
                take_block(key_dealt, k_block, 0),
                seg_query,
                take_block(segment, k_block, 0),
                index_query,
                take_block(dealt_index, k_block, 0),
                score_scale,
            )

        def running(k_block, loop_state):
            highest, row_mass = loop_state
            scores = block_scores(k_block)
            new_high = jnp.maximum(highest, jnp.max(scores, axis=-1))
            row_mass = row_mass * jnp.exp(highest - new_high) + jnp.sum(
                jnp.exp(scores - new_high[..., None]), axis=-1
            )
            return (new_high, row_mass)

        start_state = (
            jnp.full((kv_local, repeat, block_rows), MASKED, jnp.float32),
            jnp.zeros((kv_local, repeat, block_rows), jnp.float32),
        )
        highest, row_mass = lax.fori_loop(first_block[q_block], q_block + 1, running, start_state)
        log_total = highest + jnp.log(row_mass)

        def accumulate(k_block, total_acc):
            weights_low = jnp.exp(block_scores(k_block) - log_total[..., None]).astype(jnp.bfloat16)
            return total_acc + jnp.einsum(
                "grqk,kgd->qgrd",
                weights_low,
                take_block(value_dealt, k_block, 0),
                preferred_element_type=jnp.float32,
            )

        attended_block = lax.fori_loop(
            first_block[q_block],
            q_block + 1,
            accumulate,
            jnp.zeros((block_rows, kv_local, repeat, head_dim), jnp.float32),
        )
        return (attended_block, log_total)

    attended_parts, log_totals = lax.map(forward_block, jnp.arange(block_count, dtype=jnp.int32))
    attended_dealt = attended_parts.reshape(all_rows, kv_local, repeat, head_dim)
    attended_given = jnp.take(
        attended_dealt.reshape(all_rows, -1).astype(jnp.bfloat16), inverse, axis=0
    )
    attended_tok = lax.all_to_all(attended_given, "seq", split_axis=0, concat_axis=1, tiled=True)
    middle = x_in + product(attended_tok, gathered[4])
    normed_ffn = rms_norm(middle, gathered[5].astype(jnp.float32)).astype(jnp.bfloat16)
    gate_proj = product(normed_ffn, gathered[6])
    up_proj = product(normed_ffn, gathered[7])
    hidden = (jax.nn.silu(gate_proj) * up_proj).astype(jnp.bfloat16)
    block_out = (middle + product(hidden, gathered[8])).astype(jnp.bfloat16)
    weights_back = (
        lax.all_gather(attn_gain, "shard", axis=0, tiled=True),
        lax.all_gather(w_query, "shard", axis=0, tiled=True),
        lax.all_gather(w_key, "shard", axis=0, tiled=True),
        lax.all_gather(w_value, "shard", axis=0, tiled=True),
        lax.all_gather(w_out, "shard", axis=0, tiled=True),
        lax.all_gather(ffn_gain, "shard", axis=0, tiled=True),
        lax.all_gather(w_gate, "shard", axis=0, tiled=True),
        lax.all_gather(w_up, "shard", axis=0, tiled=True),
        lax.all_gather(w_down, "shard", axis=0, tiled=True),
    )
    grad_rows = cotangent[0]
    d_w_down = rows_product(hidden, grad_rows)
    d_hidden = transposed_product(grad_rows, weights_back[8])
    sigmoid_gate = jax.nn.sigmoid(gate_proj)
    d_gate = (d_hidden * up_proj * sigmoid_gate * (1.0 + gate_proj * (1.0 - sigmoid_gate))).astype(
        jnp.bfloat16
    )
    d_up = (d_hidden * gate_proj * sigmoid_gate).astype(jnp.bfloat16)
    d_w_gate = rows_product(normed_ffn, d_gate)
    d_w_up = rows_product(normed_ffn, d_up)
    d_normed_ffn = transposed_product(d_gate, weights_back[6]) + transposed_product(
        d_up, weights_back[7]
    )
    ffn_pull = jax.vjp(rms_norm, middle, weights_back[5].astype(jnp.float32))[1]
    d_middle_norm, d_ffn_gain = ffn_pull(d_normed_ffn)
    d_middle = grad_rows.astype(jnp.float32) + d_middle_norm
    d_branch = d_middle.astype(jnp.bfloat16)
    d_w_out = rows_product(attended_tok, d_branch)
    d_attended = transposed_product(d_branch, weights_back[4]).astype(jnp.bfloat16)
    d_here = lax.all_to_all(d_attended, "seq", split_axis=1, concat_axis=0, tiled=True)
    d_dealt = jnp.take(d_here, dealt_order, axis=0).reshape(all_rows, kv_local, repeat, head_dim)
    delta_rows = jnp.moveaxis(jnp.sum(d_dealt.astype(jnp.float32) * attended_dealt, axis=-1), 0, -1)

    def backward_block(q_block, grads_state):
        d_query_all, d_key_all, d_value_all = grads_state
        query_block = take_block(query_dealt, q_block, 0)
        grad_block = take_block(d_dealt, q_block, 0)
        seg_query = take_block(segment, q_block, 0)
        index_query = take_block(dealt_index, q_block, 0)
        log_total = log_totals[q_block]
        delta_block = take_block(delta_rows, q_block, 2)

        def key_step(k_block, inner_state):
            d_query_block, d_key_all, d_value_all = inner_state
            key_block = take_block(key_dealt, k_block, 0)
            value_block = take_block(value_dealt, k_block, 0)
            scores = masked_scores(
                query_block,
                key_block,
                seg_query,
                take_block(segment, k_block, 0),
                index_query,
                take_block(dealt_index, k_block, 0),
                score_scale,
            )
            weights_f32 = jnp.exp(scores - log_total[..., None])
            weights_low = weights_f32.astype(jnp.bfloat16)
            d_weights = jnp.einsum(
                "qgrd,kgd->grqk", grad_block, value_block, preferred_element_type=jnp.float32
            )
            d_scores = (weights_f32 * (d_weights - delta_block[..., None])).astype(jnp.bfloat16)
            d_query_block = (
                d_query_block
                + jnp.einsum(
                    "grqk,kgd->qgrd", d_scores, key_block, preferred_element_type=jnp.float32
                )
                * score_scale
            )
            key_part = (
                jnp.einsum(
                    "grqk,qgrd->kgd", d_scores, query_block, preferred_element_type=jnp.float32
                )
                * score_scale
            )
            value_part = jnp.einsum(
                "grqk,qgrd->kgd", weights_low, grad_block, preferred_element_type=jnp.float32
            )
            d_key_all = lax.dynamic_update_slice_in_dim(
                d_key_all, take_block(d_key_all, k_block, 0) + key_part, k_block * block_rows, 0
            )
            d_value_all = lax.dynamic_update_slice_in_dim(
                d_value_all,
                take_block(d_value_all, k_block, 0) + value_part,
                k_block * block_rows,
                0,
            )
            return (d_query_block, d_key_all, d_value_all)

        start_state = (
            jnp.zeros((block_rows, kv_local, repeat, head_dim), jnp.float32),
            d_key_all,
            d_value_all,
        )
        d_query_block, d_key_all, d_value_all = lax.fori_loop(
            first_block[q_block], q_block + 1, key_step, start_state
        )
        d_query_all = lax.dynamic_update_slice_in_dim(
            d_query_all, d_query_block, q_block * block_rows, 0
        )
        return (d_query_all, d_key_all, d_value_all)

    zero_state = (
        jnp.zeros((all_rows, kv_local, repeat, head_dim), jnp.float32),
        jnp.zeros((all_rows, kv_local, head_dim), jnp.float32),
        jnp.zeros((all_rows, kv_local, head_dim), jnp.float32),
    )
    d_query_dealt, d_key_dealt, d_value_dealt = lax.fori_loop(
        0, block_count, backward_block, zero_state
    )
    d_query_given = jnp.take(
        d_query_dealt.reshape(all_rows, -1).astype(jnp.bfloat16), inverse, axis=0
    )
    d_key_given = jnp.take(d_key_dealt.reshape(all_rows, -1).astype(jnp.bfloat16), inverse, axis=0)
    d_value_given = jnp.take(
        d_value_dealt.reshape(all_rows, -1).astype(jnp.bfloat16), inverse, axis=0
    )
    d_query_tok, d_key_tok, d_value_tok = (
        lax.all_to_all(d_query_given, "seq", split_axis=0, concat_axis=1, tiled=True),
        lax.all_to_all(d_key_given, "seq", split_axis=0, concat_axis=1, tiled=True),
        lax.all_to_all(d_value_given, "seq", split_axis=0, concat_axis=1, tiled=True),
    )
    query_pull = jax.vjp(
        lambda raw_rows, head_gain: head_prep(raw_rows, head_gain, my_places), q_raw, q_gain
    )[1]
    d_q_raw, d_query_gain = query_pull(d_query_tok.astype(jnp.float32))
    key_pull = jax.vjp(
        lambda raw_rows, head_gain: head_prep(raw_rows, head_gain, my_places), k_raw, k_gain
    )[1]
    d_k_raw, d_key_gain = key_pull(d_key_tok.astype(jnp.float32))
    d_q_low = d_q_raw.astype(jnp.bfloat16)
    d_k_low = d_k_raw.astype(jnp.bfloat16)
    d_w_query = rows_product(normed, d_q_low)
    d_w_key = rows_product(normed, d_k_low)
    d_w_value = rows_product(normed, d_value_tok)
    d_normed = (
        transposed_product(d_q_low, weights_back[1])
        + transposed_product(d_k_low, weights_back[2])
        + transposed_product(d_value_tok, weights_back[3])
    )
    attn_pull = jax.vjp(rms_norm, x_in, weights_back[0].astype(jnp.float32))[1]
    d_input_norm, d_attn_gain = attn_pull(d_normed)
    d_tokens = (d_middle + d_input_norm).astype(jnp.bfloat16)
    (
        part_attn_gain,
        part_query,
        part_key,
        part_value,
        part_out,
        part_ffn_gain,
        part_gate,
        part_up,
        part_down,
    ) = (
        lax.psum_scatter(
            d_attn_gain.astype(jnp.bfloat16), "shard", scatter_dimension=0, tiled=True
        ).astype(jnp.float32),
        lax.psum_scatter(
            d_w_query.astype(jnp.bfloat16), "shard", scatter_dimension=0, tiled=True
        ).astype(jnp.float32),
        lax.psum_scatter(
            d_w_key.astype(jnp.bfloat16), "shard", scatter_dimension=0, tiled=True
        ).astype(jnp.float32),
        lax.psum_scatter(
            d_w_value.astype(jnp.bfloat16), "shard", scatter_dimension=0, tiled=True
        ).astype(jnp.float32),
        lax.psum_scatter(
            d_w_out.astype(jnp.bfloat16), "shard", scatter_dimension=0, tiled=True
        ).astype(jnp.float32),
        lax.psum_scatter(
            d_ffn_gain.astype(jnp.bfloat16), "shard", scatter_dimension=0, tiled=True
        ).astype(jnp.float32),
        lax.psum_scatter(
            d_w_gate.astype(jnp.bfloat16), "shard", scatter_dimension=0, tiled=True
        ).astype(jnp.float32),
        lax.psum_scatter(
            d_w_up.astype(jnp.bfloat16), "shard", scatter_dimension=0, tiled=True
        ).astype(jnp.float32),
        lax.psum_scatter(
            d_w_down.astype(jnp.bfloat16), "shard", scatter_dimension=0, tiled=True
        ).astype(jnp.float32),
    )
    totals = (
        lax.psum(part_attn_gain.astype(jnp.bfloat16), "seq").astype(jnp.float32),
        lax.psum(part_query.astype(jnp.bfloat16), "seq").astype(jnp.float32),
        lax.psum(part_key.astype(jnp.bfloat16), "seq").astype(jnp.float32),
        lax.psum(part_value.astype(jnp.bfloat16), "seq").astype(jnp.float32),
        lax.psum(part_out.astype(jnp.bfloat16), "seq").astype(jnp.float32),
        lax.psum(part_ffn_gain.astype(jnp.bfloat16), "seq").astype(jnp.float32),
        lax.psum(part_gate.astype(jnp.bfloat16), "seq").astype(jnp.float32),
        lax.psum(part_up.astype(jnp.bfloat16), "seq").astype(jnp.float32),
        lax.psum(part_down.astype(jnp.bfloat16), "seq").astype(jnp.float32),
    )
    head_gains = lax.psum((d_query_gain, d_key_gain), ("seq", "shard"))
    return (
        block_out[None],
        d_tokens[None],
        totals[0],
        totals[1],
        totals[2],
        totals[3],
        head_gains[0],
        head_gains[1],
        totals[4],
        totals[5],
        totals[6],
        totals[7],
        totals[8],
    )


def solution(mesh):
    in_specs = (
        P("shard", "seq", None),
        P("shard", None),
        P("shard", None),
        P("shard"),
        P("shard", None),
        P("shard", None),
        P("shard", None),
        P(),
        P(),
        P("shard", None),
        P("shard"),
        P("shard", None),
        P("shard", None),
        P("shard", None),
        P("shard", "seq", None),
    )
    out_specs = (
        P("shard", "seq", None),
        P("shard", "seq", None),
        P("shard"),
        P("shard", None),
        P("shard", None),
        P("shard", None),
        P(),
        P(),
        P("shard", None),
        P("shard"),
        P("shard", None),
        P("shard", None),
        P("shard", None),
    )
    return jax.shard_map(body, mesh=mesh, in_specs=in_specs, out_specs=out_specs, check_vma=False)
```

profile of v0, /device:TPU:0, one launch (start us, length us, event | category | flops | bytes accessed | tf_op | source)
XLA Modules:
  0.0 1178.0 jit_solution(16855842968926135628)
XLA Ops:
  12.3 8.0 scatter_custom_fusion
  20.8 13.4 %all-gather = bf16[8,1,128]{2,1,0:T(2,128)(2,1)S(1)} all-gather(bf16[1,1,128]{2,1,0:T(2,128)(2,1)S(1)} %bitcast.397), channel_id=1, replica_groups=mesh['seq'=4,'shard'=8] {'shard'}, dimensions={0}, use_global_device_ids=true | all-gather | bytes 2304 | tf_op jit(solution)/shard_map/all_gather | solution.py:96
  34.3 11.8 %gather_fusion = s32[2048]{0:T(1024)S(1)} fusion(s32[2048]{0:T(1024)S(1)} %get-tuple-element.780, s32[2048]{0:T(1024)S(1)} %get-tuple-element.781), kind=kCustom, calls=%fused_computation.8 | custom fusion | bytes 24576 | tf_op jit(solution)/shard_map/jit(_take)/gather | solution.py:93
  51.3 4.1 all-to-all-start.1
  60.8 27.4 %all-gather.10.cloned.1.call-done = bf16[1024,1024]{1,0:T(8,128)(2,1)} async-done(((bf16[128,1024]{1,0:T(8,128)(2,1)}), bf16[1024,1024]{1,0:T(8,128)(2,1)}) %all-gather.10.cloned.1.call-update) | async-done | bytes 2097168 | tf_op jit(solution)/shard_map/all_gather | solution.py:97
  88.2 3.9 copy.133
  97.6 3.6 all-to-all-start.2
  104.8 4.9 all-to-all-done.2
  109.7 3.7 all-to-all-start
  116.2 6.2 gather_fusion.2
  122.4 6.2 gather_fusion.3
  130.8 9.1 gather_fusion.1
  142.0 89.8 %while.88 = (s32[]{:T(128)}, f32[4,512,2,2,64]{1,4,3,2,0:T(8,128)}, f32[4,2,2,512]{3,2,1,0:T(2,128)S(1)}, s32[4]{0:T(128)S(1)}, s32[4]{0:T(128)S(1)}, /*index=5*...) while((s32[]{:T(128)}, f32[4,512,2,2,64]{1,4,3,2,0:T(8,128)}, ...), condition=%wide.region_14.17_spmd.clone, body=%wide.region_7.16_spmd.clone.sunk | while | flops 415897600 | bytes 13969887 | solution.py:184
  149.7 6.1 while.92
  161.9 4.6 while.91
  166.7 11.6 while.92
  184.4 4.6 while.91
  189.1 11.6 while.92
  206.8 7.0 while.91
  213.9 17.1 %while.92 = (s32[]{:T(128)}, f32[512,2,2,64]{0,3,2,1:T(8,128)S(1)}, s32[]{:T(128)}, bf16[2048,2,64]{0,2,1:T(8,128)(2,1)}, s32[512]{0:T(512)S(1)}, /*index=5*/s32...) while((s32[]{:T(128)}, f32[512,2,2,64]{0,3,2,1:T(8,128)S(1)}, ...), condition=%wide.region_13.15_spmd, body=%wide.region_12.14_spmd.sunk | while | flops 273547264 | bytes 2122947 | solution.py:176
  234.0 3.7 copy.165
  237.7 4.4 reshape.612
  242.1 7.5 gather_fusion.4
  251.4 4.2 all-to-all-start.3
  255.5 21.8 %all-gather.1 = bf16[8,1,128]{2,1,0:T(2,128)(2,1)S(1)} all-gather(bf16[1,1,128]{2,1,0:T(2,128)(2,1)S(1)} %bitcast.398), channel_id=1, replica_groups=mesh['seq'=4,'shard'=8] {'shard'}, dimensions={0}, use_global_device_ids=true | all-gather | bytes 2304 | tf_op jit(solution)/shard_map/all_gather | solution.py:101
  278.4 3.5 multiply_reduce_fusion.4
  283.3 10.5 fusion.113
  293.8 7.0 all-gather.20.cloned.1.call-done
  300.8 10.3 fusion.114
  311.1 80.5 %all-gather.22.cloned.1.call-done = bf16[4608,1024]{1,0:T(8,128)(2,1)} async-done(((bf16[576,1024]{1,0:T(8,128)(2,1)}), bf16[4608,1024]{1,0:T(8,128)(2,1)}) %all-gather.22.cloned.1.call-update) | async-done | bytes 9437200 | tf_op jit(solution)/shard_map/all_gather | solution.py:104
  391.6 18.0 %multiply_convert_fusion = (bf16[512,4608]{1,0:T(8,128)(2,1)}, bf16[512,4608]{1,0:T(8,128)(2,1)}, bf16[512,4608]{1,0:T(8,128)(2,1)}) fusion(f32[512,4608]{1,0:T(8,128)} %fusion.113, f32[512,4608]{1,0:T(8,128)} %fusion.114, bf16[4608,1024]{1,0:T(8,128)(2,1)} %all-gather.22.cloned.1.call-done, bf16[1,512,1024]{2,1,0:T(8,128)(2,1)} %param.43), kind=kOutput, calls=%fused_computation.79 | convolution fusion | flops 4869586944 | bytes 43515904 | tf_op jit(solution)/shard_map/dot_general | solution.py:22
  409.7 9.2 fusion.115
  418.9 8.8 multiply_reduce_fusion
  431.7 3.7 all-to-all-start.4
  435.4 14.2 %all-to-all-done.4 = bf16[512,4,256]{2,0,1:T(8,128)(2,1)S(1)} async-done(((bf16[512,4,256]{2,0,1:T(8,128)(2,1)}), bf16[512,4,256]{2,0,1:T(8,128)(2,1)S(1)}, u32[]{:S(2)}, u32[]{:S(2)}) %all-to-all-start.4) | async-done | bytes 1048608 | tf_op jit(solution)/shard_map/all_to_all | solution.py:226
  449.5 7.5 gather_fusion.5
  460.6 3.8 reshape.490
  464.4 3.6 fusion.75
  470.4 95.5 %while.90 = (s32[]{:T(128)}, bf16[2048,2,2,64]{0,3,2,1:T(8,128)(2,1)}, f32[2048,2,64]{0,2,1:T(8,128)S(1)}, f32[2048,2,64]{0,2,1:T(8,128)}, s32[4]{0:T(128)S(1)},...) while((s32[]{:T(128)}, ...), condition=%wide.region_21.24_spmd.clone, body=%wide.region_18.23_spmd.clone.sunk | while | flops 682819584 | bytes 25903796 | solution.py:303
  472.3 11.0 while.93
  485.9 21.2 %while.93 = (s32[]{:T(128)}, f32[512,2,2,64]{0,3,2,1:T(8,128)S(1)}, f32[2048,2,64]{0,2,1:T(8,128)S(1)}, f32[2048,2,64]{0,2,1:T(8,128)}, s32[]{:T(128)}, /*index=...) while((s32[]{:T(128)}, f32[512,2,2,64]{0,3,2,1:T(8,128)S(1)}, ...), condition=%wide.region_20.22_spmd, body=%wide.region_19.21_spmd.sunk | while | flops 682819584 | bytes 23240952 | solution.py:290
  509.8 21.2 %while.93 = (s32[]{:T(128)}, f32[512,2,2,64]{0,3,2,1:T(8,128)S(1)}, f32[2048,2,64]{0,2,1:T(8,128)S(1)}, f32[2048,2,64]{0,2,1:T(8,128)}, s32[]{:T(128)}, /*index=...) while((s32[]{:T(128)}, f32[512,2,2,64]{0,3,2,1:T(8,128)S(1)}, ...), condition=%wide.region_20.22_spmd, body=%wide.region_19.21_spmd.sunk | while | flops 682819584 | bytes 23240952 | solution.py:290
  533.6 31.5 %while.93 = (s32[]{:T(128)}, f32[512,2,2,64]{0,3,2,1:T(8,128)S(1)}, f32[2048,2,64]{0,2,1:T(8,128)S(1)}, f32[2048,2,64]{0,2,1:T(8,128)}, s32[]{:T(128)}, /*index=...) while((s32[]{:T(128)}, f32[512,2,2,64]{0,3,2,1:T(8,128)S(1)}, ...), condition=%wide.region_20.22_spmd, body=%wide.region_19.21_spmd.sunk | while | flops 682819584 | bytes 23240952 | solution.py:290
  566.6 6.2 gather_fusion.7
  574.4 6.2 gather_fusion.8
  581.3 10.8 all_to_all.134
  597.4 9.5 all_to_all.135
  609.8 3.8 convolution_convert_fusion.3
  615.4 7.5 gather_fusion.6
  623.9 13.5 %all_to_all.136 = bf16[4,512,256]{1,2,0:T(8,128)(2,1)S(1)} all-to-all(bf16[4,512,256]{1,2,0:T(8,128)(2,1)S(1)} %copy.149), channel_id=1, replica_groups=mesh['seq'=4,'shard'=8] {'seq'}, dimensions={0} | all-to-all | bytes 2097152 | tf_op jit(solution)/shard_map/all_to_all | solution.py:314
  646.7 9.9 convolution_convert_fusion.2
  656.6 10.1 convolution_convert_fusion.1
  667.9 10.0 convolution_convert_fusion
  678.1 32.9 %reduce-scatter.14.cloned.1.call-done = bf16[128,1024]{1,0:T(8,128)(2,1)} async-done(((bf16[1024,1024]{1,0:T(8,128)(2,1)}), bf16[128,1024]{1,0:T(8,128)(2,1)}) %reduce-scatter.14.cloned.1.call-update) | async-done | bytes 262160 | tf_op jit(solution)/shard_map/reduce_scatter | solution.py:362
  710.9 37.4 %reduce-scatter.8.cloned.1.call-done = bf16[128,1024]{1,0:T(8,128)(2,1)} async-done(((bf16[1024,1024]{1,0:T(8,128)(2,1)}), bf16[128,1024]{1,0:T(8,128)(2,1)}) %reduce-scatter.8.cloned.1.call-update) | async-done | bytes 262160 | tf_op jit(solution)/shard_map/reduce_scatter | solution.py:353
  748.3 100.4 %reduce-scatter.16.cloned.1.call-done = bf16[128,4608]{1,0:T(8,128)(2,1)} async-done(((bf16[1024,4608]{1,0:T(8,128)(2,1)}), bf16[128,4608]{1,0:T(8,128)(2,1)}) %reduce-scatter.16.cloned.1.call-update) | async-done | bytes 1179664 | tf_op jit(solution)/shard_map/reduce_scatter | solution.py:368
  848.7 100.2 %reduce-scatter.18.cloned.1.call-done = bf16[128,4608]{1,0:T(8,128)(2,1)} async-done(((bf16[1024,4608]{1,0:T(8,128)(2,1)}), bf16[128,4608]{1,0:T(8,128)(2,1)}) %reduce-scatter.18.cloned.1.call-update) | async-done | bytes 1179664 | tf_op jit(solution)/shard_map/reduce_scatter | solution.py:371
  948.9 100.1 %reduce-scatter.20.cloned.1.call-done = bf16[576,1024]{1,0:T(8,128)(2,1)} async-done(((bf16[4608,1024]{1,0:T(8,128)(2,1)}), bf16[576,1024]{1,0:T(8,128)(2,1)}) %reduce-scatter.20.cloned.1.call-update) | async-done | bytes 1179664 | tf_op jit(solution)/shard_map/reduce_scatter | solution.py:374
  1050.9 9.9 fusion.76
  1066.6 13.7 %all-reduce.7 = (bf16[1024]{0:T(1024)(128)(2,1)S(1)}, bf16[1024]{0:T(1024)(128)(2,1)S(1)}) all-reduce(bf16[1024]{0:T(1024)(128)(2,1)S(1)} %get-tuple-element.612, bf16[1024]{0:T(1024)(128)(2,1)S(1)} %copy-done.66), channel_id=2, replica_groups=mesh['seq'=4,'shard'=8] {'shard'}, use_global_device_ids=true, to_apply=%region_26.29.clone | all-reduce | flops 2048 | bytes 8192
  1080.5 9.9 all-reduce.8
  1091.4 37.1 %all-reduce.6 = (f32[64]{0:T(128)}, f32[64]{0:T(128)}) all-reduce(f32[64]{0:T(128)S(1)} %get-tuple-element.610, f32[64]{0:T(128)S(1)} %get-tuple-element.614), channel_id=1, replica_groups=mesh['seq'=4,'shard'=8] {'seq','shard'}, use_global_device_ids=true, to_apply=%region_35.38 | all-reduce | flops 128 | bytes 1024 | tf_op jit(solution)/shard_map/psum | solution.py:389
  1128.6 3.1 fusion.78
  1131.7 29.8 %all-reduce.12.cloned.1.call-done = (bf16[128,1024]{1,0:T(8,128)(2,1)}, bf16[128,512]{1,0:T(8,128)(2,1)}, bf16[128,512]{1,0:T(8,128)(2,1)}, bf16[128,1024]{1,0:T...) async-done(((bf16[128,1024]{1,0:T(8,128)(2,1)}, bf16[128,512]{1,0:T(8,128)(2,1)}, bf16[128,512]{1,0:T(8,128)(2,1)}, ...) | async-done | bytes 4325392 | tf_op jit(solution)/shard_map/psum | solution.py:380
  (526 shorter events, 216.1 us)
Async XLA Ops:
  7.2 39.5 %all-gather.12.cloned.1.call-start = ((), (), s32[]{:S(2)}) async-start(), calls=%async_computation.16 | async-start | bytes 1179648 | tf_op jit(solution)/shard_map/all_gather | solution.py:98
  7.9 4.0 copy-start.69
  7.9 4.3 copy-start.49
  7.9 50.0 %all-gather.14.cloned.1.call-start = ((), (), s32[]{:S(2)}) async-start(), calls=%async_computation.17 | async-start | bytes 1179648 | tf_op jit(solution)/shard_map/all_gather | solution.py:99
  8.7 11.8 %copy-start.6 = (bf16[1,512,1024]{2,1,0:T(8,128)(2,1)S(1)}, bf16[1,512,1024]{2,1,0:T(8,128)(2,1)}, u32[]{:S(2)}) copy-start(bf16[1,512,1024]{2,1,0:T(8,128)(2,1)} %param.29) | copy-start | bytes 3145732
  8.7 79.5 %all-gather.10.cloned.1.call-start = ((), (), s32[]{:S(2)}) async-start(), calls=%async_computation.15 | async-start | bytes 2359296 | tf_op jit(solution)/shard_map/all_gather | solution.py:97
  9.4 267.9 %all-gather.16.cloned.1.call-start = ((), (), s32[]{:S(2)}) async-start(), calls=%async_computation.18 | async-start | bytes 2359296 | tf_op jit(solution)/shard_map/all_gather | solution.py:100
  10.0 10.8 copy-start.67
  10.0 24.2 %copy-start.70 = (bf16[64]{0:T(256)(128)(2,1)S(1)}, bf16[64]{0:T(256)(128)(2,1)}, u32[]{:S(2)}) copy-start(bf16[64]{0:T(256)(128)(2,1)} %param.37) | copy-start | bytes 388
  10.0 273.3 %all-gather.18.cloned.1.call-start = ((), (), s32[]{:S(2)}) async-start(), calls=%async_computation.19 | async-start | bytes 10616832 | tf_op jit(solution)/shard_map/all_gather | solution.py:102
  10.6 290.2 %all-gather.20.cloned.1.call-start = ((), (), s32[]{:S(2)}) async-start(), calls=%async_computation.20 | async-start | bytes 10616832 | tf_op jit(solution)/shard_map/all_gather | solution.py:103
  11.2 380.4 %all-gather.22.cloned.1.call-start = ((), (), s32[]{:S(2)}) async-start(), calls=%async_computation.21 | async-start | bytes 10616832 | tf_op jit(solution)/shard_map/all_gather | solution.py:104
  20.4 229.2 %copy-start.52 = (pred[2048]{0:T(1024)(128)(4,1)}, pred[2048]{0:T(1024)(128)(4,1)S(1)}, u32[]{:S(2)}) copy-start(pred[2048]{0:T(1024)(128)(4,1)S(1)} %compare_and_fusion.3) | copy-start | bytes 6148
  20.5 221.6 %copy-start.39 = (s32[2048]{0:T(1024)}, s32[2048]{0:T(1024)S(1)}, u32[]{:S(2)}) copy-start(s32[2048]{0:T(1024)S(1)} %get-tuple-element.781) | copy-start | bytes 24580
  20.8 25.3 %copy-start.58 = (f32[512]{0:T(512)}, f32[512]{0:T(512)S(1)}, u32[]{:S(2)}) copy-start(f32[512]{0:T(512)S(1)} %fusion.65) | copy-start | bytes 6148
  20.8 71.3 %copy-start.60 = (f32[512]{0:T(512)}, f32[512]{0:T(512)S(1)}, u32[]{:S(2)}) copy-start(f32[512]{0:T(512)S(1)} %fusion.103) | copy-start | bytes 6148
  34.2 57.9 %copy-start.54 = (f32[8,1,128]{2,1,0:T(1,128)}, f32[8,1,128]{2,1,0:T(1,128)S(1)}, u32[]{:S(2)}) copy-start(f32[8,1,128]{2,1,0:T(1,128)S(1)} %convert_element_type.308) | copy-start | bytes 12292
  34.2 15.8 %copy-start.64 = (f32[64]{0:T(128)}, f32[64]{0:T(128)S(1)}, u32[]{:S(2)}) copy-start(f32[64]{0:T(128)S(1)} %convert_element_type.249) | copy-start | bytes 772
  34.3 12.3 %copy-start.71 = (bf16[64]{0:T(256)(128)(2,1)S(1)}, bf16[64]{0:T(256)(128)(2,1)}, u32[]{:S(2)}) copy-start(bf16[64]{0:T(256)(128)(2,1)} %param.36) | copy-start | bytes 388
  46.5 56.5 %copy-start.16 = (f32[512,64]{0,1:T(8,128)}, f32[512,64]{0,1:T(8,128)S(1)}, u32[]{:S(2)}) copy-start(f32[512,64]{0,1:T(8,128)S(1)} %pad_maximum_fusion) | copy-start | bytes 393220
  46.5 56.5 %copy-start.18 = (f32[512,64]{0,1:T(8,128)}, f32[512,64]{0,1:T(8,128)S(1)}, u32[]{:S(2)}) copy-start(f32[512,64]{0,1:T(8,128)S(1)} %pad_maximum_fusion.1) | copy-start | bytes 393220
  46.6 93.3 %copy-start.56 = (pred[2048]{0:T(1024)(128)(4,1)}, pred[2048]{0:T(1024)(128)(4,1)S(1)}, u32[]{:S(2)}) copy-start(pred[2048]{0:T(1024)(128)(4,1)S(1)} %compare_and_fusion.4) | copy-start | bytes 6148
  46.6 56.5 %copy-start.62 = (f32[64]{0:T(128)}, f32[64]{0:T(128)S(1)}, u32[]{:S(2)}) copy-start(f32[64]{0:T(128)S(1)} %convert_element_type.245) | copy-start | bytes 772
  51.3 46.3 %all-to-all-start.1 = ((bf16[512,4,128]{0,2,1:T(8,128)(2,1)}), bf16[512,4,128]{0,2,1:T(8,128)(2,1)}, u32[]{:S(2)}, u32[]{:S(2)}) async-start(bf16[512,4,128]{0,2,1:T(8,128)(2,1)} %bitcast.44), calls=%async_computation.1 | async-start | bytes 1048576 | tf_op jit(solution)/shard_map/all_to_all | solution.py:117
  95.1 7.9 copy-start
  95.7 7.3 copy-start.35
  97.6 12.1 %all-to-all-start.2 = ((bf16[512,4,128]{0,2,1:T(8,128)(2,1)}), bf16[512,4,128]{0,2,1:T(8,128)(2,1)S(1)}, u32[]{:S(2)}, u32[]{:S(2)}) async-start(bf16[512,4,128]{0,2,1:T(8,128)(2,1)} %bitcast.379), calls=%async_computation.2 | async-start | bytes 1048576 | tf_op jit(solution)/shard_map/all_to_all | solution.py:118
  109.7 5.1 copy-start.26
  109.7 20.5 %all-to-all-start = ((bf16[512,4,256]{0,2,1:T(8,128)(2,1)}), bf16[512,4,256]{0,2,1:T(8,128)(2,1)S(1)}, u32[]{:S(2)}, u32[]{:S(2)}) async-start(bf16[512,4,256]{0,2,1:T(8,128)(2,1)} %bitcast.38), calls=%async_computation | async-start | bytes 2097152 | tf_op jit(solution)/shard_map/all_to_all | solution.py:116
  113.5 17.3 %copy-start.43 = (s32[2048]{0:T(1024)}, s32[2048]{0:T(1024)S(1)}, u32[]{:S(2)}) copy-start(s32[2048]{0:T(1024)S(1)} %fusion.98) | copy-start | bytes 24580
  231.8 2.1 copy-start.8
  250.1 5.5 copy-start.68
  251.4 26.0 %all-to-all-start.3 = ((bf16[4,512,256]{1,2,0:T(8,128)(2,1)}), bf16[4,512,256]{1,2,0:T(8,128)(2,1)S(1)}, u32[]{:S(2)}, u32[]{:S(2)}) async-start(bf16[4,512,256]{1,2,0:T(8,128)(2,1)} %copy.143), calls=%async_computation.3 | async-start | bytes 2097152 | tf_op jit(solution)/shard_map/all_to_all | solution.py:189
  281.9 145.9 %copy-start.2 = (f32[512,1024]{1,0:T(8,128)}, f32[512,1024]{1,0:T(8,128)S(1)}, u32[]{:S(2)}) copy-start(f32[512,1024]{1,0:T(8,128)S(1)} %get-tuple-element.777) | copy-start | bytes 6291460
  409.7 9.2 copy-start.73
  418.9 8.9 copy-start.30
  430.7 18.9 %copy-start.44 = (s32[2048]{0:T(1024)S(1)}, s32[2048]{0:T(1024)}, u32[]{:S(2)}) copy-start(s32[2048]{0:T(1024)} %copy-done.43) | copy-start | bytes 24580
  431.7 17.8 %all-to-all-start.4 = ((bf16[512,4,256]{2,0,1:T(8,128)(2,1)}), bf16[512,4,256]{2,0,1:T(8,128)(2,1)S(1)}, u32[]{:S(2)}, u32[]{:S(2)}) async-start(bf16[512,4,256]{2,0,1:T(8,128)(2,1)} %bitcast.282), calls=%async_computation.4 | async-start | bytes 2097152 | tf_op jit(solution)/shard_map/all_to_all | solution.py:226
  435.4 242.6 %reduce-scatter.10.cloned.1.call-start = ((), (), s32[]{:S(2)}) async-start(), calls=%async_computation.23 | async-start | bytes 1179648 | tf_op jit(solution)/shard_map/reduce_scatter | solution.py:356
  449.5 7.5 copy-start.57
  460.6 3.8 copy-start.9
  574.3 6.2 copy-start.53
  581.0 11.2 copy-start.19
  594.5 2.7 copy-start.24
  597.2 80.9 %reduce-scatter.12.cloned.1.call-start = ((), (), s32[]{:S(2)}) async-start(), calls=%async_computation.24 | async-start | bytes 1179648 | tf_op jit(solution)/shard_map/reduce_scatter | solution.py:359
  607.8 2.0 copy-start.11
  609.8 101.2 %reduce-scatter.14.cloned.1.call-start = ((), (), s32[]{:S(2)}) async-start(), calls=%async_computation.25 | async-start | bytes 2359296 | tf_op jit(solution)/shard_map/reduce_scatter | solution.py:362
  613.7 134.7 %reduce-scatter.8.cloned.1.call-start = ((), (), s32[]{:S(2)}) async-start(), calls=%async_computation.22 | async-start | bytes 2359296 | tf_op jit(solution)/shard_map/reduce_scatter | solution.py:353
  645.5 203.3 %reduce-scatter.16.cloned.1.call-start = ((), (), s32[]{:S(2)}) async-start(), calls=%async_computation.26 | async-start | bytes 10616832 | tf_op jit(solution)/shard_map/reduce_scatter | solution.py:368
  656.6 292.4 %reduce-scatter.18.cloned.1.call-start = ((), (), s32[]{:S(2)}) async-start(), calls=%async_computation.27 | async-start | bytes 10616832 | tf_op jit(solution)/shard_map/reduce_scatter | solution.py:371
  666.7 382.3 %reduce-scatter.20.cloned.1.call-start = ((), (), s32[]{:S(2)}) async-start(), calls=%async_computation.28 | async-start | bytes 10616832 | tf_op jit(solution)/shard_map/reduce_scatter | solution.py:374
  678.0 483.5 %all-reduce.12.cloned.1.call-start = ((), (), s32[]{:S(2)}) async-start(), calls=%async_computation.29 | async-start | bytes 8650752 | tf_op jit(solution)/shard_map/psum | solution.py:380
  1049.0 1.9 copy-start.3
  1050.9 9.9 copy-start.13
  1050.9 9.9 copy-start.25
  1060.8 1.9 copy-start.33
  1064.1 2.5 copy-start.66
  1064.1 64.5 %copy-start.59 = (f32[512]{0:T(512)S(1)}, f32[512]{0:T(512)}, u32[]{:S(2)}) copy-start(f32[512]{0:T(512)} %copy-done.58) | copy-start | bytes 6148
  1064.1 64.5 %copy-start.12 = (f32[512,1024]{1,0:T(8,128)S(1)}, f32[512,1024]{1,0:T(8,128)}, u32[]{:S(2)}) copy-start(f32[512,1024]{1,0:T(8,128)} %copy-done.10) | copy-start | bytes 6291460
  1161.5 3.0 copy-start.28
  1166.1 1.7 copy-start.42
  1166.1 2.6 copy-start.41
  1166.1 3.4 copy-start.46
  1166.1 4.1 copy-start.45
  (30 other events, 35.3 us)
Sparse Core Ops, SparseCore 0:
  9.6 24.7 all-gather.11
  36.0 21.8 all-gather.13
  59.5 28.6 all-gather.9
  89.6 28.5 all-gather.15
  119.7 90.2 all-gather.17
  211.5 89.2 all-gather.19
  302.4 89.1 all-gather.21
  597.3 44.4 reduce-scatter.9
  644.1 30.5 reduce-scatter.11
  676.8 34.0 reduce-scatter.13
  713.8 34.4 reduce-scatter.7
  750.5 98.2 reduce-scatter.15
  851.0 97.8 reduce-scatter.17
  951.1 97.8 reduce-scatter.19
  1053.4 107.9 all-reduce.11
where the time goes:
time: 1190 us; the launch traced here: 1180 us
  waiting for transfers between devices  542 us (46%)
  matrix products  210 us (18%)
  local copies, waits for them, and re-layouts  146 us (12%)
  blocking collectives  130 us (11%)
  loops' own time  61.4 us (5%)
  other arithmetic  53 us (4%)
  starting transfers between devices  19.9 us (2%)
  between operations  16.3 us (1%)
    reduce_scatter x1, waiting for transfers between devices, body(): lax.psum_scatter(d_w_gate.astype(jnp.bfloat16), 'shard', scatter_dimensio...  100 us
    reduce_scatter x1, waiting for transfers between devices, body(): lax.psum_scatter(d_w_up.astype(jnp.bfloat16), 'shard', scatter_dimension=...  100 us
    reduce_scatter x1, waiting for transfers between devices, body(): lax.psum_scatter(d_w_down.astype(jnp.bfloat16), 'shard', scatter_dimensio...  100 us
    all_gather x1, waiting for transfers between devices, body(): lax.all_gather(w_down, 'shard', axis=0, tiled=True)  80.5 us
    dot_general x7, matrix products, transposed_product(): lax.dot_general(left_arg, right_arg, (((1,), (1,)), ((), ())), preferred_...  41.9 us
    dot_general x7, matrix products, product(): return jnp.dot(left_arg, right_arg, preferred_element_type=jnp.float32)  40.9 us
    dot_general x7, matrix products, rows_product(): lax.dot_general(left_arg, right_arg, (((0,), (0,)), ((), ())), preferred_...  40.4 us
    reduce_scatter x1, waiting for transfers between devices, body(): lax.psum_scatter(d_w_query.astype(jnp.bfloat16), 'shard', scatter_dimensi...  37.4 us
  transfers between devices with their start and end apart: 20, of which 12 were waited for; matrix products, arithmetic and copies ran while one was open for 20% of the time, Pallas kernels for 0%

commit v1 on v0

v1 whole, which is shorter than its diff:
```python
import functools

import jax
import jax.numpy as jnp
from jax import lax
from jax.experimental import pallas as pl
from jax.experimental.pallas import tpu as pltpu
from jax.sharding import PartitionSpec as P

EPSILON = 1e-05
ROPE_BASE = 1000000.0
LOG2E = 1.4426950408889634
ROWS = 256
LANES = 128
F32 = jnp.float32
BF16 = jnp.bfloat16
VMEM_LIMIT = 58 * 1024 * 1024


def dot_nn(left, right):
    return jnp.dot(left, right, preferred_element_type=F32)


def dot_nt(left, right):
    return lax.dot_general(left, right, (((1,), (1,)), ((), ())), preferred_element_type=F32)


def dot_tn(left, right):
    return lax.dot_general(left, right, (((0,), (0,)), ((), ())), preferred_element_type=F32)


def vmem():
    return pl.BlockSpec(memory_space=pltpu.VMEM)


def smem():
    return pl.BlockSpec(memory_space=pltpu.SMEM)


def params():
    return pltpu.CompilerParams(vmem_limit_bytes=VMEM_LIMIT)


def lane_iota(rows, columns):
    return lax.broadcasted_iota(jnp.int32, (rows, columns), 1)


def row_iota(rows, columns):
    return lax.broadcasted_iota(jnp.int32, (rows, columns), 0)


def at_rows(block, rows=ROWS):
    return pl.ds(pl.multiple_of(block * rows, rows), rows)


def pair_ones(head_dim):
    return (
        row_iota(LANES, LANES) // head_dim == lane_iota(LANES, LANES) // head_dim
    ).astype(BF16)


def head_mean(values, ones, head_dim):
    high = values.astype(BF16)
    low = (values - high.astype(F32)).astype(BF16)
    return (dot_nn(high, ones) + dot_nn(low, ones)) * (1.0 / head_dim)


def turn(values, cosine, sine_up, sine_down, head_dim, sign=1.0):
    half = head_dim // 2
    up = pltpu.roll(values, LANES - half, 1) * sine_up
    down = pltpu.roll(values, half, 1) * sine_down
    return values * cosine + sign * (up + down)


def spread_heads(pair, group, head_dim, low_lanes):
    moved = pltpu.roll(pair, head_dim, 1)
    if group == 0:
        return jnp.where(low_lanes, pair, 0.0), jnp.where(low_lanes, moved, 0.0)
    return jnp.where(low_lanes, 0.0, moved), jnp.where(low_lanes, 0.0, pair)


def qkv_kernel(
    head_dim, x_ref, w_ref, gain_ref, ocol_ref, cos_ref, su_ref, sd_ref, qg_ref, kg_ref,
    normed_ref, qx_ref, k_ref, v_ref, kt_ref, vt_ref, rawq_ref, rawk_ref, raw_ref,
):
    all_rows = x_ref.shape[0]
    width = raw_ref.shape[1]
    blocks = all_rows // ROWS
    pairs = rawq_ref.shape[1] // LANES

    def project(i, carry):
        rows = at_rows(i)
        x = x_ref[rows, :].astype(F32)
        r1 = lax.rsqrt(jnp.mean(x * x, axis=1, keepdims=True) + EPSILON)
        normed = (x * r1 * gain_ref[...]).astype(BF16)
        normed_ref[rows, :] = normed
        raw_ref[rows, :] = dot_nn(normed, w_ref[:, :width]).astype(BF16)
        return carry

    lax.fori_loop(0, blocks, project, 0)
    ones = pair_ones(head_dim)
    low_lanes = lane_iota(ROWS, LANES) < head_dim

    def deal(i, carry):
        rows = at_rows(i)
        pick = (ocol_ref[rows, :] == lane_iota(ROWS, all_rows)).astype(F32).astype(BF16)
        dealt = dot_nn(pick, raw_ref[...])
        cosine, su, sd = cos_ref[rows, :], su_ref[rows, :], sd_ref[rows, :]
        for g in range(pairs):
            raw = dealt[:, g * LANES:(g + 1) * LANES]
            rawq_ref[rows, g * LANES:(g + 1) * LANES] = raw.astype(BF16)
            rq = lax.rsqrt(head_mean(raw * raw, ones, head_dim) + EPSILON)
            pair = turn(raw * rq * qg_ref[...], cosine, su, sd, head_dim)
            for r, one in enumerate(spread_heads(pair, g, head_dim, low_lanes)):
                qx_ref[2 * g + r, rows, :] = one.astype(BF16)
        raw = dealt[:, pairs * LANES:(pairs + 1) * LANES]
        rawk_ref[rows, :] = raw.astype(BF16)
        rk = lax.rsqrt(head_mean(raw * raw, ones, head_dim) + EPSILON)
        keys = turn(raw * rk * kg_ref[...], cosine, su, sd, head_dim)
        k_ref[rows, :] = keys.astype(BF16)
        kt_ref[:, rows] = jnp.transpose(keys).astype(BF16)
        values = dealt[:, (pairs + 1) * LANES:]
        v_ref[rows, :] = values.astype(BF16)
        vt_ref[:, rows] = jnp.transpose(values).astype(BF16)
        return carry

    lax.fori_loop(0, blocks, deal, 0)


def qkv(x, w, gain, ocol, cosine, su, sd, qg, kg, head_dim):
    all_rows, width = x.shape
    out = lambda *dims: jax.ShapeDtypeStruct(dims, BF16)
    return pl.pallas_call(
        functools.partial(qkv_kernel, head_dim),
        out_shape=(
            out(all_rows, width), out(4, all_rows, LANES), out(all_rows, LANES), out(all_rows, LANES),
            out(LANES, all_rows), out(LANES, all_rows), out(all_rows, 2 * LANES), out(all_rows, LANES),
        ),
        in_specs=[vmem()] * 9,
        out_specs=(vmem(),) * 8,
        scratch_shapes=[pltpu.VMEM((all_rows, 4 * LANES), BF16)],
        compiler_params=params(),
        cost_estimate=pl.CostEstimate(flops=2 * all_rows * (width + all_rows) * 512, bytes_accessed=16 << 20, transcendentals=0),
        name="qkv",
    )(x, w, gain, ocol, cosine, su, sd, qg, kg)


def row_starts(lens_ref, index):
    start = jnp.zeros_like(index)
    end = lens_ref[0, 0]
    for s in range(1, lens_ref.shape[1]):
        start = jnp.where(index >= end, end, start)
        end = end + lens_ref[0, s]
    return start


def attend_kernel(head_dim, group, lens_ref, orow_ref, qx_ref, k_ref, vt_ref, given_ref, dealt_ref, lse_ref):
    all_rows = k_ref.shape[0]
    blocks = all_rows // ROWS
    scale = LOG2E * head_dim ** -0.5

    def query_block(i, carry):
        rows = at_rows(i)
        q_index = i * ROWS + lane_iota(1, ROWS)
        start = row_starts(lens_ref, q_index)
        first = row_starts(lens_ref, i * ROWS) // ROWS
        queries = [qx_ref[r, rows, :] for r in range(2)]

        def step(j, state):
            columns = at_rows(j)
            k_index = j * ROWS + row_iota(ROWS, ROWS)
            keep = (k_index <= q_index) & (k_index >= start)
            keys = k_ref[columns, :]
            values = vt_ref[group * head_dim:(group + 1) * head_dim, columns]
            new = []
            for r in range(2):
                total, mass = state[2 * r], state[2 * r + 1]
                weights = jnp.where(keep, jnp.exp2(dot_nt(keys, queries[r]) * scale), 0.0)
                mass = mass + jnp.sum(weights, axis=0, keepdims=True)
                total = total + dot_nn(values, weights.astype(BF16))
                new += [total, mass]
            return tuple(new)

        zero = (jnp.zeros((head_dim, ROWS), F32), jnp.zeros((1, ROWS), F32)) * 2
        state = lax.fori_loop(first, i + 1, step, zero)
        pair = jnp.concatenate([state[0] / state[1], state[2] / state[3]], axis=0)
        dealt_ref[rows, :] = jnp.transpose(pair).astype(BF16)
        for r in range(2):
            lse_ref[r:r + 1, rows] = jnp.log2(state[2 * r + 1])
        return carry

    lax.fori_loop(0, blocks, query_block, 0)

    def undeal(i, carry):
        rows = at_rows(i)
        pick = (orow_ref[...] == i * ROWS + row_iota(ROWS, all_rows)).astype(F32).astype(BF16)
        given_ref[rows, :] = dot_nn(pick, dealt_ref[...]).astype(BF16)
        return carry

    lax.fori_loop(0, blocks, undeal, 0)


def attend(group, lens, orow, qx, k, vt, head_dim):
    all_rows = k.shape[0]
    whole = lambda *dims: pl.BlockSpec(dims, lambda i: (0,) * len(dims))
    return pl.pallas_call(
        functools.partial(attend_kernel, head_dim, group),
        grid=(1,),
        out_shape=(
            jax.ShapeDtypeStruct((all_rows, LANES), BF16),
            jax.ShapeDtypeStruct((all_rows, LANES), BF16),
            jax.ShapeDtypeStruct((2, all_rows), F32),
        ),
        in_specs=[
            smem(), whole(1, all_rows),
            pl.BlockSpec((2, all_rows, LANES), lambda i: (group, 0, 0)),
            whole(all_rows, LANES), whole(LANES, all_rows),
        ],
        out_specs=(whole(all_rows, LANES), whole(all_rows, LANES), whole(2, all_rows)),
        compiler_params=params(),
        cost_estimate=pl.CostEstimate(flops=12 << 30, bytes_accessed=4 << 20, transcendentals=5 << 20),
        name="attend",
    )(lens, orow, qx, k, vt)


def attend_back_kernel(
    head_dim, lens_ref, ocol_ref, orow_ref, qx_ref, k_ref, v_ref, kt_ref, lse0_ref, lse1_ref, o0_ref, o1_ref,
    d0_ref, d1_ref, d2_ref, d3_ref, rawq_ref, rawk_ref, cos_ref, su_ref, sd_ref, qg_ref, kg_ref, w_ref,
    grad_ref, gain_ref, n0_ref, n1_ref, n2_ref, n3_ref,
    dgiven_ref, dx_ref, delta_ref, dk_ref, dv_ref, draw_ref,
):
    all_rows = k_ref.shape[0]
    blocks = all_rows // ROWS
    exponent = LOG2E * head_dim ** -0.5
    scale = head_dim ** -0.5
    low_lanes = lane_iota(ROWS, LANES) < head_dim
    tok = d0_ref.shape[0]
    for d, ref in enumerate((d0_ref, d1_ref, d2_ref, d3_ref)):
        dgiven_ref[d * tok:(d + 1) * tok, :] = ref[...]
    dk_ref[...] = jnp.zeros_like(dk_ref)
    dv_ref[...] = jnp.zeros_like(dv_ref)
    gain_ref[...] = jnp.zeros_like(gain_ref)

    def deal(i, carry):
        rows = at_rows(i)
        pick = (ocol_ref[rows, :] == lane_iota(ROWS, all_rows)).astype(F32).astype(BF16)
        dealt = dot_nn(pick, dgiven_ref[...])
        for g, o_ref in enumerate((o0_ref, o1_ref)):
            pair = dealt[:, g * LANES:(g + 1) * LANES]
            for r, one in enumerate(spread_heads(pair, g, head_dim, low_lanes)):
                dx_ref[2 * g + r, rows, :] = one.astype(BF16)
            across = jnp.transpose(pair * o_ref[rows, :].astype(F32))
            for r in range(2):
                delta_ref[2 * g + r:2 * g + r + 1, rows] = jnp.sum(
                    across[r * head_dim:(r + 1) * head_dim], axis=0, keepdims=True
                )
        return carry

    lax.fori_loop(0, blocks, deal, 0)
    ones = pair_ones(head_dim)

    def query_block(i, carry):
        rows = at_rows(i)
        q_index = i * ROWS + lane_iota(1, ROWS)
        start = row_starts(lens_ref, q_index)
        first = row_starts(lens_ref, i * ROWS) // ROWS

        def step(j, state):
            columns = at_rows(j)
            k_index = j * ROWS + row_iota(ROWS, ROWS)
            keep = (k_index <= q_index) & (k_index >= start)
            keys = k_ref[columns, :]
            values = v_ref[columns, :]
            new = []
            dk, dv = dk_ref[columns, :], dv_ref[columns, :]
            for h in range(4):
                g = h // 2
                queries = qx_ref[h, rows, :]
                grads = dx_ref[h, rows, :]
                lse = (lse0_ref, lse1_ref)[g][h % 2:h % 2 + 1, rows]
                weights = jnp.where(keep, jnp.exp2(dot_nt(keys, queries) * exponent - lse), 0.0)
                d_weights = dot_nt(values, grads)
                d_scores = (weights * (d_weights - delta_ref[h:h + 1, rows])).astype(BF16)
                dv = dv + dot_nn(weights.astype(BF16), grads)
                dk = dk + dot_nn(d_scores, queries)
                new.append(state[h] + dot_nn(kt_ref[g * head_dim:(g + 1) * head_dim, columns], d_scores))
            dk_ref[columns, :] = dk
            dv_ref[columns, :] = dv
            return tuple(new)

        state = lax.fori_loop(first, i + 1, step, (jnp.zeros((head_dim, ROWS), F32),) * 4)
        cosine, su, sd = cos_ref[rows, :], su_ref[rows, :], sd_ref[rows, :]
        for g in range(2):
            pair = jnp.transpose(jnp.concatenate(state[2 * g:2 * g + 2], axis=0)) * scale
            lanes = slice(g * LANES, (g + 1) * LANES)
            draw, gain = norm_back(
                pair, rawq_ref[rows, lanes].astype(F32), qg_ref[...], cosine, su, sd, ones, head_dim
            )
            draw_ref[rows, lanes] = draw
            gain_ref[0:1, :] += gain
        return carry

    lax.fori_loop(0, blocks, query_block, 0)

    def key_block(i, carry):
        rows = at_rows(i)
        cosine, su, sd = cos_ref[rows, :], su_ref[rows, :], sd_ref[rows, :]
        draw, gain = norm_back(
            dk_ref[rows, :] * scale, rawk_ref[rows, :].astype(F32), kg_ref[...], cosine, su, sd, ones, head_dim
        )
        draw_ref[rows, 2 * LANES:3 * LANES] = draw
        draw_ref[rows, 3 * LANES:] = dv_ref[rows, :].astype(BF16)
        gain_ref[1:2, :] += gain
        return carry

    lax.fori_loop(0, blocks, key_block, 0)
    width = draw_ref.shape[1]
    for d, ref in enumerate((n0_ref, n1_ref, n2_ref, n3_ref)):

        def undeal(i, carry, d=d, ref=ref):
            rows = at_rows(d * (tok // ROWS) + i)
            pick = (
                (orow_ref[...] == d * tok + i * ROWS + row_iota(ROWS, all_rows)).astype(F32).astype(BF16)
            )
            grads = dot_nn(pick, draw_ref[...]).astype(BF16)
            grad_ref[rows, :] = grads
            ref[at_rows(i), :] = dot_nt(grads, w_ref[:, :width]).astype(BF16)
            return carry

        lax.fori_loop(0, tok // ROWS, undeal, 0)


def norm_back(pair, raw, gain, cosine, su, sd, ones, head_dim):
    pair = pair.astype(BF16).astype(F32)
    u = turn(pair, cosine, su, sd, head_dim, -1.0)
    r = lax.rsqrt(head_mean(raw * raw, ones, head_dim) + EPSILON)
    unit = raw * r
    scaled = u * gain
    draw = r * (scaled - unit * head_mean(scaled * unit, ones, head_dim))
    return draw.astype(BF16), jnp.sum(u * unit, axis=0, keepdims=True)


def attend_back(lens, ocol, orow, qx, k, v, kt, lses, dealts, grads, rawq, rawk, cosine, su, sd, qg, kg, w, head_dim):
    all_rows = k.shape[0]
    tok = grads[0].shape[0]
    width = w.shape[0]
    return pl.pallas_call(
        functools.partial(attend_back_kernel, head_dim),
        out_shape=(
            jax.ShapeDtypeStruct((all_rows, 4 * LANES), BF16),
            jax.ShapeDtypeStruct((2, LANES), F32),
        ) + (jax.ShapeDtypeStruct((tok, width), BF16),) * 4,
        in_specs=[smem()] + [vmem()] * 22,
        out_specs=(vmem(),) * 6,
        scratch_shapes=[
            pltpu.VMEM((all_rows, 2 * LANES), BF16),
            pltpu.VMEM((4, all_rows, LANES), BF16),
            pltpu.VMEM((4, all_rows), F32),
            pltpu.VMEM((all_rows, LANES), F32),
            pltpu.VMEM((all_rows, LANES), F32),
            pltpu.VMEM((all_rows, 4 * LANES), BF16),
        ],
        compiler_params=params(),
        cost_estimate=pl.CostEstimate(flops=40 << 30, bytes_accessed=12 << 20, transcendentals=10 << 20),
        name="attend_back",
    )(lens, ocol, orow, qx, k, v, kt, *lses, *dealts, *grads, rawq, rawk, cosine, su, sd, qg, kg, w)


def ffn_kernel(
    per, me_ref, *refs
):
    att = refs[:8]
    x_ref, cot_ref, wo_ref, gain_ref, wgu_ref, wd_ref = refs[8:14]
    nf_ref, hid_ref, dg_ref, du_ref, mid_ref = refs[14:19]
    dn_refs, bo_refs = refs[19:23], refs[23:27]
    i = pl.program_id(0)
    me = me_ref[0]
    hidden_units = hid_ref.shape[1]
    middle = x_ref[...].astype(F32)
    for d in range(4):
        block = jnp.concatenate([att[2 * d][...], att[2 * d + 1][...]], axis=1)
        middle = middle + dot_nn(block, wo_ref[at_rows(jnp.bitwise_xor(me, d), 2 * LANES), :])
    r2 = lax.rsqrt(jnp.mean(middle * middle, axis=1, keepdims=True) + EPSILON)
    nf = (middle * r2 * gain_ref[...]).astype(BF16)
    nf_ref[...] = nf
    wg, wu = wgu_ref[:, :hidden_units], wgu_ref[:, hidden_units:]
    gate = dot_nn(nf, wg)
    up = dot_nn(nf, wu)
    s = jax.nn.sigmoid(gate)
    silu = gate * s
    hidden = (silu * up).astype(BF16)
    hid_ref[...] = hidden
    d_hidden = dot_nt(cot_ref[...], wd_ref[...])
    d_gate = (d_hidden * up * s * (1.0 + gate * (1.0 - s))).astype(BF16)
    d_up = (d_hidden * silu).astype(BF16)
    dg_ref[...] = d_gate
    du_ref[...] = d_up
    dn = (dot_nt(d_gate, wg) + dot_nt(d_up, wu)).astype(BF16)
    bo = dot_nn(hidden, wd_ref[...]).astype(BF16)
    for d in range(4):

        @pl.when(i // per == d)
        def _(d=d):
            dn_refs[d][...] = dn
            bo_refs[d][...] = bo

    @pl.when(i < per)
    def _():
        mid_ref[...] = middle


def ffn(me, att, x, cot, wo, gain, wgu, wd, tok):
    all_rows, width = x.shape
    units = wd.shape[0]
    per = tok // ROWS
    steps = all_rows // ROWS
    fixed = lambda a: pl.BlockSpec(a.shape, lambda i: (0, 0), pipeline_mode=pl.Buffered(1))
    rows = lambda c: pl.BlockSpec((ROWS, c), lambda i: (i, 0))
    crossed = lambda d: pl.BlockSpec(
        (ROWS, LANES), lambda i: (jnp.bitwise_xor(i // per, d) * per + i % per, 0)
    )
    held = lambda d: pl.BlockSpec((ROWS, width), lambda i: (jnp.clip(i - d * per, 0, per - 1), 0))
    out = lambda r, c, t=BF16: jax.ShapeDtypeStruct((r, c), t)
    return pl.pallas_call(
        functools.partial(ffn_kernel, per),
        grid=(steps,),
        out_shape=(
            out(all_rows, width), out(all_rows, units), out(all_rows, units), out(all_rows, units),
            out(tok, width, F32),
        ) + (out(tok, width),) * 8,
        in_specs=[smem()] + [crossed(d) for d in range(4) for _ in range(2)]
        + [rows(width), rows(width), fixed(wo), fixed(gain), fixed(wgu), fixed(wd)],
        out_specs=(rows(width), rows(units), rows(units), rows(units), held(0))
        + tuple(held(d) for d in range(4)) * 2,
        compiler_params=params(),
        cost_estimate=pl.CostEstimate(flops=2 * all_rows * width * (width + 6 * units), bytes_accessed=50 << 20, transcendentals=0),
        name="ffn",
    )(me, *att, x, cot, wo, gain, wgu, wd)


def middle_kernel(me_ref, n0_ref, n1_ref, n2_ref, n3_ref, cot_ref, mid_ref, gain_ref, wo_ref,
                  dmid_ref, branch_ref, a0_ref, a1_ref, a2_ref, a3_ref):
    me = me_ref[0]
    middle = mid_ref[...]
    d_normed = (
        n0_ref[...].astype(F32) + n1_ref[...].astype(F32) + n2_ref[...].astype(F32) + n3_ref[...].astype(F32)
    )
    r2 = lax.rsqrt(jnp.mean(middle * middle, axis=1, keepdims=True) + EPSILON)
    scaled = d_normed * gain_ref[...]
    pull = jnp.mean(scaled * middle, axis=1, keepdims=True)
    d_middle = cot_ref[...].astype(F32) + r2 * scaled - middle * (r2 * r2 * r2 * pull)
    dmid_ref[...] = d_middle
    branch = d_middle.astype(BF16)
    branch_ref[...] = branch
    for d, ref in enumerate((a0_ref, a1_ref, a2_ref, a3_ref)):
        ref[...] = dot_nt(branch, wo_ref[at_rows(jnp.bitwise_xor(me, d), 2 * LANES), :]).astype(BF16)


def middle_back(me, parts, cot, middle, gain, wo):
    tok, width = middle.shape
    fixed = lambda a: pl.BlockSpec(a.shape, lambda i: (0, 0), pipeline_mode=pl.Buffered(1))
    rows = lambda c: pl.BlockSpec((ROWS, c), lambda i: (i, 0))
    out = lambda c, t: jax.ShapeDtypeStruct((tok, c), t)
    return pl.pallas_call(
        middle_kernel,
        grid=(tok // ROWS,),
        out_shape=(out(width, F32), out(width, BF16)) + (out(2 * LANES, BF16),) * 4,
        in_specs=[smem()] + [rows(width)] * 6 + [fixed(gain), fixed(wo)],
        out_specs=(rows(width), rows(width)) + (rows(2 * LANES),) * 4,
        compiler_params=params(),
        cost_estimate=pl.CostEstimate(flops=2 * tok * width * width, bytes_accessed=12 << 20, transcendentals=0),
        name="middle_back",
    )(me, *parts, cot, middle, gain, wo)


def swap(array, distance):
    return lax.ppermute(array, "seq", [(s, s ^ distance) for s in range(4)])


def gather_rows(block):
    half = block.shape[0] // 2
    one, two = swap(block, 1), swap(block, 2)
    return [block, one, two, swap(one[:half], 2), swap(two[half:], 1)]


def body(
    tokens, order, seq_lengths, attn_gain, w_query, w_key, w_value, query_gain, key_gain,
    w_out, ffn_gain, w_gate, w_up, w_down, cotangent,
):
    tok = tokens.shape[1]
    ways = lax.axis_size("seq")
    shards = lax.axis_size("shard")
    all_rows = tok * ways
    head_dim = query_gain.shape[0]
    me = lax.axis_index("seq")
    me_arr = me.astype(jnp.int32)[None]
    own = lambda a, axis: lax.dynamic_slice_in_dim(a, me * (a.shape[axis] // ways), a.shape[axis] // ways, axis)
    depth = w_gate.shape[0]
    units = w_gate.shape[1] // ways
    piece = units // shards

    gains = jnp.stack([attn_gain, ffn_gain], axis=1)
    w_first = jnp.concatenate(
        [own(w_query, 1), own(w_key, 1), own(w_value, 1), gains, jnp.zeros((depth, LANES - 2), BF16)], axis=1
    )
    w_qkv = lax.all_gather(w_first, "shard", axis=0, tiled=True)
    w_o = lax.all_gather(w_out, "shard", axis=0, tiled=True)
    cut = lambda w: own(w.reshape(depth, shards, ways, piece), 2).reshape(depth, units)
    w_gu = lax.all_gather(jnp.concatenate([cut(w_gate), cut(w_up)], axis=1), "shard", axis=0, tiled=True)
    w_d = lax.all_gather(own(w_down, 0), "shard", axis=0, tiled=True)
    first_cols = 4 * LANES
    gain_rows = jnp.transpose(w_qkv[:, first_cols:first_cols + 2]).astype(F32)
    gain_a, gain_f = gain_rows[0:1], gain_rows[1:2]

    dealt_index = jnp.arange(all_rows, dtype=jnp.int32)
    ends = jnp.cumsum(seq_lengths[0])
    start = jnp.zeros_like(dealt_index)
    for s in range(seq_lengths.shape[1] - 1):
        start = jnp.where(dealt_index >= ends[s], ends[s], start)
    places = (dealt_index - start).astype(F32)
    lane = jnp.arange(LANES, dtype=jnp.int32) % head_dim
    half = head_dim // 2
    frequency = ROPE_BASE ** (-2.0 * jnp.arange(half, dtype=F32) / head_dim)
    angles = places[:, None] * frequency[None, :]
    cosine = jnp.tile(jnp.cos(angles), (1, LANES // half))
    sine = jnp.tile(jnp.sin(angles), (1, LANES // half))
    sine_up = jnp.where(lane[None, :] < half, -sine, 0.0)
    sine_down = jnp.where(lane[None, :] < half, 0.0, sine)
    relative = jnp.bitwise_xor(order[0], me.astype(jnp.int32) * tok)
    ocol, orow = relative[:, None], relative[None, :]
    q_gain = jnp.tile(query_gain.astype(F32), LANES // head_dim)[None, :]
    k_gain = jnp.tile(key_gain.astype(F32), LANES // head_dim)[None, :]

    x_all = jnp.concatenate(gather_rows(tokens[0]), axis=0)
    normed, qx, k, v, kt, vt, rawq, rawk = qkv(
        x_all, w_qkv, gain_a, ocol, cosine, sine_up, sine_down, q_gain, k_gain, head_dim
    )
    cot = cotangent[0]
    cot_all = jnp.concatenate(gather_rows(cot), axis=0)

    att, dealts, lses = [], [], []
    for g in range(2):
        given, dealt, lse = attend(g, seq_lengths, orow, qx, k, vt, head_dim)
        att.append([given] + [swap(given, d) for d in (1, 2, 3)])
        dealts.append(dealt)
        lses.append(lse)
    att = [att[g][d] for d in range(4) for g in range(2)]

    nf, hidden, d_gate, d_up, middle, *blocks = ffn(
        me_arr, att, x_all, cot_all, w_o, gain_f, w_gu, w_d, tok
    )
    dn, bo = blocks[:4], blocks[4:]
    dn = [dn[0]] + [swap(dn[d], d) for d in (1, 2, 3)]
    rows_product = lambda a, b: dot_tn(a, b).astype(BF16)
    d_wd = lax.psum_scatter(rows_product(hidden, cot_all), "shard", scatter_dimension=0, tiled=True)
    d_wgu = lax.psum_scatter(
        jnp.concatenate([rows_product(nf, d_gate), rows_product(nf, d_up)], axis=1),
        "shard", scatter_dimension=0, tiled=True,
    )

    d_middle, branch, *d_att = middle_back(me_arr, dn, cot, middle, gain_f, w_o)
    d_att = [d_att[0]] + [swap(d_att[d], d) for d in (1, 2, 3)]
    bo = [bo[0]] + [swap(bo[d], d) for d in (1, 2, 3)]
    block_out = (middle + sum(b.astype(F32) for b in bo)).astype(BF16)
    att_own = jnp.concatenate(
        [att[2 * d + g][d * tok:(d + 1) * tok] for d in range(4) for g in range(2)], axis=1
    )
    d_wo = rows_product(att_own, branch).reshape(ways, 2 * LANES, -1)
    d_wo = jnp.take(d_wo, jnp.bitwise_xor(jnp.arange(ways), me), axis=0).reshape(ways * 2 * LANES, -1)
    d_wo = lax.psum_scatter(d_wo, "shard", scatter_dimension=0, tiled=True)

    grads, head_gains, *dm = attend_back(
        seq_lengths, ocol, orow, qx, k, v, kt, lses, dealts, d_att, rawq, rawk,
        cosine, sine_up, sine_down, q_gain, k_gain, w_qkv, head_dim,
    )
    dm = [dm[0]] + [swap(dm[d], d) for d in (1, 2, 3)]
    d_wqkv = lax.psum_scatter(rows_product(normed, grads), "shard", scatter_dimension=0, tiled=True)
    x = tokens[0].astype(F32)
    d_normed = sum(b.astype(F32) for b in dm)
    r1 = lax.rsqrt(jnp.mean(x * x, axis=1, keepdims=True) + EPSILON)
    scaled = d_normed * gain_a
    d_tokens = (
        d_middle + r1 * scaled - x * (r1 * r1 * r1 * jnp.mean(scaled * x, axis=1, keepdims=True))
    ).astype(BF16)

    def whole(part):
        return lax.all_gather(part, "seq", axis=0)

    d_wqkv = whole(d_wqkv)
    side = lambda a: jnp.moveaxis(a, 0, 1).reshape(depth, -1).astype(F32)
    d_wq, d_wk, d_wv = side(d_wqkv[:, :, :256]), side(d_wqkv[:, :, 256:384]), side(d_wqkv[:, :, 384:512])
    d_wgu = whole(d_wgu).reshape(ways, depth, 2, shards, piece)
    d_wgu = jnp.transpose(d_wgu, (2, 1, 3, 0, 4)).reshape(2, depth, -1).astype(F32)
    d_wd = whole(d_wd).reshape(-1, d_wd.shape[1]).astype(F32)
    d_wo_total = lax.psum(d_wo, "seq").astype(F32)
    dot_rows = lambda w, d: jnp.sum(w.astype(F32) * d, axis=1)
    d_attn_gain = (dot_rows(w_query, d_wq) + dot_rows(w_key, d_wk) + dot_rows(w_value, d_wv)) / attn_gain.astype(F32)
    d_ffn_gain = (dot_rows(w_gate, d_wgu[0]) + dot_rows(w_up, d_wgu[1])) / ffn_gain.astype(F32)
    head_gains = lax.psum(head_gains, ("seq", "shard"))
    head_gains = head_gains[:, :head_dim] + head_gains[:, head_dim:]
    return (
        block_out[None], d_tokens[None], d_attn_gain, d_wq, d_wk, d_wv, head_gains[0], head_gains[1],
        d_wo_total, d_ffn_gain, d_wgu[0], d_wgu[1], d_wd,
    )


def solution(mesh):
    rows, flat, wide = P("shard", None), P("shard"), P("shard", "seq", None)
    in_specs = (
        wide, rows, rows, flat, rows, rows, rows, P(), P(), rows, flat, rows, rows, rows, wide,
    )
    out_specs = (wide, wide, flat, rows, rows, rows, P(), P(), rows, flat, rows, rows, rows)
    return jax.shard_map(body, mesh=mesh, in_specs=in_specs, out_specs=out_specs, check_vma=False)
```

time: 1190 us -> 654 us (0.55)
  waiting for transfers between devices: 542 us -> 200 us
  Pallas kernels: 0 us -> 184 us
  matrix products: 210 us -> 33.1 us
  local copies, waits for them, and re-layouts: 146 us -> 68.4 us
  loops' own time: 61.4 us -> 0 us
  blocking collectives: 130 us -> 83.2 us
  other arithmetic: 53 us -> 31 us
  starting transfers between devices: 19.9 us -> 34.1 us
    reduce_scatter x7 -> x4, waiting for transfers between devices: 371 us -> 2.08 us  [the longest x1 2.03 us: body(): lax.psum_scatter(jnp.concatenate([rows_product(nf, d_gate), rows_product(...]
    pallas_call x0 -> x6, Pallas kernels: none -> 184 us  [the longest x1 56.5 us: attend_back(): pl.pallas_call(functools.partial(attend_back_kernel, head_dim), out_shape...]
    dot_general x77 -> x5, matrix products: 210 us -> 33.1 us  [dot_tn(): lax.dot_general(left, right, (((0,), (0,)), ((), ())), preferred_element_...]
    ppermute x0 -> x26, waiting for transfers between devices: none -> 153 us  [swap(): return lax.ppermute(array, 'seq', [(s, s ^ distance) for s in range(4)])]
    all_gather x7 -> x6, waiting for transfers between devices: 117 us -> 42.7 us  [the longest x2 42.6 us: whole(): return lax.all_gather(part, 'seq', axis=0)]
    gather x9 -> x1, local copies, waits for them, and re-layouts: 68.1 us -> 2.27 us  [body(): jnp.take(d_wo, jnp.bitwise_xor(jnp.arange(ways), me), axis=0)]
    another operation x14 -> x0, loops' own time: 61.4 us -> none  [the longest x4 22.6 us: backward_block(): lax.fori_loop(first_block[q_block], q_block + 1, key_step, start_state)]
    all_to_all x3 -> x0, blocking collectives: 33.8 us -> none  [the longest x1 13.5 us: body(): lax.all_to_all(d_query_given, 'seq', split_axis=0, concat_axis=1, tiled=T...]
  transfers between devices with their start and end apart: 20 -> 37, of which waited for: 12 -> 17; matrix products, arithmetic and copies ran while one was open for 20% -> 15% of each run, Pallas kernels for 0% -> 19%
where the time goes in v1:
time: 654 us; the launch traced here: 648 us
  waiting for transfers between devices  200 us (31%)
  Pallas kernels  184 us (28%)
  blocking collectives  83.2 us (13%)
  local copies, waits for them, and re-layouts  68.4 us (10%)
  starting transfers between devices  34.1 us (5%)
  matrix products  33.1 us (5%)
  other arithmetic  31 us (5%)
  between operations  15 us (2%)
    ppermute x26, waiting for transfers between devices, swap(): return lax.ppermute(array, 'seq', [(s, s ^ distance) for s in range(4)])  153 us
    psum x1, blocking collectives, body(): head_gains = lax.psum(head_gains, ('seq', 'shard'))  71.8 us
    pallas_call x1, Pallas kernels, attend_back(): pl.pallas_call(functools.partial(attend_back_kernel, head_dim), out_shape...  56.5 us
    pallas_call x1, Pallas kernels, ffn(): pl.pallas_call(functools.partial(ffn_kernel, per), grid=(steps,), out_sha...  54.7 us
    pallas_call x2, Pallas kernels, attend(): pl.pallas_call(functools.partial(attend_kernel, head_dim, group), grid=(1...  43.5 us
    all_gather x2, waiting for transfers between devices, whole(): return lax.all_gather(part, 'seq', axis=0)  42.6 us
    ppermute x26, starting transfers between devices, swap(): return lax.ppermute(array, 'seq', [(s, s ^ distance) for s in range(4)])  33.7 us
    dot_general x5, matrix products, dot_tn(): lax.dot_general(left, right, (((0,), (0,)), ((), ())), preferred_element_...  33.1 us
  transfers between devices with their start and end apart: 37, of which 17 were waited for; matrix products, arithmetic and copies ran while one was open for 15% of the time, Pallas kernels for 19%

profile of v1, /device:TPU:0, one launch (start us, length us, event | category | flops | bytes accessed | tf_op | source)
XLA Modules:
  0.0 648.5 jit_solution(10188037188575165756)
XLA Ops:
  13.0 3.0 collective-permute-start
  16.0 1.5 collective-permute-start.1
  18.9 2.1 copy.48
  34.4 6.0 collective-permute-done
  41.4 2.1 collective-permute-start.2
  44.7 1.6 collective-permute-start.3
  46.2 16.6 %collective-permute-done.10 = bf16[512,1024]{1,0:T(8,128)(2,1)} collective-permute-done((bf16[512,1024]{1,0:T(8,128)(2,1)}, bf16[512,1024]{1,0:T(8,128)(2,1)}, u32[]{:S(2)}, u32[]{:S(2)}) %collective-permute-start.10) | collective-permute-done | bytes 1048608 | tf_op jit(solution)/shard_map/ppermute | solution.py:477
  63.9 2.1 collective-permute-start.12
  67.1 1.6 collective-permute-start.13
  71.3 2.3 constant_dynamic-update-slice_fusion.8
  73.6 2.3 constant_dynamic-update-slice_fusion.7
  76.1 9.7 %collective-permute-done.12 = bf16[256,1024]{1,0:T(8,128)(2,1)S(1)} collective-permute-done((bf16[256,1024]{1,0:T(8,128)(2,1)S(1)}, bf16[256,1024]{1,0:T(8,128)(2,1)S(1)}, u32[]{:S(2)}, u32[]{:S(2)}) %collective-permute-start.12) | collective-permute-done | bytes 524320 | tf_op jit(solution)/shard_map/ppermute | solution.py:477
  89.6 22.2 %qkv.1 = (bf16[2048,1024]{1,0:T(8,128)(2,1)}, bf16[4,2048,128]{2,1,0:T(8,128)(2,1)}, bf16[2048,128]{1,0:T(8,128)(2,1)}, bf16[2048,128]{1,0:T(8,128)(2,1)}, bf16[...) custom-call(bf16[2048,1024]{1,0:T(8,128)(2,1)} %copy-done.21, ...), custom_call_target="tpu_custom_call" | custom-call | flops 6442450944 | bytes 16777216 | tf_op jit(solution)/shard_map/qkv/pallas_call | solution.py:133
  111.9 21.7 %attend.2 = (bf16[2048,128]{1,0:T(8,128)(2,1)}, bf16[2048,128]{1,0:T(8,128)(2,1)}, f32[2,2048]{1,0:T(2,128)}) custom-call(s32[1,3]{1,0:T(1,128)} %lens_ref.5, s32[1,2048]{1,0:T(1,128)} %broadcast_xor_fusion.orow_ref, bf16[4,2048,128]{2,1,0:T(8,128)(2,1)} %get-tuple-element.52.qx_ref, bf16[2048,128]{1,0:T(8,128)(2,1)} %get-tuple-element.53.k_ref, ...), custom_call_target="tpu_custom_call" | custom-call | flops 12884901888 | bytes 4194304 | tf_op jit(solution)/shard_map/attend/pallas_call | solution.py:206
  134.1 21.8 %attend.3 = (bf16[2048,128]{1,0:T(8,128)(2,1)}, bf16[2048,128]{1,0:T(8,128)(2,1)}, f32[2,2048]{1,0:T(2,128)}) custom-call(s32[1,3]{1,0:T(1,128)} %lens_ref.5, s32[1,2048]{1,0:T(1,128)} %broadcast_xor_fusion.orow_ref, bf16[4,2048,128]{2,1,0:T(8,128)(2,1)} %get-tuple-element.52.qx_ref, bf16[2048,128]{1,0:T(8,128)(2,1)} %get-tuple-element.53.k_ref, ...), custom_call_target="tpu_custom_call" | custom-call | flops 12884901888 | bytes 4194304 | tf_op jit(solution)/shard_map/attend/pallas_call | solution.py:206
  155.9 1.6 collective-permute-start.5
  157.4 1.5 collective-permute-start.7
  159.3 1.7 collective-permute-start.6
  163.8 1.6 slice_dynamic-update-slice_fusion.6
  166.1 4.8 collective-permute-done.5.refs_3_
  170.9 24.0 %collective-permute-done.7.refs_5_ = bf16[2048,128]{1,0:T(8,128)(2,1)S(1)} collective-permute-done((bf16[2048,128]{1,0:T(8,128)(2,1)}, bf16[2048,128]{1,0:T(8,128)(2,1)S(1)}, u32[]{:S(2)}, u32[]{:S(2)}) %collective-permute-start.7) | collective-permute-done | bytes 524320 | tf_op jit(solution)/shard_map/ppermute | solution.py:477
  195.0 8.5 %collective-permute-done.6.refs_4_ = bf16[2048,128]{1,0:T(8,128)(2,1)} collective-permute-done((bf16[2048,128]{1,0:T(8,128)(2,1)S(1)}, bf16[2048,128]{1,0:T(8,128)(2,1)}, u32[]{:S(2)}, u32[]{:S(2)}) %collective-permute-start.6) | collective-permute-done | bytes 524320 | tf_op jit(solution)/shard_map/ppermute | solution.py:477
  203.5 54.7 %ffn.1 = (bf16[2048,1024]{1,0:T(8,128)(2,1)}, bf16[2048,1152]{1,0:T(8,128)(2,1)}, bf16[2048,1152]{1,0:T(8,128)(2,1)}, bf16[2048,1152]{1,0:T(8,128)(2,1)}, f32[51...) custom-call(s32[1]{0:T(128)} %bitcast.me_ref, ...), custom_call_target="tpu_custom_call" | custom-call | flops 33285996544 | bytes 52428800 | tf_op jit(solution)/shard_map/ffn/pallas_call | solution.py:424
  261.8 1.6 slice_dynamic-update-slice_fusion.4
  263.4 1.6 slice_dynamic-update-slice_fusion.3
  265.0 1.6 slice_dynamic-update-slice_fusion.2
  266.5 1.6 slice_dynamic-update-slice_fusion.1
  268.1 1.6 slice_dynamic-update-slice_fusion
  269.7 15.0 %collective-permute-done.17.n1_ref = bf16[512,1024]{1,0:T(8,128)(2,1)S(1)} collective-permute-done((bf16[512,1024]{1,0:T(8,128)(2,1)}, bf16[512,1024]{1,0:T(8,128)(2,1)S(1)}, u32[]{:S(2)}, u32[]{:S(2)}) %collective-permute-start.17) | collective-permute-done | bytes 1048608 | tf_op jit(solution)/shard_map/ppermute | solution.py:477
  284.6 18.2 %collective-permute-done.18.n2_ref = bf16[512,1024]{1,0:T(8,128)(2,1)S(1)} collective-permute-done((bf16[512,1024]{1,0:T(8,128)(2,1)}, bf16[512,1024]{1,0:T(8,128)(2,1)S(1)}, u32[]{:S(2)}, u32[]{:S(2)}) %collective-permute-start.18) | collective-permute-done | bytes 1048608 | tf_op jit(solution)/shard_map/ppermute | solution.py:477
  302.9 1.7 collective-permute-done.19.n3_ref
  305.6 6.7 %middle_back.1 = (f32[512,1024]{1,0:T(8,128)}, bf16[512,1024]{1,0:T(8,128)(2,1)}, bf16[512,256]{1,0:T(8,128)(2,1)}, bf16[512,256]{1,0:T(8,128)(2,1)}, bf16[512,2...) custom-call(s32[1]{0:T(128)} %bitcast.me_ref, bf16[512,1024]{1,0:T(8,128)(2,1)} %get-tuple-element.62.n0_ref, ...), custom_call_target="tpu_custom_call" | custom-call | flops 1073741824 | bytes 12582912 | tf_op jit(solution)/shard_map/middle_back/pallas_call | solution.py:464
  312.3 3.8 convolution_convert_fusion.3
  316.1 2.3 gather_fusion
  318.4 1.8 bitcast_select_fusion
  320.3 9.3 %convolution_convert_fusion = bf16[1152,1024]{1,0:T(8,128)(2,1)} fusion(bf16[2048,1152]{1,0:T(8,128)(2,1)} %get-tuple-element.90, bf16[2048,1024]{1,0:T(8,128)(2,1)} %constant_dynamic-update-slice_fusion.5.refs_9_), kind=kOutput, calls=%fused_computation.2 | convolution fusion | flops 4833017856 | bytes 11272192 | tf_op jit(solution)/shard_map/dot_general | solution.py:29
  329.7 9.0 %convolution_convert_fusion.2 = bf16[1024,1152]{1,0:T(8,128)(2,1)S(1)} fusion(bf16[2048,1024]{1,0:T(8,128)(2,1)} %get-tuple-element.87, bf16[2048,1152]{1,0:T(8,128)(2,1)} %get-tuple-element.88), kind=kOutput, calls=%fused_computation.4 | convolution fusion | flops 4833017856 | bytes 11272192 | tf_op jit(solution)/shard_map/dot_general | solution.py:29
  338.8 6.1 convolution_convert_fusion.1
  344.8 2.5 pad_maximum_fusion
  349.2 1.7 collective-permute-start.21
  351.8 4.2 collective-permute-done.20.d1_ref
  356.0 2.9 collective-permute-done.21.d2_ref
  359.7 56.5 %attend_back.1 = (bf16[2048,512]{1,0:T(8,128)(2,1)}, f32[2,128]{1,0:T(2,128)}, bf16[512,1024]{1,0:T(8,128)(2,1)}, bf16[512,1024]{1,0:T(8,128)(2,1)}, bf16[512,10...) custom-call(s32[1,3]{1,0:T(1,128)} %lens_ref.5, s32[2048,1]{1,0:T(8,128)} %copy.45.ocol_ref, ...), custom_call_target="tpu_custom_call" | custom-call | flops 42949672960 | bytes 12582912 | tf_op jit(solution)/shard_map/attend_back/pallas_call | solution.py:347
  416.2 4.9 convolution_convert_fusion.4
  422.5 1.7 collective-permute-start.14
  426.1 1.7 collective-permute-start.23
  428.1 20.7 %collective-permute-done.14 = bf16[512,1024]{1,0:T(8,128)(2,1)S(1)} collective-permute-done((bf16[512,1024]{1,0:T(8,128)(2,1)}, bf16[512,1024]{1,0:T(8,128)(2,1)S(1)}, u32[]{:S(2)}, u32[]{:S(2)}) %collective-permute-start.14) | collective-permute-done | bytes 1048608 | tf_op jit(solution)/shard_map/ppermute | solution.py:477
  448.9 1.5 collective-permute-start.25
  450.4 2.0 reduce-scatter.9.cloned.1.call-done
  452.4 20.7 %collective-permute-done.15 = bf16[512,1024]{1,0:T(8,128)(2,1)} collective-permute-done((bf16[512,1024]{1,0:T(8,128)(2,1)}, bf16[512,1024]{1,0:T(8,128)(2,1)}, u32[]{:S(2)}, u32[]{:S(2)}) %collective-permute-start.15) | collective-permute-done | bytes 1048608 | tf_op jit(solution)/shard_map/ppermute | solution.py:477
  473.2 4.3 fusion.4
  477.4 71.8 %psum.14 = f32[2,128]{1,0:T(2,128)S(1)} all-reduce(f32[2,128]{1,0:T(2,128)S(1)} %copy-done.33), channel_id=1, replica_groups=mesh['seq'=4,'shard'=8] {'seq','shard'}, use_global_device_ids=true, to_apply=%region_7.8 | all-reduce | flops 256 | bytes 2048 | tf_op jit(solution)/shard_map/psum | solution.py:599
  549.9 3.3 fusion
  553.2 3.8 fusion.5
  557.1 11.4 %all-gather = bf16[512,512]{1,0:T(8,128)(2,1)S(1)} all-gather(bf16[128,512]{1,0:T(8,128)(2,1)} %reduce-scatter.5.cloned.1.call-done), channel_id=2, replica_groups=mesh['seq'=4,'shard'=8] {'seq'}, dimensions={0}, use_global_device_ids=true | all-gather | bytes 655360 | tf_op jit(solution)/shard_map/all_gather | solution.py:587
  570.7 1.8 convert_element_type.165
  572.5 6.1 all-gather.20.cloned.1.call-done
  578.6 3.0 convert_element_type.187
  581.6 36.5 %all-gather.18.cloned.1.call-done = bf16[512,2304]{1,0:T(8,128)(2,1)} async-done(((bf16[128,2304]{1,0:T(8,128)(2,1)}), bf16[512,2304]{1,0:T(8,128)(2,1)}) %all-gather.18.cloned.1.call-update) | async-done | bytes 2359312 | tf_op jit(solution)/shard_map/all_gather | solution.py:587
  618.1 4.6 copy.59
  622.7 6.3 reshape.225
  629.1 2.7 fusion.9
  635.9 3.0 copy.63
  639.0 1.9 copy.64
  (219 shorter events, 54.8 us)
Async XLA Ops:
  7.2 5.0 copy-start
  7.2 11.0 %copy-start.15 = (bf16[128,4608]{1,0:T(8,128)(2,1)S(1)}, bf16[128,4608]{1,0:T(8,128)(2,1)}, u32[]{:S(2)}) copy-start(bf16[128,4608]{1,0:T(8,128)(2,1)} %param.26) | copy-start | bytes 3538948
  7.2 80.3 %all-gather.10.cloned.1.call-start = ((), (), s32[]{:S(2)}) async-start(), calls=%async_computation.4 | async-start | bytes 1474560 | tf_op jit(solution)/shard_map/all_gather | solution.py:506
  11.4 192.1 %all-gather.12.cloned.1.call-start = ((), (), s32[]{:S(2)}) async-start(), calls=%async_computation.5 | async-start | bytes 2359296 | tf_op jit(solution)/shard_map/all_gather | solution.py:507
  12.2 191.3 %all-gather.16.cloned.1.call-start = ((), (), s32[]{:S(2)}) async-start(), calls=%async_computation.7 | async-start | bytes 2654208 | tf_op jit(solution)/shard_map/all_gather | solution.py:510
  13.0 190.5 %all-gather.14.cloned.1.call-start = ((), (), s32[]{:S(2)}) async-start(), calls=%async_computation.6 | async-start | bytes 5308416 | tf_op jit(solution)/shard_map/all_gather | solution.py:509
  13.0 27.3 %collective-permute-start = (bf16[512,1024]{1,0:T(8,128)(2,1)}, bf16[512,1024]{1,0:T(8,128)(2,1)}, u32[]{:S(2)}, u32[]{:S(2)}) collective-permute-start(bf16[512,1024]{1,0:T(8,128)(2,1)} %bitcast.73), channel_id=1, source_target_pairs={{0,8},{8,0},{16,24},{24,16},{1,9},{9,1},{17,25},{25,17},{2,10},{10... | collective-permute-start | bytes 3145736 | tf_op jit(solution)/shard_map/ppermute | solution.py:477
  16.0 27.5 %collective-permute-start.1 = (bf16[512,1024]{1,0:T(8,128)(2,1)}, bf16[512,1024]{1,0:T(8,128)(2,1)}, u32[]{:S(2)}, u32[]{:S(2)}) collective-permute-start(bf16[512,1024]{1,0:T(8,128)(2,1)} %bitcast.74), channel_id=1, source_target_pairs={{0,16},{8,24},{16,0},{24,8},{1,17},{9,25},{17,1},{25,9},{2,18},{10... | collective-permute-start | bytes 3145736 | tf_op jit(solution)/shard_map/ppermute | solution.py:477
  17.6 45.3 %collective-permute-start.10 = (bf16[512,1024]{1,0:T(8,128)(2,1)}, bf16[512,1024]{1,0:T(8,128)(2,1)}, u32[]{:S(2)}, u32[]{:S(2)}) collective-permute-start(bf16[512,1024]{1,0:T(8,128)(2,1)} %bitcast.77), channel_id=1, source_target_pairs={{0,8},{8,0},{16,24},{24,16},{1,9},{9,1},{17,25},{25,17},{2,10},{10... | collective-permute-start | bytes 3145736 | tf_op jit(solution)/shard_map/ppermute | solution.py:477
  18.1 48.0 %collective-permute-start.11 = (bf16[512,1024]{1,0:T(8,128)(2,1)}, bf16[512,1024]{1,0:T(8,128)(2,1)}, u32[]{:S(2)}, u32[]{:S(2)}) collective-permute-start(bf16[512,1024]{1,0:T(8,128)(2,1)} %bitcast.78), channel_id=1, source_target_pairs={{0,16},{8,24},{16,0},{24,8},{1,17},{9,25},{17,1},{25,9},{2,18},{10... | collective-permute-start | bytes 3145736 | tf_op jit(solution)/shard_map/ppermute | solution.py:477
  22.4 398.8 %reduce-scatter.7.cloned.1.call-start = ((), (), s32[]{:S(2)}) async-start(), calls=%async_computation.9 | async-start | bytes 2359296 | tf_op jit(solution)/shard_map/reduce_scatter | solution.py:570
  27.0 3.4 copy-start.41
  27.0 4.1 copy-start.3
  41.4 34.6 %collective-permute-start.2 = (bf16[256,1024]{1,0:T(8,128)(2,1)S(1)}, bf16[256,1024]{1,0:T(8,128)(2,1)S(1)}, u32[]{:S(2)}, u32[]{:S(2)}) collective-permute-start(bf16[256,1024]{1,0:T(8,128)(2,1)S(1)} %slice.114), channel_id=1, source_target_pairs={{0,16},{8,24},{16,0},{24,8},{1,17},{9,25},{17,1},{25,9},{2,18},{10... | collective-permute-start | bytes 1572872 | tf_op jit(solution)/shard_map/ppermute | solution.py:477
  44.7 31.4 %collective-permute-start.3 = (bf16[256,1024]{1,0:T(8,128)(2,1)S(1)}, bf16[256,1024]{1,0:T(8,128)(2,1)S(1)}, u32[]{:S(2)}, u32[]{:S(2)}) collective-permute-start(bf16[256,1024]{1,0:T(8,128)(2,1)S(1)} %slice.115), channel_id=1, source_target_pairs={{0,8},{8,0},{16,24},{24,16},{1,9},{9,1},{17,25},{25,17},{2,10},{10... | collective-permute-start | bytes 1572872 | tf_op jit(solution)/shard_map/ppermute | solution.py:477
  63.9 21.9 %collective-permute-start.12 = (bf16[256,1024]{1,0:T(8,128)(2,1)S(1)}, bf16[256,1024]{1,0:T(8,128)(2,1)S(1)}, u32[]{:S(2)}, u32[]{:S(2)}) collective-permute-start(bf16[256,1024]{1,0:T(8,128)(2,1)S(1)} %slice.118), channel_id=1, source_target_pairs={{0,16},{8,24},{16,0},{24,8},{1,17},{9,25},{17,1},{25,9},{2,18},{10... | collective-permute-start | bytes 1572872 | tf_op jit(solution)/shard_map/ppermute | solution.py:477
  67.1 19.5 %collective-permute-start.13 = (bf16[256,1024]{1,0:T(8,128)(2,1)S(1)}, bf16[256,1024]{1,0:T(8,128)(2,1)S(1)}, u32[]{:S(2)}, u32[]{:S(2)}) collective-permute-start(bf16[256,1024]{1,0:T(8,128)(2,1)S(1)} %slice.119), channel_id=1, source_target_pairs={{0,8},{8,0},{16,24},{24,16},{1,9},{9,1},{17,25},{25,17},{2,10},{10... | collective-permute-start | bytes 1572872 | tf_op jit(solution)/shard_map/ppermute | solution.py:477
  76.1 10.5 %copy-start.21 = (bf16[2048,1024]{1,0:T(8,128)(2,1)}, bf16[2048,1024]{1,0:T(8,128)(2,1)S(1)}, u32[]{:S(2)}) copy-start(bf16[2048,1024]{1,0:T(8,128)(2,1)S(1)} %constant_dynamic-update-slice_fusion.x_ref.refs_8_) | copy-start | bytes 12582916
  133.6 25.7 %copy-start.26 = (bf16[2048,128]{1,0:T(8,128)(2,1)S(1)}, bf16[2048,128]{1,0:T(8,128)(2,1)}, u32[]{:S(2)}) copy-start(bf16[2048,128]{1,0:T(8,128)(2,1)} %get-tuple-element.55.refs_0_) | copy-start | bytes 1572868
  133.6 27.4 %collective-permute-start.4 = (bf16[2048,128]{1,0:T(8,128)(2,1)}, bf16[2048,128]{1,0:T(8,128)(2,1)S(1)}, u32[]{:S(2)}, u32[]{:S(2)}) collective-permute-start(bf16[2048,128]{1,0:T(8,128)(2,1)} %get-tuple-element.55.refs_0_), channel_id=1, source_target_pairs={{0,8},{8,0},{16,24},{24,16},{1,9},{9,1},{17,25},{25,17},{2,10},{10... | collective-permute-start | bytes 1572872 | tf_op jit(solution)/shard_map/ppermute | solution.py:477
  155.9 15.1 %collective-permute-start.5 = (bf16[2048,128]{1,0:T(8,128)(2,1)}, bf16[2048,128]{1,0:T(8,128)(2,1)S(1)}, u32[]{:S(2)}, u32[]{:S(2)}) collective-permute-start(bf16[2048,128]{1,0:T(8,128)(2,1)} %get-tuple-element.56.refs_1_), channel_id=1, source_target_pairs={{0,8},{8,0},{16,24},{24,16},{1,9},{9,1},{17,25},{25,17},{2,10},{10... | collective-permute-start | bytes 1572872 | tf_op jit(solution)/shard_map/ppermute | solution.py:477
  157.4 37.5 %collective-permute-start.7 = (bf16[2048,128]{1,0:T(8,128)(2,1)}, bf16[2048,128]{1,0:T(8,128)(2,1)S(1)}, u32[]{:S(2)}, u32[]{:S(2)}) collective-permute-start(bf16[2048,128]{1,0:T(8,128)(2,1)} %get-tuple-element.56.refs_1_), channel_id=1, source_target_pairs={{0,16},{8,24},{16,0},{24,8},{1,17},{9,25},{17,1},{25,9},{2,18},{10... | collective-permute-start | bytes 1572872 | tf_op jit(solution)/shard_map/ppermute | solution.py:477
  159.0 36.0 %collective-permute-start.9 = (bf16[2048,128]{1,0:T(8,128)(2,1)}, bf16[2048,128]{1,0:T(8,128)(2,1)S(1)}, u32[]{:S(2)}, u32[]{:S(2)}) collective-permute-start(bf16[2048,128]{1,0:T(8,128)(2,1)} %get-tuple-element.56.refs_1_), channel_id=1, source_target_pairs={{0,24},{8,16},{16,8},{24,0},{1,25},{9,17},{17,9},{25,1},{2,26},{10... | collective-permute-start | bytes 1572872 | tf_op jit(solution)/shard_map/ppermute | solution.py:477
  159.3 44.1 %collective-permute-start.6 = (bf16[2048,128]{1,0:T(8,128)(2,1)S(1)}, bf16[2048,128]{1,0:T(8,128)(2,1)}, u32[]{:S(2)}, u32[]{:S(2)}) collective-permute-start(bf16[2048,128]{1,0:T(8,128)(2,1)S(1)} %copy-done.26), channel_id=1, source_target_pairs={{0,16},{8,24},{16,0},{24,8},{1,17},{9,25},{17,1},{25,9},{2,18},{10... | collective-permute-start | bytes 1572872 | tf_op jit(solution)/shard_map/ppermute | solution.py:477
  161.0 42.5 %copy-start.28 = (bf16[2048,128]{1,0:T(8,128)(2,1)}, bf16[2048,128]{1,0:T(8,128)(2,1)S(1)}, u32[]{:S(2)}) copy-start(bf16[2048,128]{1,0:T(8,128)(2,1)S(1)} %collective-permute-done.4.refs_2_) | copy-start | bytes 1572868
  161.0 42.5 %collective-permute-start.8 = (bf16[2048,128]{1,0:T(8,128)(2,1)S(1)}, bf16[2048,128]{1,0:T(8,128)(2,1)}, u32[]{:S(2)}, u32[]{:S(2)}) collective-permute-start(bf16[2048,128]{1,0:T(8,128)(2,1)S(1)} %copy-done.26), channel_id=1, source_target_pairs={{0,24},{8,16},{16,8},{24,0},{1,25},{9,17},{17,9},{25,1},{2,26},{10... | collective-permute-start | bytes 1572872 | tf_op jit(solution)/shard_map/ppermute | solution.py:477
  170.9 32.6 %copy-start.27 = (bf16[2048,128]{1,0:T(8,128)(2,1)}, bf16[2048,128]{1,0:T(8,128)(2,1)S(1)}, u32[]{:S(2)}) copy-start(bf16[2048,128]{1,0:T(8,128)(2,1)S(1)} %collective-permute-done.5.refs_3_) | copy-start | bytes 1572868
  195.0 8.6 %copy-start.25 = (bf16[2048,128]{1,0:T(8,128)(2,1)}, bf16[2048,128]{1,0:T(8,128)(2,1)S(1)}, u32[]{:S(2)}) copy-start(bf16[2048,128]{1,0:T(8,128)(2,1)S(1)} %collective-permute-done.7.refs_5_) | copy-start | bytes 1572868
  195.0 8.6 %copy-start.24 = (bf16[2048,128]{1,0:T(8,128)(2,1)}, bf16[2048,128]{1,0:T(8,128)(2,1)S(1)}, u32[]{:S(2)}) copy-start(bf16[2048,128]{1,0:T(8,128)(2,1)S(1)} %collective-permute-done.9.refs_7_) | copy-start | bytes 1572868
  258.3 26.4 %collective-permute-start.17 = (bf16[512,1024]{1,0:T(8,128)(2,1)}, bf16[512,1024]{1,0:T(8,128)(2,1)S(1)}, u32[]{:S(2)}, u32[]{:S(2)}) collective-permute-start(bf16[512,1024]{1,0:T(8,128)(2,1)} %get-tuple-element.63), channel_id=1, source_target_pairs={{0,8},{8,0},{16,24},{24,16},{1,9},{9,1},{17,25},{25,17},{2,10},{10... | collective-permute-start | bytes 3145736 | tf_op jit(solution)/shard_map/ppermute | solution.py:477
  259.1 43.7 %collective-permute-start.18 = (bf16[512,1024]{1,0:T(8,128)(2,1)}, bf16[512,1024]{1,0:T(8,128)(2,1)S(1)}, u32[]{:S(2)}, u32[]{:S(2)}) collective-permute-start(bf16[512,1024]{1,0:T(8,128)(2,1)} %get-tuple-element.64), channel_id=1, source_target_pairs={{0,16},{8,24},{16,0},{24,8},{1,17},{9,25},{17,1},{25,9},{2,18},{10... | collective-permute-start | bytes 3145736 | tf_op jit(solution)/shard_map/ppermute | solution.py:477
  260.4 44.1 %collective-permute-start.19 = (bf16[512,1024]{1,0:T(8,128)(2,1)}, bf16[512,1024]{1,0:T(8,128)(2,1)S(1)}, u32[]{:S(2)}, u32[]{:S(2)}) collective-permute-start(bf16[512,1024]{1,0:T(8,128)(2,1)} %get-tuple-element.65), channel_id=1, source_target_pairs={{0,24},{8,16},{16,8},{24,0},{1,25},{9,17},{17,9},{25,1},{2,26},{10... | collective-permute-start | bytes 3145736 | tf_op jit(solution)/shard_map/ppermute | solution.py:477
  284.6 19.9 %copy-start.17 = (bf16[512,1024]{1,0:T(8,128)(2,1)}, bf16[512,1024]{1,0:T(8,128)(2,1)S(1)}, u32[]{:S(2)}) copy-start(bf16[512,1024]{1,0:T(8,128)(2,1)S(1)} %collective-permute-done.17.n1_ref) | copy-start | bytes 3145732
  305.6 6.7 %copy-start.30 = (bf16[512,1024]{1,0:T(8,128)(2,1)S(1)}, bf16[512,1024]{1,0:T(8,128)(2,1)}, u32[]{:S(2)}) copy-start(bf16[512,1024]{1,0:T(8,128)(2,1)} %slice_dynamic-update-slice_fusion) | copy-start | bytes 3145732
  320.2 101.7 %reduce-scatter.11.cloned.1.call-start = ((), (), s32[]{:S(2)}) async-start(), calls=%async_computation.12 | async-start | bytes 2654208 | tf_op jit(solution)/shard_map/reduce_scatter | solution.py:555
  329.6 9.1 %slice-start = ((s8[4718592]{0:T(1024)(128)(4,1)}), s8[524288]{0:T(1024)(128)(4,1)S(1)}, s32[]{:S(2)}) async-start(s8[4718592]{0:T(1024)(128)(4,1)} %bitcast.92), calls=%async_computation.15 | async-start | bytes 1048576
  329.6 122.8 %reduce-scatter.9.cloned.1.call-start = ((), (), s32[]{:S(2)}) async-start(), calls=%async_computation.11 | async-start | bytes 5308416 | tf_op jit(solution)/shard_map/reduce_scatter | solution.py:556
  329.7 9.1 %slice-start.1 = ((s8[4718592]{0:T(1024)(128)(4,1)}), s8[4194304]{0:T(1024)(128)(4,1)S(1)}, s32[]{:S(2)}) async-start(s8[4718592]{0:T(1024)(128)(4,1)} %bitcast.92), calls=%async_computation.16 | async-start | bytes 8388608
  329.7 9.1 %copy-start.44 = (bf16[2048,1024]{1,0:T(8,128)(2,1)S(1)}, bf16[2048,1024]{1,0:T(8,128)(2,1)}, u32[]{:S(2)}) copy-start(bf16[2048,1024]{1,0:T(8,128)(2,1)} %get-tuple-element.87) | copy-start | bytes 12582916
  347.3 3.6 copy-start.34
  347.4 209.7 %reduce-scatter.5.cloned.1.call-start = ((), (), s32[]{:S(2)}) async-start(), calls=%async_computation.8 | async-start | bytes 1179648 | tf_op jit(solution)/shard_map/reduce_scatter | solution.py:577
  348.3 7.7 %collective-permute-start.20 = (bf16[512,256]{1,0:T(8,128)(2,1)S(1)}, bf16[512,256]{1,0:T(8,128)(2,1)S(1)}, u32[]{:S(2)}, u32[]{:S(2)}) collective-permute-start(bf16[512,256]{1,0:T(8,128)(2,1)S(1)} %copy-done.36), channel_id=1, source_target_pairs={{0,8},{8,0},{16,24},{24,16},{1,9},{9,1},{17,25},{25,17},{2,10},{10... | collective-permute-start | bytes 786440 | tf_op jit(solution)/shard_map/ppermute | solution.py:477
  349.2 9.7 %collective-permute-start.21 = (bf16[512,256]{1,0:T(8,128)(2,1)S(1)}, bf16[512,256]{1,0:T(8,128)(2,1)S(1)}, u32[]{:S(2)}, u32[]{:S(2)}) collective-permute-start(bf16[512,256]{1,0:T(8,128)(2,1)S(1)} %copy-done.35), channel_id=1, source_target_pairs={{0,16},{8,24},{16,0},{24,8},{1,17},{9,25},{17,1},{25,9},{2,18},{10... | collective-permute-start | bytes 786440 | tf_op jit(solution)/shard_map/ppermute | solution.py:477
  351.0 7.9 %collective-permute-start.22 = (bf16[512,256]{1,0:T(8,128)(2,1)S(1)}, bf16[512,256]{1,0:T(8,128)(2,1)S(1)}, u32[]{:S(2)}, u32[]{:S(2)}) collective-permute-start(bf16[512,256]{1,0:T(8,128)(2,1)S(1)} %copy-done.34), channel_id=1, source_target_pairs={{0,24},{8,16},{16,8},{24,0},{1,25},{9,17},{17,9},{25,1},{2,26},{10... | collective-permute-start | bytes 786440 | tf_op jit(solution)/shard_map/ppermute | solution.py:477
  359.7 56.5 %copy-start.43 = (bf16[2048,1024]{1,0:T(8,128)(2,1)S(1)}, bf16[2048,1024]{1,0:T(8,128)(2,1)}, u32[]{:S(2)}) copy-start(bf16[2048,1024]{1,0:T(8,128)(2,1)} %get-tuple-element.83) | copy-start | bytes 12582916
  421.1 52.0 %copy-start.5 = (f32[512,1024]{1,0:T(8,128)S(1)}, f32[512,1024]{1,0:T(8,128)}, u32[]{:S(2)}) copy-start(f32[512,1024]{1,0:T(8,128)} %get-tuple-element.57.mid_ref) | copy-start | bytes 6291460
  421.1 149.6 %all-reduce.2.cloned.1.call-start = ((), (), s32[]{:S(2)}) async-start(), calls=%async_computation.10 | async-start | bytes 524288 | tf_op jit(solution)/shard_map/psum | solution.py:595
  421.9 156.8 %all-gather.20.cloned.1.call-start = ((), (), s32[]{:S(2)}) async-start(), calls=%async_computation.14 | async-start | bytes 1474560 | tf_op jit(solution)/shard_map/all_gather | solution.py:587
  422.4 195.7 %all-gather.18.cloned.1.call-start = ((), (), s32[]{:S(2)}) async-start(), calls=%async_computation.13 | async-start | bytes 2949120 | tf_op jit(solution)/shard_map/all_gather | solution.py:587
  422.5 26.4 %collective-permute-start.14 = (bf16[512,1024]{1,0:T(8,128)(2,1)}, bf16[512,1024]{1,0:T(8,128)(2,1)S(1)}, u32[]{:S(2)}, u32[]{:S(2)}) collective-permute-start(bf16[512,1024]{1,0:T(8,128)(2,1)} %get-tuple-element.59), channel_id=1, source_target_pairs={{0,8},{8,0},{16,24},{24,16},{1,9},{9,1},{17,25},{25,17},{2,10},{10... | collective-permute-start | bytes 3145736 | tf_op jit(solution)/shard_map/ppermute | solution.py:477
  424.2 48.9 %collective-permute-start.15 = (bf16[512,1024]{1,0:T(8,128)(2,1)}, bf16[512,1024]{1,0:T(8,128)(2,1)}, u32[]{:S(2)}, u32[]{:S(2)}) collective-permute-start(bf16[512,1024]{1,0:T(8,128)(2,1)} %get-tuple-element.60), channel_id=1, source_target_pairs={{0,16},{8,24},{16,0},{24,8},{1,17},{9,25},{17,1},{25,9},{2,18},{10... | collective-permute-start | bytes 3145736 | tf_op jit(solution)/shard_map/ppermute | solution.py:477
  424.6 48.5 %collective-permute-start.16 = (bf16[512,1024]{1,0:T(8,128)(2,1)}, bf16[512,1024]{1,0:T(8,128)(2,1)}, u32[]{:S(2)}, u32[]{:S(2)}) collective-permute-start(bf16[512,1024]{1,0:T(8,128)(2,1)} %get-tuple-element.61), channel_id=1, source_target_pairs={{0,24},{8,16},{16,8},{24,0},{1,25},{9,17},{17,9},{25,1},{2,26},{10... | collective-permute-start | bytes 3145736 | tf_op jit(solution)/shard_map/ppermute | solution.py:477
  426.1 123.8 %collective-permute-start.23 = (bf16[512,1024]{1,0:T(8,128)(2,1)}, bf16[512,1024]{1,0:T(8,128)(2,1)}, u32[]{:S(2)}, u32[]{:S(2)}) collective-permute-start(bf16[512,1024]{1,0:T(8,128)(2,1)} %get-tuple-element.80), channel_id=1, source_target_pairs={{0,8},{8,0},{16,24},{24,16},{1,9},{9,1},{17,25},{25,17},{2,10},{10... | collective-permute-start | bytes 3145736 | tf_op jit(solution)/shard_map/ppermute | solution.py:477
  427.7 122.1 %collective-permute-start.24 = (bf16[512,1024]{1,0:T(8,128)(2,1)}, bf16[512,1024]{1,0:T(8,128)(2,1)}, u32[]{:S(2)}, u32[]{:S(2)}) collective-permute-start(bf16[512,1024]{1,0:T(8,128)(2,1)} %get-tuple-element.81), channel_id=1, source_target_pairs={{0,16},{8,24},{16,0},{24,8},{1,17},{9,25},{17,1},{25,9},{2,18},{10... | collective-permute-start | bytes 3145736 | tf_op jit(solution)/shard_map/ppermute | solution.py:477
  448.9 24.3 %copy-start.16 = (bf16[512,1024]{1,0:T(8,128)(2,1)}, bf16[512,1024]{1,0:T(8,128)(2,1)S(1)}, u32[]{:S(2)}) copy-start(bf16[512,1024]{1,0:T(8,128)(2,1)S(1)} %collective-permute-done.14) | copy-start | bytes 3145732
  448.9 101.0 %collective-permute-start.25 = (bf16[512,1024]{1,0:T(8,128)(2,1)}, bf16[512,1024]{1,0:T(8,128)(2,1)}, u32[]{:S(2)}, u32[]{:S(2)}) collective-permute-start(bf16[512,1024]{1,0:T(8,128)(2,1)} %get-tuple-element.82), channel_id=1, source_target_pairs={{0,24},{8,16},{16,8},{24,0},{1,25},{9,17},{17,9},{25,1},{2,26},{10... | collective-permute-start | bytes 3145736 | tf_op jit(solution)/shard_map/ppermute | solution.py:477
  473.1 4.3 copy-start.33
  473.2 76.7 %copy-start.4 = (bf16[1,512,1024]{2,1,0:T(8,128)(2,1)S(1)}, bf16[1,512,1024]{2,1,0:T(8,128)(2,1)}, u32[]{:S(2)}) copy-start(bf16[1,512,1024]{2,1,0:T(8,128)(2,1)} %param.15) | copy-start | bytes 3145732
  549.9 3.3 copy-start.10
  549.9 3.3 copy-start.13
  557.0 11.5 %copy-start.20 = (bf16[128,1024]{1,0:T(8,128)(2,1)S(1)}, bf16[128,1024]{1,0:T(8,128)(2,1)}, u32[]{:S(2)}) copy-start(bf16[128,1024]{1,0:T(8,128)(2,1)} %param.19) | copy-start | bytes 786436
  557.0 11.7 %copy-start.22 = (bf16[128,512]{1,0:T(8,128)(2,1)S(1)}, bf16[128,512]{1,0:T(8,128)(2,1)}, u32[]{:S(2)}) copy-start(bf16[128,512]{1,0:T(8,128)(2,1)} %param.20) | copy-start | bytes 393220
  557.0 12.5 %copy-start.23 = (bf16[128,512]{1,0:T(8,128)(2,1)S(1)}, bf16[128,512]{1,0:T(8,128)(2,1)}, u32[]{:S(2)}) copy-start(bf16[128,512]{1,0:T(8,128)(2,1)} %param.21) | copy-start | bytes 393220
  568.5 13.1 %copy-start.14 = (f32[4,16,8,256]{3,2,0,1:T(8,128)}, f32[4,16,8,256]{3,2,0,1:T(8,128)S(1)}, u32[]{:S(2)}) copy-start(f32[4,16,8,256]{3,2,0,1:T(8,128)S(1)} %copy.65) | copy-start | bytes 1572868
  (20 other events, 38.7 us)
Sparse Core Ops, SparseCore 0:
  11.5 26.1 all-gather.9
  39.3 28.5 all-gather.11
  69.6 31.1 all-gather.15
  102.8 50.8 all-gather.13
  320.4 37.6 reduce-scatter.6
  360.8 34.8 reduce-scatter.10
  398.1 54.2 reduce-scatter.8
  455.3 30.4 reduce-scatter.4
  488.7 58.5 all-reduce.1
  549.2 29.4 all-gather.19
  580.6 37.4 all-gather.17

commit v2 on v1

v2 whole, which is shorter than its diff:
```python
import functools

import jax
import jax.numpy as jnp
from jax import lax
from jax.experimental import pallas as pl
from jax.experimental.pallas import tpu as pltpu
from jax.sharding import PartitionSpec as P

EPSILON = 1e-05
ROPE_BASE = 1000000.0
LOG2E = 1.4426950408889634
ROWS = 256
LANES = 128
F32 = jnp.float32
BF16 = jnp.bfloat16
COST = pl.CostEstimate(flops=1 << 20, bytes_accessed=1 << 16, transcendentals=0)
VMEM_LIMIT = 58 * 1024 * 1024


def dot_nn(left, right):
    return jnp.dot(left, right, preferred_element_type=F32)


def dot_nt(left, right):
    return lax.dot_general(left, right, (((1,), (1,)), ((), ())), preferred_element_type=F32)


def dot_tn(left, right):
    return lax.dot_general(left, right, (((0,), (0,)), ((), ())), preferred_element_type=F32)


def vmem():
    return pl.BlockSpec(memory_space=pltpu.VMEM)


def smem():
    return pl.BlockSpec(memory_space=pltpu.SMEM)


def params():
    return pltpu.CompilerParams(vmem_limit_bytes=VMEM_LIMIT)


def lane_iota(rows, columns):
    return lax.broadcasted_iota(jnp.int32, (rows, columns), 1)


def row_iota(rows, columns):
    return lax.broadcasted_iota(jnp.int32, (rows, columns), 0)


def at_rows(block, rows=ROWS):
    return pl.ds(pl.multiple_of(block * rows, rows), rows)


def pair_ones(head_dim):
    return (
        row_iota(LANES, LANES) // head_dim == lane_iota(LANES, LANES) // head_dim
    ).astype(BF16)


def head_mean(values, ones, head_dim):
    high = values.astype(BF16)
    low = (values - high.astype(F32)).astype(BF16)
    return (dot_nn(high, ones) + dot_nn(low, ones)) * (1.0 / head_dim)


def turn(values, cosine, sine_up, sine_down, head_dim, sign=1.0):
    half = head_dim // 2
    up = pltpu.roll(values, LANES - half, 1) * sine_up
    down = pltpu.roll(values, half, 1) * sine_down
    return values * cosine + sign * (up + down)


def spread_heads(pair, group, head_dim, low_lanes):
    moved = pltpu.roll(pair, head_dim, 1)
    if group == 0:
        return jnp.where(low_lanes, pair, 0.0), jnp.where(low_lanes, moved, 0.0)
    return jnp.where(low_lanes, 0.0, moved), jnp.where(low_lanes, 0.0, pair)


def first_kernel(me_ref, q_ref, k_ref, v_ref, ga_ref, gf_ref, out_ref):
    at = 0
    for ref in (q_ref, k_ref, v_ref):
        size = ref.shape[1] // 4
        out_ref[:, at:at + size] = ref[:, pl.ds(pl.multiple_of(me_ref[0] * size, size), size)]
        at += size
    depth = out_ref.shape[0]
    row = row_iota(LANES, depth)
    gains = jnp.where(row == 0, ga_ref[...].astype(F32), jnp.where(row == 1, gf_ref[...].astype(F32), 0.0))
    out_ref[:, at:] = jnp.transpose(gains).astype(BF16)


def first_weights(me, w_query, w_key, w_value, attn_gain, ffn_gain):
    depth = w_query.shape[0]
    width = (w_query.shape[1] + w_key.shape[1] + w_value.shape[1]) // 4 + LANES
    return pl.pallas_call(
        first_kernel,
        out_shape=jax.ShapeDtypeStruct((depth, width), BF16),
        in_specs=[smem()] + [vmem()] * 5,
        out_specs=vmem(),
        compiler_params=params(),
        cost_estimate=COST,
        name="first_weights",
    )(me, w_query, w_key, w_value, attn_gain[None], ffn_gain[None])


def qkv_kernel(
    head_dim, x0_ref, x1_ref, x2_ref, x3a_ref, x3b_ref, w_ref, ocol_ref, cos_ref, su_ref, sd_ref,
    qg_ref, kg_ref, normed_ref, qx_ref, k_ref, v_ref, vx_ref, kt_ref, rawq_ref, rawk_ref, gain_ref, raw_ref,
):
    i = pl.program_id(0)
    tok = x0_ref.shape[0]
    all_rows, width = raw_ref.shape
    pairs = rawq_ref.shape[1] // LANES

    @pl.when(i == 0)
    def _():
        gain_ref[...] = jnp.transpose(w_ref[:, width:].astype(F32))[:8]

    def project(x, rows):
        x = x.astype(F32)
        r1 = lax.rsqrt(jnp.mean(x * x, axis=1, keepdims=True) + EPSILON)
        normed = (x * r1 * gain_ref[0:1, :]).astype(BF16)
        normed_ref[...] = normed
        raw_ref[rows, :] = dot_nn(normed, w_ref[:, :width]).astype(BF16)

    for d, refs in enumerate(((x0_ref,), (x1_ref,), (x2_ref,), (x3a_ref, x3b_ref))):

        @pl.when(i == d)
        def _(d=d, refs=refs):
            project(jnp.concatenate([ref[...] for ref in refs], axis=1), slice(d * tok, (d + 1) * tok))

    @pl.when(i >= 4)
    def _():
        ones = pair_ones(head_dim)
        low_lanes = lane_iota(tok, LANES) < head_dim
        pick = (ocol_ref[...] == lane_iota(tok, all_rows)).astype(F32).astype(BF16)
        dealt = dot_nn(pick, raw_ref[...])
        cosine, su, sd = cos_ref[...], su_ref[...], sd_ref[...]
        for g in range(pairs):
            raw = dealt[:, g * LANES:(g + 1) * LANES]
            rawq_ref[:, g * LANES:(g + 1) * LANES] = raw.astype(BF16)
            rq = lax.rsqrt(head_mean(raw * raw, ones, head_dim) + EPSILON)
            pair = turn(raw * rq * qg_ref[...], cosine, su, sd, head_dim)
            for r, one in enumerate(spread_heads(pair, g, head_dim, low_lanes)):
                qx_ref[2 * g + r] = one.astype(BF16)
        raw = dealt[:, pairs * LANES:(pairs + 1) * LANES]
        rawk_ref[...] = raw.astype(BF16)
        rk = lax.rsqrt(head_mean(raw * raw, ones, head_dim) + EPSILON)
        keys = turn(raw * rk * kg_ref[...], cosine, su, sd, head_dim)
        k_ref[...] = keys.astype(BF16)
        kt_ref[...] = jnp.transpose(keys).astype(BF16)
        values = dealt[:, (pairs + 1) * LANES:]
        v_ref[...] = values.astype(BF16)
        vx_ref[0] = jnp.where(low_lanes, values, 1.0).astype(BF16)
        vx_ref[1] = jnp.where(low_lanes, 1.0, values).astype(BF16)


def fixed(array):
    return pl.BlockSpec(array.shape, lambda i: (0,) * array.ndim, pipeline_mode=pl.Buffered(1))


def qkv(xs, w, ocol, cosine, su, sd, qg, kg, head_dim):
    tok, width = xs[0].shape
    all_rows = 4 * tok
    out = lambda *dims: jax.ShapeDtypeStruct(dims, BF16)
    late = lambda c: pl.BlockSpec((tok, c), lambda i: (jnp.maximum(i - 4, 0), 0))
    heads = lambda n: pl.BlockSpec((n, tok, LANES), lambda i: (0, jnp.maximum(i - 4, 0), 0))
    return pl.pallas_call(
        functools.partial(qkv_kernel, head_dim),
        grid=(8,),
        out_shape=(
            out(all_rows, width), out(4, all_rows, LANES), out(all_rows, LANES), out(all_rows, LANES),
            out(2, all_rows, LANES), out(LANES, all_rows), out(all_rows, 2 * LANES), out(all_rows, LANES),
            jax.ShapeDtypeStruct((8, width), F32),
        ),
        in_specs=[fixed(x) for x in xs] + [fixed(w), late(1)] + [late(LANES)] * 3 + [fixed(qg), fixed(kg)],
        out_specs=(
            pl.BlockSpec((tok, width), lambda i: (jnp.minimum(i, 3), 0)),
            heads(4), late(LANES), late(LANES), heads(2),
            pl.BlockSpec((LANES, tok), lambda i: (0, jnp.maximum(i - 4, 0))), late(2 * LANES), late(LANES),
            pl.BlockSpec((8, width), lambda i: (0, 0)),
        ),
        scratch_shapes=[pltpu.VMEM((all_rows, 4 * LANES), BF16)],
        compiler_params=params(),
        cost_estimate=COST,
        name="qkv",
    )(*xs, w, ocol, cosine, su, sd, qg, kg)


def row_starts(lens_ref, index):
    start = jnp.zeros_like(index)
    end = lens_ref[0, 0]
    for s in range(1, lens_ref.shape[1]):
        start = jnp.where(index >= end, end, start)
        end = end + lens_ref[0, s]
    return start


def attend_kernel(head_dim, group, block, lens_ref, orow_ref, qx_ref, k_ref, vx_ref, *refs):
    given_ref, dealt_ref, lse_ref = refs[-3:]
    all_rows = k_ref.shape[0]
    scale = LOG2E * head_dim ** -0.5
    low_lanes = lane_iota(block, LANES) < head_dim
    mass_row = head_dim if group == 0 else 0

    def query_block(i, carry):
        rows = at_rows(i, block)
        q_index = i * block + row_iota(block, 1)
        start = row_starts(lens_ref, q_index)
        first = row_starts(lens_ref, i * block) // block
        clear = jnp.minimum((row_starts(lens_ref, i * block + block - 1) + block - 1) // block, i)
        queries = [qx_ref[r, rows, :] for r in range(2)]

        def step(j, state, masked):
            columns = at_rows(j, block)
            keys, values = k_ref[columns, :], vx_ref[0, columns, :]
            k_index = j * block + lane_iota(block, block)
            keep = (k_index <= q_index) & (k_index >= start)
            new = []
            for r in range(2):
                weights = jnp.exp2(dot_nt(queries[r], keys) * scale)
                if masked:
                    weights = jnp.where(keep, weights, 0.0)
                new.append(state[r] + dot_nn(weights.astype(BF16), values))
            return tuple(new)

        state = (jnp.zeros((block, LANES), F32),) * 2
        state = lax.fori_loop(first, clear, functools.partial(step, masked=True), state)
        state = lax.fori_loop(clear, i, functools.partial(step, masked=False), state)
        state = step(i, state, True)
        out = []
        for r in range(2):
            lse_ref[r:r + 1, rows] = jnp.log2(jnp.transpose(state[r])[mass_row:mass_row + 1, :])
            out.append(state[r] / pltpu.roll(state[r], head_dim, 1))
        if group == 0:
            pair = jnp.where(low_lanes, out[0], pltpu.roll(out[1], head_dim, 1))
        else:
            pair = jnp.where(low_lanes, pltpu.roll(out[0], head_dim, 1), out[1])
        dealt_ref[rows, :] = pair.astype(BF16)
        return carry

    lax.fori_loop(0, all_rows // block, query_block, 0)

    def undeal(i, carry):
        rows = at_rows(i, block)
        pick = (orow_ref[...] == i * block + row_iota(block, all_rows)).astype(F32).astype(BF16)
        given_ref[rows, :] = dot_nn(pick, dealt_ref[...]).astype(BF16)
        return carry

    lax.fori_loop(0, all_rows // block, undeal, 0)


def attend(group, lens, orow, qx, k, vx, head_dim, after):
    all_rows = k.shape[0]
    whole = lambda *dims: pl.BlockSpec(dims, lambda i: (0,) * len(dims))
    return pl.pallas_call(
        functools.partial(attend_kernel, head_dim, group, all_rows // 4),
        grid=(1,),
        out_shape=(
            jax.ShapeDtypeStruct((all_rows, LANES), BF16),
            jax.ShapeDtypeStruct((all_rows, LANES), BF16),
            jax.ShapeDtypeStruct((2, all_rows), F32),
        ),
        in_specs=[
            smem(), whole(1, all_rows),
            pl.BlockSpec((2, all_rows, LANES), lambda i: (group, 0, 0)),
            whole(all_rows, LANES),
            pl.BlockSpec((1, all_rows, LANES), lambda i: (group, 0, 0)),
        ] + anywhere(after),
        out_specs=(whole(all_rows, LANES), whole(all_rows, LANES), whole(2, all_rows)),
        compiler_params=params(),
        cost_estimate=COST,
        name="attend",
    )(lens, orow, qx, k, vx, *after)


def attend_back_kernel(head_dim, *refs):
    (lens_ref, ocol_ref, qx_ref, k_ref, v_ref, kt_ref, lse0_ref, lse1_ref, o0_ref, o1_ref,
     d0_ref, d1_ref, d2_ref, d3_ref, rawq_ref, rawk_ref, cos_ref, su_ref, sd_ref, qg_ref, kg_ref) = refs[:21]
    draw_ref, gain_ref, dgiven_ref, dx_ref, delta_ref, dk_ref, dv_ref = refs[-7:]
    all_rows = k_ref.shape[0]
    blocks = all_rows // ROWS
    exponent = LOG2E * head_dim ** -0.5
    scale = head_dim ** -0.5
    low_lanes = lane_iota(ROWS, LANES) < head_dim
    tok = d0_ref.shape[0]
    for d, ref in enumerate((d0_ref, d1_ref, d2_ref, d3_ref)):
        dgiven_ref[d * tok:(d + 1) * tok, :] = ref[...]
    dk_ref[...] = jnp.zeros_like(dk_ref)
    dv_ref[...] = jnp.zeros_like(dv_ref)
    gain_ref[...] = jnp.zeros_like(gain_ref)

    def deal(i, carry):
        rows = at_rows(i)
        pick = (ocol_ref[rows, :] == lane_iota(ROWS, all_rows)).astype(F32).astype(BF16)
        dealt = dot_nn(pick, dgiven_ref[...])
        for g, o_ref in enumerate((o0_ref, o1_ref)):
            pair = dealt[:, g * LANES:(g + 1) * LANES]
            for r, one in enumerate(spread_heads(pair, g, head_dim, low_lanes)):
                dx_ref[2 * g + r, rows, :] = one.astype(BF16)
            across = jnp.transpose(pair * o_ref[rows, :].astype(F32))
            for r in range(2):
                delta_ref[2 * g + r:2 * g + r + 1, rows] = jnp.sum(
                    across[r * head_dim:(r + 1) * head_dim], axis=0, keepdims=True
                )
        return carry

    lax.fori_loop(0, blocks, deal, 0)
    ones = pair_ones(head_dim)

    def query_block(i, carry):
        rows = at_rows(i)
        q_index = i * ROWS + lane_iota(1, ROWS)
        start = row_starts(lens_ref, q_index)
        first = row_starts(lens_ref, i * ROWS) // ROWS

        def step(j, state):
            columns = at_rows(j)
            k_index = j * ROWS + row_iota(ROWS, ROWS)
            keep = (k_index <= q_index) & (k_index >= start)
            keys = k_ref[columns, :]
            values = v_ref[columns, :]
            new = []
            dk, dv = dk_ref[columns, :], dv_ref[columns, :]
            for h in range(4):
                g = h // 2
                queries = qx_ref[h, rows, :]
                grads = dx_ref[h, rows, :]
                lse = (lse0_ref, lse1_ref)[g][h % 2:h % 2 + 1, rows]
                weights = jnp.where(keep, jnp.exp2(dot_nt(keys, queries) * exponent - lse), 0.0)
                d_weights = dot_nt(values, grads)
                d_scores = (weights * (d_weights - delta_ref[h:h + 1, rows])).astype(BF16)
                dv = dv + dot_nn(weights.astype(BF16), grads)
                dk = dk + dot_nn(d_scores, queries)
                new.append(state[h] + dot_nn(kt_ref[g * head_dim:(g + 1) * head_dim, columns], d_scores))
            dk_ref[columns, :] = dk
            dv_ref[columns, :] = dv
            return tuple(new)

        state = lax.fori_loop(first, i + 1, step, (jnp.zeros((head_dim, ROWS), F32),) * 4)
        cosine, su, sd = cos_ref[rows, :], su_ref[rows, :], sd_ref[rows, :]
        for g in range(2):
            pair = jnp.transpose(jnp.concatenate(state[2 * g:2 * g + 2], axis=0)) * scale
            lanes = slice(g * LANES, (g + 1) * LANES)
            draw, gain = norm_back(
                pair, rawq_ref[rows, lanes].astype(F32), qg_ref[...], cosine, su, sd, ones, head_dim
            )
            draw_ref[rows, lanes] = draw
            gain_ref[0:1, :] += gain
        return carry

    lax.fori_loop(0, blocks, query_block, 0)

    def key_block(i, carry):
        rows = at_rows(i)
        cosine, su, sd = cos_ref[rows, :], su_ref[rows, :], sd_ref[rows, :]
        draw, gain = norm_back(
            dk_ref[rows, :] * scale, rawk_ref[rows, :].astype(F32), kg_ref[...], cosine, su, sd, ones, head_dim
        )
        draw_ref[rows, 2 * LANES:3 * LANES] = draw
        draw_ref[rows, 3 * LANES:] = dv_ref[rows, :].astype(BF16)
        gain_ref[1:2, :] += gain
        return carry

    lax.fori_loop(0, blocks, key_block, 0)


def rows_back_kernel(orow_ref, draw_ref, *refs):
    grad_ref, refs = refs[-5], refs[-4:]
    i = pl.program_id(0)
    all_rows = draw_ref.shape[0]
    rows = grad_ref.shape[0]
    pick = (orow_ref[...] == i * rows + row_iota(rows, all_rows)).astype(F32).astype(BF16)
    grads = dot_nn(pick, draw_ref[...]).astype(BF16)
    grad_ref[...] = grads
    for d, ref in enumerate(refs):

        @pl.when(i == d)
        def _(ref=ref):
            ref[...] = grads


def norm_back(pair, raw, gain, cosine, su, sd, ones, head_dim):
    pair = pair.astype(BF16).astype(F32)
    u = turn(pair, cosine, su, sd, head_dim, -1.0)
    r = lax.rsqrt(head_mean(raw * raw, ones, head_dim) + EPSILON)
    unit = raw * r
    scaled = u * gain
    draw = r * (scaled - unit * head_mean(scaled * unit, ones, head_dim))
    return draw.astype(BF16), jnp.sum(u * unit, axis=0, keepdims=True)


def anywhere(arrays):
    return [pl.BlockSpec(memory_space=pl.ANY)] * len(arrays)


def attend_back(lens, ocol, qx, k, v, kt, lses, dealts, grads, rawq, rawk, cosine, su, sd, qg, kg, head_dim, after):
    all_rows = k.shape[0]
    return pl.pallas_call(
        functools.partial(attend_back_kernel, head_dim),
        out_shape=(
            jax.ShapeDtypeStruct((all_rows, 4 * LANES), BF16),
            jax.ShapeDtypeStruct((2, LANES), F32),
        ),
        in_specs=[smem()] + [vmem()] * 20 + anywhere(after),
        out_specs=(vmem(),) * 2,
        scratch_shapes=[
            pltpu.VMEM((all_rows, 2 * LANES), BF16),
            pltpu.VMEM((4, all_rows, LANES), BF16),
            pltpu.VMEM((4, all_rows), F32),
            pltpu.VMEM((all_rows, LANES), F32),
            pltpu.VMEM((all_rows, LANES), F32),
        ],
        compiler_params=params(),
        cost_estimate=COST,
        name="attend_back",
    )(lens, ocol, qx, k, v, kt, *lses, *dealts, *grads, rawq, rawk, cosine, su, sd, qg, kg, *after)


def rows_back(orow, draw, after):
    all_rows, width = draw.shape
    tok = all_rows // 4
    block = pl.BlockSpec((tok, width), lambda i: (i, 0))
    return pl.pallas_call(
        rows_back_kernel,
        grid=(4,),
        out_shape=(jax.ShapeDtypeStruct(draw.shape, BF16),) + (jax.ShapeDtypeStruct((tok, width), BF16),) * 4,
        in_specs=[fixed(orow), fixed(draw)] + anywhere(after),
        out_specs=(block,) + (pl.BlockSpec((tok, width), lambda i: (0, 0)),) * 4,
        compiler_params=params(),
        cost_estimate=COST,
        name="rows_back",
    )(orow, draw, *after)


def tokens_kernel(me_ref, g0_ref, g1_ref, g2_ref, g3_ref, w_ref, x_ref, mid_ref, gain_ref, *refs):
    out_ref = refs[-1]
    me = me_ref[0]
    d_normed = jnp.zeros(x_ref.shape, F32)
    span, width = 2 * LANES, 8 * LANES
    for d, ref in enumerate((g0_ref, g1_ref, g2_ref, g3_ref)):
        other = jnp.bitwise_xor(me, d)
        take = lambda at, size: w_ref[:, pl.ds(pl.multiple_of(at + other * size, size), size)]
        weights = jnp.concatenate([take(0, span), take(width, LANES), take(width + 4 * LANES, LANES)], axis=1)
        d_normed = d_normed + dot_nt(ref[...], weights)
    x = x_ref[...].astype(F32)
    r1 = lax.rsqrt(jnp.mean(x * x, axis=1, keepdims=True) + EPSILON)
    scaled = d_normed * gain_ref[...]
    pull = jnp.mean(scaled * x, axis=1, keepdims=True)
    out_ref[...] = (mid_ref[...] + r1 * scaled - x * (r1 * r1 * r1 * pull)).astype(BF16)


def tokens_back(me, grads, w, x, d_middle, gain, after):
    tok, width = x.shape
    rows = lambda c: pl.BlockSpec((ROWS, c), lambda i: (i, 0))
    return pl.pallas_call(
        tokens_kernel,
        grid=(tok // ROWS,),
        out_shape=jax.ShapeDtypeStruct((tok, width), BF16),
        in_specs=[smem()] + [rows(grads[0].shape[1])] * 4 + [fixed(w), rows(width), rows(width), fixed(gain)] + anywhere(after),
        out_specs=rows(width),
        compiler_params=params(),
        cost_estimate=COST,
        name="tokens_back",
    )(me, *grads, w, x, d_middle, gain, *after)


def ffn_kernel(per, blocks, n_carried, *refs):
    me_ref, att, refs = refs[0], refs[1:9], list(refs[9:])
    take = lambda n: [refs.pop(0) for _ in range(n)]
    xs = [take(2 if d == 3 else 1) for d in blocks]
    cots = [take(2 if d == 3 else 1) for d in blocks]
    wo_ref, gain_ref, wgu_ref, wd_ref = take(4)
    diag = take(2) if blocks == (1, 2) else None
    take(n_carried)
    nf_ref, hid_ref, dgu_ref, cot_ref = take(4)
    i = pl.program_id(0)
    me = me_ref[0]
    hidden_units = hid_ref.shape[1]
    which = i // per

    def read(lists):
        parts = [jnp.concatenate([ref[...] for ref in one], axis=1) for one in lists]
        return parts[0] if len(parts) == 1 else jnp.where(which == 0, parts[0], parts[1])

    middle = read(xs).astype(F32)
    for d in range(4):
        block = jnp.concatenate([att[2 * d][...], att[2 * d + 1][...]], axis=1)
        middle = middle + dot_nn(block, wo_ref[at_rows(jnp.bitwise_xor(me, d), 2 * LANES), :])
    r2 = lax.rsqrt(jnp.mean(middle * middle, axis=1, keepdims=True) + EPSILON)
    nf = (middle * r2 * gain_ref[...]).astype(BF16)
    nf_ref[...] = nf
    cot = read(cots)
    cot_ref[...] = cot
    wg, wu = wgu_ref[:, :hidden_units], wgu_ref[:, hidden_units:]
    gate = dot_nn(nf, wg)
    up = dot_nn(nf, wu)
    s = jax.nn.sigmoid(gate)
    silu = gate * s
    hidden = (silu * up).astype(BF16)
    hid_ref[...] = hidden
    d_hidden = dot_nt(cot, wd_ref[...])
    d_gate = (d_hidden * up * s * (1.0 + gate * (1.0 - s))).astype(BF16)
    d_up = (d_hidden * silu).astype(BF16)
    dgu_ref[:, :hidden_units] = d_gate
    dgu_ref[:, hidden_units:] = d_up
    dn = dot_nt(d_gate, wg) + dot_nt(d_up, wu)
    bo = dot_nn(hidden, wd_ref[...])
    half = dn.shape[1] // 2
    if blocks == (3,):
        dna_ref, dnb_ref, bo_ref = take(3)
        dna_ref[...] = dn[:, :half].astype(BF16)
        dnb_ref[...] = dn[:, half:].astype(BF16)
        bo_ref[...] = bo.astype(BF16)
    elif blocks == (0,):
        dn_ref, bo_ref, mid_ref = take(3)
        dn_ref[...] = dn.astype(BF16)
        bo_ref[...] = bo.astype(BF16)
        mid_ref[...] = middle
    else:
        dn1_ref, dn2_ref, bo1_ref, bo2_ref = take(4)

        @pl.when(which == 0)
        def _():
            dn1_ref[:, :half] = dn[:, :half].astype(BF16)
            dn1_ref[:, half:] = (dn[:, half:] + diag[1][...].astype(F32)).astype(BF16)
            bo1_ref[...] = bo.astype(BF16)

        @pl.when(which == 1)
        def _():
            dn2_ref[:, :half] = (dn[:, :half] + diag[0][...].astype(F32)).astype(BF16)
            dn2_ref[:, half:] = dn[:, half:].astype(BF16)
            bo2_ref[...] = bo.astype(BF16)


def ffn(me, blocks, att, xs, cots, wo, gain, wgu, wd, diag, carried):
    all_rows = att[0].shape[0]
    width, units = wo.shape[1], wd.shape[0]
    tok = all_rows // 4
    per = tok // ROWS
    block_of = lambda i: blocks[0] + (i // per) * (blocks[-1] - blocks[0])
    everywhere = lambda c: pl.BlockSpec((ROWS, c), lambda i: (block_of(i) * per + i % per, 0))
    crossed = lambda d: pl.BlockSpec(
        (ROWS, LANES), lambda i: (jnp.bitwise_xor(block_of(i), d) * per + i % per, 0)
    )
    held = lambda n, c: pl.BlockSpec((ROWS, c), lambda i: (jnp.clip(i - n * per, 0, per - 1), 0))
    out = lambda r, c, t=BF16: jax.ShapeDtypeStruct((r, c), t)
    pieces = lambda arrays: [held(n, a.shape[1]) for n, d in enumerate(blocks) for a in arrays[d]]
    shapes = [out(all_rows, width), out(all_rows, units), out(all_rows, 2 * units), out(all_rows, width)]
    specs = [everywhere(width), everywhere(units), everywhere(2 * units), everywhere(width)]
    if blocks == (3,):
        shapes += [out(tok, width // 2)] * 2 + [out(tok, width)]
        specs += [held(0, width // 2)] * 2 + [held(0, width)]
    elif blocks == (0,):
        shapes += [out(tok, width)] * 2 + [out(tok, width, F32)]
        specs += [held(0, width)] * 3
    else:
        shapes += [out(tok, width)] * 4
        specs += [held(0, width), held(1, width)] * 2
    diag_specs = [held(1, width // 2), held(0, width // 2)] if diag else []
    operands = (
        [me] + list(att) + [a for d in blocks for a in xs[d]] + [a for d in blocks for a in cots[d]]
        + [wo, gain, wgu, wd] + list(diag) + list(carried)
    )
    first = len(operands) - len(carried)
    return pl.pallas_call(
        functools.partial(ffn_kernel, per, blocks, len(carried)),
        grid=(len(blocks) * per,),
        out_shape=tuple(shapes),
        in_specs=[smem()] + [crossed(d) for d in range(4) for _ in range(2)] + pieces(xs) + pieces(cots)
        + [fixed(wo), fixed(gain), fixed(wgu), fixed(wd)] + diag_specs + anywhere(carried),
        out_specs=tuple(specs),
        input_output_aliases={first + n: n for n in range(len(carried))},
        compiler_params=params(),
        cost_estimate=COST,
        name="ffn",
    )(*operands)


def weights_kernel(left_ref, right_ref, out_ref):
    out_ref[...] = dot_tn(left_ref[...], right_ref[...]).astype(BF16)


def weights_back(left, right, steps):
    rows, depth = left.shape
    return pl.pallas_call(
        weights_kernel,
        grid=(steps,),
        out_shape=jax.ShapeDtypeStruct((depth, right.shape[1]), BF16),
        in_specs=[pl.BlockSpec((rows, depth // steps), lambda i: (0, i)), fixed(right)],
        out_specs=pl.BlockSpec((depth // steps, right.shape[1]), lambda i: (i, 0)),
        compiler_params=params(),
        cost_estimate=COST,
        name="weights_back",
    )(left, right)


def last_kernel(period, normed_ref, grads_ref, o0_ref, o1_ref, o2_ref, o3_ref, gain_ref, out_ref):
    width, extra = grads_ref.shape[1], o0_ref.shape[1]
    out_ref[:, :width] = dot_tn(normed_ref[...], grads_ref[...]).astype(BF16)
    total = o0_ref[...].astype(F32)
    for ref in (o1_ref, o2_ref, o3_ref):
        total = total + ref[...].astype(F32)
    out_ref[:, width:width + extra] = total.astype(BF16)
    place = row_iota(out_ref.shape[0], LANES) % period
    gains = jnp.where(place == 0, gain_ref[0:1, :], jnp.where(place == 1, gain_ref[1:2, :], 0.0))
    out_ref[:, width + extra:] = gains.astype(BF16)


def last_weights(normed, grads, parts, gains, shards):
    rows, depth = normed.shape
    steps, extra = 4, parts[0].shape[1]
    block = lambda c: pl.BlockSpec((depth // steps, c), lambda i: (i, 0))
    return pl.pallas_call(
        functools.partial(last_kernel, depth // shards),
        grid=(steps,),
        out_shape=jax.ShapeDtypeStruct((depth, grads.shape[1] + extra + LANES), BF16),
        in_specs=[pl.BlockSpec((rows, depth // steps), lambda i: (0, i)), fixed(grads)] + [block(extra)] * 4 + [fixed(gains)],
        out_specs=block(grads.shape[1] + extra + LANES),
        compiler_params=params(),
        cost_estimate=COST,
        name="last_weights",
    )(normed, grads, *parts, gains)


def middle_kernel(*refs):
    me_ref, dn_refs = refs[0], refs[1:4]
    cot_ref, mid_ref, gain_ref, wo_ref = refs[4:8]
    dmid_ref, branch_ref, da_refs = refs[-6], refs[-5], refs[-4:]
    me = me_ref[0]
    tok = mid_ref.shape[0]

    def rows_of(i, carry):
        rows = at_rows(i)
        middle = mid_ref[rows, :]
        d_normed = dn_refs[0][rows, :].astype(F32)
        for ref in dn_refs[1:]:
            d_normed = d_normed + ref[rows, :].astype(F32)
        r2 = lax.rsqrt(jnp.mean(middle * middle, axis=1, keepdims=True) + EPSILON)
        scaled = d_normed * gain_ref[...]
        pull = jnp.mean(scaled * middle, axis=1, keepdims=True)
        d_middle = cot_ref[rows, :].astype(F32) + r2 * scaled - middle * (r2 * r2 * r2 * pull)
        dmid_ref[rows, :] = d_middle
        branch_ref[rows, :] = d_middle.astype(BF16)
        return carry

    lax.fori_loop(0, tok // ROWS, rows_of, 0)
    span = 2 * LANES
    for d in range(4):
        there = pl.ds(pl.multiple_of(jnp.bitwise_xor(me, d) * span, span), span)
        da_refs[d][...] = dot_nt(branch_ref[...], wo_ref[there, :]).astype(BF16)


def out_kernel(me_ref, *refs):
    att_refs, branch_ref, outs = refs[:8], refs[8], refs[9:]
    span = 2 * LANES
    for d in range(4):
        there = pl.ds(pl.multiple_of(jnp.bitwise_xor(me_ref[0], d) * span, span), span)
        rows = jnp.concatenate([att_refs[2 * d][...], att_refs[2 * d + 1][...]], axis=1)
        for e in range(4):
            columns = pl.ds(pl.multiple_of(jnp.bitwise_xor(me_ref[0], e) * span, span), span)
            outs[e][there, :] = dot_tn(rows, branch_ref[:, columns]).astype(BF16)


def out_weights(me, att, branch):
    tok, width = branch.shape
    whole = lambda r, c: pl.BlockSpec((r, c), lambda i: (0, 0))
    own = lambda d: pl.BlockSpec((tok, LANES), lambda i: (d, 0))
    return pl.pallas_call(
        out_kernel,
        grid=(1,),
        out_shape=(jax.ShapeDtypeStruct((width, width // 4), BF16),) * 4,
        in_specs=[smem()] + [own(d) for d in range(4) for _ in range(2)] + [whole(tok, width)],
        out_specs=(whole(width, width // 4),) * 4,
        compiler_params=params(),
        cost_estimate=COST,
        name="out_weights",
    )(me, *att, branch)


def middle_back(me, parts, cot, middle, gain, wo, after):
    tok, width = middle.shape
    whole = lambda r, c: pl.BlockSpec((r, c), lambda i: (0, 0))
    out = lambda r, c, t=BF16: jax.ShapeDtypeStruct((r, c), t)
    return pl.pallas_call(
        middle_kernel,
        grid=(1,),
        out_shape=(out(tok, width, F32), out(tok, width)) + (out(tok, 2 * LANES),) * 4,
        in_specs=[smem()] + [whole(tok, width)] * 5 + [whole(1, width), whole(*wo.shape)] + anywhere(after),
        out_specs=(whole(tok, width),) * 2 + (whole(tok, 2 * LANES),) * 4,
        compiler_params=params(),
        cost_estimate=COST,
        name="middle_back",
    )(me, *parts, cot, middle, gain, wo, *after)


def swap(array, distance):
    return lax.ppermute(array, "seq", [(s, s ^ distance) for s in range(4)])


def gather_rows(block, meanwhile):
    half = block.shape[1] // 2
    one, two = swap(block, 1), swap(block, 2)
    one, two, meanwhile = lax.optimization_barrier((one, two, meanwhile))
    return [meanwhile, [one], [two], [swap(one[:, :half], 2), swap(two[:, half:], 1)]]


def after(value, *others):
    return lax.optimization_barrier((value, others))[0]


def body(
    tokens, order, seq_lengths, attn_gain, w_query, w_key, w_value, query_gain, key_gain,
    w_out, ffn_gain, w_gate, w_up, w_down, cotangent,
):
    tok = tokens.shape[1]
    ways = lax.axis_size("seq")
    shards = lax.axis_size("shard")
    all_rows = tok * ways
    head_dim = query_gain.shape[0]
    me = lax.axis_index("seq")
    me_arr = me.astype(jnp.int32)[None]
    own = lambda a, axis: lax.dynamic_slice_in_dim(a, me * (a.shape[axis] // ways), a.shape[axis] // ways, axis)
    depth = w_gate.shape[0]
    units = w_gate.shape[1] // ways
    piece = units // shards

    dealt_index = jnp.arange(all_rows, dtype=jnp.int32)
    ends = jnp.cumsum(seq_lengths[0])
    start = jnp.zeros_like(dealt_index)
    for s in range(seq_lengths.shape[1] - 1):
        start = jnp.where(dealt_index >= ends[s], ends[s], start)
    places = (dealt_index - start).astype(F32)
    lane = jnp.arange(LANES, dtype=jnp.int32) % head_dim
    half = head_dim // 2
    frequency = ROPE_BASE ** (-2.0 * jnp.arange(half, dtype=F32) / head_dim)
    angles = places[:, None] * frequency[None, :]
    cosine = jnp.tile(jnp.cos(angles), (1, LANES // half))
    sine = jnp.tile(jnp.sin(angles), (1, LANES // half))
    sine_up = jnp.where(lane[None, :] < half, -sine, 0.0)
    sine_down = jnp.where(lane[None, :] < half, 0.0, sine)
    relative = jnp.bitwise_xor(order[0], me.astype(jnp.int32) * tok)
    ocol, orow = relative[:, None], relative[None, :]
    q_gain = jnp.tile(query_gain.astype(F32), LANES // head_dim)[None, :]
    k_gain = jnp.tile(key_gain.astype(F32), LANES // head_dim)[None, :]

    tables = (cosine, sine_up, sine_down, ocol, orow, q_gain, k_gain)

    xs = gather_rows(tokens[0], tables)
    w_first = first_weights(me_arr, w_query, w_key, w_value, attn_gain, ffn_gain)
    w_qkv = lax.all_gather(w_first, "shard", axis=0, tiled=True)
    w_o = lax.all_gather(w_out, "shard", axis=0, tiled=True)
    cut = lambda w: own(w.reshape(depth, shards, ways, piece), 2).reshape(depth, units)
    w_gate_now, w_up_now, w_down_now = after((w_gate, w_up, w_down), tables)
    w_gu = lax.all_gather(jnp.concatenate([cut(w_gate_now), cut(w_up_now)], axis=1), "shard", axis=0, tiled=True)
    w_d = lax.all_gather(own(w_down_now, 0), "shard", axis=0, tiled=True)

    cosine, sine_up, sine_down, ocol, orow, q_gain, k_gain = xs[0]
    xs = [[tokens[0]]] + xs[1:]
    normed, qx, k, v, vx, kt, rawq, rawk, gains = qkv(
        [x for one in xs for x in one], w_qkv, ocol, cosine, sine_up, sine_down, q_gain, k_gain, head_dim
    )
    cot = cotangent[0]
    cots = [[cot]] + gather_rows(after(cot, xs[3]), ())[1:]
    gain_a, gain_f = gains[0:1], gains[1:2]
    w_rows = jnp.concatenate(after([w_query, w_key, w_value], xs[3]), axis=1)
    w_all = lax.all_gather(w_rows, "shard", axis=0, tiled=True)

    att, dealts, lses = [], [], []
    for g in range(2):
        given, dealt, lse = attend(g, seq_lengths, orow, qx, k, vx, head_dim, cots[3] if g else [])
        att.append([given] + [swap(given, d) for d in (1, 2, 3)])
        dealts.append(dealt)
        lses.append(lse)
    att = [att[g][d] for d in range(4) for g in range(2)]

    feed = lambda blocks, diag, carried: ffn(
        me_arr, blocks, att, xs, cots, w_o, gain_f, w_gu, w_d, diag, carried
    )
    *carried, dn3a, dn3b, bo3 = feed((3,), (), ())
    diag = (swap(dn3a, 1), swap(dn3b, 2))
    *carried, dn0, bo0, middle = feed((0,), (), carried)
    bo3 = swap(after(bo3, diag), 3)
    *carried, dn1, dn2, bo1, bo2 = feed((1, 2), diag, carried)
    nf, hidden, d_gu, cot_all = carried
    dn1, dn2 = after((dn1, dn2), bo3)
    dn = (dn0, swap(dn1, 1), swap(dn2, 2))
    scatter = lambda a: lax.psum_scatter(a, "shard", scatter_dimension=0, tiled=True)
    p_wd, p_wgu = weights_back(hidden, cot_all, 3), weights_back(nf, d_gu, 4)
    p_wd, p_wgu = after((p_wd, p_wgu), dn)
    d_wd, d_wgu = scatter(p_wd), scatter(p_wgu)

    d_middle, branch, *d_att = middle_back(me_arr, dn, cot, middle, gain_f, w_o, (p_wd, p_wgu, w_all))
    p_wo = out_weights(me_arr, att, branch)
    d_att = [d_att[0]] + [swap(d_att[d], d) for d in (1, 2, 3)]
    draw, head_gains = attend_back(
        seq_lengths, ocol, qx, k, v, kt, lses, dealts, d_att, rawq, rawk,
        cosine, sine_up, sine_down, q_gain, k_gain, head_dim, (d_wd,),
    )
    bo1, bo2, *p_wo = after([bo1, bo2] + list(p_wo), d_att)
    bo = [bo0, swap(bo1, 1), swap(bo2, 2), bo3]
    p_wo = [p_wo[0]] + [swap(p_wo[d], d) for d in (1, 2, 3)]
    grads, *d_raw = rows_back(orow, draw, bo[1:3] + p_wo[1:])
    block_out = (middle + sum(b.astype(F32) for b in after(bo, grads))).astype(BF16)
    d_raw = [d_raw[0]] + [swap(d_raw[d], d) for d in (1, 2, 3)]
    p_last = last_weights(normed, grads, p_wo, head_gains, shards)
    d_last = scatter(after(p_last, d_wgu))
    d_tokens = tokens_back(me_arr, d_raw, w_all, tokens[0], d_middle, gain_a, (p_last,))
    d_wgu, d_wd = after((d_wgu, d_wd), d_raw, p_last)

    odd, high = me % 2 == 1, me // 2 == 1

    def in_order(parts):
        parts = list(parts)
        for a, b, which in ((0, 1, odd), (2, 3, odd), (0, 2, high), (1, 3, high)):
            parts[a], parts[b] = jnp.where(which, parts[b], parts[a]), jnp.where(which, parts[a], parts[b])
        return parts

    def quarters(part):
        return in_order([part] + [swap(part, d) for d in (1, 2, 3)])

    d_wd = quarters(d_wd)
    d_wd = jnp.concatenate(d_wd, axis=0).astype(F32)
    columns = lambda parts, at: jnp.stack(
        [p[:, at:at + units].reshape(depth, shards, piece) for p in parts], axis=2
    ).reshape(depth, -1).astype(F32)
    d_wgu = quarters(d_wgu)
    d_wg, d_wu = columns(d_wgu, 0), columns(d_wgu, units)
    last = quarters(after(d_last, d_wgu))
    beside = lambda parts, lo, hi: jnp.concatenate([p[:, lo:hi] for p in parts], axis=1).astype(F32)
    d_wq, d_wk, d_wv = beside(last, 0, 256), beside(last, 256, 384), beside(last, 384, 512)
    d_wo = beside(last, 512, 768)
    dot_rows = lambda w, d: jnp.sum(w.astype(F32) * d, axis=1)
    d_attn_gain = (dot_rows(w_query, d_wq) + dot_rows(w_key, d_wk) + dot_rows(w_value, d_wv)) / attn_gain.astype(F32)
    d_ffn_gain = (dot_rows(w_gate, d_wg) + dot_rows(w_up, d_wu)) / ffn_gain.astype(F32)
    head_gains = sum(p[0:2, 768:768 + LANES].astype(F32) for p in last)
    head_gains = head_gains[:, :head_dim] + head_gains[:, head_dim:]
    return (
        block_out[None], d_tokens[None], d_attn_gain, d_wq, d_wk, d_wv, head_gains[0], head_gains[1],
        d_wo, d_ffn_gain, d_wg, d_wu, d_wd,
    )


def solution(mesh):
    rows, flat, wide = P("shard", None), P("shard"), P("shard", "seq", None)
    in_specs = (
        wide, rows, rows, flat, rows, rows, rows, P(), P(), rows, flat, rows, rows, rows, wide,
    )
    out_specs = (wide, wide, flat, rows, rows, rows, P(), P(), rows, flat, rows, rows, rows)
    return jax.shard_map(body, mesh=mesh, in_specs=in_specs, out_specs=out_specs, check_vma=False)
```

time: 654 us -> 475 us (0.73)
  waiting for transfers between devices: 200 us -> 116 us
  blocking collectives: 83.2 us -> 0 us
  Pallas kernels: 184 us -> 218 us
  matrix products: 33.1 us -> 0 us
  local copies, waits for them, and re-layouts: 68.4 us -> 43.1 us
  starting transfers between devices: 34.1 us -> 56.6 us
    psum x1 -> x0, blocking collectives: 71.8 us -> none  [body(): head_gains = lax.psum(head_gains, ('seq', 'shard'))]
    ppermute x26 -> x39, waiting for transfers between devices: 153 us -> 105 us  [swap(): return lax.ppermute(array, 'seq', [(s, s ^ distance) for s in range(4)])]
    pallas_call x5 -> x14, Pallas kernels: 127 us -> 171 us  [the longest x3 65.3 us: ffn(): pl.pallas_call(functools.partial(ffn_kernel, per, blocks, len(carried)),...]
    all_gather x4 -> x3, waiting for transfers between devices: 42.7 us -> 0.02 us  [the longest x1 0.01 us: body(): lax.all_gather(jnp.concatenate([cut(w_gate_now), cut(w_up_now)], axis=1),...]
    dot_general x5 -> x0, matrix products: 33.1 us -> none  [dot_tn(): lax.dot_general(left, right, (((0,), (0,)), ((), ())), preferred_element_...]
    ppermute x26 -> x39, starting transfers between devices: 33.7 us -> 56.3 us  [swap(): return lax.ppermute(array, 'seq', [(s, s ^ distance) for s in range(4)])]
    unnamed x113 -> x96, local copies, waits for them, and re-layouts: 31.5 us -> 14.4 us
    all_gather x1 -> x0, blocking collectives: 11.4 us -> none  [whole(): return lax.all_gather(part, 'seq', axis=0)]
  transfers between devices with their start and end apart: 37 -> 47, of which waited for: 17 -> 23; matrix products, arithmetic and copies ran while one was open for 15% -> 12% of each run, Pallas kernels for 19% -> 45%
where the time goes in v2:
time: 475 us
  Pallas kernels  218 us (46%)
  waiting for transfers between devices  116 us (24%)
  starting transfers between devices  56.6 us (12%)
  local copies, waits for them, and re-layouts  43.1 us (9%)
  other arithmetic  27.6 us (6%)
  between operations  15 us (3%)
    ppermute x39, waiting for transfers between devices, swap(): return lax.ppermute(array, 'seq', [(s, s ^ distance) for s in range(4)])  105 us
    pallas_call x3, Pallas kernels, ffn(): pl.pallas_call(functools.partial(ffn_kernel, per, blocks, len(carried)),...  65.3 us
    ppermute x39, starting transfers between devices, swap(): return lax.ppermute(array, 'seq', [(s, s ^ distance) for s in range(4)])  56.3 us
    pallas_call x1, Pallas kernels, attend_back(): pl.pallas_call(functools.partial(attend_back_kernel, head_dim), out_shape...  46.9 us
    pallas_call x2, Pallas kernels, attend(): pl.pallas_call(functools.partial(attend_kernel, head_dim, group, all_rows...  27.6 us
    pallas_call x2, Pallas kernels, weights_back(): pl.pallas_call(weights_kernel, grid=(steps,), out_shape=jax.ShapeDtypeStr...  24.8 us
    pallas_call x1, Pallas kernels, qkv(): pl.pallas_call(functools.partial(qkv_kernel, head_dim), grid=(8,), out_sh...  17.4 us
    unnamed x96, local copies, waits for them, and re-layouts  14.4 us
  transfers between devices with their start and end apart: 47, of which 23 were waited for; matrix products, arithmetic and copies ran while one was open for 12% of the time, Pallas kernels for 45%

profile of v2, /device:TPU:0, one launch (start us, length us, event | category | flops | bytes accessed | tf_op | source)
XLA Modules:
  0.0 475.5 jit_solution(7286059225880098869)
XLA Ops:
  7.2 1.9 first_weights.1
  12.8 1.8 multiply_sine_fusion
  16.8 1.5 broadcast_select_fusion.8
  18.3 2.1 tile.12
  25.9 3.0 collective-permute-start
  28.9 1.5 collective-permute-start.1
  30.4 21.6 %collective-permute-done.x1_ref.refs_9_ = bf16[512,1024]{1,0:T(8,128)(2,1)S(1)} collective-permute-done((bf16[512,1024]{1,0:T(8,128)(2,1)S(1)}, bf16[512,1024]{1,0:T(8,128)(2,1)S(1)}, u32[]{:S(2)}, u32[]{:S(2)}) %collective-permute-start) | collective-permute-done | bytes 1048608 | tf_op jit(solution)/shard_map/ppermute | solution.py:701
  52.1 1.5 collective-permute-done.1.x2_ref.refs_10_
  53.6 1.6 collective-permute-start.2
  55.8 10.5 %collective-permute-done.2.x3a_ref.refs_9_ = bf16[512,512]{1,0:T(8,128)(2,1)} collective-permute-done((bf16[512,512]{1,0:T(8,128)(2,1)S(1)}, bf16[512,512]{1,0:T(8,128)(2,1)}, u32[]{:S(2)}, u32[]{:S(2)}) %collective-permute-start.2) | collective-permute-done | bytes 524320 | tf_op jit(solution)/shard_map/ppermute | solution.py:701
  67.7 1.7 pad_maximum_fusion.1
  73.4 17.4 %qkv.1 = (bf16[2048,1024]{1,0:T(8,128)(2,1)}, bf16[4,2048,128]{2,1,0:T(8,128)(2,1)}, bf16[2048,128]{1,0:T(8,128)(2,1)}, bf16[2048,128]{1,0:T(8,128)(2,1)}, bf16[...) custom-call(bf16[512,1024]{1,0:T(8,128)(2,1)} %bitcast.37, ...), custom_call_target="tpu_custom_call" | custom-call | flops 1048576 | bytes 65536 | tf_op jit(solution)/shard_map/qkv/pallas_call | solution.py:171
  90.9 1.6 collective-permute-done.4.refs_11_
  97.0 13.7 %attend.2 = (bf16[2048,128]{1,0:T(8,128)(2,1)}, bf16[2048,128]{1,0:T(8,128)(2,1)}, f32[2,2048]{1,0:T(2,128)}) custom-call(s32[1,3]{1,0:T(1,128)} %refs_0_.1, s32[1,2048]{1,0:T(1,128)} %broadcast_xor_fusion.orow_ref, bf16[4,2048,128]{2,1,0:T(8,128)(2,1)} %get-tuple-element.113.qx_ref.refs_2_, bf16[2048,128]{1,0:T(8,128)(2,1)} %get-tuple-element.114.k_ref.refs_3_, ...), custom_call_target="tpu_custom_call" | custom-call | flops 1048576 | bytes 65536 | tf_op jit(solution)/shard_map/attend/pallas_call | solution.py:259
  110.7 1.5 collective-permute-start.10
  115.9 13.9 %attend.3 = (bf16[2048,128]{1,0:T(8,128)(2,1)}, bf16[2048,128]{1,0:T(8,128)(2,1)}, f32[2,2048]{1,0:T(2,128)}) custom-call(s32[1,3]{1,0:T(1,128)} %refs_0_.1, s32[1,2048]{1,0:T(1,128)} %broadcast_xor_fusion.orow_ref, bf16[4,2048,128]{2,1,0:T(8,128)(2,1)} %get-tuple-element.113.qx_ref.refs_2_, bf16[2048,128]{1,0:T(8,128)(2,1)} %get-tuple-element.114.k_ref.refs_3_, ...), custom_call_target="tpu_custom_call" | custom-call | flops 1048576 | bytes 65536 | tf_op jit(solution)/shard_map/attend/pallas_call | solution.py:259
  129.8 1.5 collective-permute-start.11
  132.2 12.4 %collective-permute-done.10.refs_5_.refs_4_ = bf16[2048,128]{1,0:T(8,128)(2,1)S(1)} collective-permute-done((bf16[2048,128]{1,0:T(8,128)(2,1)}, bf16[2048,128]{1,0:T(8,128)(2,1)S(1)}, u32[]{:S(2)}, u32[]{:S(2)}) %collective-permute-start.10) | collective-permute-done | bytes 524320 | tf_op jit(solution)/shard_map/ppermute | solution.py:701
  145.3 1.4 fusion.14
  146.7 9.3 %collective-permute-done.11.refs_6_.refs_5_ = bf16[2048,128]{1,0:T(8,128)(2,1)S(1)} collective-permute-done((bf16[2048,128]{1,0:T(8,128)(2,1)}, bf16[2048,128]{1,0:T(8,128)(2,1)S(1)}, u32[]{:S(2)}, u32[]{:S(2)}) %collective-permute-start.11) | collective-permute-done | bytes 524320 | tf_op jit(solution)/shard_map/ppermute | solution.py:701
  158.1 17.3 %ffn.3 = (bf16[2048,1024]{1,0:T(8,128)(2,1)}, bf16[2048,1152]{1,0:T(8,128)(2,1)}, bf16[2048,2304]{1,0:T(8,128)(2,1)}, bf16[2048,1024]{1,0:T(8,128)(2,1)}, bf16[5...) custom-call(s32[1]{0:T(128)} %bitcast.me_ref.refs_0_, ...), custom_call_target="tpu_custom_call" | custom-call | flops 1048576 | bytes 65536 | tf_op jit(solution)/shard_map/ffn/pallas_call | solution.py:569
  175.4 1.4 collective-permute-start.14
  177.6 8.9 %collective-permute-done.14.refs_17_ = bf16[512,512]{1,0:T(8,128)(2,1)S(1)} collective-permute-done((bf16[512,512]{1,0:T(8,128)(2,1)}, bf16[512,512]{1,0:T(8,128)(2,1)S(1)}, u32[]{:S(2)}, u32[]{:S(2)}) %collective-permute-start.14) | collective-permute-done | bytes 524320 | tf_op jit(solution)/shard_map/ppermute | solution.py:701
  187.9 10.8 %collective-permute-start.16 = (bf16[512,1024]{1,0:T(8,128)(2,1)}, bf16[512,1024]{1,0:T(8,128)(2,1)S(1)}, u32[]{:S(2)}, u32[]{:S(2)}) collective-permute-start(bf16[512,1024]{1,0:T(8,128)(2,1)} %get-tuple-element.143), channel_id=1, source_target_pairs={{0,24},{8,16},{16,8},{24,0},{1,25},{9,17},{17,9},{25,1},{2,26},{10... | collective-permute-start | bytes 3145736 | tf_op jit(solution)/shard_map/ppermute | solution.py:701
  198.7 16.9 %ffn.4 = (bf16[2048,1024]{1,0:T(8,128)(2,1)}, bf16[2048,1152]{1,0:T(8,128)(2,1)}, bf16[2048,2304]{1,0:T(8,128)(2,1)}, bf16[2048,1024]{1,0:T(8,128)(2,1)}, bf16[5...) custom-call(s32[1]{0:T(128)} %bitcast.me_ref.refs_0_, ...), custom_call_target="tpu_custom_call", output_to_operand_aliasing={{0}: (15, {}), {1}: (16, {}), {2}: (17, {}), {3}: (18, {})} | custom-call | flops 1048576 | bytes 65536 | tf_op jit(solution)/shard_map/ffn/pallas_call | solution.py:569
  215.5 31.2 %ffn.5 = (bf16[2048,1024]{1,0:T(8,128)(2,1)}, bf16[2048,1152]{1,0:T(8,128)(2,1)}, bf16[2048,2304]{1,0:T(8,128)(2,1)}, bf16[2048,1024]{1,0:T(8,128)(2,1)}, bf16[5...) custom-call(s32[1]{0:T(128)} %bitcast.me_ref.refs_0_, ...), custom_call_target="tpu_custom_call", output_to_operand_aliasing={{0}: (19, {}), {1}: (20, {}), {2}: (21, {}), {3}: (22, {})} | custom-call | flops 1048576 | bytes 65536 | tf_op jit(solution)/shard_map/ffn/pallas_call | solution.py:569
  249.2 15.7 %weights_back.3.refs_9_ = bf16[1024,2304]{1,0:T(8,128)(2,1)} custom-call(bf16[2048,1024]{1,0:T(8,128)(2,1)} %get-tuple-element.148.left_ref, bf16[2048,2304]{1,0:T(8,128)(2,1)} %get-tuple-element.149.right_ref), custom_call_target="tpu_custom_call" | custom-call | flops 1048576 | bytes 65536 | tf_op jit(solution)/shard_map/weights_back/pallas_call | solution.py:589
  265.0 9.0 %weights_back.2.refs_8_ = bf16[1152,1024]{1,0:T(8,128)(2,1)} custom-call(bf16[2048,1152]{1,0:T(8,128)(2,1)} %get-tuple-element.146.left_ref, bf16[2048,1024]{1,0:T(8,128)(2,1)} %get-tuple-element.147.right_ref), custom_call_target="tpu_custom_call" | custom-call | flops 1048576 | bytes 65536 | tf_op jit(solution)/shard_map/weights_back/pallas_call | solution.py:589
  275.4 6.8 %middle_back.1 = (f32[512,1024]{1,0:T(8,128)}, bf16[512,1024]{1,0:T(8,128)(2,1)}, bf16[512,256]{1,0:T(8,128)(2,1)}, bf16[512,256]{1,0:T(8,128)(2,1)}, bf16[512,2...) custom-call(s32[1]{0:T(128)} %bitcast.me_ref.refs_0_, bf16[512,1024]{1,0:T(8,128)(2,1)} %get-tuple-element.139.refs_1_, ...), custom_call_target="tpu_custom_call" | custom-call | flops 1048576 | bytes 65536 | tf_op jit(solution)/shard_map/middle_back/pallas_call | solution.py:688
  282.2 1.9 collective-permute-start.19
  284.2 1.5 collective-permute-start.21
  285.7 4.2 out_weights.1
  289.9 1.8 collective-permute-done.19.refs_11_
  291.7 3.8 collective-permute-done.20.refs_12_
  295.5 1.9 collective-permute-done.21.refs_13_
  299.4 2.0 collective-permute-start.23
  302.1 2.8 collective-permute-start.26
  304.9 5.4 %reduce-scatter.4.cloned.1.call-done.refs_21_ = bf16[144,1024]{1,0:T(8,128)(2,1)} async-done(((bf16[1152,1024]{1,0:T(8,128)(2,1)}), bf16[144,1024]{1,0:T(8,128)(2,1)}) %reduce-scatter.4.cloned.1.call-update) | async-done | bytes 294928 | tf_op jit(solution)/shard_map/reduce_scatter | solution.py:791
  310.3 46.9 %attend_back.1 = (bf16[2048,512]{1,0:T(8,128)(2,1)}, f32[2,128]{1,0:T(2,128)}) custom-call(s32[1,3]{1,0:T(1,128)} %refs_0_.1, s32[2048,1]{1,0:T(8,128)} %copy.42.ocol_ref.refs_1_, bf16[4,2048,128]{2,1,0:T(8,128)(2,1)} %get-tuple-element.113.qx_ref.refs_2_, bf16[2048,128]{1,0:T(8,128)(2,1)} %get-tuple-element.114.k_ref.refs_3_, ...), custom_call_target="tpu_custom_call" | custom-call | flops 1048576 | bytes 65536 | tf_op jit(solution)/shard_map/attend_back/pallas_call | solution.py:402
  358.9 8.3 %rows_back.1 = (bf16[2048,512]{1,0:T(8,128)(2,1)}, bf16[512,512]{1,0:T(8,128)(2,1)}, bf16[512,512]{1,0:T(8,128)(2,1)}, bf16[512,512]{1,0:T(8,128)(2,1)}, bf16[512,512]{1,0:T(8,128)(2,1)}) custom-call(s32[1,2048]{1,0:T(1,128)} %broadcast_xor_fusion.orow_ref, bf16[2048,512]{1,0:T(8,128)(2,1)} %get-tuple-element.174.draw_ref, bf16[512,1024]{1,0:T(8,128)(2,1)} %copy-done.17, ...), custom_call_target="tpu_custom_call" | custom-call | flops 1048576 | bytes 65536 | tf_op jit(solution)/shard_map/rows_back/pallas_call | solution.py:427
  367.2 1.5 collective-permute-start.27
  368.7 1.5 collective-permute-start.28
  370.7 7.2 %last_weights.1.refs_0_ = bf16[1024,896]{1,0:T(8,128)(2,1)} custom-call(bf16[2048,1024]{1,0:T(8,128)(2,1)} %get-tuple-element.188.normed_ref, bf16[2048,512]{1,0:T(8,128)(2,1)} %get-tuple-element.178.grads_ref, bf16[1024,256]{1,0:T(8,128)(2,1)} %get-tuple-element.189.o0_ref, bf16[1024,256]{1,0:T(8,128)(2,1)} %copy-done.23, bf16[1024,256]{1,0:T(8,128)(2,1)} %copy-done.24, ...), custom_call_target="tpu_custom_call" | custom-call | flops 1048576 | bytes 65536 | tf_op jit(solution)/shard_map/last_weights/pallas_call | solution.py:617
  377.9 4.4 collective-permute-done.27.g1_ref
  382.3 11.3 %collective-permute-done.28.g2_ref = bf16[512,512]{1,0:T(8,128)(2,1)S(1)} collective-permute-done((bf16[512,512]{1,0:T(8,128)(2,1)}, bf16[512,512]{1,0:T(8,128)(2,1)S(1)}, u32[]{:S(2)}, u32[]{:S(2)}) %collective-permute-start.28) | collective-permute-done | bytes 524320 | tf_op jit(solution)/shard_map/ppermute | solution.py:701
  395.9 1.7 copy.50
  397.7 2.4 collective-permute-start.37
  405.9 4.1 fusion
  410.0 7.2 %tokens_back.1 = bf16[512,1024]{1,0:T(8,128)(2,1)} custom-call(s32[1]{0:T(128)} %bitcast.me_ref.refs_0_, bf16[512,512]{1,0:T(8,128)(2,1)} %get-tuple-element.183.g0_ref, bf16[512,512]{1,0:T(8,128)(2,1)} %copy-done.34, bf16[512,512]{1,0:T(8,128)(2,1)} %copy-done.35, bf16[512,512]{1,0:T(8,128)(2,1)} %copy-done.36, ...), custom_call_target="tpu_custom_call" | custom-call | flops 1048576 | bytes 65536 | tf_op jit(solution)/shard_map/tokens_back/pallas_call | solution.py:459
  417.2 2.4 collective-permute-done.37
  420.9 1.7 maximum_convert_fusion.2
  423.8 6.0 %collective-permute-done.31 = bf16[128,2304]{1,0:T(8,128)(2,1)} collective-permute-done((bf16[128,2304]{1,0:T(8,128)(2,1)}, bf16[128,2304]{1,0:T(8,128)(2,1)}, u32[]{:S(2)}, u32[]{:S(2)}) %collective-permute-start.31) | collective-permute-done | bytes 589856 | tf_op jit(solution)/shard_map/ppermute | solution.py:701
  431.0 1.6 broadcast_select_fusion.4
  437.0 1.9 copy.51
  438.8 1.8 copy.52
  440.7 1.8 copy.53
  442.5 1.8 copy.54
  444.4 1.4 maximum_convert_fusion
  445.8 1.6 copy.55
  448.1 3.2 reduce-scatter.8.cloned.1.call-done
  451.2 2.4 collective-permute-start.33
  454.7 2.3 multiply_reduce_fusion.1
  457.0 1.9 copy.63
  459.0 3.1 copy.62
  (220 shorter events, 64.0 us)
Async XLA Ops:
  7.2 13.2 %copy-start = (bf16[576,1024]{1,0:T(8,128)(2,1)S(1)}, bf16[576,1024]{1,0:T(8,128)(2,1)}, u32[]{:S(2)}) copy-start(bf16[576,1024]{1,0:T(8,128)(2,1)} %param.28) | copy-start | bytes 3538948
  7.2 66.2 %all-gather.6.cloned.1.call-start = ((), (), s32[]{:S(2)}) async-start(), calls=%async_computation.3 | async-start | bytes 1474560 | tf_op jit(solution)/shard_map/all_gather | solution.py:754
  9.2 148.1 %all-gather.8.cloned.1.call-start = ((), (), s32[]{:S(2)}) async-start(), calls=%async_computation.4 | async-start | bytes 2359296 | tf_op jit(solution)/shard_map/all_gather | solution.py:755
  10.0 147.3 %all-gather.12.cloned.1.call-start = ((), (), s32[]{:S(2)}) async-start(), calls=%async_computation.6 | async-start | bytes 2654208 | tf_op jit(solution)/shard_map/all_gather | solution.py:759
  21.2 136.1 %all-gather.10.cloned.1.call-start = ((), (), s32[]{:S(2)}) async-start(), calls=%async_computation.5 | async-start | bytes 5308416 | tf_op jit(solution)/shard_map/all_gather | solution.py:758
  24.7 43.0 %copy-start.19 = (bf16[128,1024]{1,0:T(8,128)(2,1)S(1)}, bf16[128,1024]{1,0:T(8,128)(2,1)}, u32[]{:S(2)}) copy-start(bf16[128,1024]{1,0:T(8,128)(2,1)} %q_ref.1) | copy-start | bytes 786436
  24.7 42.9 %copy-start.25 = (bf16[128,512]{1,0:T(8,128)(2,1)S(1)}, bf16[128,512]{1,0:T(8,128)(2,1)}, u32[]{:S(2)}) copy-start(bf16[128,512]{1,0:T(8,128)(2,1)} %k_ref.1) | copy-start | bytes 393220
  25.8 249.6 %all-gather.14.cloned.1.call-start = ((), (), s32[]{:S(2)}) async-start(), calls=%async_computation.7 | async-start | bytes 4718592 | tf_op jit(solution)/shard_map/all_gather | solution.py:770
  25.9 26.2 %collective-permute-start = (bf16[512,1024]{1,0:T(8,128)(2,1)S(1)}, bf16[512,1024]{1,0:T(8,128)(2,1)S(1)}, u32[]{:S(2)}, u32[]{:S(2)}) collective-permute-start(bf16[512,1024]{1,0:T(8,128)(2,1)S(1)} %bitcast.40), channel_id=1, source_target_pairs={{0,8},{8,0},{16,24},{24,16},{1,9},{9,1},{17,25},{25,17},{2,10},{10... | collective-permute-start | bytes 3145736 | tf_op jit(solution)/shard_map/ppermute | solution.py:701
  28.9 24.6 %collective-permute-start.1 = (bf16[512,1024]{1,0:T(8,128)(2,1)S(1)}, bf16[512,1024]{1,0:T(8,128)(2,1)S(1)}, u32[]{:S(2)}, u32[]{:S(2)}) collective-permute-start(bf16[512,1024]{1,0:T(8,128)(2,1)S(1)} %bitcast.41), channel_id=1, source_target_pairs={{0,16},{8,24},{16,0},{24,8},{1,17},{9,25},{17,1},{25,9},{2,18},{10... | collective-permute-start | bytes 3145736 | tf_op jit(solution)/shard_map/ppermute | solution.py:701
  52.1 20.1 %copy-start.10 = (bf16[512,1024]{1,0:T(8,128)(2,1)}, bf16[512,1024]{1,0:T(8,128)(2,1)S(1)}, u32[]{:S(2)}) copy-start(bf16[512,1024]{1,0:T(8,128)(2,1)S(1)} %collective-permute-done.x1_ref.refs_9_) | copy-start | bytes 3145732
  53.5 18.6 %copy-start.11 = (bf16[512,1024]{1,0:T(8,128)(2,1)}, bf16[512,1024]{1,0:T(8,128)(2,1)S(1)}, u32[]{:S(2)}) copy-start(bf16[512,1024]{1,0:T(8,128)(2,1)S(1)} %collective-permute-done.1.x2_ref.refs_10_) | copy-start | bytes 3145732
  53.6 18.6 %copy-start.16 = (f32[2048,4,32]{0,2,1:T(8,128)S(1)}, f32[2048,4,32]{0,2,1:T(8,128)}, u32[]{:S(2)}) copy-start(f32[2048,4,32]{0,2,1:T(8,128)} %tile.12) | copy-start | bytes 3145732
  53.6 12.7 %collective-permute-start.2 = (bf16[512,512]{1,0:T(8,128)(2,1)S(1)}, bf16[512,512]{1,0:T(8,128)(2,1)}, u32[]{:S(2)}, u32[]{:S(2)}) collective-permute-start(bf16[512,512]{1,0:T(8,128)(2,1)S(1)} %slice.126), channel_id=1, source_target_pairs={{0,16},{8,24},{16,0},{24,8},{1,17},{9,25},{17,1},{25,9},{2,18},{10... | collective-permute-start | bytes 1572872 | tf_op jit(solution)/shard_map/ppermute | solution.py:701
  55.2 12.5 %collective-permute-start.3 = (bf16[512,512]{1,0:T(8,128)(2,1)S(1)}, bf16[512,512]{1,0:T(8,128)(2,1)}, u32[]{:S(2)}, u32[]{:S(2)}) collective-permute-start(bf16[512,512]{1,0:T(8,128)(2,1)S(1)} %slice.127), channel_id=1, source_target_pairs={{0,8},{8,0},{16,24},{24,16},{1,9},{9,1},{17,25},{25,17},{2,10},{10... | collective-permute-start | bytes 1572872 | tf_op jit(solution)/shard_map/ppermute | solution.py:701
  69.4 240.9 %reduce-scatter.4.cloned.1.call-start = ((), (), s32[]{:S(2)}) async-start(), calls=%async_computation.8 | async-start | bytes 2654208 | tf_op jit(solution)/shard_map/reduce_scatter | solution.py:791
  69.5 23.0 %collective-permute-start.4 = (bf16[512,1024]{1,0:T(8,128)(2,1)}, bf16[512,1024]{1,0:T(8,128)(2,1)}, u32[]{:S(2)}, u32[]{:S(2)}) collective-permute-start(bf16[512,1024]{1,0:T(8,128)(2,1)} %bitcast.42), channel_id=1, source_target_pairs={{0,8},{8,0},{16,24},{24,16},{1,9},{9,1},{17,25},{25,17},{2,10},{10... | collective-permute-start | bytes 3145736 | tf_op jit(solution)/shard_map/ppermute | solution.py:701
  70.2 22.7 %collective-permute-start.5 = (bf16[512,1024]{1,0:T(8,128)(2,1)}, bf16[512,1024]{1,0:T(8,128)(2,1)}, u32[]{:S(2)}, u32[]{:S(2)}) collective-permute-start(bf16[512,1024]{1,0:T(8,128)(2,1)} %bitcast.43), channel_id=1, source_target_pairs={{0,16},{8,24},{16,0},{24,8},{1,17},{9,25},{17,1},{25,9},{2,18},{10... | collective-permute-start | bytes 3145736 | tf_op jit(solution)/shard_map/ppermute | solution.py:701
  93.9 20.3 %collective-permute-start.6 = (bf16[512,512]{1,0:T(8,128)(2,1)S(1)}, bf16[512,512]{1,0:T(8,128)(2,1)S(1)}, u32[]{:S(2)}, u32[]{:S(2)}) collective-permute-start(bf16[512,512]{1,0:T(8,128)(2,1)S(1)} %slice.128), channel_id=1, source_target_pairs={{0,16},{8,24},{16,0},{24,8},{1,17},{9,25},{17,1},{25,9},{2,18},{10... | collective-permute-start | bytes 1572872 | tf_op jit(solution)/shard_map/ppermute | solution.py:701
  95.9 18.3 %collective-permute-start.7 = (bf16[512,512]{1,0:T(8,128)(2,1)S(1)}, bf16[512,512]{1,0:T(8,128)(2,1)S(1)}, u32[]{:S(2)}, u32[]{:S(2)}) collective-permute-start(bf16[512,512]{1,0:T(8,128)(2,1)S(1)} %slice.129), channel_id=1, source_target_pairs={{0,8},{8,0},{16,24},{24,16},{1,9},{9,1},{17,25},{25,17},{2,10},{10... | collective-permute-start | bytes 1572872 | tf_op jit(solution)/shard_map/ppermute | solution.py:701
  110.7 33.9 %collective-permute-start.10 = (bf16[2048,128]{1,0:T(8,128)(2,1)}, bf16[2048,128]{1,0:T(8,128)(2,1)S(1)}, u32[]{:S(2)}, u32[]{:S(2)}) collective-permute-start(bf16[2048,128]{1,0:T(8,128)(2,1)} %get-tuple-element.116.refs_1_.refs_0_), channel_id=1, source_target_pairs={{0,16},{8,24},{16,0},{24,8},{1,17},{9,25},{17,1},{25,9},{2,18},{10... | collective-permute-start | bytes 1572872 | tf_op jit(solution)/shard_map/ppermute | solution.py:701
  112.3 34.5 %collective-permute-start.12 = (bf16[2048,128]{1,0:T(8,128)(2,1)}, bf16[2048,128]{1,0:T(8,128)(2,1)S(1)}, u32[]{:S(2)}, u32[]{:S(2)}) collective-permute-start(bf16[2048,128]{1,0:T(8,128)(2,1)} %get-tuple-element.116.refs_1_.refs_0_), channel_id=1, source_target_pairs={{0,24},{8,16},{16,8},{24,0},{1,25},{9,17},{17,9},{25,1},{2,26},{10... | collective-permute-start | bytes 1572872 | tf_op jit(solution)/shard_map/ppermute | solution.py:701
  113.2 33.5 %collective-permute-start.8 = (bf16[2048,128]{1,0:T(8,128)(2,1)}, bf16[2048,128]{1,0:T(8,128)(2,1)S(1)}, u32[]{:S(2)}, u32[]{:S(2)}) collective-permute-start(bf16[2048,128]{1,0:T(8,128)(2,1)} %get-tuple-element.116.refs_1_.refs_0_), channel_id=1, source_target_pairs={{0,8},{8,0},{16,24},{24,16},{1,9},{9,1},{17,25},{25,17},{2,10},{10... | collective-permute-start | bytes 1572872 | tf_op jit(solution)/shard_map/ppermute | solution.py:701
  129.8 26.2 %collective-permute-start.11 = (bf16[2048,128]{1,0:T(8,128)(2,1)}, bf16[2048,128]{1,0:T(8,128)(2,1)S(1)}, u32[]{:S(2)}, u32[]{:S(2)}) collective-permute-start(bf16[2048,128]{1,0:T(8,128)(2,1)} %get-tuple-element.120.refs_2_.refs_1_), channel_id=1, source_target_pairs={{0,16},{8,24},{16,0},{24,8},{1,17},{9,25},{17,1},{25,9},{2,18},{10... | collective-permute-start | bytes 1572872 | tf_op jit(solution)/shard_map/ppermute | solution.py:701
  131.3 24.7 %collective-permute-start.13 = (bf16[2048,128]{1,0:T(8,128)(2,1)}, bf16[2048,128]{1,0:T(8,128)(2,1)S(1)}, u32[]{:S(2)}, u32[]{:S(2)}) collective-permute-start(bf16[2048,128]{1,0:T(8,128)(2,1)} %get-tuple-element.120.refs_2_.refs_1_), channel_id=1, source_target_pairs={{0,24},{8,16},{16,8},{24,0},{1,25},{9,17},{17,9},{25,1},{2,26},{10... | collective-permute-start | bytes 1572872 | tf_op jit(solution)/shard_map/ppermute | solution.py:701
  144.6 12.7 %copy-start.3 = (bf16[2048,128]{1,0:T(8,128)(2,1)}, bf16[2048,128]{1,0:T(8,128)(2,1)S(1)}, u32[]{:S(2)}) copy-start(bf16[2048,128]{1,0:T(8,128)(2,1)S(1)} %collective-permute-done.10.refs_5_.refs_4_) | copy-start | bytes 1572868
  144.6 12.7 %collective-permute-start.9 = (bf16[2048,128]{1,0:T(8,128)(2,1)}, bf16[2048,128]{1,0:T(8,128)(2,1)S(1)}, u32[]{:S(2)}, u32[]{:S(2)}) collective-permute-start(bf16[2048,128]{1,0:T(8,128)(2,1)} %get-tuple-element.120.refs_2_.refs_1_), channel_id=1, source_target_pairs={{0,8},{8,0},{16,24},{24,16},{1,9},{9,1},{17,25},{25,17},{2,10},{10... | collective-permute-start | bytes 1572872 | tf_op jit(solution)/shard_map/ppermute | solution.py:701
  146.7 10.6 %copy-start.4 = (bf16[2048,128]{1,0:T(8,128)(2,1)}, bf16[2048,128]{1,0:T(8,128)(2,1)S(1)}, u32[]{:S(2)}) copy-start(bf16[2048,128]{1,0:T(8,128)(2,1)S(1)} %collective-permute-done.12.refs_7_.refs_6_) | copy-start | bytes 1572868
  146.7 10.6 %copy-start.5 = (bf16[2048,128]{1,0:T(8,128)(2,1)}, bf16[2048,128]{1,0:T(8,128)(2,1)S(1)}, u32[]{:S(2)}) copy-start(bf16[2048,128]{1,0:T(8,128)(2,1)S(1)} %collective-permute-done.8.refs_3_.refs_2_) | copy-start | bytes 1572868
  175.4 11.1 %collective-permute-start.14 = (bf16[512,512]{1,0:T(8,128)(2,1)}, bf16[512,512]{1,0:T(8,128)(2,1)S(1)}, u32[]{:S(2)}, u32[]{:S(2)}) collective-permute-start(bf16[512,512]{1,0:T(8,128)(2,1)} %get-tuple-element.131), channel_id=1, source_target_pairs={{0,8},{8,0},{16,24},{24,16},{1,9},{9,1},{17,25},{25,17},{2,10},{10... | collective-permute-start | bytes 1572872 | tf_op jit(solution)/shard_map/ppermute | solution.py:701
  176.8 11.1 %collective-permute-start.15 = (bf16[512,512]{1,0:T(8,128)(2,1)}, bf16[512,512]{1,0:T(8,128)(2,1)S(1)}, u32[]{:S(2)}, u32[]{:S(2)}) collective-permute-start(bf16[512,512]{1,0:T(8,128)(2,1)} %get-tuple-element.132), channel_id=1, source_target_pairs={{0,16},{8,24},{16,0},{24,8},{1,17},{9,25},{17,1},{25,9},{2,18},{10... | collective-permute-start | bytes 1572872 | tf_op jit(solution)/shard_map/ppermute | solution.py:701
  186.5 29.1 %copy-start.32 = (bf16[512,512]{1,0:T(8,128)(2,1)}, bf16[512,512]{1,0:T(8,128)(2,1)S(1)}, u32[]{:S(2)}) copy-start(bf16[512,512]{1,0:T(8,128)(2,1)S(1)} %collective-permute-done.14.refs_17_) | copy-start | bytes 1572868
  187.9 27.7 %copy-start.33 = (bf16[512,512]{1,0:T(8,128)(2,1)}, bf16[512,512]{1,0:T(8,128)(2,1)S(1)}, u32[]{:S(2)}) copy-start(bf16[512,512]{1,0:T(8,128)(2,1)S(1)} %collective-permute-done.15.refs_18_) | copy-start | bytes 1572868
  187.9 58.9 %collective-permute-start.16 = (bf16[512,1024]{1,0:T(8,128)(2,1)}, bf16[512,1024]{1,0:T(8,128)(2,1)S(1)}, u32[]{:S(2)}, u32[]{:S(2)}) collective-permute-start(bf16[512,1024]{1,0:T(8,128)(2,1)} %get-tuple-element.143), channel_id=1, source_target_pairs={{0,24},{8,16},{16,8},{24,0},{1,25},{9,17},{17,9},{25,1},{2,26},{10... | collective-permute-start | bytes 3145736 | tf_op jit(solution)/shard_map/ppermute | solution.py:701
  246.8 18.2 %copy-start.28 = (bf16[512,1024]{1,0:T(8,128)(2,1)}, bf16[512,1024]{1,0:T(8,128)(2,1)S(1)}, u32[]{:S(2)}) copy-start(bf16[512,1024]{1,0:T(8,128)(2,1)S(1)} %collective-permute-done.16) | copy-start | bytes 3145732
  246.8 27.3 %collective-permute-start.17 = (bf16[512,1024]{1,0:T(8,128)(2,1)}, bf16[512,1024]{1,0:T(8,128)(2,1)S(1)}, u32[]{:S(2)}, u32[]{:S(2)}) collective-permute-start(bf16[512,1024]{1,0:T(8,128)(2,1)} %get-tuple-element.144), channel_id=1, source_target_pairs={{0,8},{8,0},{16,24},{24,16},{1,9},{9,1},{17,25},{25,17},{2,10},{10... | collective-permute-start | bytes 3145736 | tf_op jit(solution)/shard_map/ppermute | solution.py:701
  247.9 26.2 %collective-permute-start.18 = (bf16[512,1024]{1,0:T(8,128)(2,1)}, bf16[512,1024]{1,0:T(8,128)(2,1)S(1)}, u32[]{:S(2)}, u32[]{:S(2)}) collective-permute-start(bf16[512,1024]{1,0:T(8,128)(2,1)} %get-tuple-element.145), channel_id=1, source_target_pairs={{0,16},{8,24},{16,0},{24,8},{1,17},{9,25},{17,1},{25,9},{2,18},{10... | collective-permute-start | bytes 3145736 | tf_op jit(solution)/shard_map/ppermute | solution.py:701
  274.1 119.5 %reduce-scatter.6.cloned.1.call-start = ((), (), s32[]{:S(2)}) async-start(), calls=%async_computation.9 | async-start | bytes 5308416 | tf_op jit(solution)/shard_map/reduce_scatter | solution.py:791
  275.4 175.8 %reduce-scatter.8.cloned.1.call-start = ((), (), s32[]{:S(2)}) async-start(), calls=%async_computation.10 | async-start | bytes 2064384 | tf_op jit(solution)/shard_map/reduce_scatter | solution.py:791
  282.2 9.5 %collective-permute-start.19 = (bf16[512,256]{1,0:T(8,128)(2,1)}, bf16[512,256]{1,0:T(8,128)(2,1)S(1)}, u32[]{:S(2)}, u32[]{:S(2)}) collective-permute-start(bf16[512,256]{1,0:T(8,128)(2,1)} %get-tuple-element.161), channel_id=1, source_target_pairs={{0,8},{8,0},{16,24},{24,16},{1,9},{9,1},{17,25},{25,17},{2,10},{10... | collective-permute-start | bytes 786440 | tf_op jit(solution)/shard_map/ppermute | solution.py:701
  284.2 11.3 %collective-permute-start.20 = (bf16[512,256]{1,0:T(8,128)(2,1)}, bf16[512,256]{1,0:T(8,128)(2,1)S(1)}, u32[]{:S(2)}, u32[]{:S(2)}) collective-permute-start(bf16[512,256]{1,0:T(8,128)(2,1)} %get-tuple-element.162), channel_id=1, source_target_pairs={{0,16},{8,24},{16,0},{24,8},{1,17},{9,25},{17,1},{25,9},{2,18},{10... | collective-permute-start | bytes 786440 | tf_op jit(solution)/shard_map/ppermute | solution.py:701
  284.2 13.2 %collective-permute-start.21 = (bf16[512,256]{1,0:T(8,128)(2,1)}, bf16[512,256]{1,0:T(8,128)(2,1)S(1)}, u32[]{:S(2)}, u32[]{:S(2)}) collective-permute-start(bf16[512,256]{1,0:T(8,128)(2,1)} %get-tuple-element.163), channel_id=1, source_target_pairs={{0,24},{8,16},{16,8},{24,0},{1,25},{9,17},{17,9},{25,1},{2,26},{10... | collective-permute-start | bytes 786440 | tf_op jit(solution)/shard_map/ppermute | solution.py:701
  291.7 18.6 %copy-start.37 = (bf16[512,256]{1,0:T(8,128)(2,1)}, bf16[512,256]{1,0:T(8,128)(2,1)S(1)}, u32[]{:S(2)}) copy-start(bf16[512,256]{1,0:T(8,128)(2,1)S(1)} %collective-permute-done.19.refs_11_) | copy-start | bytes 786436
  298.1 59.2 %collective-permute-start.22 = (bf16[512,1024]{1,0:T(8,128)(2,1)}, bf16[512,1024]{1,0:T(8,128)(2,1)S(1)}, u32[]{:S(2)}, u32[]{:S(2)}) collective-permute-start(bf16[512,1024]{1,0:T(8,128)(2,1)} %get-tuple-element.164), channel_id=1, source_target_pairs={{0,8},{8,0},{16,24},{24,16},{1,9},{9,1},{17,25},{25,17},{2,10},{10... | collective-permute-start | bytes 3145736 | tf_op jit(solution)/shard_map/ppermute | solution.py:701
  299.4 57.9 %collective-permute-start.23 = (bf16[512,1024]{1,0:T(8,128)(2,1)}, bf16[512,1024]{1,0:T(8,128)(2,1)S(1)}, u32[]{:S(2)}, u32[]{:S(2)}) collective-permute-start(bf16[512,1024]{1,0:T(8,128)(2,1)} %get-tuple-element.165), channel_id=1, source_target_pairs={{0,16},{8,24},{16,0},{24,8},{1,17},{9,25},{17,1},{25,9},{2,18},{10... | collective-permute-start | bytes 3145736 | tf_op jit(solution)/shard_map/ppermute | solution.py:701
  301.4 55.8 %collective-permute-start.24 = (bf16[1024,256]{1,0:T(8,128)(2,1)}, bf16[1024,256]{1,0:T(8,128)(2,1)S(1)}, u32[]{:S(2)}, u32[]{:S(2)}) collective-permute-start(bf16[1024,256]{1,0:T(8,128)(2,1)} %get-tuple-element.175), channel_id=1, source_target_pairs={{0,8},{8,0},{16,24},{24,16},{1,9},{9,1},{17,25},{25,17},{2,10},{10... | collective-permute-start | bytes 1572872 | tf_op jit(solution)/shard_map/ppermute | solution.py:701
  301.5 55.8 %collective-permute-start.25 = (bf16[1024,256]{1,0:T(8,128)(2,1)}, bf16[1024,256]{1,0:T(8,128)(2,1)S(1)}, u32[]{:S(2)}, u32[]{:S(2)}) collective-permute-start(bf16[1024,256]{1,0:T(8,128)(2,1)} %get-tuple-element.176), channel_id=1, source_target_pairs={{0,16},{8,24},{16,0},{24,8},{1,17},{9,25},{17,1},{25,9},{2,18},{10... | collective-permute-start | bytes 1572872 | tf_op jit(solution)/shard_map/ppermute | solution.py:701
  302.1 55.1 %collective-permute-start.26 = (bf16[1024,256]{1,0:T(8,128)(2,1)}, bf16[1024,256]{1,0:T(8,128)(2,1)}, u32[]{:S(2)}, u32[]{:S(2)}) collective-permute-start(bf16[1024,256]{1,0:T(8,128)(2,1)} %get-tuple-element.177), channel_id=1, source_target_pairs={{0,24},{8,16},{16,8},{24,0},{1,25},{9,17},{17,9},{25,1},{2,26},{10... | collective-permute-start | bytes 1572872 | tf_op jit(solution)/shard_map/ppermute | solution.py:701
  367.2 15.1 %collective-permute-start.27 = (bf16[512,512]{1,0:T(8,128)(2,1)}, bf16[512,512]{1,0:T(8,128)(2,1)S(1)}, u32[]{:S(2)}, u32[]{:S(2)}) collective-permute-start(bf16[512,512]{1,0:T(8,128)(2,1)} %get-tuple-element.184), channel_id=1, source_target_pairs={{0,8},{8,0},{16,24},{24,16},{1,9},{9,1},{17,25},{25,17},{2,10},{10... | collective-permute-start | bytes 1572872 | tf_op jit(solution)/shard_map/ppermute | solution.py:701
  368.7 24.8 %collective-permute-start.28 = (bf16[512,512]{1,0:T(8,128)(2,1)}, bf16[512,512]{1,0:T(8,128)(2,1)S(1)}, u32[]{:S(2)}, u32[]{:S(2)}) collective-permute-start(bf16[512,512]{1,0:T(8,128)(2,1)} %get-tuple-element.185), channel_id=1, source_target_pairs={{0,16},{8,24},{16,0},{24,8},{1,17},{9,25},{17,1},{25,9},{2,18},{10... | collective-permute-start | bytes 1572872 | tf_op jit(solution)/shard_map/ppermute | solution.py:701
  370.2 23.4 %collective-permute-start.29 = (bf16[512,512]{1,0:T(8,128)(2,1)}, bf16[512,512]{1,0:T(8,128)(2,1)S(1)}, u32[]{:S(2)}, u32[]{:S(2)}) collective-permute-start(bf16[512,512]{1,0:T(8,128)(2,1)} %get-tuple-element.186), channel_id=1, source_target_pairs={{0,24},{8,16},{16,8},{24,0},{1,25},{9,17},{17,9},{25,1},{2,26},{10... | collective-permute-start | bytes 1572872 | tf_op jit(solution)/shard_map/ppermute | solution.py:701
  370.7 23.8 %copy-start.13 = (bf16[128,4608]{1,0:T(8,128)(2,1)S(1)}, bf16[128,4608]{1,0:T(8,128)(2,1)}, u32[]{:S(2)}) copy-start(bf16[128,4608]{1,0:T(8,128)(2,1)} %param.27) | copy-start | bytes 3538948
  382.3 11.4 %copy-start.34 = (bf16[512,512]{1,0:T(8,128)(2,1)}, bf16[512,512]{1,0:T(8,128)(2,1)S(1)}, u32[]{:S(2)}) copy-start(bf16[512,512]{1,0:T(8,128)(2,1)S(1)} %collective-permute-done.27.g1_ref) | copy-start | bytes 1572868
  393.6 11.3 %collective-permute-start.36 = (bf16[144,1024]{1,0:T(8,128)(2,1)}, bf16[144,1024]{1,0:T(8,128)(2,1)}, u32[]{:S(2)}, u32[]{:S(2)}) collective-permute-start(bf16[144,1024]{1,0:T(8,128)(2,1)} %reduce-scatter.4.cloned.1.call-done.refs_21_), channel_id=1, source_target_pairs={{0,24},{8,16},{16,8},{24,0},{1,25},{9,17},{17,9},{25,1},{2,26},{10... | collective-permute-start | bytes 884744 | tf_op jit(solution)/shard_map/ppermute | solution.py:701
  394.5 11.3 %copy-start.9 = (f32[512,1024]{1,0:T(8,128)S(1)}, f32[512,1024]{1,0:T(8,128)}, u32[]{:S(2)}) copy-start(f32[512,1024]{1,0:T(8,128)} %get-tuple-element.129.refs_5_) | copy-start | bytes 6291460
  397.7 21.9 %collective-permute-start.37 = (bf16[144,1024]{1,0:T(8,128)(2,1)}, bf16[144,1024]{1,0:T(8,128)(2,1)}, u32[]{:S(2)}, u32[]{:S(2)}) collective-permute-start(bf16[144,1024]{1,0:T(8,128)(2,1)} %reduce-scatter.4.cloned.1.call-done.refs_21_), channel_id=1, source_target_pairs={{0,16},{8,24},{16,0},{24,8},{1,17},{9,25},{17,1},{25,9},{2,18},{10... | collective-permute-start | bytes 884744 | tf_op jit(solution)/shard_map/ppermute | solution.py:701
  400.1 19.5 %collective-permute-start.38 = (bf16[144,1024]{1,0:T(8,128)(2,1)}, bf16[144,1024]{1,0:T(8,128)(2,1)}, u32[]{:S(2)}, u32[]{:S(2)}) collective-permute-start(bf16[144,1024]{1,0:T(8,128)(2,1)} %reduce-scatter.4.cloned.1.call-done.refs_21_), channel_id=1, source_target_pairs={{0,8},{8,0},{16,24},{24,16},{1,9},{9,1},{17,25},{25,17},{2,10},{10... | collective-permute-start | bytes 884744 | tf_op jit(solution)/shard_map/ppermute | solution.py:701
  400.8 23.0 %collective-permute-start.30 = (bf16[128,2304]{1,0:T(8,128)(2,1)}, bf16[128,2304]{1,0:T(8,128)(2,1)}, u32[]{:S(2)}, u32[]{:S(2)}) collective-permute-start(bf16[128,2304]{1,0:T(8,128)(2,1)} %reduce-scatter.6.cloned.1.call-done), channel_id=1, source_target_pairs={{0,24},{8,16},{16,8},{24,0},{1,25},{9,17},{17,9},{25,1},{2,26},{10... | collective-permute-start | bytes 1769480 | tf_op jit(solution)/shard_map/ppermute | solution.py:701
  402.2 27.6 %collective-permute-start.31 = (bf16[128,2304]{1,0:T(8,128)(2,1)}, bf16[128,2304]{1,0:T(8,128)(2,1)}, u32[]{:S(2)}, u32[]{:S(2)}) collective-permute-start(bf16[128,2304]{1,0:T(8,128)(2,1)} %reduce-scatter.6.cloned.1.call-done), channel_id=1, source_target_pairs={{0,16},{8,24},{16,0},{24,8},{1,17},{9,25},{17,1},{25,9},{2,18},{10... | collective-permute-start | bytes 1769480 | tf_op jit(solution)/shard_map/ppermute | solution.py:701
  404.9 26.1 %collective-permute-start.32 = (bf16[128,2304]{1,0:T(8,128)(2,1)}, bf16[128,2304]{1,0:T(8,128)(2,1)}, u32[]{:S(2)}, u32[]{:S(2)}) collective-permute-start(bf16[128,2304]{1,0:T(8,128)(2,1)} %reduce-scatter.6.cloned.1.call-done), channel_id=1, source_target_pairs={{0,8},{8,0},{16,24},{24,16},{1,9},{9,1},{17,25},{25,17},{2,10},{10... | collective-permute-start | bytes 1769480 | tf_op jit(solution)/shard_map/ppermute | solution.py:701
  420.9 10.1 %copy-start.31 = (bf16[128,2304]{1,0:T(8,128)(2,1)S(1)}, bf16[128,2304]{1,0:T(8,128)(2,1)}, u32[]{:S(2)}) copy-start(bf16[128,2304]{1,0:T(8,128)(2,1)} %reduce-scatter.6.cloned.1.call-done) | copy-start | bytes 1769476
  451.2 11.3 %collective-permute-start.33 = (bf16[128,896]{1,0:T(8,128)(2,1)}, bf16[128,896]{1,0:T(8,128)(2,1)}, u32[]{:S(2)}, u32[]{:S(2)}) collective-permute-start(bf16[128,896]{1,0:T(8,128)(2,1)} %reduce-scatter.8.cloned.1.call-done), channel_id=1, source_target_pairs={{0,24},{8,16},{16,8},{24,0},{1,25},{9,17},{17,9},{25,1},{2,26},{10... | collective-permute-start | bytes 688136 | tf_op jit(solution)/shard_map/ppermute | solution.py:701
  453.7 8.9 %collective-permute-start.34 = (bf16[128,896]{1,0:T(8,128)(2,1)}, bf16[128,896]{1,0:T(8,128)(2,1)}, u32[]{:S(2)}, u32[]{:S(2)}) collective-permute-start(bf16[128,896]{1,0:T(8,128)(2,1)} %reduce-scatter.8.cloned.1.call-done), channel_id=1, source_target_pairs={{0,16},{8,24},{16,0},{24,8},{1,17},{9,25},{17,1},{25,9},{2,18},{10... | collective-permute-start | bytes 688136 | tf_op jit(solution)/shard_map/ppermute | solution.py:701
  454.2 8.4 %collective-permute-start.35 = (bf16[128,896]{1,0:T(8,128)(2,1)}, bf16[128,896]{1,0:T(8,128)(2,1)}, u32[]{:S(2)}, u32[]{:S(2)}) collective-permute-start(bf16[128,896]{1,0:T(8,128)(2,1)} %reduce-scatter.8.cloned.1.call-done), channel_id=1, source_target_pairs={{0,8},{8,0},{16,24},{24,16},{1,9},{9,1},{17,25},{25,17},{2,10},{10... | collective-permute-start | bytes 688136 | tf_op jit(solution)/shard_map/ppermute | solution.py:701
  (29 other events, 72.5 us)
Sparse Core Ops, SparseCore 0:
  10.2 26.1 all-gather.5
  38.0 28.5 all-gather.7
  68.3 31.1 all-gather.11
  101.5 50.8 all-gather.9
  153.8 45.9 all-gather.13
  274.2 36.0 reduce-scatter.3
  312.6 54.2 reduce-scatter.5
  417.4 33.8 reduce-scatter.7

commit v3 on v2

--- a/solution.py
+++ b/solution.py
@@ -106,6 +106,144 @@
     )(me, w_query, w_key, w_value, attn_gain[None], ffn_gain[None])
 
 
+def cut_kernel(shards, me_ref, gate_ref, up_ref, down_ref, wo_ref, out_ref):
+    whole, units = gate_ref.shape[1], down_ref.shape[1]
+    piece, span = units // shards, whole // shards
+    for at, ref in ((0, gate_ref), (units, up_ref)):
+        turned = pltpu.roll(ref[...].astype(F32), whole - piece * me_ref[0], 1)
+        parts = [turned[:, span * k:span * k + piece] for k in range(shards)]
+        out_ref[:, at:at + units] = jnp.concatenate(parts, axis=1).astype(BF16)
+    out_ref[:, 2 * units:3 * units] = down_ref[...]
+    width = wo_ref.shape[1]
+    out_ref[:, 3 * units:3 * units + width] = wo_ref[...]
+    out_ref[:, 3 * units + width:] = jnp.zeros((out_ref.shape[0], units - width), BF16)
+
+
+def cut_weights(me, w_gate, w_up, w_down, w_out, shards):
+    depth, whole = w_gate.shape
+    return pl.pallas_call(
+        functools.partial(cut_kernel, shards),
+        out_shape=jax.ShapeDtypeStruct((depth, whole), BF16),
+        in_specs=[smem()] + [vmem()] * 4,
+        out_specs=vmem(),
+        compiler_params=params(),
+        cost_estimate=COST,
+        name="cut_weights",
+    )(me, w_gate, w_up, w_down, w_out)
+
+
+def join_kernel(shards, me_ref, p0_ref, p1_ref, p2_ref, p3_ref, gate_ref, up_ref, dgate_ref, dup_ref, dot_ref, st_ref):
+    for d, ref in enumerate((p0_ref, p1_ref, p2_ref, p3_ref)):
+        st_ref[d] = ref[...]
+    units = p0_ref.shape[1] // 2
+    piece = units // shards
+    quarters = [st_ref[jnp.bitwise_xor(me_ref[0], q)] for q in range(4)]
+    total = 0.0
+    for at, w_ref, out_ref in ((0, gate_ref, dgate_ref), (units, up_ref, dup_ref)):
+        parts = [q[:, at:at + units].astype(F32) for q in quarters]
+        parts = [q[:, piece * k:piece * (k + 1)] for k in range(shards) for q in parts]
+        joined = jnp.concatenate(parts, axis=1)
+        out_ref[...] = joined
+        total = total + jnp.sum(joined * w_ref[...].astype(F32), axis=1, keepdims=True)
+    dot_ref[...] = total
+
+
+def join_weights(me, parts, w_gate, w_up, shards):
+    depth, whole = w_gate.shape
+    return pl.pallas_call(
+        functools.partial(join_kernel, shards),
+        out_shape=(jax.ShapeDtypeStruct((depth, whole), F32),) * 2 + (jax.ShapeDtypeStruct((depth, 1), F32),),
+        in_specs=[smem()] + [vmem()] * 6,
+        out_specs=(vmem(),) * 3,
+        scratch_shapes=[pltpu.VMEM((4,) + parts[0].shape, BF16)],
+        compiler_params=params(),
+        cost_estimate=COST,
+        name="join_weights",
+    )(me, *parts, w_gate, w_up)
+
+
+def join_last_kernel(me_ref, p0_ref, p1_ref, p2_ref, p3_ref, q_ref, k_ref, v_ref,
+                     dq_ref, dk_ref, dv_ref, do_ref, dot_ref, gain_ref):
+    at = 0
+    parts = (p0_ref, p1_ref, p2_ref, p3_ref)
+    total = jnp.zeros(dot_ref.shape, F32)
+    for out_ref, w_ref in ((dq_ref, q_ref), (dk_ref, k_ref), (dv_ref, v_ref), (do_ref, None)):
+        size = out_ref.shape[1] // 4
+        for d, ref in enumerate(parts):
+            there = pl.ds(pl.multiple_of(jnp.bitwise_xor(me_ref[0], d) * size, size), size)
+            part = ref[:, at:at + size].astype(F32)
+            out_ref[:, there] = part
+            if w_ref is not None:
+                total = total + jnp.sum(part * w_ref[:, there].astype(F32), axis=1, keepdims=True)
+        at += size
+    dot_ref[...] = total
+    gains = jnp.zeros(gain_ref.shape, F32)
+    for ref in parts:
+        gains = gains + ref[0:16, at:].astype(F32)[:8]
+    gain_ref[...] = gains
+
+
+def join_last(me, parts, w_query, w_key, w_value, out_width):
+    depth = w_query.shape[0]
+    out = lambda c: jax.ShapeDtypeStruct((depth, c), F32)
+    return pl.pallas_call(
+        join_last_kernel,
+        out_shape=(
+            out(w_query.shape[1]), out(w_key.shape[1]), out(w_value.shape[1]), out(out_width), out(1),
+            jax.ShapeDtypeStruct((8, LANES), F32),
+        ),
+        in_specs=[smem()] + [vmem()] * 7,
+        out_specs=(vmem(),) * 6,
+        compiler_params=params(),
+        cost_estimate=COST,
+        name="join_last",
+    )(me, *parts, w_query, w_key, w_value)
+
+
+def table_kernel(half, me_ref, lens_ref, order_ref, freq_ref, cos_ref, up_ref, down_ref, ocol_ref, orow_ref):
+    all_rows = order_ref.shape[1]
+    groups = LANES // half
+    rows = all_rows // groups
+    lane = lane_iota(rows, LANES)
+    index = lane // half * rows + row_iota(rows, LANES)
+    angles = (index - row_starts(lens_ref, index)).astype(F32) * freq_ref[...]
+    cosine, sine = jnp.cos(angles), jnp.sin(angles)
+    first = lane % (2 * half) < half
+    for q in range(groups):
+
+        def spread(table, q=q):
+            one = jnp.where(lane < half, pltpu.roll(table, LANES - half * q, 1) if q else table, 0.0)
+            return one + pltpu.roll(one, half, 1) + pltpu.roll(one, 2 * half, 1) + pltpu.roll(one, 3 * half, 1)
+
+        here = slice(q * rows, (q + 1) * rows)
+        cos_ref[here, :] = spread(cosine)
+        wide = spread(sine)
+        up_ref[here, :] = jnp.where(first, -wide, 0.0)
+        down_ref[here, :] = jnp.where(first, 0.0, wide)
+    relative = jnp.bitwise_xor(order_ref[...], me_ref[0] * (all_rows // 4))
+    orow_ref[...] = relative
+    for c in range(all_rows // LANES):
+        here = slice(c * LANES, (c + 1) * LANES)
+        across = jnp.broadcast_to(relative[:, here].astype(F32), (LANES, LANES))
+        ocol_ref[here, :] = jnp.transpose(across).astype(jnp.int32)
+
+
+def make_tables(me, lens, order, head_dim):
+    all_rows = order.shape[1]
+    half = head_dim // 2
+    frequency = ROPE_BASE ** (-2.0 * jnp.arange(half, dtype=F32) / head_dim)
+    out = lambda r, c, t: jax.ShapeDtypeStruct((r, c), t)
+    return pl.pallas_call(
+        functools.partial(table_kernel, half),
+        out_shape=(out(all_rows, LANES, F32),) * 3 + (out(all_rows, LANES, jnp.int32), out(1, all_rows, jnp.int32)),
+        in_specs=[smem(), smem(), vmem(), vmem()],
+        out_specs=(vmem(),) * 5,
+        compiler_params=params(),
+        cost_estimate=COST,
+        name="make_tables",
+    )(me, lens, order, jnp.tile(frequency, LANES // half)[None, :])
+
+
 def qkv_kernel(
     head_dim, x0_ref, x1_ref, x2_ref, x3a_ref, x3b_ref, w_ref, ocol_ref, cos_ref, su_ref, sd_ref,
     qg_ref, kg_ref, normed_ref, qx_ref, k_ref, v_ref, vx_ref, kt_ref, rawq_ref, rawk_ref, gain_ref, raw_ref,
@@ -136,7 +274,7 @@
     def _():
         ones = pair_ones(head_dim)
         low_lanes = lane_iota(tok, LANES) < head_dim
-        pick = (ocol_ref[...] == lane_iota(tok, all_rows)).astype(F32).astype(BF16)
+        pick = (ocol_ref[:, 0:1] == lane_iota(tok, all_rows)).astype(F32).astype(BF16)
         dealt = dot_nn(pick, raw_ref[...])
         cosine, su, sd = cos_ref[...], su_ref[...], sd_ref[...]
         for g in range(pairs):
@@ -176,7 +314,7 @@
             out(2, all_rows, LANES), out(LANES, all_rows), out(all_rows, 2 * LANES), out(all_rows, LANES),
             jax.ShapeDtypeStruct((8, width), F32),
         ),
-        in_specs=[fixed(x) for x in xs] + [fixed(w), late(1)] + [late(LANES)] * 3 + [fixed(qg), fixed(kg)],
+        in_specs=[fixed(x) for x in xs] + [fixed(w)] + [late(LANES)] * 4 + [fixed(qg), fixed(kg)],
         out_specs=(
             pl.BlockSpec((tok, width), lambda i: (jnp.minimum(i, 3), 0)),
             heads(4), late(LANES), late(LANES), heads(2),
@@ -295,7 +433,7 @@
 
     def deal(i, carry):
         rows = at_rows(i)
-        pick = (ocol_ref[rows, :] == lane_iota(ROWS, all_rows)).astype(F32).astype(BF16)
+        pick = (ocol_ref[rows, 0:1] == lane_iota(ROWS, all_rows)).astype(F32).astype(BF16)
         dealt = dot_nn(pick, dgiven_ref[...])
         for g, o_ref in enumerate((o0_ref, o1_ref)):
             pair = dealt[:, g * LANES:(g + 1) * LANES]
@@ -368,19 +506,31 @@
     lax.fori_loop(0, blocks, key_block, 0)
 
 
-def rows_back_kernel(orow_ref, draw_ref, *refs):
-    grad_ref, refs = refs[-5], refs[-4:]
+def rows_back_kernel(period, orow_ref, draw_ref, normed_ref, o0_ref, o1_ref, o2_ref, o3_ref, gain_ref, *refs):
+    d_refs, out_ref, grad_ref = refs[-6:-2], refs[-2], refs[-1]
     i = pl.program_id(0)
-    all_rows = draw_ref.shape[0]
-    rows = grad_ref.shape[0]
-    pick = (orow_ref[...] == i * rows + row_iota(rows, all_rows)).astype(F32).astype(BF16)
-    grads = dot_nn(pick, draw_ref[...]).astype(BF16)
-    grad_ref[...] = grads
-    for d, ref in enumerate(refs):
+    all_rows, width = draw_ref.shape
+    rows = all_rows // 4
+    for d, ref in enumerate(d_refs):
 
         @pl.when(i == d)
-        def _(ref=ref):
+        def _(d=d, ref=ref):
+            pick = (orow_ref[...] == d * rows + row_iota(rows, all_rows)).astype(F32).astype(BF16)
+            grads = dot_nn(pick, draw_ref[...]).astype(BF16)
+            grad_ref[d * rows:(d + 1) * rows, :] = grads
             ref[...] = grads
+
+    @pl.when(i >= 4)
+    def _():
+        extra = o0_ref.shape[1]
+        out_ref[:, :width] = dot_tn(normed_ref[...], grad_ref[...]).astype(BF16)
+        total = o0_ref[...].astype(F32)
+        for ref in (o1_ref, o2_ref, o3_ref):
+            total = total + ref[...].astype(F32)
+        out_ref[:, width:width + extra] = total.astype(BF16)
+        place = row_iota(out_ref.shape[0], LANES) % period
+        gains = jnp.where(place == 0, gain_ref[0:1, :], jnp.where(place == 1, gain_ref[1:2, :], 0.0))
+        out_ref[:, width + extra:] = gains.astype(BF16)
 
 
 def norm_back(pair, raw, gain, cosine, su, sd, ones, head_dim):
@@ -420,20 +570,24 @@
     )(lens, ocol, qx, k, v, kt, *lses, *dealts, *grads, rawq, rawk, cosine, su, sd, qg, kg, *after)
 
 
-def rows_back(orow, draw, after):
+def rows_back(orow, draw, normed, parts, gains, shards, after):
     all_rows, width = draw.shape
+    depth, extra = normed.shape[1], parts[0].shape[1]
     tok = all_rows // 4
-    block = pl.BlockSpec((tok, width), lambda i: (i, 0))
-    return pl.pallas_call(
-        rows_back_kernel,
-        grid=(4,),
-        out_shape=(jax.ShapeDtypeStruct(draw.shape, BF16),) + (jax.ShapeDtypeStruct((tok, width), BF16),) * 4,
-        in_specs=[fixed(orow), fixed(draw)] + anywhere(after),
-        out_specs=(block,) + (pl.BlockSpec((tok, width), lambda i: (0, 0)),) * 4,
+    late = lambda c: pl.BlockSpec((depth // 4, c), lambda i: (jnp.maximum(i - 4, 0), 0))
+    wide = width + extra + LANES
+    return pl.pallas_call(
+        functools.partial(rows_back_kernel, depth // shards),
+        grid=(8,),
+        out_shape=(jax.ShapeDtypeStruct((tok, width), BF16),) * 4 + (jax.ShapeDtypeStruct((depth, wide), BF16),),
+        in_specs=[fixed(orow), fixed(draw), pl.BlockSpec((all_rows, depth // 4), lambda i: (0, jnp.maximum(i - 4, 0)))]
+        + [late(extra)] * 4 + [fixed(gains)] + anywhere(after),
+        out_specs=(pl.BlockSpec((tok, width), lambda i: (0, 0)),) * 4 + (late(wide),),
+        scratch_shapes=[pltpu.VMEM((all_rows, width), BF16)],
         compiler_params=params(),
         cost_estimate=COST,
         name="rows_back",
-    )(orow, draw, *after)
+    )(orow, draw, normed, *parts, gains, *after)
 
 
 def tokens_kernel(me_ref, g0_ref, g1_ref, g2_ref, g3_ref, w_ref, x_ref, mid_ref, gain_ref, *refs):
@@ -469,12 +623,14 @@
 
 
 def ffn_kernel(per, blocks, n_carried, *refs):
-    me_ref, att, refs = refs[0], refs[1:9], list(refs[9:])
+    refs = list(refs)
     take = lambda n: [refs.pop(0) for _ in range(n)]
+    me_ref = take(1)[0]
+    att = [take(2 if d < 3 else 2 * len(blocks)) for d in range(4)]
     xs = [take(2 if d == 3 else 1) for d in blocks]
     cots = [take(2 if d == 3 else 1) for d in blocks]
-    wo_ref, gain_ref, wgu_ref, wd_ref = take(4)
-    diag = take(2) if blocks == (1, 2) else None
+    wo_ref, gain_ref, wg_ref, wu_ref, wd_ref = take(5)
+    diag = take(4) if blocks == (1, 2) else None
     take(n_carried)
     nf_ref, hid_ref, dgu_ref, cot_ref = take(4)
     i = pl.program_id(0)
@@ -488,14 +644,14 @@
 
     middle = read(xs).astype(F32)
     for d in range(4):
-        block = jnp.concatenate([att[2 * d][...], att[2 * d + 1][...]], axis=1)
-        middle = middle + dot_nn(block, wo_ref[at_rows(jnp.bitwise_xor(me, d), 2 * LANES), :])
+        block = read([att[d][2 * n:2 * n + 2] for n in range(len(att[d]) // 2)])
+        middle = middle + dot_nn(block, wo_ref[at_rows(jnp.bitwise_xor(me, d), 2 * LANES), :middle.shape[1]])
     r2 = lax.rsqrt(jnp.mean(middle * middle, axis=1, keepdims=True) + EPSILON)
     nf = (middle * r2 * gain_ref[...]).astype(BF16)
     nf_ref[...] = nf
     cot = read(cots)
     cot_ref[...] = cot
-    wg, wu = wgu_ref[:, :hidden_units], wgu_ref[:, hidden_units:]
+    wg, wu = wg_ref[...], wu_ref[...]
     gate = dot_nn(nf, wg)
     up = dot_nn(nf, wu)
     s = jax.nn.sigmoid(gate)
@@ -511,10 +667,8 @@
     bo = dot_nn(hidden, wd_ref[...])
     half = dn.shape[1] // 2
     if blocks == (3,):
-        dna_ref, dnb_ref, bo_ref = take(3)
-        dna_ref[...] = dn[:, :half].astype(BF16)
-        dnb_ref[...] = dn[:, half:].astype(BF16)
-        bo_ref[...] = bo.astype(BF16)
+        for ref, value in zip(take(4), (dn[:, :half], dn[:, half:], bo[:, :half], bo[:, half:])):
+            ref[...] = value.astype(BF16)
     elif blocks == (0,):
         dn_ref, bo_ref, mid_ref = take(3)
         dn_ref[...] = dn.astype(BF16)
@@ -525,20 +679,20 @@
 
         @pl.when(which == 0)
         def _():
-            dn1_ref[:, :half] = dn[:, :half].astype(BF16)
-            dn1_ref[:, half:] = (dn[:, half:] + diag[1][...].astype(F32)).astype(BF16)
-            bo1_ref[...] = bo.astype(BF16)
+            for ref, value, extra in ((dn1_ref, dn, diag[1]), (bo1_ref, bo, diag[3])):
+                ref[:, :half] = value[:, :half].astype(BF16)
+                ref[:, half:] = (value[:, half:] + extra[...].astype(F32)).astype(BF16)
 
         @pl.when(which == 1)
         def _():
-            dn2_ref[:, :half] = (dn[:, :half] + diag[0][...].astype(F32)).astype(BF16)
-            dn2_ref[:, half:] = dn[:, half:].astype(BF16)
-            bo2_ref[...] = bo.astype(BF16)
-
-
-def ffn(me, blocks, att, xs, cots, wo, gain, wgu, wd, diag, carried):
+            for ref, value, extra in ((dn2_ref, dn, diag[0]), (bo2_ref, bo, diag[2])):
+                ref[:, :half] = (value[:, :half] + extra[...].astype(F32)).astype(BF16)
+                ref[:, half:] = value[:, half:].astype(BF16)
+
+
+def ffn(me, blocks, att, xs, cots, gain, wide, wd, diag, carried, after):
     all_rows = att[0].shape[0]
-    width, units = wo.shape[1], wd.shape[0]
+    units, width = wd.shape
     tok = all_rows // 4
     per = tok // ROWS
     block_of = lambda i: blocks[0] + (i // per) * (blocks[-1] - blocks[0])
@@ -547,31 +701,37 @@
         (ROWS, LANES), lambda i: (jnp.bitwise_xor(block_of(i), d) * per + i % per, 0)
     )
     held = lambda n, c: pl.BlockSpec((ROWS, c), lambda i: (jnp.clip(i - n * per, 0, per - 1), 0))
+    halves = {0: 1, 1: 1, 2: 0, 3: 0}
+    last = []
+    for n, d in enumerate(blocks):
+        local = lambda i, n=n, d=d: ((3 - d) % 2 * per + jnp.clip(i - n * per, 0, per - 1), 0)
+        last += [(att[6], crossed(3)), (att[7 + halves[d]], pl.BlockSpec((ROWS, LANES), local))]
+    weight = lambda n: pl.BlockSpec((wide.shape[0], units), lambda i: (0, n), pipeline_mode=pl.Buffered(1))
     out = lambda r, c, t=BF16: jax.ShapeDtypeStruct((r, c), t)
     pieces = lambda arrays: [held(n, a.shape[1]) for n, d in enumerate(blocks) for a in arrays[d]]
     shapes = [out(all_rows, width), out(all_rows, units), out(all_rows, 2 * units), out(all_rows, width)]
     specs = [everywhere(width), everywhere(units), everywhere(2 * units), everywhere(width)]
     if blocks == (3,):
-        shapes += [out(tok, width // 2)] * 2 + [out(tok, width)]
-        specs += [held(0, width // 2)] * 2 + [held(0, width)]
+        shapes += [out(tok, width // 2)] * 4
+        specs += [held(0, width // 2)] * 4
     elif blocks == (0,):
         shapes += [out(tok, width)] * 2 + [out(tok, width, F32)]
         specs += [held(0, width)] * 3
     else:
         shapes += [out(tok, width)] * 4
         specs += [held(0, width), held(1, width)] * 2
-    diag_specs = [held(1, width // 2), held(0, width // 2)] if diag else []
+    diag_specs = [held(1, width // 2), held(0, width // 2)] * 2 if diag else []
     operands = (
-        [me] + list(att) + [a for d in blocks for a in xs[d]] + [a for d in blocks for a in cots[d]]
-        + [wo, gain, wgu, wd] + list(diag) + list(carried)
+        [me] + list(att[:6]) + [a for a, _ in last] + [a for d in blocks for a in xs[d]] + [a for d in blocks for a in cots[d]]
+        + [wide, gain, wide, wide, wd] + list(diag) + list(carried) + list(after)
     )
-    first = len(operands) - len(carried)
-    return pl.pallas_call(
-        functools.partial(ffn_kernel, per, blocks, len(carried)),
+    first = len(operands) - len(carried) - len(after)
+    return pl.pallas_call(
+        functools.partial(ffn_kernel, per, blocks, len(carried) + len(after)),
         grid=(len(blocks) * per,),
         out_shape=tuple(shapes),
-        in_specs=[smem()] + [crossed(d) for d in range(4) for _ in range(2)] + pieces(xs) + pieces(cots)
-        + [fixed(wo), fixed(gain), fixed(wgu), fixed(wd)] + diag_specs + anywhere(carried),
+        in_specs=[smem()] + [crossed(d) for d in range(3) for _ in range(2)] + [spec for _, spec in last]
+        + pieces(xs) + pieces(cots) + [weight(3), fixed(gain), weight(0), weight(1), fixed(wd)] + diag_specs + anywhere(carried) + anywhere(after),
         out_specs=tuple(specs),
         input_output_aliases={first + n: n for n in range(len(carried))},
         compiler_params=params(),
@@ -596,34 +756,6 @@
         cost_estimate=COST,
         name="weights_back",
     )(left, right)
-
-
-def last_kernel(period, normed_ref, grads_ref, o0_ref, o1_ref, o2_ref, o3_ref, gain_ref, out_ref):
-    width, extra = grads_ref.shape[1], o0_ref.shape[1]
-    out_ref[:, :width] = dot_tn(normed_ref[...], grads_ref[...]).astype(BF16)
-    total = o0_ref[...].astype(F32)
-    for ref in (o1_ref, o2_ref, o3_ref):
-        total = total + ref[...].astype(F32)
-    out_ref[:, width:width + extra] = total.astype(BF16)
-    place = row_iota(out_ref.shape[0], LANES) % period
-    gains = jnp.where(place == 0, gain_ref[0:1, :], jnp.where(place == 1, gain_ref[1:2, :], 0.0))
-    out_ref[:, width + extra:] = gains.astype(BF16)
-
-
-def last_weights(normed, grads, parts, gains, shards):
-    rows, depth = normed.shape
-    steps, extra = 4, parts[0].shape[1]
-    block = lambda c: pl.BlockSpec((depth // steps, c), lambda i: (i, 0))
-    return pl.pallas_call(
-        functools.partial(last_kernel, depth // shards),
-        grid=(steps,),
-        out_shape=jax.ShapeDtypeStruct((depth, grads.shape[1] + extra + LANES), BF16),
-        in_specs=[pl.BlockSpec((rows, depth // steps), lambda i: (0, i)), fixed(grads)] + [block(extra)] * 4 + [fixed(gains)],
-        out_specs=block(grads.shape[1] + extra + LANES),
-        compiler_params=params(),
-        cost_estimate=COST,
-        name="last_weights",
-    )(normed, grads, *parts, gains)
 
 
 def middle_kernel(*refs):
@@ -651,7 +783,7 @@
     span = 2 * LANES
     for d in range(4):
         there = pl.ds(pl.multiple_of(jnp.bitwise_xor(me, d) * span, span), span)
-        da_refs[d][...] = dot_nt(branch_ref[...], wo_ref[there, :]).astype(BF16)
+        da_refs[d][...] = dot_nt(branch_ref[...], wo_ref[there, :branch_ref.shape[1]]).astype(BF16)
 
 
 def out_kernel(me_ref, *refs):
@@ -673,28 +805,29 @@
         out_kernel,
         grid=(1,),
         out_shape=(jax.ShapeDtypeStruct((width, width // 4), BF16),) * 4,
-        in_specs=[smem()] + [own(d) for d in range(4) for _ in range(2)] + [whole(tok, width)],
+        in_specs=[smem()] + [own(d) for d in (0, 0, 1, 1, 2, 2, 3, 1)] + [whole(tok, width)],
         out_specs=(whole(width, width // 4),) * 4,
         compiler_params=params(),
         cost_estimate=COST,
         name="out_weights",
-    )(me, *att, branch)
-
-
-def middle_back(me, parts, cot, middle, gain, wo, after):
+    )(me, *att[:7], att[8], branch)
+
+
+def middle_back(me, parts, cot, middle, gain, wide, after):
     tok, width = middle.shape
+    wo = pl.BlockSpec((wide.shape[0], wide.shape[1] // 4), lambda i: (0, 3))
     whole = lambda r, c: pl.BlockSpec((r, c), lambda i: (0, 0))
     out = lambda r, c, t=BF16: jax.ShapeDtypeStruct((r, c), t)
     return pl.pallas_call(
         middle_kernel,
         grid=(1,),
         out_shape=(out(tok, width, F32), out(tok, width)) + (out(tok, 2 * LANES),) * 4,
-        in_specs=[smem()] + [whole(tok, width)] * 5 + [whole(1, width), whole(*wo.shape)] + anywhere(after),
+        in_specs=[smem()] + [whole(tok, width)] * 5 + [whole(1, width), wo] + anywhere(after),
         out_specs=(whole(tok, width),) * 2 + (whole(tok, 2 * LANES),) * 4,
         compiler_params=params(),
         cost_estimate=COST,
         name="middle_back",
-    )(me, *parts, cot, middle, gain, wo, *after)
+    )(me, *parts, cot, middle, gain, wide, *after)
 
 
 def swap(array, distance):
@@ -728,22 +861,7 @@
     units = w_gate.shape[1] // ways
     piece = units // shards
 
-    dealt_index = jnp.arange(all_rows, dtype=jnp.int32)
-    ends = jnp.cumsum(seq_lengths[0])
-    start = jnp.zeros_like(dealt_index)
-    for s in range(seq_lengths.shape[1] - 1):
-        start = jnp.where(dealt_index >= ends[s], ends[s], start)
-    places = (dealt_index - start).astype(F32)
-    lane = jnp.arange(LANES, dtype=jnp.int32) % head_dim
-    half = head_dim // 2
-    frequency = ROPE_BASE ** (-2.0 * jnp.arange(half, dtype=F32) / head_dim)
-    angles = places[:, None] * frequency[None, :]
-    cosine = jnp.tile(jnp.cos(angles), (1, LANES // half))
-    sine = jnp.tile(jnp.sin(angles), (1, LANES // half))
-    sine_up = jnp.where(lane[None, :] < half, -sine, 0.0)
-    sine_down = jnp.where(lane[None, :] < half, 0.0, sine)
-    relative = jnp.bitwise_xor(order[0], me.astype(jnp.int32) * tok)
-    ocol, orow = relative[:, None], relative[None, :]
+    cosine, sine_up, sine_down, ocol, orow = make_tables(me_arr, seq_lengths, order, head_dim)
     q_gain = jnp.tile(query_gain.astype(F32), LANES // head_dim)[None, :]
     k_gain = jnp.tile(key_gain.astype(F32), LANES // head_dim)[None, :]
 
@@ -752,11 +870,9 @@
     xs = gather_rows(tokens[0], tables)
     w_first = first_weights(me_arr, w_query, w_key, w_value, attn_gain, ffn_gain)
     w_qkv = lax.all_gather(w_first, "shard", axis=0, tiled=True)
-    w_o = lax.all_gather(w_out, "shard", axis=0, tiled=True)
-    cut = lambda w: own(w.reshape(depth, shards, ways, piece), 2).reshape(depth, units)
-    w_gate_now, w_up_now, w_down_now = after((w_gate, w_up, w_down), tables)
-    w_gu = lax.all_gather(jnp.concatenate([cut(w_gate_now), cut(w_up_now)], axis=1), "shard", axis=0, tiled=True)
-    w_d = lax.all_gather(own(w_down_now, 0), "shard", axis=0, tiled=True)
+    w_cut = cut_weights(me_arr, w_gate, w_up, own(w_down, 0).reshape(depth, units), w_out, shards)
+    w_wide = lax.all_gather(after(w_cut, xs[1]), "shard", axis=0, tiled=True)
+    w_d = w_wide[:, 2 * units:3 * units].reshape(units, -1)
 
     cosine, sine_up, sine_down, ocol, orow, q_gain, k_gain = xs[0]
     xs = [[tokens[0]]] + xs[1:]
@@ -764,80 +880,69 @@
         [x for one in xs for x in one], w_qkv, ocol, cosine, sine_up, sine_down, q_gain, k_gain, head_dim
     )
     cot = cotangent[0]
-    cots = [[cot]] + gather_rows(after(cot, xs[3]), ())[1:]
+    cots = gather_rows(after(cot, xs[3]), gains)
+    gains, cots = cots[0], [[cot]] + cots[1:]
     gain_a, gain_f = gains[0:1], gains[1:2]
     w_rows = jnp.concatenate(after([w_query, w_key, w_value], xs[3]), axis=1)
     w_all = lax.all_gather(w_rows, "shard", axis=0, tiled=True)
 
     att, dealts, lses = [], [], []
     for g in range(2):
-        given, dealt, lse = attend(g, seq_lengths, orow, qx, k, vx, head_dim, cots[3] if g else [])
-        att.append([given] + [swap(given, d) for d in (1, 2, 3)])
+        given, dealt, lse = attend(g, seq_lengths, orow, qx, k, vx, head_dim, [])
+        one, two = swap(given, 1), swap(given, 2)
+        half = given.shape[0] // 2
+        three = [swap(one[:half], 2), swap(two[half:], 1)] if g else [swap(given, 3)]
+        att.append([given, one, two] + three)
         dealts.append(dealt)
         lses.append(lse)
-    att = [att[g][d] for d in range(4) for g in range(2)]
-
-    feed = lambda blocks, diag, carried: ffn(
-        me_arr, blocks, att, xs, cots, w_o, gain_f, w_gu, w_d, diag, carried
+    att = [att[g][d] for d in range(3) for g in range(2)] + att[0][3:] + att[1][3:]
+
+    feed = lambda blocks, diag, carried, after=(): ffn(
+        me_arr, blocks, att, xs, cots, gain_f, w_wide, w_d, diag, carried, after
     )
-    *carried, dn3a, dn3b, bo3 = feed((3,), (), ())
-    diag = (swap(dn3a, 1), swap(dn3b, 2))
+    *carried, dn3a, dn3b, bo3a, bo3b = feed((3,), (), (), att[8:])
+    diag = (swap(dn3a, 1), swap(dn3b, 2), swap(bo3a, 1), swap(bo3b, 2))
     *carried, dn0, bo0, middle = feed((0,), (), carried)
-    bo3 = swap(after(bo3, diag), 3)
     *carried, dn1, dn2, bo1, bo2 = feed((1, 2), diag, carried)
     nf, hidden, d_gu, cot_all = carried
-    dn1, dn2 = after((dn1, dn2), bo3)
     dn = (dn0, swap(dn1, 1), swap(dn2, 2))
     scatter = lambda a: lax.psum_scatter(a, "shard", scatter_dimension=0, tiled=True)
-    p_wd, p_wgu = weights_back(hidden, cot_all, 3), weights_back(nf, d_gu, 4)
+    p_wd = weights_back(hidden, cot_all, 3)
+    p_wgu = weights_back(nf, after(d_gu, p_wd), 4)
     p_wd, p_wgu = after((p_wd, p_wgu), dn)
     d_wd, d_wgu = scatter(p_wd), scatter(p_wgu)
 
-    d_middle, branch, *d_att = middle_back(me_arr, dn, cot, middle, gain_f, w_o, (p_wd, p_wgu, w_all))
+    d_middle, branch, *d_att = middle_back(me_arr, dn, cot, middle, gain_f, w_wide, (p_wd, p_wgu, w_all))
     p_wo = out_weights(me_arr, att, branch)
     d_att = [d_att[0]] + [swap(d_att[d], d) for d in (1, 2, 3)]
     draw, head_gains = attend_back(
         seq_lengths, ocol, qx, k, v, kt, lses, dealts, d_att, rawq, rawk,
-        cosine, sine_up, sine_down, q_gain, k_gain, head_dim, (d_wd,),
+        cosine, sine_up, sine_down, q_gain, k_gain, head_dim, (),
     )
     bo1, bo2, *p_wo = after([bo1, bo2] + list(p_wo), d_att)
-    bo = [bo0, swap(bo1, 1), swap(bo2, 2), bo3]
+    bo = [bo0, swap(bo1, 1), swap(bo2, 2)]
     p_wo = [p_wo[0]] + [swap(p_wo[d], d) for d in (1, 2, 3)]
-    grads, *d_raw = rows_back(orow, draw, bo[1:3] + p_wo[1:])
-    block_out = (middle + sum(b.astype(F32) for b in after(bo, grads))).astype(BF16)
+    *d_raw, p_last = rows_back(orow, draw, normed, p_wo, head_gains, shards, bo[1:3] + [d_wd])
+    block_out = (middle + sum(b.astype(F32) for b in after(bo, p_last))).astype(BF16)
     d_raw = [d_raw[0]] + [swap(d_raw[d], d) for d in (1, 2, 3)]
-    p_last = last_weights(normed, grads, p_wo, head_gains, shards)
     d_last = scatter(after(p_last, d_wgu))
     d_tokens = tokens_back(me_arr, d_raw, w_all, tokens[0], d_middle, gain_a, (p_last,))
     d_wgu, d_wd = after((d_wgu, d_wd), d_raw, p_last)
 
-    odd, high = me % 2 == 1, me // 2 == 1
-
-    def in_order(parts):
-        parts = list(parts)
-        for a, b, which in ((0, 1, odd), (2, 3, odd), (0, 2, high), (1, 3, high)):
-            parts[a], parts[b] = jnp.where(which, parts[b], parts[a]), jnp.where(which, parts[a], parts[b])
-        return parts
-
-    def quarters(part):
-        return in_order([part] + [swap(part, d) for d in (1, 2, 3)])
-
-    d_wd = quarters(d_wd)
+    def parts_of(part):
+        return [part] + [swap(part, d) for d in (1, 2, 3)]
+
+    d_wd = parts_of(d_wd)
+    for a, b, which in ((0, 1, me % 2), (2, 3, me % 2), (0, 2, me // 2), (1, 3, me // 2)):
+        d_wd[a], d_wd[b] = jnp.where(which == 1, d_wd[b], d_wd[a]), jnp.where(which == 1, d_wd[a], d_wd[b])
     d_wd = jnp.concatenate(d_wd, axis=0).astype(F32)
-    columns = lambda parts, at: jnp.stack(
-        [p[:, at:at + units].reshape(depth, shards, piece) for p in parts], axis=2
-    ).reshape(depth, -1).astype(F32)
-    d_wgu = quarters(d_wgu)
-    d_wg, d_wu = columns(d_wgu, 0), columns(d_wgu, units)
-    last = quarters(after(d_last, d_wgu))
-    beside = lambda parts, lo, hi: jnp.concatenate([p[:, lo:hi] for p in parts], axis=1).astype(F32)
-    d_wq, d_wk, d_wv = beside(last, 0, 256), beside(last, 256, 384), beside(last, 384, 512)
-    d_wo = beside(last, 512, 768)
-    dot_rows = lambda w, d: jnp.sum(w.astype(F32) * d, axis=1)
-    d_attn_gain = (dot_rows(w_query, d_wq) + dot_rows(w_key, d_wk) + dot_rows(w_value, d_wv)) / attn_gain.astype(F32)
-    d_ffn_gain = (dot_rows(w_gate, d_wg) + dot_rows(w_up, d_wu)) / ffn_gain.astype(F32)
-    head_gains = sum(p[0:2, 768:768 + LANES].astype(F32) for p in last)
-    head_gains = head_gains[:, :head_dim] + head_gains[:, head_dim:]
+    d_wg, d_wu, ffn_dots = join_weights(me_arr, parts_of(d_wgu), w_gate, w_up, shards)
+    d_wq, d_wk, d_wv, d_wo, attn_dots, head_gains = join_last(
+        me_arr, parts_of(after(d_last, d_wgu)), w_query, w_key, w_value, w_out.shape[1]
+    )
+    d_attn_gain = attn_dots[:, 0] / attn_gain.astype(F32)
+    d_ffn_gain = ffn_dots[:, 0] / ffn_gain.astype(F32)
+    head_gains = head_gains[0:2, :head_dim] + head_gains[0:2, head_dim:]
     return (
         block_out[None], d_tokens[None], d_attn_gain, d_wq, d_wk, d_wv, head_gains[0], head_gains[1],
         d_wo, d_ffn_gain, d_wg, d_wu, d_wd,

time: 475 us -> 428 us (0.901)
  waiting for transfers between devices: 116 us -> 92.3 us
  local copies, waits for them, and re-layouts: 43.1 us -> 23.3 us
  Pallas kernels: 218 us -> 236 us
  other arithmetic: 27.6 us -> 11.5 us
  starting transfers between devices: 56.6 us -> 46.1 us
    ppermute x39 -> x41, waiting for transfers between devices: 105 us -> 87.2 us  [swap(): return lax.ppermute(array, 'seq', [(s, s ^ distance) for s in range(4)])]
    pallas_call x5 -> x8, Pallas kernels: 80.8 us -> 97.9 us  [the longest x3 65.2 us: ffn(): pl.pallas_call(functools.partial(ffn_kernel, per, blocks, len(carried) +...]
    ppermute x39 -> x41, starting transfers between devices: 56.3 us -> 45.3 us  [swap(): return lax.ppermute(array, 'seq', [(s, s ^ distance) for s in range(4)])]
    slice x21 -> x4, local copies, waits for them, and re-layouts: 12 us -> 3.09 us  [the longest x2 1.65 us: body(): w_d = w_wide[:, 2 * units:3 * units].reshape(units, -1)]
    unnamed x96 -> x74, local copies, waits for them, and re-layouts: 14.4 us -> 6.06 us
    reduce_sum x5 -> x0, other arithmetic: 5.25 us -> none  [body(): dot_rows = lambda w, d: jnp.sum(w.astype(F32) * d, axis=1)]
    reshape x2, local copies, waits for them, and re-layouts: 0.41 us -> 5.59 us  [the longest x1 3.58 us: body(): w_d = w_wide[:, 2 * units:3 * units].reshape(units, -1)]
    optimization_barrier x4 -> x0, local copies, waits for them, and re-layouts: 4.79 us -> none  [the longest x2 2.66 us: gather_rows(): one, two, meanwhile = lax.optimization_barrier((one, two, meanwhile))]
  transfers between devices with their start and end apart: 47 -> 47, of which waited for: 23 -> 17; matrix products, arithmetic and copies ran while one was open for 12% -> 6% of each run, Pallas kernels for 45% -> 55%
where the time goes in v3:
time: 428 us; the launch traced here: 424 us
  Pallas kernels  236 us (55%)
  waiting for transfers between devices  92.3 us (22%)
  starting transfers between devices  46.1 us (11%)
  local copies, waits for them, and re-layouts  23.3 us (5%)
  between operations  15 us (4%)
  other arithmetic  11.5 us (3%)
    ppermute x41, waiting for transfers between devices, swap(): return lax.ppermute(array, 'seq', [(s, s ^ distance) for s in range(4)])  87.2 us
    pallas_call x3, Pallas kernels, ffn(): pl.pallas_call(functools.partial(ffn_kernel, per, blocks, len(carried) +...  65.2 us
    pallas_call x1, Pallas kernels, attend_back(): pl.pallas_call(functools.partial(attend_back_kernel, head_dim), out_shape...  48.2 us
    ppermute x41, starting transfers between devices, swap(): return lax.ppermute(array, 'seq', [(s, s ^ distance) for s in range(4)])  45.3 us
    pallas_call x2, Pallas kernels, attend(): pl.pallas_call(functools.partial(attend_kernel, head_dim, group, all_rows...  27.6 us
    pallas_call x2, Pallas kernels, weights_back(): pl.pallas_call(weights_kernel, grid=(steps,), out_shape=jax.ShapeDtypeStr...  24.7 us
    pallas_call x1, Pallas kernels, qkv(): pl.pallas_call(functools.partial(qkv_kernel, head_dim), grid=(8,), out_sh...  16.9 us
    pallas_call x1, Pallas kernels, rows_back(): pl.pallas_call(functools.partial(rows_back_kernel, depth // shards), grid...  13.7 us
  transfers between devices with their start and end apart: 47, of which 17 were waited for; matrix products, arithmetic and copies ran while one was open for 6% of the time, Pallas kernels for 55%

profile of v3, /device:TPU:0, one launch (start us, length us, event | category | flops | bytes accessed | tf_op | source)
XLA Modules:
  0.0 423.9 jit_solution(11249702969050708199)
XLA Ops:
  7.2 1.9 first_weights.1
  9.2 3.0 collective-permute-start
  12.2 1.5 collective-permute-start.1
  17.6 2.0 reshape.39.down_ref
  19.6 5.5 %make_tables.1 = (f32[2048,128]{1,0:T(8,128)}, f32[2048,128]{1,0:T(8,128)}, f32[2048,128]{1,0:T(8,128)}, s32[2048,128]{1,0:T(8,128)}, s32[1,2048]{1,0:T(1,128)}) custom-call(s32[1]{0:T(128)} %bitcast.me_ref.refs_0_, s32[1,3]{1,0:T(1,128)} %refs_0_.1, s32[1,2048]{1,0:T(1,128)} %order_ref.1, f32[1,128]{1,0:T(1,128)} %broadcast_in_dim_tile.9.freq_ref), custom_call_target="tpu_custom_call" | custom-call | flops 1048576 | bytes 65536 | tf_op jit(solution)/shard_map/make_tables/pallas_call | solution.py:236
  25.1 4.8 %cut_weights.1 = bf16[128,4608]{1,0:T(8,128)(2,1)} custom-call(s32[1]{0:T(128)} %bitcast.me_ref.refs_0_, bf16[128,4608]{1,0:T(8,128)(2,1)} %gate_ref.3, bf16[128,4608]{1,0:T(8,128)(2,1)} %up_ref.3, bf16[128,1152]{1,0:T(8,128)(2,1)} %reshape.39.down_ref, bf16[128,1024]{1,0:T(8,128)(2,1)} %wo_ref.1), custom_call_target="tpu_custom_call" | custom-call | flops 1048576 | bytes 65536 | tf_op jit(solution)/shard_map/cut_weights/pallas_call | solution.py:124
  29.9 5.7 %collective-permute-done.x1_ref.refs_11_ = bf16[512,1024]{1,0:T(8,128)(2,1)S(1)} collective-permute-done((bf16[512,1024]{1,0:T(8,128)(2,1)}, bf16[512,1024]{1,0:T(8,128)(2,1)S(1)}, u32[]{:S(2)}, u32[]{:S(2)}) %collective-permute-start) | collective-permute-done | bytes 1048608 | tf_op jit(solution)/shard_map/ppermute | solution.py:834
  35.6 1.5 collective-permute-done.1.x2_ref.refs_12_
  37.2 1.6 collective-permute-start.2
  39.4 10.4 %collective-permute-done.2.x3a_ref.refs_9_ = bf16[512,512]{1,0:T(8,128)(2,1)} collective-permute-done((bf16[512,512]{1,0:T(8,128)(2,1)S(1)}, bf16[512,512]{1,0:T(8,128)(2,1)}, u32[]{:S(2)}, u32[]{:S(2)}) %collective-permute-start.2) | collective-permute-done | bytes 524320 | tf_op jit(solution)/shard_map/ppermute | solution.py:834
  49.8 1.3 collective-permute-done.3.x3b_ref.refs_10_
  51.2 1.7 pad_maximum_fusion
  54.9 16.9 %qkv.1 = (bf16[2048,1024]{1,0:T(8,128)(2,1)}, bf16[4,2048,128]{2,1,0:T(8,128)(2,1)}, bf16[2048,128]{1,0:T(8,128)(2,1)}, bf16[2048,128]{1,0:T(8,128)(2,1)}, bf16[...) custom-call(bf16[512,1024]{1,0:T(8,128)(2,1)} %bitcast.14, ...), custom_call_target="tpu_custom_call" | custom-call | flops 1048576 | bytes 65536 | tf_op jit(solution)/shard_map/qkv/pallas_call | solution.py:309
  71.8 13.7 %attend.3 = (bf16[2048,128]{1,0:T(8,128)(2,1)}, bf16[2048,128]{1,0:T(8,128)(2,1)}, f32[2,2048]{1,0:T(2,128)}) custom-call(s32[1,3]{1,0:T(1,128)} %refs_0_.1, s32[1,2048]{1,0:T(1,128)} %get-tuple-element.120.orow_ref, bf16[4,2048,128]{2,1,0:T(8,128)(2,1)} %get-tuple-element.129.qx_ref.refs_2_, bf16[2048,128]{1,0:T(8,128)(2,1)} %get-tuple-element.130.k_ref.refs_3_, ...), custom_call_target="tpu_custom_call" | custom-call | flops 1048576 | bytes 65536 | tf_op jit(solution)/shard_map/attend/pallas_call | solution.py:397
  85.6 1.2 collective-permute-start.5
  86.8 1.5 collective-permute-start.7
  88.3 13.9 %attend.2 = (bf16[2048,128]{1,0:T(8,128)(2,1)}, bf16[2048,128]{1,0:T(8,128)(2,1)}, f32[2,2048]{1,0:T(2,128)}) custom-call(s32[1,3]{1,0:T(1,128)} %refs_0_.1, s32[1,2048]{1,0:T(1,128)} %get-tuple-element.120.orow_ref, bf16[4,2048,128]{2,1,0:T(8,128)(2,1)} %get-tuple-element.129.qx_ref.refs_2_, bf16[2048,128]{1,0:T(8,128)(2,1)} %get-tuple-element.130.k_ref.refs_3_, ...), custom_call_target="tpu_custom_call" | custom-call | flops 1048576 | bytes 65536 | tf_op jit(solution)/shard_map/attend/pallas_call | solution.py:397
  103.5 2.1 collective-permute-start.8
  106.5 1.9 slice.46
  111.2 6.2 %collective-permute-done.4.refs_3_.refs_2_ = bf16[2048,128]{1,0:T(8,128)(2,1)} collective-permute-done((bf16[2048,128]{1,0:T(8,128)(2,1)}, bf16[2048,128]{1,0:T(8,128)(2,1)}, u32[]{:S(2)}, u32[]{:S(2)}) %collective-permute-start.4) | collective-permute-done | bytes 524320 | tf_op jit(solution)/shard_map/ppermute | solution.py:834
  117.9 11.5 %collective-permute-done.6.refs_5_.refs_4_ = bf16[2048,128]{1,0:T(8,128)(2,1)} collective-permute-done((bf16[2048,128]{1,0:T(8,128)(2,1)}, bf16[2048,128]{1,0:T(8,128)(2,1)}, u32[]{:S(2)}, u32[]{:S(2)}) %collective-permute-start.6) | collective-permute-done | bytes 524320 | tf_op jit(solution)/shard_map/ppermute | solution.py:834
  129.3 1.3 collective-permute-start.9
  130.6 1.4 fusion.1
  132.1 1.7 slice-done
  133.7 3.6 reshape.40.refs_17_.refs_15_.refs_19_
  137.3 4.3 %collective-permute-done.12.refs_8_.refs_10_ = bf16[1024,128]{1,0:T(8,128)(2,1)} collective-permute-done((bf16[1024,128]{1,0:T(8,128)(2,1)}, bf16[1024,128]{1,0:T(8,128)(2,1)}, u32[]{:S(2)}, u32[]{:S(2)}) %collective-permute-start.12) | collective-permute-done | bytes 262176 | tf_op jit(solution)/shard_map/ppermute | solution.py:834
  141.6 16.9 %ffn.3 = (bf16[2048,1024]{1,0:T(8,128)(2,1)}, bf16[2048,1152]{1,0:T(8,128)(2,1)}, bf16[2048,2304]{1,0:T(8,128)(2,1)}, bf16[2048,1024]{1,0:T(8,128)(2,1)}, bf16[5...) custom-call(s32[1]{0:T(128)} %bitcast.me_ref.refs_0_, ...), custom_call_target="tpu_custom_call" | custom-call | flops 1048576 | bytes 65536 | tf_op jit(solution)/shard_map/ffn/pallas_call | solution.py:729
  158.6 1.1 collective-permute-start.15
  160.2 1.2 collective-permute-start.17
  161.4 1.3 collective-permute-start.18
  162.7 17.0 %ffn.4 = (bf16[2048,1024]{1,0:T(8,128)(2,1)}, bf16[2048,1152]{1,0:T(8,128)(2,1)}, bf16[2048,2304]{1,0:T(8,128)(2,1)}, bf16[2048,1024]{1,0:T(8,128)(2,1)}, bf16[5...) custom-call(s32[1]{0:T(128)} %bitcast.me_ref.refs_0_, ...), custom_call_target="tpu_custom_call", output_to_operand_aliasing={{0}: (16, {}), {1}: (17, {}), {2}: (18, {}), {3}: (19, {})} | custom-call | flops 1048576 | bytes 65536 | tf_op jit(solution)/shard_map/ffn/pallas_call | solution.py:729
  181.1 31.2 %ffn.5 = (bf16[2048,1024]{1,0:T(8,128)(2,1)}, bf16[2048,1152]{1,0:T(8,128)(2,1)}, bf16[2048,2304]{1,0:T(8,128)(2,1)}, bf16[2048,1024]{1,0:T(8,128)(2,1)}, bf16[5...) custom-call(s32[1]{0:T(128)} %bitcast.me_ref.refs_0_, ...), custom_call_target="tpu_custom_call", output_to_operand_aliasing={{0}: (24, {}), {1}: (25, {}), {2}: (26, {}), {3}: (27, {})} | custom-call | flops 1048576 | bytes 65536 | tf_op jit(solution)/shard_map/ffn/pallas_call | solution.py:729
  212.4 1.1 collective-permute-start.19
  214.5 9.0 %weights_back.2.refs_8_ = bf16[1152,1024]{1,0:T(8,128)(2,1)} custom-call(bf16[2048,1152]{1,0:T(8,128)(2,1)} %get-tuple-element.159.left_ref, bf16[2048,1024]{1,0:T(8,128)(2,1)} %get-tuple-element.160.right_ref), custom_call_target="tpu_custom_call" | custom-call | flops 1048576 | bytes 65536 | tf_op jit(solution)/shard_map/weights_back/pallas_call | solution.py:749
  223.5 15.7 %weights_back.3.refs_9_ = bf16[1024,2304]{1,0:T(8,128)(2,1)} custom-call(bf16[2048,1024]{1,0:T(8,128)(2,1)} %get-tuple-element.161.left_ref, bf16[2048,2304]{1,0:T(8,128)(2,1)} %get-tuple-element.163.right_ref), custom_call_target="tpu_custom_call" | custom-call | flops 1048576 | bytes 65536 | tf_op jit(solution)/shard_map/weights_back/pallas_call | solution.py:749
  240.6 7.0 %middle_back.1 = (f32[512,1024]{1,0:T(8,128)}, bf16[512,1024]{1,0:T(8,128)(2,1)}, bf16[512,256]{1,0:T(8,128)(2,1)}, bf16[512,256]{1,0:T(8,128)(2,1)}, bf16[512,2...) custom-call(s32[1]{0:T(128)} %bitcast.me_ref.refs_0_, bf16[512,1024]{1,0:T(8,128)(2,1)} %get-tuple-element.156.refs_1_, ...), custom_call_target="tpu_custom_call" | custom-call | flops 1048576 | bytes 65536 | tf_op jit(solution)/shard_map/middle_back/pallas_call | solution.py:821
  248.3 1.3 collective-permute-start.22
  249.6 1.4 collective-permute-start.23
  251.0 4.2 %out_weights.1 = (bf16[1024,256]{1,0:T(8,128)(2,1)}, bf16[1024,256]{1,0:T(8,128)(2,1)}, bf16[1024,256]{1,0:T(8,128)(2,1)}, bf16[1024,256]{1,0:T(8,128)(2,1)}) custom-call(s32[1]{0:T(128)} %bitcast.me_ref.refs_0_, bf16[2048,128]{1,0:T(8,128)(2,1)} %get-tuple-element.132.refs_1_.refs_0_, bf16[2048,128]{1,0:T(8,128)(2,1)} %get-tuple-element.133.refs_2_.refs_1_, ...), custom_call_target="tpu_custom_call" | custom-call | flops 1048576 | bytes 65536 | tf_op jit(solution)/shard_map/out_weights/pallas_call | solution.py:804
  255.5 5.6 %collective-permute-done.23.refs_13_ = bf16[512,256]{1,0:T(8,128)(2,1)S(1)} collective-permute-done((bf16[512,256]{1,0:T(8,128)(2,1)}, bf16[512,256]{1,0:T(8,128)(2,1)S(1)}, u32[]{:S(2)}, u32[]{:S(2)}) %collective-permute-start.23) | collective-permute-done | bytes 262176 | tf_op jit(solution)/shard_map/ppermute | solution.py:834
  262.3 1.8 collective-permute-start.26
  264.1 1.1 collective-permute-start.27
  265.8 48.2 %attend_back.1 = (bf16[2048,512]{1,0:T(8,128)(2,1)}, f32[2,128]{1,0:T(2,128)}) custom-call(s32[1,3]{1,0:T(1,128)} %refs_0_.1, s32[2048,128]{1,0:T(8,128)} %get-tuple-element.123.ocol_ref.refs_1_, bf16[4,2048,128]{2,1,0:T(8,128)(2,1)} %get-tuple-element.129.qx_ref.refs_2_, bf16[2048,128]{1,0:T(8,128)(2,1)} %get-tuple-element.130.k_ref.refs_3_, ...), custom_call_target="tpu_custom_call" | custom-call | flops 1048576 | bytes 65536 | tf_op jit(solution)/shard_map/attend_back/pallas_call | solution.py:552
  316.1 13.7 %rows_back.1 = (bf16[512,512]{1,0:T(8,128)(2,1)}, bf16[512,512]{1,0:T(8,128)(2,1)}, bf16[512,512]{1,0:T(8,128)(2,1)}, bf16[512,512]{1,0:T(8,128)(2,1)}, bf16[1024,896]{1,0:T(8,128)(2,1)}) custom-call(s32[1,2048]{1,0:T(1,128)} %get-tuple-element.120.orow_ref, bf16[2048,512]{1,0:T(8,128)(2,1)} %get-tuple-element.188.draw_ref, ...), custom_call_target="tpu_custom_call" | custom-call | flops 1048576 | bytes 65536 | tf_op jit(solution)/shard_map/rows_back/pallas_call | solution.py:579
  329.8 4.4 %reduce-scatter.6.cloned.1.call-done.p0_ref = bf16[128,2304]{1,0:T(8,128)(2,1)} async-done(((bf16[1024,2304]{1,0:T(8,128)(2,1)}), bf16[128,2304]{1,0:T(8,128)(2,1)}) %reduce-scatter.6.cloned.1.call-update) | async-done | bytes 589840 | tf_op jit(solution)/shard_map/reduce_scatter | solution.py:909
  334.2 1.5 collective-permute-start.29
  335.7 1.5 collective-permute-start.30
  337.7 11.6 %collective-permute-done.29.g1_ref = bf16[512,512]{1,0:T(8,128)(2,1)S(1)} collective-permute-done((bf16[512,512]{1,0:T(8,128)(2,1)}, bf16[512,512]{1,0:T(8,128)(2,1)S(1)}, u32[]{:S(2)}, u32[]{:S(2)}) %collective-permute-start.29) | collective-permute-done | bytes 524320 | tf_op jit(solution)/shard_map/ppermute | solution.py:834
  349.3 9.1 %collective-permute-done.30.g2_ref = bf16[512,512]{1,0:T(8,128)(2,1)S(1)} collective-permute-done((bf16[512,512]{1,0:T(8,128)(2,1)}, bf16[512,512]{1,0:T(8,128)(2,1)S(1)}, u32[]{:S(2)}, u32[]{:S(2)}) %collective-permute-start.30) | collective-permute-done | bytes 524320 | tf_op jit(solution)/shard_map/ppermute | solution.py:834
  359.4 1.5 collective-permute-start.38
  361.9 1.0 collective-permute-start.40
  363.9 1.0 collective-permute-start.36
  364.9 5.4 %collective-permute-done.38 = bf16[144,1024]{1,0:T(8,128)(2,1)} collective-permute-done((bf16[144,1024]{1,0:T(8,128)(2,1)S(1)}, bf16[144,1024]{1,0:T(8,128)(2,1)}, u32[]{:S(2)}, u32[]{:S(2)}) %collective-permute-start.38) | collective-permute-done | bytes 294944 | tf_op jit(solution)/shard_map/ppermute | solution.py:834
  370.3 1.5 collective-permute-start.37
  371.8 3.3 fusion
  375.1 7.3 %tokens_back.1 = bf16[512,1024]{1,0:T(8,128)(2,1)} custom-call(s32[1]{0:T(128)} %bitcast.me_ref.refs_0_, bf16[512,512]{1,0:T(8,128)(2,1)} %get-tuple-element.199.g0_ref, bf16[512,512]{1,0:T(8,128)(2,1)} %copy-done.21, bf16[512,512]{1,0:T(8,128)(2,1)} %copy-done.22, bf16[512,512]{1,0:T(8,128)(2,1)} %copy-done.23, ...), custom_call_target="tpu_custom_call" | custom-call | flops 1048576 | bytes 65536 | tf_op jit(solution)/shard_map/tokens_back/pallas_call | solution.py:613
  382.4 1.1 broadcast_select_fusion.7
  383.5 1.5 collective-permute-start.32
  385.5 3.8 collective-permute-done.35.p1_ref
  390.3 1.7 maximum_convert_fusion
  392.0 4.2 collective-permute-done.36.p2_ref
  396.2 5.8 %collective-permute-done.37.p3_ref = bf16[128,2304]{1,0:T(8,128)(2,1)} collective-permute-done((bf16[128,2304]{1,0:T(8,128)(2,1)}, bf16[128,2304]{1,0:T(8,128)(2,1)}, u32[]{:S(2)}, u32[]{:S(2)}) %collective-permute-start.37) | collective-permute-done | bytes 589856 | tf_op jit(solution)/shard_map/ppermute | solution.py:834
  402.0 6.0 %join_weights.1 = (f32[128,4608]{1,0:T(8,128)}, f32[128,4608]{1,0:T(8,128)}, f32[128,1]{1,0:T(8,128)}) custom-call(s32[1]{0:T(128)} %bitcast.me_ref.refs_0_, bf16[128,2304]{1,0:T(8,128)(2,1)} %reduce-scatter.6.cloned.1.call-done.p0_ref, bf16[128,2304]{1,0:T(8,128)(2,1)} %collective-permute-done.35.p1_ref, bf16[128,2304]{1,0:T(8,128)(2,1)} %collective-permute-done.36.p2_ref, ...), custom_call_target="tpu_custom_call" | custom-call | flops 1048576 | bytes 65536 | tf_op jit(solution)/shard_map/join_weights/pallas_call | solution.py:153
  411.1 2.7 join_last.1
  (157 shorter events, 31.9 us)
Async XLA Ops:
  7.2 47.8 %all-gather.4.cloned.1.call-start = ((), (), s32[]{:S(2)}) async-start(), calls=%async_computation.3 | async-start | bytes 1474560 | tf_op jit(solution)/shard_map/all_gather | solution.py:872
  9.2 122.8 %all-gather.6.cloned.1.call-start = ((), (), s32[]{:S(2)}) async-start(), calls=%async_computation.4 | async-start | bytes 10616832 | tf_op jit(solution)/shard_map/all_gather | solution.py:874
  9.2 26.4 %collective-permute-start = (bf16[512,1024]{1,0:T(8,128)(2,1)}, bf16[512,1024]{1,0:T(8,128)(2,1)S(1)}, u32[]{:S(2)}, u32[]{:S(2)}) collective-permute-start(bf16[512,1024]{1,0:T(8,128)(2,1)} %bitcast.12), channel_id=1, source_target_pairs={{0,8},{8,0},{16,24},{24,16},{1,9},{9,1},{17,25},{25,17},{2,10},{10... | collective-permute-start | bytes 3145736 | tf_op jit(solution)/shard_map/ppermute | solution.py:834
  12.2 24.8 %collective-permute-start.1 = (bf16[512,1024]{1,0:T(8,128)(2,1)}, bf16[512,1024]{1,0:T(8,128)(2,1)S(1)}, u32[]{:S(2)}, u32[]{:S(2)}) collective-permute-start(bf16[512,1024]{1,0:T(8,128)(2,1)} %bitcast.13), channel_id=1, source_target_pairs={{0,16},{8,24},{16,0},{24,8},{1,17},{9,25},{17,1},{25,9},{2,18},{10... | collective-permute-start | bytes 3145736 | tf_op jit(solution)/shard_map/ppermute | solution.py:834
  29.9 21.3 %copy-start.12 = (bf16[128,1024]{1,0:T(8,128)(2,1)S(1)}, bf16[128,1024]{1,0:T(8,128)(2,1)}, u32[]{:S(2)}) copy-start(bf16[128,1024]{1,0:T(8,128)(2,1)} %q_ref.3) | copy-start | bytes 786436
  29.9 21.3 %copy-start.14 = (bf16[128,512]{1,0:T(8,128)(2,1)S(1)}, bf16[128,512]{1,0:T(8,128)(2,1)}, u32[]{:S(2)}) copy-start(bf16[128,512]{1,0:T(8,128)(2,1)} %k_ref.3) | copy-start | bytes 393220
  35.6 17.3 %copy-start.6 = (bf16[512,1024]{1,0:T(8,128)(2,1)}, bf16[512,1024]{1,0:T(8,128)(2,1)S(1)}, u32[]{:S(2)}) copy-start(bf16[512,1024]{1,0:T(8,128)(2,1)S(1)} %collective-permute-done.x1_ref.refs_11_) | copy-start | bytes 3145732
  37.1 15.9 %copy-start.7 = (bf16[512,1024]{1,0:T(8,128)(2,1)}, bf16[512,1024]{1,0:T(8,128)(2,1)S(1)}, u32[]{:S(2)}) copy-start(bf16[512,1024]{1,0:T(8,128)(2,1)S(1)} %collective-permute-done.1.x2_ref.refs_12_) | copy-start | bytes 3145732
  37.1 16.5 %copy-start.8 = (bf16[1,512,1024]{2,1,0:T(8,128)(2,1)S(1)}, bf16[1,512,1024]{2,1,0:T(8,128)(2,1)}, u32[]{:S(2)}) copy-start(bf16[1,512,1024]{2,1,0:T(8,128)(2,1)} %param.29) | copy-start | bytes 3145732
  37.1 203.5 %all-gather.8.cloned.1.call-start = ((), (), s32[]{:S(2)}) async-start(), calls=%async_computation.5 | async-start | bytes 4718592 | tf_op jit(solution)/shard_map/all_gather | solution.py:887
  37.2 12.6 %collective-permute-start.2 = (bf16[512,512]{1,0:T(8,128)(2,1)S(1)}, bf16[512,512]{1,0:T(8,128)(2,1)}, u32[]{:S(2)}, u32[]{:S(2)}) collective-permute-start(bf16[512,512]{1,0:T(8,128)(2,1)S(1)} %slice.39), channel_id=1, source_target_pairs={{0,16},{8,24},{16,0},{24,8},{1,17},{9,25},{17,1},{25,9},{2,18},{10... | collective-permute-start | bytes 1572872 | tf_op jit(solution)/shard_map/ppermute | solution.py:834
  38.8 12.4 %collective-permute-start.3 = (bf16[512,512]{1,0:T(8,128)(2,1)S(1)}, bf16[512,512]{1,0:T(8,128)(2,1)}, u32[]{:S(2)}, u32[]{:S(2)}) collective-permute-start(bf16[512,512]{1,0:T(8,128)(2,1)S(1)} %slice.40), channel_id=1, source_target_pairs={{0,8},{8,0},{16,24},{24,16},{1,9},{9,1},{17,25},{25,17},{2,10},{10... | collective-permute-start | bytes 1572872 | tf_op jit(solution)/shard_map/ppermute | solution.py:834
  53.0 262.1 %reduce-scatter.4.cloned.1.call-start = ((), (), s32[]{:S(2)}) async-start(), calls=%async_computation.6 | async-start | bytes 2654208 | tf_op jit(solution)/shard_map/reduce_scatter | solution.py:909
  53.6 49.3 %collective-permute-start.10 = (bf16[512,1024]{1,0:T(8,128)(2,1)S(1)}, bf16[512,1024]{1,0:T(8,128)(2,1)S(1)}, u32[]{:S(2)}, u32[]{:S(2)}) collective-permute-start(bf16[512,1024]{1,0:T(8,128)(2,1)S(1)} %bitcast.19), channel_id=1, source_target_pairs={{0,8},{8,0},{16,24},{24,16},{1,9},{9,1},{17,25},{25,17},{2,10},{10... | collective-permute-start | bytes 3145736 | tf_op jit(solution)/shard_map/ppermute | solution.py:834
  54.3 49.2 %collective-permute-start.11 = (bf16[512,1024]{1,0:T(8,128)(2,1)S(1)}, bf16[512,1024]{1,0:T(8,128)(2,1)}, u32[]{:S(2)}, u32[]{:S(2)}) collective-permute-start(bf16[512,1024]{1,0:T(8,128)(2,1)S(1)} %bitcast.20), channel_id=1, source_target_pairs={{0,16},{8,24},{16,0},{24,8},{1,17},{9,25},{17,1},{25,9},{2,18},{10... | collective-permute-start | bytes 3145736 | tf_op jit(solution)/shard_map/ppermute | solution.py:834
  85.6 22.8 %collective-permute-start.5 = (bf16[2048,128]{1,0:T(8,128)(2,1)}, bf16[2048,128]{1,0:T(8,128)(2,1)S(1)}, u32[]{:S(2)}, u32[]{:S(2)}) collective-permute-start(bf16[2048,128]{1,0:T(8,128)(2,1)} %get-tuple-element.133.refs_2_.refs_1_), channel_id=1, source_target_pairs={{0,8},{8,0},{16,24},{24,16},{1,9},{9,1},{17,25},{25,17},{2,10},{10... | collective-permute-start | bytes 1572872 | tf_op jit(solution)/shard_map/ppermute | solution.py:834
  86.8 22.1 %collective-permute-start.7 = (bf16[2048,128]{1,0:T(8,128)(2,1)}, bf16[2048,128]{1,0:T(8,128)(2,1)S(1)}, u32[]{:S(2)}, u32[]{:S(2)}) collective-permute-start(bf16[2048,128]{1,0:T(8,128)(2,1)} %get-tuple-element.133.refs_2_.refs_1_), channel_id=1, source_target_pairs={{0,16},{8,24},{16,0},{24,8},{1,17},{9,25},{17,1},{25,9},{2,18},{10... | collective-permute-start | bytes 1572872 | tf_op jit(solution)/shard_map/ppermute | solution.py:834
  102.2 15.2 %collective-permute-start.4 = (bf16[2048,128]{1,0:T(8,128)(2,1)}, bf16[2048,128]{1,0:T(8,128)(2,1)}, u32[]{:S(2)}, u32[]{:S(2)}) collective-permute-start(bf16[2048,128]{1,0:T(8,128)(2,1)} %get-tuple-element.132.refs_1_.refs_0_), channel_id=1, source_target_pairs={{0,8},{8,0},{16,24},{24,16},{1,9},{9,1},{17,25},{25,17},{2,10},{10... | collective-permute-start | bytes 1572872 | tf_op jit(solution)/shard_map/ppermute | solution.py:834
  102.9 29.1 %copy-start.11 = (bf16[512,1024]{1,0:T(8,128)(2,1)}, bf16[512,1024]{1,0:T(8,128)(2,1)S(1)}, u32[]{:S(2)}) copy-start(bf16[512,1024]{1,0:T(8,128)(2,1)S(1)} %collective-permute-done.10.refs_13_) | copy-start | bytes 3145732
  102.9 26.4 %collective-permute-start.6 = (bf16[2048,128]{1,0:T(8,128)(2,1)}, bf16[2048,128]{1,0:T(8,128)(2,1)}, u32[]{:S(2)}, u32[]{:S(2)}) collective-permute-start(bf16[2048,128]{1,0:T(8,128)(2,1)} %get-tuple-element.132.refs_1_.refs_0_), channel_id=1, source_target_pairs={{0,16},{8,24},{16,0},{24,8},{1,17},{9,25},{17,1},{25,9},{2,18},{10... | collective-permute-start | bytes 1572872 | tf_op jit(solution)/shard_map/ppermute | solution.py:834
  103.5 33.8 %collective-permute-start.8 = (bf16[2048,128]{1,0:T(8,128)(2,1)}, bf16[2048,128]{1,0:T(8,128)(2,1)S(1)}, u32[]{:S(2)}, u32[]{:S(2)}) collective-permute-start(bf16[2048,128]{1,0:T(8,128)(2,1)} %get-tuple-element.132.refs_1_.refs_0_), channel_id=1, source_target_pairs={{0,24},{8,16},{16,8},{24,0},{1,25},{9,17},{17,9},{25,1},{2,26},{10... | collective-permute-start | bytes 1572872 | tf_op jit(solution)/shard_map/ppermute | solution.py:834
  108.4 23.7 %copy-start.3 = (bf16[2048,128]{1,0:T(8,128)(2,1)}, bf16[2048,128]{1,0:T(8,128)(2,1)S(1)}, u32[]{:S(2)}) copy-start(bf16[2048,128]{1,0:T(8,128)(2,1)S(1)} %collective-permute-done.5.refs_4_.refs_3_) | copy-start | bytes 1572868
  108.4 33.3 %collective-permute-start.13 = (bf16[512,512]{1,0:T(8,128)(2,1)}, bf16[512,512]{1,0:T(8,128)(2,1)}, u32[]{:S(2)}, u32[]{:S(2)}) collective-permute-start(bf16[512,512]{1,0:T(8,128)(2,1)} %slice.45), channel_id=1, source_target_pairs={{0,16},{8,24},{16,0},{24,8},{1,17},{9,25},{17,1},{25,9},{2,18},{10... | collective-permute-start | bytes 1572872 | tf_op jit(solution)/shard_map/ppermute | solution.py:834
  108.9 32.8 %collective-permute-start.14 = (bf16[512,512]{1,0:T(8,128)(2,1)}, bf16[512,512]{1,0:T(8,128)(2,1)}, u32[]{:S(2)}, u32[]{:S(2)}) collective-permute-start(bf16[512,512]{1,0:T(8,128)(2,1)} %slice.46), channel_id=1, source_target_pairs={{0,8},{8,0},{16,24},{24,16},{1,9},{9,1},{17,25},{25,17},{2,10},{10... | collective-permute-start | bytes 1572872 | tf_op jit(solution)/shard_map/ppermute | solution.py:834
  117.3 24.3 %collective-permute-start.12 = (bf16[1024,128]{1,0:T(8,128)(2,1)}, bf16[1024,128]{1,0:T(8,128)(2,1)}, u32[]{:S(2)}, u32[]{:S(2)}) collective-permute-start(bf16[1024,128]{1,0:T(8,128)(2,1)} %slice.54), channel_id=1, source_target_pairs={{0,16},{8,24},{16,0},{24,8},{1,17},{9,25},{17,1},{25,9},{2,18},{10... | collective-permute-start | bytes 786440 | tf_op jit(solution)/shard_map/ppermute | solution.py:834
  129.3 12.3 %collective-permute-start.9 = (bf16[1024,128]{1,0:T(8,128)(2,1)}, bf16[1024,128]{1,0:T(8,128)(2,1)}, u32[]{:S(2)}, u32[]{:S(2)}) collective-permute-start(bf16[1024,128]{1,0:T(8,128)(2,1)} %slice.52), channel_id=1, source_target_pairs={{0,8},{8,0},{16,24},{24,16},{1,9},{9,1},{17,25},{25,17},{2,10},{10... | collective-permute-start | bytes 786440 | tf_op jit(solution)/shard_map/ppermute | solution.py:834
  158.6 21.2 %collective-permute-start.15 = (bf16[512,512]{1,0:T(8,128)(2,1)}, bf16[512,512]{1,0:T(8,128)(2,1)S(1)}, u32[]{:S(2)}, u32[]{:S(2)}) collective-permute-start(bf16[512,512]{1,0:T(8,128)(2,1)} %get-tuple-element.146), channel_id=1, source_target_pairs={{0,8},{8,0},{16,24},{24,16},{1,9},{9,1},{17,25},{25,17},{2,10},{10... | collective-permute-start | bytes 1572872 | tf_op jit(solution)/shard_map/ppermute | solution.py:834
  159.7 20.1 %collective-permute-start.16 = (bf16[512,512]{1,0:T(8,128)(2,1)}, bf16[512,512]{1,0:T(8,128)(2,1)S(1)}, u32[]{:S(2)}, u32[]{:S(2)}) collective-permute-start(bf16[512,512]{1,0:T(8,128)(2,1)} %get-tuple-element.147), channel_id=1, source_target_pairs={{0,16},{8,24},{16,0},{24,8},{1,17},{9,25},{17,1},{25,9},{2,18},{10... | collective-permute-start | bytes 1572872 | tf_op jit(solution)/shard_map/ppermute | solution.py:834
  160.2 19.6 %collective-permute-start.17 = (bf16[512,512]{1,0:T(8,128)(2,1)}, bf16[512,512]{1,0:T(8,128)(2,1)S(1)}, u32[]{:S(2)}, u32[]{:S(2)}) collective-permute-start(bf16[512,512]{1,0:T(8,128)(2,1)} %get-tuple-element.148), channel_id=1, source_target_pairs={{0,8},{8,0},{16,24},{24,16},{1,9},{9,1},{17,25},{25,17},{2,10},{10... | collective-permute-start | bytes 1572872 | tf_op jit(solution)/shard_map/ppermute | solution.py:834
  161.4 19.0 %collective-permute-start.18 = (bf16[512,512]{1,0:T(8,128)(2,1)}, bf16[512,512]{1,0:T(8,128)(2,1)S(1)}, u32[]{:S(2)}, u32[]{:S(2)}) collective-permute-start(bf16[512,512]{1,0:T(8,128)(2,1)} %get-tuple-element.149), channel_id=1, source_target_pairs={{0,16},{8,24},{16,0},{24,8},{1,17},{9,25},{17,1},{25,9},{2,18},{10... | collective-permute-start | bytes 1572872 | tf_op jit(solution)/shard_map/ppermute | solution.py:834
  212.4 26.8 %collective-permute-start.19 = (bf16[512,1024]{1,0:T(8,128)(2,1)}, bf16[512,1024]{1,0:T(8,128)(2,1)S(1)}, u32[]{:S(2)}, u32[]{:S(2)}) collective-permute-start(bf16[512,1024]{1,0:T(8,128)(2,1)} %get-tuple-element.157), channel_id=1, source_target_pairs={{0,8},{8,0},{16,24},{24,16},{1,9},{9,1},{17,25},{25,17},{2,10},{10... | collective-permute-start | bytes 3145736 | tf_op jit(solution)/shard_map/ppermute | solution.py:834
  213.5 25.8 %collective-permute-start.20 = (bf16[512,1024]{1,0:T(8,128)(2,1)}, bf16[512,1024]{1,0:T(8,128)(2,1)S(1)}, u32[]{:S(2)}, u32[]{:S(2)}) collective-permute-start(bf16[512,1024]{1,0:T(8,128)(2,1)} %get-tuple-element.158), channel_id=1, source_target_pairs={{0,16},{8,24},{16,0},{24,8},{1,17},{9,25},{17,1},{25,9},{2,18},{10... | collective-permute-start | bytes 3145736 | tf_op jit(solution)/shard_map/ppermute | solution.py:834
  239.3 94.9 %reduce-scatter.6.cloned.1.call-start = ((), (), s32[]{:S(2)}) async-start(), calls=%async_computation.7 | async-start | bytes 5308416 | tf_op jit(solution)/shard_map/reduce_scatter | solution.py:909
  240.6 142.9 %reduce-scatter.8.cloned.1.call-start = ((), (), s32[]{:S(2)}) async-start(), calls=%async_computation.8 | async-start | bytes 2064384 | tf_op jit(solution)/shard_map/reduce_scatter | solution.py:909
  247.6 7.7 %collective-permute-start.21 = (bf16[512,256]{1,0:T(8,128)(2,1)}, bf16[512,256]{1,0:T(8,128)(2,1)S(1)}, u32[]{:S(2)}, u32[]{:S(2)}) collective-permute-start(bf16[512,256]{1,0:T(8,128)(2,1)} %get-tuple-element.175), channel_id=1, source_target_pairs={{0,8},{8,0},{16,24},{24,16},{1,9},{9,1},{17,25},{25,17},{2,10},{10... | collective-permute-start | bytes 786440 | tf_op jit(solution)/shard_map/ppermute | solution.py:834
  248.3 7.1 %collective-permute-start.22 = (bf16[512,256]{1,0:T(8,128)(2,1)}, bf16[512,256]{1,0:T(8,128)(2,1)S(1)}, u32[]{:S(2)}, u32[]{:S(2)}) collective-permute-start(bf16[512,256]{1,0:T(8,128)(2,1)} %get-tuple-element.176), channel_id=1, source_target_pairs={{0,16},{8,24},{16,0},{24,8},{1,17},{9,25},{17,1},{25,9},{2,18},{10... | collective-permute-start | bytes 786440 | tf_op jit(solution)/shard_map/ppermute | solution.py:834
  249.6 11.5 %collective-permute-start.23 = (bf16[512,256]{1,0:T(8,128)(2,1)}, bf16[512,256]{1,0:T(8,128)(2,1)S(1)}, u32[]{:S(2)}, u32[]{:S(2)}) collective-permute-start(bf16[512,256]{1,0:T(8,128)(2,1)} %get-tuple-element.177), channel_id=1, source_target_pairs={{0,24},{8,16},{16,8},{24,0},{1,25},{9,17},{17,9},{25,1},{2,26},{10... | collective-permute-start | bytes 786440 | tf_op jit(solution)/shard_map/ppermute | solution.py:834
  251.0 10.1 %copy-start.36 = (bf16[512,1024]{1,0:T(8,128)(2,1)S(1)}, bf16[512,1024]{1,0:T(8,128)(2,1)}, u32[]{:S(2)}) copy-start(bf16[512,1024]{1,0:T(8,128)(2,1)} %get-tuple-element.178) | copy-start | bytes 3145732
  251.0 11.1 %copy-start.35 = (bf16[512,1024]{1,0:T(8,128)(2,1)S(1)}, bf16[512,1024]{1,0:T(8,128)(2,1)}, u32[]{:S(2)}) copy-start(bf16[512,1024]{1,0:T(8,128)(2,1)} %get-tuple-element.179) | copy-start | bytes 3145732
  255.3 10.5 %copy-start.27 = (bf16[512,256]{1,0:T(8,128)(2,1)}, bf16[512,256]{1,0:T(8,128)(2,1)S(1)}, u32[]{:S(2)}) copy-start(bf16[512,256]{1,0:T(8,128)(2,1)S(1)} %collective-permute-done.21.refs_11_) | copy-start | bytes 786436
  255.5 10.3 %copy-start.28 = (bf16[512,256]{1,0:T(8,128)(2,1)}, bf16[512,256]{1,0:T(8,128)(2,1)S(1)}, u32[]{:S(2)}) copy-start(bf16[512,256]{1,0:T(8,128)(2,1)S(1)} %collective-permute-done.22.refs_12_) | copy-start | bytes 786436
  261.1 52.9 %collective-permute-start.24 = (bf16[512,1024]{1,0:T(8,128)(2,1)S(1)}, bf16[512,1024]{1,0:T(8,128)(2,1)S(1)}, u32[]{:S(2)}, u32[]{:S(2)}) collective-permute-start(bf16[512,1024]{1,0:T(8,128)(2,1)S(1)} %copy-done.36), channel_id=1, source_target_pairs={{0,8},{8,0},{16,24},{24,16},{1,9},{9,1},{17,25},{25,17},{2,10},{10... | collective-permute-start | bytes 3145736 | tf_op jit(solution)/shard_map/ppermute | solution.py:834
  262.1 53.0 %collective-permute-start.25 = (bf16[512,1024]{1,0:T(8,128)(2,1)S(1)}, bf16[512,1024]{1,0:T(8,128)(2,1)}, u32[]{:S(2)}, u32[]{:S(2)}) collective-permute-start(bf16[512,1024]{1,0:T(8,128)(2,1)S(1)} %copy-done.35), channel_id=1, source_target_pairs={{0,16},{8,24},{16,0},{24,8},{1,17},{9,25},{17,1},{25,9},{2,18},{10... | collective-permute-start | bytes 3145736 | tf_op jit(solution)/shard_map/ppermute | solution.py:834
  262.3 51.7 %collective-permute-start.26 = (bf16[1024,256]{1,0:T(8,128)(2,1)}, bf16[1024,256]{1,0:T(8,128)(2,1)S(1)}, u32[]{:S(2)}, u32[]{:S(2)}) collective-permute-start(bf16[1024,256]{1,0:T(8,128)(2,1)} %get-tuple-element.191), channel_id=1, source_target_pairs={{0,8},{8,0},{16,24},{24,16},{1,9},{9,1},{17,25},{25,17},{2,10},{10... | collective-permute-start | bytes 1572872 | tf_op jit(solution)/shard_map/ppermute | solution.py:834
  264.1 49.9 %collective-permute-start.27 = (bf16[1024,256]{1,0:T(8,128)(2,1)}, bf16[1024,256]{1,0:T(8,128)(2,1)S(1)}, u32[]{:S(2)}, u32[]{:S(2)}) collective-permute-start(bf16[1024,256]{1,0:T(8,128)(2,1)} %get-tuple-element.192), channel_id=1, source_target_pairs={{0,16},{8,24},{16,0},{24,8},{1,17},{9,25},{17,1},{25,9},{2,18},{10... | collective-permute-start | bytes 1572872 | tf_op jit(solution)/shard_map/ppermute | solution.py:834
  265.2 48.8 %collective-permute-start.28 = (bf16[1024,256]{1,0:T(8,128)(2,1)}, bf16[1024,256]{1,0:T(8,128)(2,1)S(1)}, u32[]{:S(2)}, u32[]{:S(2)}) collective-permute-start(bf16[1024,256]{1,0:T(8,128)(2,1)} %get-tuple-element.193), channel_id=1, source_target_pairs={{0,24},{8,16},{16,8},{24,0},{1,25},{9,17},{17,9},{25,1},{2,26},{10... | collective-permute-start | bytes 1572872 | tf_op jit(solution)/shard_map/ppermute | solution.py:834
  316.1 43.3 %copy-start.13 = (bf16[144,1024]{1,0:T(8,128)(2,1)S(1)}, bf16[144,1024]{1,0:T(8,128)(2,1)}, u32[]{:S(2)}) copy-start(bf16[144,1024]{1,0:T(8,128)(2,1)} %reduce-scatter.4.cloned.1.call-done.refs_2_) | copy-start | bytes 884740
  316.1 55.7 %copy-start.5 = (f32[512,1024]{1,0:T(8,128)S(1)}, f32[512,1024]{1,0:T(8,128)}, u32[]{:S(2)}) copy-start(f32[512,1024]{1,0:T(8,128)} %get-tuple-element.144.refs_5_) | copy-start | bytes 6291460
  329.8 42.0 %copy-start.10 = (bf16[512,1024]{1,0:T(8,128)(2,1)S(1)}, bf16[512,1024]{1,0:T(8,128)(2,1)}, u32[]{:S(2)}) copy-start(bf16[512,1024]{1,0:T(8,128)(2,1)} %copy-done.9) | copy-start | bytes 3145732
  334.2 15.1 %collective-permute-start.29 = (bf16[512,512]{1,0:T(8,128)(2,1)}, bf16[512,512]{1,0:T(8,128)(2,1)S(1)}, u32[]{:S(2)}, u32[]{:S(2)}) collective-permute-start(bf16[512,512]{1,0:T(8,128)(2,1)} %get-tuple-element.200), channel_id=1, source_target_pairs={{0,8},{8,0},{16,24},{24,16},{1,9},{9,1},{17,25},{25,17},{2,10},{10... | collective-permute-start | bytes 1572872 | tf_op jit(solution)/shard_map/ppermute | solution.py:834
  335.7 22.7 %collective-permute-start.30 = (bf16[512,512]{1,0:T(8,128)(2,1)}, bf16[512,512]{1,0:T(8,128)(2,1)S(1)}, u32[]{:S(2)}, u32[]{:S(2)}) collective-permute-start(bf16[512,512]{1,0:T(8,128)(2,1)} %get-tuple-element.201), channel_id=1, source_target_pairs={{0,16},{8,24},{16,0},{24,8},{1,17},{9,25},{17,1},{25,9},{2,18},{10... | collective-permute-start | bytes 1572872 | tf_op jit(solution)/shard_map/ppermute | solution.py:834
  337.2 21.2 %collective-permute-start.31 = (bf16[512,512]{1,0:T(8,128)(2,1)}, bf16[512,512]{1,0:T(8,128)(2,1)S(1)}, u32[]{:S(2)}, u32[]{:S(2)}) collective-permute-start(bf16[512,512]{1,0:T(8,128)(2,1)} %get-tuple-element.202), channel_id=1, source_target_pairs={{0,24},{8,16},{16,8},{24,0},{1,25},{9,17},{17,9},{25,1},{2,26},{10... | collective-permute-start | bytes 1572872 | tf_op jit(solution)/shard_map/ppermute | solution.py:834
  359.4 10.9 %collective-permute-start.38 = (bf16[144,1024]{1,0:T(8,128)(2,1)S(1)}, bf16[144,1024]{1,0:T(8,128)(2,1)}, u32[]{:S(2)}, u32[]{:S(2)}) collective-permute-start(bf16[144,1024]{1,0:T(8,128)(2,1)S(1)} %copy-done.13), channel_id=1, source_target_pairs={{0,24},{8,16},{16,8},{24,0},{1,25},{9,17},{17,9},{25,1},{2,26},{10... | collective-permute-start | bytes 884744 | tf_op jit(solution)/shard_map/ppermute | solution.py:834
  360.8 21.5 %collective-permute-start.39 = (bf16[144,1024]{1,0:T(8,128)(2,1)S(1)}, bf16[144,1024]{1,0:T(8,128)(2,1)S(1)}, u32[]{:S(2)}, u32[]{:S(2)}) collective-permute-start(bf16[144,1024]{1,0:T(8,128)(2,1)S(1)} %copy-done.13), channel_id=1, source_target_pairs={{0,16},{8,24},{16,0},{24,8},{1,17},{9,25},{17,1},{25,9},{2,18},{10... | collective-permute-start | bytes 884744 | tf_op jit(solution)/shard_map/ppermute | solution.py:834
  361.9 20.5 %collective-permute-start.40 = (bf16[144,1024]{1,0:T(8,128)(2,1)S(1)}, bf16[144,1024]{1,0:T(8,128)(2,1)S(1)}, u32[]{:S(2)}, u32[]{:S(2)}) collective-permute-start(bf16[144,1024]{1,0:T(8,128)(2,1)S(1)} %copy-done.13), channel_id=1, source_target_pairs={{0,8},{8,0},{16,24},{24,16},{1,9},{9,1},{17,25},{25,17},{2,10},{10... | collective-permute-start | bytes 884744 | tf_op jit(solution)/shard_map/ppermute | solution.py:834
  362.9 26.4 %collective-permute-start.35 = (bf16[128,2304]{1,0:T(8,128)(2,1)}, bf16[128,2304]{1,0:T(8,128)(2,1)}, u32[]{:S(2)}, u32[]{:S(2)}) collective-permute-start(bf16[128,2304]{1,0:T(8,128)(2,1)} %reduce-scatter.6.cloned.1.call-done.p0_ref), channel_id=1, source_target_pairs={{0,8},{8,0},{16,24},{24,16},{1,9},{9,1},{17,25},{25,17},{2,10},{10... | collective-permute-start | bytes 1769480 | tf_op jit(solution)/shard_map/ppermute | solution.py:834
  363.9 32.3 %collective-permute-start.36 = (bf16[128,2304]{1,0:T(8,128)(2,1)}, bf16[128,2304]{1,0:T(8,128)(2,1)}, u32[]{:S(2)}, u32[]{:S(2)}) collective-permute-start(bf16[128,2304]{1,0:T(8,128)(2,1)} %reduce-scatter.6.cloned.1.call-done.p0_ref), channel_id=1, source_target_pairs={{0,16},{8,24},{16,0},{24,8},{1,17},{9,25},{17,1},{25,9},{2,18},{10... | collective-permute-start | bytes 1769480 | tf_op jit(solution)/shard_map/ppermute | solution.py:834
  370.3 31.7 %collective-permute-start.37 = (bf16[128,2304]{1,0:T(8,128)(2,1)}, bf16[128,2304]{1,0:T(8,128)(2,1)}, u32[]{:S(2)}, u32[]{:S(2)}) collective-permute-start(bf16[128,2304]{1,0:T(8,128)(2,1)} %reduce-scatter.6.cloned.1.call-done.p0_ref), channel_id=1, source_target_pairs={{0,24},{8,16},{16,8},{24,0},{1,25},{9,17},{17,9},{25,1},{2,26},{10... | collective-permute-start | bytes 1769480 | tf_op jit(solution)/shard_map/ppermute | solution.py:834
  383.5 26.1 %collective-permute-start.32 = (bf16[128,896]{1,0:T(8,128)(2,1)}, bf16[128,896]{1,0:T(8,128)(2,1)S(1)}, u32[]{:S(2)}, u32[]{:S(2)}) collective-permute-start(bf16[128,896]{1,0:T(8,128)(2,1)} %reduce-scatter.8.cloned.1.call-done.p0_ref), channel_id=1, source_target_pairs={{0,8},{8,0},{16,24},{24,16},{1,9},{9,1},{17,25},{25,17},{2,10},{10... | collective-permute-start | bytes 688136 | tf_op jit(solution)/shard_map/ppermute | solution.py:834
  385.0 24.5 %collective-permute-start.33 = (bf16[128,896]{1,0:T(8,128)(2,1)}, bf16[128,896]{1,0:T(8,128)(2,1)S(1)}, u32[]{:S(2)}, u32[]{:S(2)}) collective-permute-start(bf16[128,896]{1,0:T(8,128)(2,1)} %reduce-scatter.8.cloned.1.call-done.p0_ref), channel_id=1, source_target_pairs={{0,16},{8,24},{16,0},{24,8},{1,17},{9,25},{17,1},{25,9},{2,18},{10... | collective-permute-start | bytes 688136 | tf_op jit(solution)/shard_map/ppermute | solution.py:834
  389.3 20.3 %collective-permute-start.34 = (bf16[128,896]{1,0:T(8,128)(2,1)}, bf16[128,896]{1,0:T(8,128)(2,1)S(1)}, u32[]{:S(2)}, u32[]{:S(2)}) collective-permute-start(bf16[128,896]{1,0:T(8,128)(2,1)} %reduce-scatter.8.cloned.1.call-done.p0_ref), channel_id=1, source_target_pairs={{0,24},{8,16},{16,8},{24,0},{1,25},{9,17},{17,9},{25,1},{2,26},{10... | collective-permute-start | bytes 688136 | tf_op jit(solution)/shard_map/ppermute | solution.py:834
  390.3 26.2 %copy-start.1 = (bf16[576,1024]{1,0:T(8,128)(2,1)S(1)}, bf16[576,1024]{1,0:T(8,128)(2,1)}, u32[]{:S(2)}) copy-start(bf16[576,1024]{1,0:T(8,128)(2,1)} %param.28) | copy-start | bytes 3538948
  392.0 17.0 %copy-start.33 = (bf16[128]{0:T(256)(128)(2,1)S(1)}, bf16[128]{0:T(256)(128)(2,1)}, u32[]{:S(2)}) copy-start(bf16[128]{0:T(256)(128)(2,1)} %param.25) | copy-start | bytes 772
  392.0 24.0 %copy-start.34 = (bf16[128]{0:T(256)(128)(2,1)S(1)}, bf16[128]{0:T(256)(128)(2,1)}, u32[]{:S(2)}) copy-start(bf16[128]{0:T(256)(128)(2,1)} %param.18) | copy-start | bytes 772
  (21 other events, 44.7 us)
Sparse Core Ops, SparseCore 0:
  10.2 26.1 all-gather.3
  38.6 90.2 all-gather.5
  130.5 45.5 all-gather.7
  239.4 38.4 reduce-scatter.3
  280.1 54.0 reduce-scatter.5
  336.9 36.2 reduce-scatter.7

commit v4 on v3

--- a/solution.py
+++ b/solution.py
@@ -106,14 +106,26 @@
     )(me, w_query, w_key, w_value, attn_gain[None], ffn_gain[None])
 
 
+def pack_rows(block, rows):
+    rest = [block[rows:, c:c + LANES] for c in range(0, block.shape[1], LANES)]
+    return jnp.concatenate([block[:rows], jnp.concatenate(rest, axis=0)], axis=1)
+
+
+def unpack_rows(block, width):
+    rows = block.shape[0]
+    extra = rows * LANES // width
+    rest = [block[extra * c:extra * (c + 1), width:] for c in range(width // LANES)]
+    return jnp.concatenate([block[:, :width], jnp.concatenate(rest, axis=1)], axis=0)
+
+
 def cut_kernel(shards, me_ref, gate_ref, up_ref, down_ref, wo_ref, out_ref):
-    whole, units = gate_ref.shape[1], down_ref.shape[1]
+    whole, units = gate_ref.shape[1], gate_ref.shape[1] // 4
     piece, span = units // shards, whole // shards
     for at, ref in ((0, gate_ref), (units, up_ref)):
         turned = pltpu.roll(ref[...].astype(F32), whole - piece * me_ref[0], 1)
         parts = [turned[:, span * k:span * k + piece] for k in range(shards)]
         out_ref[:, at:at + units] = jnp.concatenate(parts, axis=1).astype(BF16)
-    out_ref[:, 2 * units:3 * units] = down_ref[...]
+    out_ref[:, 2 * units:3 * units] = pack_rows(down_ref[...].astype(F32), out_ref.shape[0]).astype(BF16)
     width = wo_ref.shape[1]
     out_ref[:, 3 * units:3 * units + width] = wo_ref[...]
     out_ref[:, 3 * units + width:] = jnp.zeros((out_ref.shape[0], units - width), BF16)
@@ -132,10 +144,10 @@
     )(me, w_gate, w_up, w_down, w_out)
 
 
-def join_kernel(shards, me_ref, p0_ref, p1_ref, p2_ref, p3_ref, gate_ref, up_ref, dgate_ref, dup_ref, dot_ref, st_ref):
+def join_kernel(shards, me_ref, p0_ref, p1_ref, p2_ref, p3_ref, gate_ref, up_ref, dgate_ref, dup_ref, ddown_ref, dot_ref, st_ref):
     for d, ref in enumerate((p0_ref, p1_ref, p2_ref, p3_ref)):
         st_ref[d] = ref[...]
-    units = p0_ref.shape[1] // 2
+    units = p0_ref.shape[1] // 3
     piece = units // shards
     quarters = [st_ref[jnp.bitwise_xor(me_ref[0], q)] for q in range(4)]
     total = 0.0
@@ -146,15 +158,19 @@
         out_ref[...] = joined
         total = total + jnp.sum(joined * w_ref[...].astype(F32), axis=1, keepdims=True)
     dot_ref[...] = total
-
-
-def join_weights(me, parts, w_gate, w_up, shards):
+    for q, quarter in enumerate(quarters):
+        block = unpack_rows(quarter[:, 2 * units:].astype(F32), ddown_ref.shape[1])
+        ddown_ref[q * piece:(q + 1) * piece, :] = block
+
+
+def join_weights(me, parts, w_gate, w_up, down_shape, shards):
     depth, whole = w_gate.shape
     return pl.pallas_call(
         functools.partial(join_kernel, shards),
-        out_shape=(jax.ShapeDtypeStruct((depth, whole), F32),) * 2 + (jax.ShapeDtypeStruct((depth, 1), F32),),
+        out_shape=(jax.ShapeDtypeStruct((depth, whole), F32),) * 2
+        + (jax.ShapeDtypeStruct(down_shape, F32), jax.ShapeDtypeStruct((depth, 1), F32)),
         in_specs=[smem()] + [vmem()] * 6,
-        out_specs=(vmem(),) * 3,
+        out_specs=(vmem(),) * 4,
         scratch_shapes=[pltpu.VMEM((4,) + parts[0].shape, BF16)],
         compiler_params=params(),
         cost_estimate=COST,
@@ -415,15 +431,19 @@
     )(lens, orow, qx, k, vx, *after)
 
 
-def attend_back_kernel(head_dim, *refs):
-    (lens_ref, ocol_ref, qx_ref, k_ref, v_ref, kt_ref, lse0_ref, lse1_ref, o0_ref, o1_ref,
-     d0_ref, d1_ref, d2_ref, d3_ref, rawq_ref, rawk_ref, cos_ref, su_ref, sd_ref, qg_ref, kg_ref) = refs[:21]
-    draw_ref, gain_ref, dgiven_ref, dx_ref, delta_ref, dk_ref, dv_ref = refs[-7:]
+def attend_back_kernel(head_dim, n_late, *refs):
+    (lens_ref, ocol_ref, lse0_ref, lse1_ref, o0_ref, o1_ref, d0_ref, d1_ref, d2_ref, d3_ref, qg_ref, kg_ref) = refs[:12]
+    late, refs = refs[12:12 + n_late], refs[-(2 + 5 + n_late + 1):]
+    draw_ref, gain_ref, dgiven_ref, dx_ref, delta_ref, dk_ref, dv_ref = refs[:7]
+    here, sems = refs[7:7 + n_late], refs[7 + n_late]
+    qx_ref, k_ref, v_ref, kt_ref, rawq_ref, rawk_ref, cos_ref, su_ref, sd_ref = here
+    copies = [pltpu.make_async_copy(late[n], here[n], sems.at[n]) for n in range(n_late)]
+    for copy in copies:
+        copy.start()
     all_rows = k_ref.shape[0]
     blocks = all_rows // ROWS
     exponent = LOG2E * head_dim ** -0.5
     scale = head_dim ** -0.5
-    low_lanes = lane_iota(ROWS, LANES) < head_dim
     tok = d0_ref.shape[0]
     for d, ref in enumerate((d0_ref, d1_ref, d2_ref, d3_ref)):
         dgiven_ref[d * tok:(d + 1) * tok, :] = ref[...]
@@ -432,8 +452,9 @@
     gain_ref[...] = jnp.zeros_like(gain_ref)
 
     def deal(i, carry):
-        rows = at_rows(i)
-        pick = (ocol_ref[rows, 0:1] == lane_iota(ROWS, all_rows)).astype(F32).astype(BF16)
+        rows = at_rows(i, tok)
+        low_lanes = lane_iota(tok, LANES) < head_dim
+        pick = (ocol_ref[rows, 0:1] == lane_iota(tok, all_rows)).astype(F32).astype(BF16)
         dealt = dot_nn(pick, dgiven_ref[...])
         for g, o_ref in enumerate((o0_ref, o1_ref)):
             pair = dealt[:, g * LANES:(g + 1) * LANES]
@@ -446,7 +467,9 @@
                 )
         return carry
 
-    lax.fori_loop(0, blocks, deal, 0)
+    lax.fori_loop(0, all_rows // tok, deal, 0)
+    for copy in copies:
+        copy.wait()
     ones = pair_ones(head_dim)
 
     def query_block(i, carry):
@@ -454,10 +477,13 @@
         q_index = i * ROWS + lane_iota(1, ROWS)
         start = row_starts(lens_ref, q_index)
         first = row_starts(lens_ref, i * ROWS) // ROWS
-
-        def step(j, state):
-            columns = at_rows(j)
-            k_index = j * ROWS + row_iota(ROWS, ROWS)
+        count = (i + 2 - first) // 2
+        base = jnp.maximum(i + 1 - 2 * count, 0)
+
+        def step(n, state):
+            at = base + 2 * n
+            columns = pl.ds(pl.multiple_of(at * ROWS, ROWS), 2 * ROWS)
+            k_index = at * ROWS + row_iota(2 * ROWS, ROWS)
             keep = (k_index <= q_index) & (k_index >= start)
             keys = k_ref[columns, :]
             values = v_ref[columns, :]
@@ -478,7 +504,7 @@
             dv_ref[columns, :] = dv
             return tuple(new)
 
-        state = lax.fori_loop(first, i + 1, step, (jnp.zeros((head_dim, ROWS), F32),) * 4)
+        state = lax.fori_loop(0, count, step, (jnp.zeros((head_dim, ROWS), F32),) * 4)
         cosine, su, sd = cos_ref[rows, :], su_ref[rows, :], sd_ref[rows, :]
         for g in range(2):
             pair = jnp.transpose(jnp.concatenate(state[2 * g:2 * g + 2], axis=0)) * scale
@@ -493,7 +519,7 @@
     lax.fori_loop(0, blocks, query_block, 0)
 
     def key_block(i, carry):
-        rows = at_rows(i)
+        rows = at_rows(i, tok)
         cosine, su, sd = cos_ref[rows, :], su_ref[rows, :], sd_ref[rows, :]
         draw, gain = norm_back(
             dk_ref[rows, :] * scale, rawk_ref[rows, :].astype(F32), kg_ref[...], cosine, su, sd, ones, head_dim
@@ -503,7 +529,7 @@
         gain_ref[1:2, :] += gain
         return carry
 
-    lax.fori_loop(0, blocks, key_block, 0)
+    lax.fori_loop(0, all_rows // tok, key_block, 0)
 
 
 def rows_back_kernel(period, orow_ref, draw_ref, normed_ref, o0_ref, o1_ref, o2_ref, o3_ref, gain_ref, *refs):
@@ -547,15 +573,16 @@
     return [pl.BlockSpec(memory_space=pl.ANY)] * len(arrays)
 
 
-def attend_back(lens, ocol, qx, k, v, kt, lses, dealts, grads, rawq, rawk, cosine, su, sd, qg, kg, head_dim, after):
+def attend_back(lens, ocol, qx, k, v, kt, lses, dealts, grads, rawq, rawk, cosine, su, sd, qg, kg, head_dim):
     all_rows = k.shape[0]
-    return pl.pallas_call(
-        functools.partial(attend_back_kernel, head_dim),
+    late = (qx, k, v, kt, rawq, rawk, cosine, su, sd)
+    return pl.pallas_call(
+        functools.partial(attend_back_kernel, head_dim, len(late)),
         out_shape=(
             jax.ShapeDtypeStruct((all_rows, 4 * LANES), BF16),
             jax.ShapeDtypeStruct((2, LANES), F32),
         ),
-        in_specs=[smem()] + [vmem()] * 20 + anywhere(after),
+        in_specs=[smem()] + [vmem()] * 11 + anywhere(late),
         out_specs=(vmem(),) * 2,
         scratch_shapes=[
             pltpu.VMEM((all_rows, 2 * LANES), BF16),
@@ -563,11 +590,11 @@
             pltpu.VMEM((4, all_rows), F32),
             pltpu.VMEM((all_rows, LANES), F32),
             pltpu.VMEM((all_rows, LANES), F32),
-        ],
+        ] + [pltpu.VMEM(a.shape, a.dtype) for a in late] + [pltpu.SemaphoreType.DMA((len(late),))],
         compiler_params=params(),
         cost_estimate=COST,
         name="attend_back",
-    )(lens, ocol, qx, k, v, kt, *lses, *dealts, *grads, rawq, rawk, cosine, su, sd, qg, kg, *after)
+    )(lens, ocol, *lses, *dealts, *grads, qg, kg, *late)
 
 
 def rows_back(orow, draw, normed, parts, gains, shards, after):
@@ -622,7 +649,7 @@
     )(me, *grads, w, x, d_middle, gain, *after)
 
 
-def ffn_kernel(per, blocks, n_carried, *refs):
+def ffn_kernel(per, shards, blocks, n_carried, *refs):
     refs = list(refs)
     take = lambda n: [refs.pop(0) for _ in range(n)]
     me_ref = take(1)[0]
@@ -633,10 +660,20 @@
     diag = take(4) if blocks == (1, 2) else None
     take(n_carried)
     nf_ref, hid_ref, dgu_ref, cot_ref = take(4)
+    packed_ref, wd_ref = wd_ref, refs.pop()
     i = pl.program_id(0)
     me = me_ref[0]
     hidden_units = hid_ref.shape[1]
     which = i // per
+
+    @pl.when(i == 0)
+    def _():
+        rows, piece = packed_ref.shape[0] // shards, wd_ref.shape[0] // shards
+        for k in range(shards):
+            block = packed_ref[k * rows:(k + 1) * rows, :]
+            if piece % 16:
+                block = block.astype(F32)
+            wd_ref[k * piece:(k + 1) * piece, :] = unpack_rows(block, wd_ref.shape[1]).astype(BF16)
 
     def read(lists):
         parts = [jnp.concatenate([ref[...] for ref in one], axis=1) for one in lists]
@@ -690,9 +727,9 @@
                 ref[:, half:] = value[:, half:].astype(BF16)
 
 
-def ffn(me, blocks, att, xs, cots, gain, wide, wd, diag, carried, after):
+def ffn(me, blocks, att, xs, cots, gain, wide, shards, diag, carried, after):
     all_rows = att[0].shape[0]
-    units, width = wd.shape
+    units, width = wide.shape[1] // 4, wide.shape[0]
     tok = all_rows // 4
     per = tok // ROWS
     block_of = lambda i: blocks[0] + (i // per) * (blocks[-1] - blocks[0])
@@ -723,39 +760,61 @@
     diag_specs = [held(1, width // 2), held(0, width // 2)] * 2 if diag else []
     operands = (
         [me] + list(att[:6]) + [a for a, _ in last] + [a for d in blocks for a in xs[d]] + [a for d in blocks for a in cots[d]]
-        + [wide, gain, wide, wide, wd] + list(diag) + list(carried) + list(after)
+        + [wide, gain, wide, wide, wide] + list(diag) + list(carried) + list(after)
     )
     first = len(operands) - len(carried) - len(after)
     return pl.pallas_call(
-        functools.partial(ffn_kernel, per, blocks, len(carried) + len(after)),
+        functools.partial(ffn_kernel, per, shards, blocks, len(carried) + len(after)),
         grid=(len(blocks) * per,),
         out_shape=tuple(shapes),
         in_specs=[smem()] + [crossed(d) for d in range(3) for _ in range(2)] + [spec for _, spec in last]
-        + pieces(xs) + pieces(cots) + [weight(3), fixed(gain), weight(0), weight(1), fixed(wd)] + diag_specs + anywhere(carried) + anywhere(after),
+        + pieces(xs) + pieces(cots) + [weight(3), fixed(gain), weight(0), weight(1), weight(2)] + diag_specs + anywhere(carried) + anywhere(after),
         out_specs=tuple(specs),
         input_output_aliases={first + n: n for n in range(len(carried))},
+        scratch_shapes=[pltpu.VMEM((units, width), BF16)],
         compiler_params=params(),
         cost_estimate=COST,
         name="ffn",
     )(*operands)
 
 
-def weights_kernel(left_ref, right_ref, out_ref):
-    out_ref[...] = dot_tn(left_ref[...], right_ref[...]).astype(BF16)
-
-
-def weights_back(left, right, steps):
-    rows, depth = left.shape
-    return pl.pallas_call(
-        weights_kernel,
-        grid=(steps,),
-        out_shape=jax.ShapeDtypeStruct((depth, right.shape[1]), BF16),
-        in_specs=[pl.BlockSpec((rows, depth // steps), lambda i: (0, i)), fixed(right)],
-        out_specs=pl.BlockSpec((depth // steps, right.shape[1]), lambda i: (i, 0)),
+def weights_kernel(shards, nf_ref, dgu_ref, hid_ref, cot_ref, out_ref, down_ref):
+    i = pl.program_id(0)
+
+    @pl.when(i == 0)
+    def _():
+        down_ref[...] = dot_tn(hid_ref[...], cot_ref[...])
+
+    @pl.when(i > 0)
+    def _():
+        out_ref[:, :dgu_ref.shape[1]] = dot_tn(nf_ref[...], dgu_ref[...]).astype(BF16)
+
+    per, piece = shards // 4, down_ref.shape[0] // shards
+    rows = out_ref.shape[0] // per
+    for k in range(shards):
+
+        @pl.when(i == 1 + k // per)
+        def _(k=k):
+            block = pack_rows(down_ref[k * piece:(k + 1) * piece, :], rows)
+            at = k % per * rows
+            out_ref[at:at + rows, dgu_ref.shape[1]:] = block.astype(BF16)
+
+
+def weights_back(nf, d_gu, hidden, cot, shards):
+    rows, depth = nf.shape
+    late = lambda i: jnp.maximum(i - 1, 0)
+    wide = d_gu.shape[1] + hidden.shape[1]
+    return pl.pallas_call(
+        functools.partial(weights_kernel, shards),
+        grid=(5,),
+        out_shape=jax.ShapeDtypeStruct((depth, wide), BF16),
+        in_specs=[pl.BlockSpec((rows, depth // 4), lambda i: (0, late(i))), fixed(d_gu), fixed(hidden), fixed(cot)],
+        out_specs=pl.BlockSpec((depth // 4, wide), lambda i: (late(i), 0)),
+        scratch_shapes=[pltpu.VMEM((hidden.shape[1], cot.shape[1]), F32)],
         compiler_params=params(),
         cost_estimate=COST,
         name="weights_back",
-    )(left, right)
+    )(nf, d_gu, hidden, cot)
 
 
 def middle_kernel(*refs):
@@ -870,9 +929,8 @@
     xs = gather_rows(tokens[0], tables)
     w_first = first_weights(me_arr, w_query, w_key, w_value, attn_gain, ffn_gain)
     w_qkv = lax.all_gather(w_first, "shard", axis=0, tiled=True)
-    w_cut = cut_weights(me_arr, w_gate, w_up, own(w_down, 0).reshape(depth, units), w_out, shards)
+    w_cut = cut_weights(me_arr, w_gate, w_up, own(w_down, 0), w_out, shards)
     w_wide = lax.all_gather(after(w_cut, xs[1]), "shard", axis=0, tiled=True)
-    w_d = w_wide[:, 2 * units:3 * units].reshape(units, -1)
 
     cosine, sine_up, sine_down, ocol, orow, q_gain, k_gain = xs[0]
     xs = [[tokens[0]]] + xs[1:]
@@ -898,7 +956,7 @@
     att = [att[g][d] for d in range(3) for g in range(2)] + att[0][3:] + att[1][3:]
 
     feed = lambda blocks, diag, carried, after=(): ffn(
-        me_arr, blocks, att, xs, cots, gain_f, w_wide, w_d, diag, carried, after
+        me_arr, blocks, att, xs, cots, gain_f, w_wide, shards, diag, carried, after
     )
     *carried, dn3a, dn3b, bo3a, bo3b = feed((3,), (), (), att[8:])
     diag = (swap(dn3a, 1), swap(dn3b, 2), swap(bo3a, 1), swap(bo3b, 2))
@@ -907,38 +965,32 @@
     nf, hidden, d_gu, cot_all = carried
     dn = (dn0, swap(dn1, 1), swap(dn2, 2))
     scatter = lambda a: lax.psum_scatter(a, "shard", scatter_dimension=0, tiled=True)
-    p_wd = weights_back(hidden, cot_all, 3)
-    p_wgu = weights_back(nf, after(d_gu, p_wd), 4)
-    p_wd, p_wgu = after((p_wd, p_wgu), dn)
-    d_wd, d_wgu = scatter(p_wd), scatter(p_wgu)
-
-    d_middle, branch, *d_att = middle_back(me_arr, dn, cot, middle, gain_f, w_wide, (p_wd, p_wgu, w_all))
+    p_ffn = weights_back(nf, d_gu, hidden, cot_all, shards)
+    d_ffn = scatter(after(p_ffn, dn))
+
+    d_middle, branch, *d_att = middle_back(me_arr, dn, cot, middle, gain_f, w_wide, (p_ffn, w_all))
     p_wo = out_weights(me_arr, att, branch)
     d_att = [d_att[0]] + [swap(d_att[d], d) for d in (1, 2, 3)]
     draw, head_gains = attend_back(
         seq_lengths, ocol, qx, k, v, kt, lses, dealts, d_att, rawq, rawk,
-        cosine, sine_up, sine_down, q_gain, k_gain, head_dim, (),
+        cosine, sine_up, sine_down, q_gain, k_gain, head_dim,
     )
     bo1, bo2, *p_wo = after([bo1, bo2] + list(p_wo), d_att)
     bo = [bo0, swap(bo1, 1), swap(bo2, 2)]
     p_wo = [p_wo[0]] + [swap(p_wo[d], d) for d in (1, 2, 3)]
-    *d_raw, p_last = rows_back(orow, draw, normed, p_wo, head_gains, shards, bo[1:3] + [d_wd])
+    *d_raw, p_last = rows_back(orow, draw, normed, p_wo, head_gains, shards, bo[1:3])
     block_out = (middle + sum(b.astype(F32) for b in after(bo, p_last))).astype(BF16)
     d_raw = [d_raw[0]] + [swap(d_raw[d], d) for d in (1, 2, 3)]
-    d_last = scatter(after(p_last, d_wgu))
+    d_last = scatter(after(p_last, d_ffn))
     d_tokens = tokens_back(me_arr, d_raw, w_all, tokens[0], d_middle, gain_a, (p_last,))
-    d_wgu, d_wd = after((d_wgu, d_wd), d_raw, p_last)
+    d_ffn = after(d_ffn, d_raw, p_last)
 
     def parts_of(part):
         return [part] + [swap(part, d) for d in (1, 2, 3)]
 
-    d_wd = parts_of(d_wd)
-    for a, b, which in ((0, 1, me % 2), (2, 3, me % 2), (0, 2, me // 2), (1, 3, me // 2)):
-        d_wd[a], d_wd[b] = jnp.where(which == 1, d_wd[b], d_wd[a]), jnp.where(which == 1, d_wd[a], d_wd[b])
-    d_wd = jnp.concatenate(d_wd, axis=0).astype(F32)
-    d_wg, d_wu, ffn_dots = join_weights(me_arr, parts_of(d_wgu), w_gate, w_up, shards)
+    d_wg, d_wu, d_wd, ffn_dots = join_weights(me_arr, parts_of(d_ffn), w_gate, w_up, w_down.shape, shards)
     d_wq, d_wk, d_wv, d_wo, attn_dots, head_gains = join_last(
-        me_arr, parts_of(after(d_last, d_wgu)), w_query, w_key, w_value, w_out.shape[1]
+        me_arr, parts_of(after(d_last, d_ffn, d_tokens, block_out)), w_query, w_key, w_value, w_out.shape[1]
     )
     d_attn_gain = attn_dots[:, 0] / attn_gain.astype(F32)
     d_ffn_gain = ffn_dots[:, 0] / ffn_gain.astype(F32)

time: 428 us -> 420 us (0.981)
  waiting for transfers between devices: 92.3 us -> 107 us
  Pallas kernels: 236 us -> 226 us
  local copies, waits for them, and re-layouts: 23.3 us -> 14.5 us
    ppermute x41 -> x38, waiting for transfers between devices: 87.2 us -> 102 us  [swap(): return lax.ppermute(array, 'seq', [(s, s ^ distance) for s in range(4)])]
    pallas_call x6 -> x5, Pallas kernels: 138 us -> 126 us  [the longest x3 66.2 us: ffn(): pl.pallas_call(functools.partial(ffn_kernel, per, shards, blocks, len(car...]
    reshape x2 -> x0, local copies, waits for them, and re-layouts: 5.59 us -> none  [the longest x1 3.58 us: body(): w_d = w_wide[:, 2 * units:3 * units].reshape(units, -1)]
    ppermute x41 -> x38, starting transfers between devices: 45.3 us -> 42.9 us  [swap(): return lax.ppermute(array, 'seq', [(s, s ^ distance) for s in range(4)])]
  transfers between devices with their start and end apart: 47 -> 43, of which waited for: 17 -> 17; matrix products, arithmetic and copies ran while one was open for 6% -> 3% of each run, Pallas kernels for 55% -> 53%
where the time goes in v4:
time: 420 us; the launch traced here: 414 us
  Pallas kernels  226 us (54%)
  waiting for transfers between devices  107 us (25%)
  starting transfers between devices  43.6 us (10%)
  local copies, waits for them, and re-layouts  14.5 us (3%)
  between operations  14.4 us (3%)
  other arithmetic  8.9 us (2%)
    ppermute x38, waiting for transfers between devices, swap(): return lax.ppermute(array, 'seq', [(s, s ^ distance) for s in range(4)])  102 us
    pallas_call x3, Pallas kernels, ffn(): pl.pallas_call(functools.partial(ffn_kernel, per, shards, blocks, len(car...  66.2 us
    ppermute x38, starting transfers between devices, swap(): return lax.ppermute(array, 'seq', [(s, s ^ distance) for s in range(4)])  42.9 us
    pallas_call x1, Pallas kernels, attend_back(): pl.pallas_call(functools.partial(attend_back_kernel, head_dim, len(late))...  36 us
    pallas_call x2, Pallas kernels, attend(): pl.pallas_call(functools.partial(attend_kernel, head_dim, group, all_rows...  27.6 us
    pallas_call x1, Pallas kernels, weights_back(): pl.pallas_call(functools.partial(weights_kernel, shards), grid=(5,), out_...  24 us
    pallas_call x1, Pallas kernels, qkv(): pl.pallas_call(functools.partial(qkv_kernel, head_dim), grid=(8,), out_sh...  16.9 us
    pallas_call x1, Pallas kernels, rows_back(): pl.pallas_call(functools.partial(rows_back_kernel, depth // shards), grid...  13.6 us
  transfers between devices with their start and end apart: 43, of which 17 were waited for; matrix products, arithmetic and copies ran while one was open for 3% of the time, Pallas kernels for 53%

profile of v4, /device:TPU:0, one launch (start us, length us, event | category | flops | bytes accessed | tf_op | source)
XLA Modules:
  0.0 413.9 jit_solution(6916923406446688003)
XLA Ops:
  7.2 1.9 first_weights.1
  9.2 3.0 collective-permute-start
  12.2 1.5 collective-permute-start.1
  16.9 5.5 %make_tables.1 = (f32[2048,128]{1,0:T(8,128)}, f32[2048,128]{1,0:T(8,128)}, f32[2048,128]{1,0:T(8,128)}, s32[2048,128]{1,0:T(8,128)}, s32[1,2048]{1,0:T(1,128)}) custom-call(s32[1]{0:T(128)} %bitcast.me_ref.refs_0_, s32[1,3]{1,0:T(1,128)} %refs_0_.1, s32[1,2048]{1,0:T(1,128)} %order_ref.1, f32[1,128]{1,0:T(1,128)} %broadcast_in_dim_tile.9.freq_ref), custom_call_target="tpu_custom_call" | custom-call | flops 1048576 | bytes 65536 | tf_op jit(solution)/shard_map/make_tables/pallas_call | solution.py:252
  23.1 4.7 %cut_weights.1 = bf16[128,4608]{1,0:T(8,128)(2,1)} custom-call(s32[1]{0:T(128)} %bitcast.me_ref.refs_0_, bf16[128,4608]{1,0:T(8,128)(2,1)} %gate_ref.3, bf16[128,4608]{1,0:T(8,128)(2,1)} %up_ref.3, bf16[144,1024]{1,0:T(8,128)(2,1)} %constant_dynamic-slice_fusion.down_ref, bf16[128,1024]{1,0:T(8,128)(2,1)} %wo_ref.1), custom_call_target="tpu_custom_call" | custom-call | flops 1048576 | bytes 65536 | tf_op jit(solution)/shard_map/cut_weights/pallas_call | solution.py:136
  27.8 7.8 %collective-permute-done.x1_ref.refs_11_ = bf16[512,1024]{1,0:T(8,128)(2,1)S(1)} collective-permute-done((bf16[512,1024]{1,0:T(8,128)(2,1)}, bf16[512,1024]{1,0:T(8,128)(2,1)S(1)}, u32[]{:S(2)}, u32[]{:S(2)}) %collective-permute-start) | collective-permute-done | bytes 1048608 | tf_op jit(solution)/shard_map/ppermute | solution.py:893
  35.6 1.5 collective-permute-done.1.x2_ref.refs_12_
  37.2 1.6 collective-permute-start.2
  39.4 10.3 %collective-permute-done.2.x3a_ref.refs_9_ = bf16[512,512]{1,0:T(8,128)(2,1)S(1)} collective-permute-done((bf16[512,512]{1,0:T(8,128)(2,1)S(1)}, bf16[512,512]{1,0:T(8,128)(2,1)S(1)}, u32[]{:S(2)}, u32[]{:S(2)}) %collective-permute-start.2) | collective-permute-done | bytes 524320 | tf_op jit(solution)/shard_map/ppermute | solution.py:893
  49.7 1.3 collective-permute-done.3.x3b_ref.refs_10_
  51.1 1.9 pad_maximum_fusion
  55.0 16.9 %qkv.1 = (bf16[2048,1024]{1,0:T(8,128)(2,1)}, bf16[4,2048,128]{2,1,0:T(8,128)(2,1)}, bf16[2048,128]{1,0:T(8,128)(2,1)}, bf16[2048,128]{1,0:T(8,128)(2,1)}, bf16[...) custom-call(bf16[512,1024]{1,0:T(8,128)(2,1)} %bitcast.13, ...), custom_call_target="tpu_custom_call" | custom-call | flops 1048576 | bytes 65536 | tf_op jit(solution)/shard_map/qkv/pallas_call | solution.py:325
  71.9 13.7 %attend.3 = (bf16[2048,128]{1,0:T(8,128)(2,1)}, bf16[2048,128]{1,0:T(8,128)(2,1)}, f32[2,2048]{1,0:T(2,128)}) custom-call(s32[1,3]{1,0:T(1,128)} %refs_0_.1, s32[1,2048]{1,0:T(1,128)} %get-tuple-element.118.orow_ref, bf16[4,2048,128]{2,1,0:T(8,128)(2,1)} %get-tuple-element.127.qx_ref.refs_12_, bf16[2048,128]{1,0:T(8,128)(2,1)} %get-tuple-element.128.k_ref.refs_13_, ...), custom_call_target="tpu_custom_call" | custom-call | flops 1048576 | bytes 65536 | tf_op jit(solution)/shard_map/attend/pallas_call | solution.py:413
  85.6 1.2 collective-permute-start.5
  86.8 1.5 collective-permute-start.7
  88.3 13.9 %attend.2 = (bf16[2048,128]{1,0:T(8,128)(2,1)}, bf16[2048,128]{1,0:T(8,128)(2,1)}, f32[2,2048]{1,0:T(2,128)}) custom-call(s32[1,3]{1,0:T(1,128)} %refs_0_.1, s32[1,2048]{1,0:T(1,128)} %get-tuple-element.118.orow_ref, bf16[4,2048,128]{2,1,0:T(8,128)(2,1)} %get-tuple-element.127.qx_ref.refs_12_, bf16[2048,128]{1,0:T(8,128)(2,1)} %get-tuple-element.128.k_ref.refs_13_, ...), custom_call_target="tpu_custom_call" | custom-call | flops 1048576 | bytes 65536 | tf_op jit(solution)/shard_map/attend/pallas_call | solution.py:413
  103.6 2.1 collective-permute-start.8
  105.7 1.1 slice.41
  106.7 1.1 slice.42
  108.4 0.9 collective-permute-start.14
  109.4 7.9 %collective-permute-done.4.refs_3_.refs_2_ = bf16[2048,128]{1,0:T(8,128)(2,1)S(1)} collective-permute-done((bf16[2048,128]{1,0:T(8,128)(2,1)}, bf16[2048,128]{1,0:T(8,128)(2,1)S(1)}, u32[]{:S(2)}, u32[]{:S(2)}) %collective-permute-start.4) | collective-permute-done | bytes 524320 | tf_op jit(solution)/shard_map/ppermute | solution.py:893
  117.8 11.5 %collective-permute-done.6.refs_5_.refs_4_ = bf16[2048,128]{1,0:T(8,128)(2,1)S(1)} collective-permute-done((bf16[2048,128]{1,0:T(8,128)(2,1)}, bf16[2048,128]{1,0:T(8,128)(2,1)S(1)}, u32[]{:S(2)}, u32[]{:S(2)}) %collective-permute-start.6) | collective-permute-done | bytes 524320 | tf_op jit(solution)/shard_map/ppermute | solution.py:893
  129.2 1.3 collective-permute-start.9
  130.5 1.4 fusion
  132.0 9.4 %collective-permute-done.12.refs_8_.refs_10_ = bf16[1024,128]{1,0:T(8,128)(2,1)S(1)} collective-permute-done((bf16[1024,128]{1,0:T(8,128)(2,1)S(1)}, bf16[1024,128]{1,0:T(8,128)(2,1)S(1)}, u32[]{:S(2)}, u32[]{:S(2)}) %collective-permute-start.12) | collective-permute-done | bytes 262176 | tf_op jit(solution)/shard_map/ppermute | solution.py:893
  142.1 17.1 %ffn.3 = (bf16[2048,1024]{1,0:T(8,128)(2,1)}, bf16[2048,1152]{1,0:T(8,128)(2,1)}, bf16[2048,2304]{1,0:T(8,128)(2,1)}, bf16[2048,1024]{1,0:T(8,128)(2,1)}, bf16[5...) custom-call(s32[1]{0:T(128)} %bitcast.me_ref.refs_0_, ...), custom_call_target="tpu_custom_call" | custom-call | flops 1048576 | bytes 65536 | tf_op jit(solution)/shard_map/ffn/pallas_call | solution.py:766
  159.2 1.1 collective-permute-start.15
  160.8 1.3 collective-permute-start.17
  162.1 1.2 collective-permute-start.18
  163.3 17.3 %ffn.4 = (bf16[2048,1024]{1,0:T(8,128)(2,1)}, bf16[2048,1152]{1,0:T(8,128)(2,1)}, bf16[2048,2304]{1,0:T(8,128)(2,1)}, bf16[2048,1024]{1,0:T(8,128)(2,1)}, bf16[5...) custom-call(s32[1]{0:T(128)} %bitcast.me_ref.refs_0_, ...), custom_call_target="tpu_custom_call", output_to_operand_aliasing={{0}: (16, {}), {1}: (17, {}), {2}: (18, {}), {3}: (19, {})} | custom-call | flops 1048576 | bytes 65536 | tf_op jit(solution)/shard_map/ffn/pallas_call | solution.py:766
  182.0 31.8 %ffn.5 = (bf16[2048,1024]{1,0:T(8,128)(2,1)}, bf16[2048,1152]{1,0:T(8,128)(2,1)}, bf16[2048,2304]{1,0:T(8,128)(2,1)}, bf16[2048,1024]{1,0:T(8,128)(2,1)}, bf16[5...) custom-call(s32[1]{0:T(128)} %bitcast.me_ref.refs_0_, ...), custom_call_target="tpu_custom_call", output_to_operand_aliasing={{0}: (24, {}), {1}: (25, {}), {2}: (26, {}), {3}: (27, {})} | custom-call | flops 1048576 | bytes 65536 | tf_op jit(solution)/shard_map/ffn/pallas_call | solution.py:766
  213.8 1.1 collective-permute-start.19
  215.6 24.0 %weights_back.1.refs_8_ = bf16[1024,3456]{1,0:T(8,128)(2,1)} custom-call(bf16[2048,1024]{1,0:T(8,128)(2,1)} %get-tuple-element.157.nf_ref, bf16[2048,2304]{1,0:T(8,128)(2,1)} %get-tuple-element.158.dgu_ref, bf16[2048,1152]{1,0:T(8,128)(2,1)} %get-tuple-element.159.hid_ref, bf16[2048,1024]{1,0:T(8,128)(2,1)} %get-tuple-element.160.cot_ref), custom_call_target="tpu_custom_call" | custom-call | flops 1048576 | bytes 65536 | tf_op jit(solution)/shard_map/weights_back/pallas_call | solution.py:807
  239.7 1.0 copy-done.19
  241.1 7.2 %middle_back.1 = (f32[512,1024]{1,0:T(8,128)}, bf16[512,1024]{1,0:T(8,128)(2,1)}, bf16[512,256]{1,0:T(8,128)(2,1)}, bf16[512,256]{1,0:T(8,128)(2,1)}, bf16[512,2...) custom-call(s32[1]{0:T(128)} %bitcast.me_ref.refs_0_, bf16[512,1024]{1,0:T(8,128)(2,1)} %get-tuple-element.154.refs_1_, ...), custom_call_target="tpu_custom_call" | custom-call | flops 1048576 | bytes 65536 | tf_op jit(solution)/shard_map/middle_back/pallas_call | solution.py:880
  248.3 1.1 collective-permute-start.21
  249.3 1.2 collective-permute-start.22
  250.6 1.2 collective-permute-start.23
  251.8 4.7 %out_weights.1 = (bf16[1024,256]{1,0:T(8,128)(2,1)}, bf16[1024,256]{1,0:T(8,128)(2,1)}, bf16[1024,256]{1,0:T(8,128)(2,1)}, bf16[1024,256]{1,0:T(8,128)(2,1)}) custom-call(s32[1]{0:T(128)} %bitcast.me_ref.refs_0_, bf16[2048,128]{1,0:T(8,128)(2,1)} %get-tuple-element.130.refs_1_.refs_0_, bf16[2048,128]{1,0:T(8,128)(2,1)} %get-tuple-element.131.refs_2_.refs_1_, ...), custom_call_target="tpu_custom_call" | custom-call | flops 1048576 | bytes 65536 | tf_op jit(solution)/shard_map/out_weights/pallas_call | solution.py:863
  256.5 0.8 collective-permute-done.22.refs_8_
  257.3 4.9 %collective-permute-done.23.refs_9_ = bf16[512,256]{1,0:T(8,128)(2,1)S(1)} collective-permute-done((bf16[512,256]{1,0:T(8,128)(2,1)}, bf16[512,256]{1,0:T(8,128)(2,1)S(1)}, u32[]{:S(2)}, u32[]{:S(2)}) %collective-permute-start.23) | collective-permute-done | bytes 262176 | tf_op jit(solution)/shard_map/ppermute | solution.py:893
  263.5 0.8 collective-permute-start.26
  264.3 1.9 collective-permute-start.27
  267.0 36.0 %attend_back.1 = (bf16[2048,512]{1,0:T(8,128)(2,1)}, f32[2,128]{1,0:T(2,128)}) custom-call(s32[1,3]{1,0:T(1,128)} %refs_0_.1, s32[2048,128]{1,0:T(8,128)} %get-tuple-element.121.ocol_ref.refs_1_, f32[2,2048]{1,0:T(2,128)} %get-tuple-element.175.refs_2_, f32[2,2048]{1,0:T(2,128)} %get-tuple-element.176.refs_3_, bf16[2048,128]{1,0:T(8,128)(2,1)} %get-tuple-element.177.refs_4_, ...), custom_call_target="tpu_custom_call" | custom-call | flops 1048576 | bytes 65536 | tf_op jit(solution)/shard_map/attend_back/pallas_call | solution.py:579
  305.3 13.6 %rows_back.1 = (bf16[512,512]{1,0:T(8,128)(2,1)}, bf16[512,512]{1,0:T(8,128)(2,1)}, bf16[512,512]{1,0:T(8,128)(2,1)}, bf16[512,512]{1,0:T(8,128)(2,1)}, bf16[1024,896]{1,0:T(8,128)(2,1)}) custom-call(s32[1,2048]{1,0:T(1,128)} %get-tuple-element.118.orow_ref, bf16[2048,512]{1,0:T(8,128)(2,1)} %get-tuple-element.183.draw_ref, ...), custom_call_target="tpu_custom_call" | custom-call | flops 1048576 | bytes 65536 | tf_op jit(solution)/shard_map/rows_back/pallas_call | solution.py:606
  319.0 4.9 %reduce-scatter.3.cloned.1.call-done.p0_ref = bf16[128,3456]{1,0:T(8,128)(2,1)} async-done(((bf16[1024,3456]{1,0:T(8,128)(2,1)}), bf16[128,3456]{1,0:T(8,128)(2,1)}) %reduce-scatter.3.cloned.1.call-update) | async-done | bytes 884752 | tf_op jit(solution)/shard_map/reduce_scatter | solution.py:967
  323.9 1.5 collective-permute-start.29
  325.5 1.5 collective-permute-start.30
  327.5 11.6 %collective-permute-done.29.g1_ref = bf16[512,512]{1,0:T(8,128)(2,1)S(1)} collective-permute-done((bf16[512,512]{1,0:T(8,128)(2,1)}, bf16[512,512]{1,0:T(8,128)(2,1)S(1)}, u32[]{:S(2)}, u32[]{:S(2)}) %collective-permute-start.29) | collective-permute-done | bytes 524320 | tf_op jit(solution)/shard_map/ppermute | solution.py:893
  339.1 8.9 %collective-permute-done.30.g2_ref = bf16[512,512]{1,0:T(8,128)(2,1)S(1)} collective-permute-done((bf16[512,512]{1,0:T(8,128)(2,1)}, bf16[512,512]{1,0:T(8,128)(2,1)S(1)}, u32[]{:S(2)}, u32[]{:S(2)}) %collective-permute-start.30) | collective-permute-done | bytes 524320 | tf_op jit(solution)/shard_map/ppermute | solution.py:893
  348.3 1.4 collective-permute-start.35
  350.3 1.4 collective-permute-start.37
  351.8 3.3 add_convert_fusion
  355.1 7.4 %tokens_back.1 = bf16[512,1024]{1,0:T(8,128)(2,1)} custom-call(s32[1]{0:T(128)} %bitcast.me_ref.refs_0_, bf16[512,512]{1,0:T(8,128)(2,1)} %get-tuple-element.194.g0_ref, bf16[512,512]{1,0:T(8,128)(2,1)} %copy-done.28, bf16[512,512]{1,0:T(8,128)(2,1)} %copy-done.29, bf16[512,512]{1,0:T(8,128)(2,1)} %copy-done.30, ...), custom_call_target="tpu_custom_call" | custom-call | flops 1048576 | bytes 65536 | tf_op jit(solution)/shard_map/tokens_back/pallas_call | solution.py:640
  362.5 1.4 collective-permute-start.32
  363.9 1.2 collective-permute-start.33
  365.1 6.1 %collective-permute-done.35.p1_ref = bf16[128,3456]{1,0:T(8,128)(2,1)} collective-permute-done((bf16[128,3456]{1,0:T(8,128)(2,1)}, bf16[128,3456]{1,0:T(8,128)(2,1)}, u32[]{:S(2)}, u32[]{:S(2)}) %collective-permute-start.35) | collective-permute-done | bytes 884768 | tf_op jit(solution)/shard_map/ppermute | solution.py:893
  371.2 1.5 collective-permute-start.34
  372.7 18.9 %collective-permute-done.36.p2_ref = bf16[128,3456]{1,0:T(8,128)(2,1)} collective-permute-done((bf16[128,3456]{1,0:T(8,128)(2,1)}, bf16[128,3456]{1,0:T(8,128)(2,1)}, u32[]{:S(2)}, u32[]{:S(2)}) %collective-permute-start.36) | collective-permute-done | bytes 884768 | tf_op jit(solution)/shard_map/ppermute | solution.py:893
  391.6 7.1 %join_weights.1 = (f32[128,4608]{1,0:T(8,128)}, f32[128,4608]{1,0:T(8,128)}, f32[576,1024]{1,0:T(8,128)}, f32[128,1]{1,0:T(8,128)}) custom-call(s32[1]{0:T(128)} %bitcast.me_ref.refs_0_, bf16[128,3456]{1,0:T(8,128)(2,1)} %reduce-scatter.3.cloned.1.call-done.p0_ref, bf16[128,3456]{1,0:T(8,128)(2,1)} %collective-permute-done.35.p1_ref, ...), custom_call_target="tpu_custom_call" | custom-call | flops 1048576 | bytes 65536 | tf_op jit(solution)/shard_map/join_weights/pallas_call | solution.py:168
  398.7 0.9 reduce.1
  401.6 2.7 join_last.1
  404.3 0.8 slice_add_fusion
  405.7 0.9 reduce
  (147 shorter events, 21.8 us)
Async XLA Ops:
  7.2 15.2 %copy-start = (bf16[576,1024]{1,0:T(8,128)(2,1)S(1)}, bf16[576,1024]{1,0:T(8,128)(2,1)}, u32[]{:S(2)}) copy-start(bf16[576,1024]{1,0:T(8,128)(2,1)} %param.28) | copy-start | bytes 3538948
  7.2 47.8 %all-gather.4.cloned.1.call-start = ((), (), s32[]{:S(2)}) async-start(), calls=%async_computation.2 | async-start | bytes 1474560 | tf_op jit(solution)/shard_map/all_gather | solution.py:931
  9.2 132.2 %all-gather.6.cloned.1.call-start = ((), (), s32[]{:S(2)}) async-start(), calls=%async_computation.3 | async-start | bytes 10616832 | tf_op jit(solution)/shard_map/all_gather | solution.py:933
  9.2 26.4 %collective-permute-start = (bf16[512,1024]{1,0:T(8,128)(2,1)}, bf16[512,1024]{1,0:T(8,128)(2,1)S(1)}, u32[]{:S(2)}, u32[]{:S(2)}) collective-permute-start(bf16[512,1024]{1,0:T(8,128)(2,1)} %bitcast.11), channel_id=1, source_target_pairs={{0,8},{8,0},{16,24},{24,16},{1,9},{9,1},{17,25},{25,17},{2,10},{10... | collective-permute-start | bytes 3145736 | tf_op jit(solution)/shard_map/ppermute | solution.py:893
  12.2 24.8 %collective-permute-start.1 = (bf16[512,1024]{1,0:T(8,128)(2,1)}, bf16[512,1024]{1,0:T(8,128)(2,1)S(1)}, u32[]{:S(2)}, u32[]{:S(2)}) collective-permute-start(bf16[512,1024]{1,0:T(8,128)(2,1)} %bitcast.12), channel_id=1, source_target_pairs={{0,16},{8,24},{16,0},{24,8},{1,17},{9,25},{17,1},{25,9},{2,18},{10... | collective-permute-start | bytes 3145736 | tf_op jit(solution)/shard_map/ppermute | solution.py:893
  27.8 23.3 %copy-start.14 = (bf16[128,1024]{1,0:T(8,128)(2,1)S(1)}, bf16[128,1024]{1,0:T(8,128)(2,1)}, u32[]{:S(2)}) copy-start(bf16[128,1024]{1,0:T(8,128)(2,1)} %q_ref.3) | copy-start | bytes 786436
  27.8 23.3 %copy-start.17 = (bf16[128,512]{1,0:T(8,128)(2,1)S(1)}, bf16[128,512]{1,0:T(8,128)(2,1)}, u32[]{:S(2)}) copy-start(bf16[128,512]{1,0:T(8,128)(2,1)} %k_ref.3) | copy-start | bytes 393220
  35.6 17.4 %copy-start.8 = (bf16[512,1024]{1,0:T(8,128)(2,1)}, bf16[512,1024]{1,0:T(8,128)(2,1)S(1)}, u32[]{:S(2)}) copy-start(bf16[512,1024]{1,0:T(8,128)(2,1)S(1)} %collective-permute-done.x1_ref.refs_11_) | copy-start | bytes 3145732
  37.1 15.9 %copy-start.9 = (bf16[512,1024]{1,0:T(8,128)(2,1)}, bf16[512,1024]{1,0:T(8,128)(2,1)S(1)}, u32[]{:S(2)}) copy-start(bf16[512,1024]{1,0:T(8,128)(2,1)S(1)} %collective-permute-done.1.x2_ref.refs_12_) | copy-start | bytes 3145732
  37.1 204.0 %all-gather.8.cloned.1.call-start = ((), (), s32[]{:S(2)}) async-start(), calls=%async_computation.4 | async-start | bytes 4718592 | tf_op jit(solution)/shard_map/all_gather | solution.py:945
  37.2 12.5 %collective-permute-start.2 = (bf16[512,512]{1,0:T(8,128)(2,1)S(1)}, bf16[512,512]{1,0:T(8,128)(2,1)S(1)}, u32[]{:S(2)}, u32[]{:S(2)}) collective-permute-start(bf16[512,512]{1,0:T(8,128)(2,1)S(1)} %slice.36), channel_id=1, source_target_pairs={{0,16},{8,24},{16,0},{24,8},{1,17},{9,25},{17,1},{25,9},{2,18},{10... | collective-permute-start | bytes 1572872 | tf_op jit(solution)/shard_map/ppermute | solution.py:893
  38.8 12.3 %collective-permute-start.3 = (bf16[512,512]{1,0:T(8,128)(2,1)S(1)}, bf16[512,512]{1,0:T(8,128)(2,1)S(1)}, u32[]{:S(2)}, u32[]{:S(2)}) collective-permute-start(bf16[512,512]{1,0:T(8,128)(2,1)S(1)} %slice.37), channel_id=1, source_target_pairs={{0,8},{8,0},{16,24},{24,16},{1,9},{9,1},{17,25},{25,17},{2,10},{10... | collective-permute-start | bytes 1572872 | tf_op jit(solution)/shard_map/ppermute | solution.py:893
  53.0 270.9 %reduce-scatter.3.cloned.1.call-start = ((), (), s32[]{:S(2)}) async-start(), calls=%async_computation.5 | async-start | bytes 7962624 | tf_op jit(solution)/shard_map/reduce_scatter | solution.py:967
  53.6 49.3 %collective-permute-start.10 = (bf16[512,1024]{1,0:T(8,128)(2,1)}, bf16[512,1024]{1,0:T(8,128)(2,1)}, u32[]{:S(2)}, u32[]{:S(2)}) collective-permute-start(bf16[512,1024]{1,0:T(8,128)(2,1)} %bitcast.4.refs_10_.refs_4_), channel_id=1, source_target_pairs={{0,8},{8,0},{16,24},{24,16},{1,9},{9,1},{17,25},{25,17},{2,10},{10... | collective-permute-start | bytes 3145736 | tf_op jit(solution)/shard_map/ppermute | solution.py:893
  54.4 49.2 %collective-permute-start.11 = (bf16[512,1024]{1,0:T(8,128)(2,1)}, bf16[512,1024]{1,0:T(8,128)(2,1)}, u32[]{:S(2)}, u32[]{:S(2)}) collective-permute-start(bf16[512,1024]{1,0:T(8,128)(2,1)} %bitcast.4.refs_10_.refs_4_), channel_id=1, source_target_pairs={{0,16},{8,24},{16,0},{24,8},{1,17},{9,25},{17,1},{25,9},{2,18},{10... | collective-permute-start | bytes 3145736 | tf_op jit(solution)/shard_map/ppermute | solution.py:893
  85.6 22.2 %collective-permute-start.5 = (bf16[2048,128]{1,0:T(8,128)(2,1)}, bf16[2048,128]{1,0:T(8,128)(2,1)S(1)}, u32[]{:S(2)}, u32[]{:S(2)}) collective-permute-start(bf16[2048,128]{1,0:T(8,128)(2,1)} %get-tuple-element.131.refs_2_.refs_1_), channel_id=1, source_target_pairs={{0,8},{8,0},{16,24},{24,16},{1,9},{9,1},{17,25},{25,17},{2,10},{10... | collective-permute-start | bytes 1572872 | tf_op jit(solution)/shard_map/ppermute | solution.py:893
  86.8 21.7 %collective-permute-start.7 = (bf16[2048,128]{1,0:T(8,128)(2,1)}, bf16[2048,128]{1,0:T(8,128)(2,1)S(1)}, u32[]{:S(2)}, u32[]{:S(2)}) collective-permute-start(bf16[2048,128]{1,0:T(8,128)(2,1)} %get-tuple-element.131.refs_2_.refs_1_), channel_id=1, source_target_pairs={{0,16},{8,24},{16,0},{24,8},{1,17},{9,25},{17,1},{25,9},{2,18},{10... | collective-permute-start | bytes 1572872 | tf_op jit(solution)/shard_map/ppermute | solution.py:893
  102.2 15.1 %collective-permute-start.4 = (bf16[2048,128]{1,0:T(8,128)(2,1)}, bf16[2048,128]{1,0:T(8,128)(2,1)S(1)}, u32[]{:S(2)}, u32[]{:S(2)}) collective-permute-start(bf16[2048,128]{1,0:T(8,128)(2,1)} %get-tuple-element.130.refs_1_.refs_0_), channel_id=1, source_target_pairs={{0,8},{8,0},{16,24},{24,16},{1,9},{9,1},{17,25},{25,17},{2,10},{10... | collective-permute-start | bytes 1572872 | tf_op jit(solution)/shard_map/ppermute | solution.py:893
  102.9 26.3 %collective-permute-start.6 = (bf16[2048,128]{1,0:T(8,128)(2,1)}, bf16[2048,128]{1,0:T(8,128)(2,1)S(1)}, u32[]{:S(2)}, u32[]{:S(2)}) collective-permute-start(bf16[2048,128]{1,0:T(8,128)(2,1)} %get-tuple-element.130.refs_1_.refs_0_), channel_id=1, source_target_pairs={{0,16},{8,24},{16,0},{24,8},{1,17},{9,25},{17,1},{25,9},{2,18},{10... | collective-permute-start | bytes 1572872 | tf_op jit(solution)/shard_map/ppermute | solution.py:893
  103.6 28.4 %collective-permute-start.8 = (bf16[2048,128]{1,0:T(8,128)(2,1)}, bf16[2048,128]{1,0:T(8,128)(2,1)S(1)}, u32[]{:S(2)}, u32[]{:S(2)}) collective-permute-start(bf16[2048,128]{1,0:T(8,128)(2,1)} %get-tuple-element.130.refs_1_.refs_0_), channel_id=1, source_target_pairs={{0,24},{8,16},{16,8},{24,0},{1,25},{9,17},{17,9},{25,1},{2,26},{10... | collective-permute-start | bytes 1572872 | tf_op jit(solution)/shard_map/ppermute | solution.py:893
  107.8 33.5 %copy-start.3 = (bf16[2048,128]{1,0:T(8,128)(2,1)}, bf16[2048,128]{1,0:T(8,128)(2,1)S(1)}, u32[]{:S(2)}) copy-start(bf16[2048,128]{1,0:T(8,128)(2,1)S(1)} %collective-permute-done.5.refs_4_.refs_3_) | copy-start | bytes 1572868
  107.9 33.5 %collective-permute-start.13 = (bf16[512,512]{1,0:T(8,128)(2,1)S(1)}, bf16[512,512]{1,0:T(8,128)(2,1)}, u32[]{:S(2)}, u32[]{:S(2)}) collective-permute-start(bf16[512,512]{1,0:T(8,128)(2,1)S(1)} %slice.41), channel_id=1, source_target_pairs={{0,16},{8,24},{16,0},{24,8},{1,17},{9,25},{17,1},{25,9},{2,18},{10... | collective-permute-start | bytes 1572872 | tf_op jit(solution)/shard_map/ppermute | solution.py:893
  108.4 33.0 %copy-start.4 = (bf16[2048,128]{1,0:T(8,128)(2,1)}, bf16[2048,128]{1,0:T(8,128)(2,1)S(1)}, u32[]{:S(2)}) copy-start(bf16[2048,128]{1,0:T(8,128)(2,1)S(1)} %collective-permute-done.7.refs_6_.refs_5_) | copy-start | bytes 1572868
  108.4 32.9 %collective-permute-start.14 = (bf16[512,512]{1,0:T(8,128)(2,1)S(1)}, bf16[512,512]{1,0:T(8,128)(2,1)}, u32[]{:S(2)}, u32[]{:S(2)}) collective-permute-start(bf16[512,512]{1,0:T(8,128)(2,1)S(1)} %slice.42), channel_id=1, source_target_pairs={{0,8},{8,0},{16,24},{24,16},{1,9},{9,1},{17,25},{25,17},{2,10},{10... | collective-permute-start | bytes 1572872 | tf_op jit(solution)/shard_map/ppermute | solution.py:893
  117.3 24.2 %copy-start.5 = (bf16[2048,128]{1,0:T(8,128)(2,1)}, bf16[2048,128]{1,0:T(8,128)(2,1)S(1)}, u32[]{:S(2)}) copy-start(bf16[2048,128]{1,0:T(8,128)(2,1)S(1)} %collective-permute-done.4.refs_3_.refs_2_) | copy-start | bytes 1572868
  117.3 24.1 %collective-permute-start.12 = (bf16[1024,128]{1,0:T(8,128)(2,1)S(1)}, bf16[1024,128]{1,0:T(8,128)(2,1)S(1)}, u32[]{:S(2)}, u32[]{:S(2)}) collective-permute-start(bf16[1024,128]{1,0:T(8,128)(2,1)S(1)} %slice.49), channel_id=1, source_target_pairs={{0,16},{8,24},{16,0},{24,8},{1,17},{9,25},{17,1},{25,9},{2,18},{10... | collective-permute-start | bytes 786440 | tf_op jit(solution)/shard_map/ppermute | solution.py:893
  129.2 12.2 %copy-start.6 = (bf16[2048,128]{1,0:T(8,128)(2,1)}, bf16[2048,128]{1,0:T(8,128)(2,1)S(1)}, u32[]{:S(2)}) copy-start(bf16[2048,128]{1,0:T(8,128)(2,1)S(1)} %collective-permute-done.6.refs_5_.refs_4_) | copy-start | bytes 1572868
  129.2 12.1 %collective-permute-start.9 = (bf16[1024,128]{1,0:T(8,128)(2,1)S(1)}, bf16[1024,128]{1,0:T(8,128)(2,1)S(1)}, u32[]{:S(2)}, u32[]{:S(2)}) collective-permute-start(bf16[1024,128]{1,0:T(8,128)(2,1)S(1)} %slice.48), channel_id=1, source_target_pairs={{0,8},{8,0},{16,24},{24,16},{1,9},{9,1},{17,25},{25,17},{2,10},{10... | collective-permute-start | bytes 786440 | tf_op jit(solution)/shard_map/ppermute | solution.py:893
  132.0 9.5 %copy-start.2 = (bf16[2048,128]{1,0:T(8,128)(2,1)}, bf16[2048,128]{1,0:T(8,128)(2,1)S(1)}, u32[]{:S(2)}) copy-start(bf16[2048,128]{1,0:T(8,128)(2,1)S(1)} %collective-permute-done.8.refs_7_.refs_9_.refs_6_) | copy-start | bytes 1572868
  159.2 21.4 %collective-permute-start.15 = (bf16[512,512]{1,0:T(8,128)(2,1)}, bf16[512,512]{1,0:T(8,128)(2,1)S(1)}, u32[]{:S(2)}, u32[]{:S(2)}) collective-permute-start(bf16[512,512]{1,0:T(8,128)(2,1)} %get-tuple-element.144), channel_id=1, source_target_pairs={{0,8},{8,0},{16,24},{24,16},{1,9},{9,1},{17,25},{25,17},{2,10},{10... | collective-permute-start | bytes 1572872 | tf_op jit(solution)/shard_map/ppermute | solution.py:893
  160.3 20.3 %collective-permute-start.16 = (bf16[512,512]{1,0:T(8,128)(2,1)}, bf16[512,512]{1,0:T(8,128)(2,1)S(1)}, u32[]{:S(2)}, u32[]{:S(2)}) collective-permute-start(bf16[512,512]{1,0:T(8,128)(2,1)} %get-tuple-element.145), channel_id=1, source_target_pairs={{0,16},{8,24},{16,0},{24,8},{1,17},{9,25},{17,1},{25,9},{2,18},{10... | collective-permute-start | bytes 1572872 | tf_op jit(solution)/shard_map/ppermute | solution.py:893
  160.8 19.9 %collective-permute-start.17 = (bf16[512,512]{1,0:T(8,128)(2,1)}, bf16[512,512]{1,0:T(8,128)(2,1)S(1)}, u32[]{:S(2)}, u32[]{:S(2)}) collective-permute-start(bf16[512,512]{1,0:T(8,128)(2,1)} %get-tuple-element.146), channel_id=1, source_target_pairs={{0,8},{8,0},{16,24},{24,16},{1,9},{9,1},{17,25},{25,17},{2,10},{10... | collective-permute-start | bytes 1572872 | tf_op jit(solution)/shard_map/ppermute | solution.py:893
  162.1 18.8 %collective-permute-start.18 = (bf16[512,512]{1,0:T(8,128)(2,1)}, bf16[512,512]{1,0:T(8,128)(2,1)S(1)}, u32[]{:S(2)}, u32[]{:S(2)}) collective-permute-start(bf16[512,512]{1,0:T(8,128)(2,1)} %get-tuple-element.147), channel_id=1, source_target_pairs={{0,16},{8,24},{16,0},{24,8},{1,17},{9,25},{17,1},{25,9},{2,18},{10... | collective-permute-start | bytes 1572872 | tf_op jit(solution)/shard_map/ppermute | solution.py:893
  213.8 25.8 %collective-permute-start.19 = (bf16[512,1024]{1,0:T(8,128)(2,1)}, bf16[512,1024]{1,0:T(8,128)(2,1)S(1)}, u32[]{:S(2)}, u32[]{:S(2)}) collective-permute-start(bf16[512,1024]{1,0:T(8,128)(2,1)} %get-tuple-element.155), channel_id=1, source_target_pairs={{0,8},{8,0},{16,24},{24,16},{1,9},{9,1},{17,25},{25,17},{2,10},{10... | collective-permute-start | bytes 3145736 | tf_op jit(solution)/shard_map/ppermute | solution.py:893
  214.9 24.7 %collective-permute-start.20 = (bf16[512,1024]{1,0:T(8,128)(2,1)}, bf16[512,1024]{1,0:T(8,128)(2,1)S(1)}, u32[]{:S(2)}, u32[]{:S(2)}) collective-permute-start(bf16[512,1024]{1,0:T(8,128)(2,1)} %get-tuple-element.156), channel_id=1, source_target_pairs={{0,16},{8,24},{16,0},{24,8},{1,17},{9,25},{17,1},{25,9},{2,18},{10... | collective-permute-start | bytes 3145736 | tf_op jit(solution)/shard_map/ppermute | solution.py:893
  241.1 121.4 %reduce-scatter.5.cloned.1.call-start = ((), (), s32[]{:S(2)}) async-start(), calls=%async_computation.6 | async-start | bytes 2064384 | tf_op jit(solution)/shard_map/reduce_scatter | solution.py:967
  248.3 8.2 %collective-permute-start.21 = (bf16[512,256]{1,0:T(8,128)(2,1)}, bf16[512,256]{1,0:T(8,128)(2,1)S(1)}, u32[]{:S(2)}, u32[]{:S(2)}) collective-permute-start(bf16[512,256]{1,0:T(8,128)(2,1)} %get-tuple-element.170), channel_id=1, source_target_pairs={{0,8},{8,0},{16,24},{24,16},{1,9},{9,1},{17,25},{25,17},{2,10},{10... | collective-permute-start | bytes 786440 | tf_op jit(solution)/shard_map/ppermute | solution.py:893
  249.3 8.0 %collective-permute-start.22 = (bf16[512,256]{1,0:T(8,128)(2,1)}, bf16[512,256]{1,0:T(8,128)(2,1)S(1)}, u32[]{:S(2)}, u32[]{:S(2)}) collective-permute-start(bf16[512,256]{1,0:T(8,128)(2,1)} %get-tuple-element.171), channel_id=1, source_target_pairs={{0,16},{8,24},{16,0},{24,8},{1,17},{9,25},{17,1},{25,9},{2,18},{10... | collective-permute-start | bytes 786440 | tf_op jit(solution)/shard_map/ppermute | solution.py:893
  250.6 11.6 %collective-permute-start.23 = (bf16[512,256]{1,0:T(8,128)(2,1)}, bf16[512,256]{1,0:T(8,128)(2,1)S(1)}, u32[]{:S(2)}, u32[]{:S(2)}) collective-permute-start(bf16[512,256]{1,0:T(8,128)(2,1)} %get-tuple-element.172), channel_id=1, source_target_pairs={{0,24},{8,16},{16,8},{24,0},{1,25},{9,17},{17,9},{25,1},{2,26},{10... | collective-permute-start | bytes 786440 | tf_op jit(solution)/shard_map/ppermute | solution.py:893
  251.8 11.2 %copy-start.39 = (bf16[512,1024]{1,0:T(8,128)(2,1)S(1)}, bf16[512,1024]{1,0:T(8,128)(2,1)}, u32[]{:S(2)}) copy-start(bf16[512,1024]{1,0:T(8,128)(2,1)} %get-tuple-element.174) | copy-start | bytes 3145732
  256.5 10.5 %copy-start.31 = (bf16[512,256]{1,0:T(8,128)(2,1)}, bf16[512,256]{1,0:T(8,128)(2,1)S(1)}, u32[]{:S(2)}) copy-start(bf16[512,256]{1,0:T(8,128)(2,1)S(1)} %collective-permute-done.21.refs_7_) | copy-start | bytes 786436
  257.3 9.7 %copy-start.32 = (bf16[512,256]{1,0:T(8,128)(2,1)}, bf16[512,256]{1,0:T(8,128)(2,1)S(1)}, u32[]{:S(2)}) copy-start(bf16[512,256]{1,0:T(8,128)(2,1)S(1)} %collective-permute-done.22.refs_8_) | copy-start | bytes 786436
  262.2 41.5 %collective-permute-start.24 = (bf16[512,1024]{1,0:T(8,128)(2,1)}, bf16[512,1024]{1,0:T(8,128)(2,1)S(1)}, u32[]{:S(2)}, u32[]{:S(2)}) collective-permute-start(bf16[512,1024]{1,0:T(8,128)(2,1)} %get-tuple-element.173), channel_id=1, source_target_pairs={{0,8},{8,0},{16,24},{24,16},{1,9},{9,1},{17,25},{25,17},{2,10},{10... | collective-permute-start | bytes 3145736 | tf_op jit(solution)/shard_map/ppermute | solution.py:893
  262.9 40.8 %collective-permute-start.25 = (bf16[512,1024]{1,0:T(8,128)(2,1)S(1)}, bf16[512,1024]{1,0:T(8,128)(2,1)S(1)}, u32[]{:S(2)}, u32[]{:S(2)}) collective-permute-start(bf16[512,1024]{1,0:T(8,128)(2,1)S(1)} %copy-done.39), channel_id=1, source_target_pairs={{0,16},{8,24},{16,0},{24,8},{1,17},{9,25},{17,1},{25,9},{2,18},{10... | collective-permute-start | bytes 3145736 | tf_op jit(solution)/shard_map/ppermute | solution.py:893
  263.5 39.5 %collective-permute-start.26 = (bf16[1024,256]{1,0:T(8,128)(2,1)}, bf16[1024,256]{1,0:T(8,128)(2,1)S(1)}, u32[]{:S(2)}, u32[]{:S(2)}) collective-permute-start(bf16[1024,256]{1,0:T(8,128)(2,1)} %get-tuple-element.186), channel_id=1, source_target_pairs={{0,8},{8,0},{16,24},{24,16},{1,9},{9,1},{17,25},{25,17},{2,10},{10... | collective-permute-start | bytes 1572872 | tf_op jit(solution)/shard_map/ppermute | solution.py:893
  264.3 39.3 %collective-permute-start.27 = (bf16[1024,256]{1,0:T(8,128)(2,1)}, bf16[1024,256]{1,0:T(8,128)(2,1)S(1)}, u32[]{:S(2)}, u32[]{:S(2)}) collective-permute-start(bf16[1024,256]{1,0:T(8,128)(2,1)} %get-tuple-element.187), channel_id=1, source_target_pairs={{0,16},{8,24},{16,0},{24,8},{1,17},{9,25},{17,1},{25,9},{2,18},{10... | collective-permute-start | bytes 1572872 | tf_op jit(solution)/shard_map/ppermute | solution.py:893
  266.2 37.4 %collective-permute-start.28 = (bf16[1024,256]{1,0:T(8,128)(2,1)}, bf16[1024,256]{1,0:T(8,128)(2,1)S(1)}, u32[]{:S(2)}, u32[]{:S(2)}) collective-permute-start(bf16[1024,256]{1,0:T(8,128)(2,1)} %get-tuple-element.188), channel_id=1, source_target_pairs={{0,24},{8,16},{16,8},{24,0},{1,25},{9,17},{17,9},{25,1},{2,26},{10... | collective-permute-start | bytes 1572872 | tf_op jit(solution)/shard_map/ppermute | solution.py:893
  305.3 46.5 %copy-start.7 = (f32[512,1024]{1,0:T(8,128)S(1)}, f32[512,1024]{1,0:T(8,128)}, u32[]{:S(2)}) copy-start(f32[512,1024]{1,0:T(8,128)} %get-tuple-element.142.refs_5_) | copy-start | bytes 6291460
  319.0 32.8 %copy-start.12 = (bf16[512,1024]{1,0:T(8,128)(2,1)S(1)}, bf16[512,1024]{1,0:T(8,128)(2,1)}, u32[]{:S(2)}) copy-start(bf16[512,1024]{1,0:T(8,128)(2,1)} %copy-done.11) | copy-start | bytes 3145732
  323.9 15.1 %collective-permute-start.29 = (bf16[512,512]{1,0:T(8,128)(2,1)}, bf16[512,512]{1,0:T(8,128)(2,1)S(1)}, u32[]{:S(2)}, u32[]{:S(2)}) collective-permute-start(bf16[512,512]{1,0:T(8,128)(2,1)} %get-tuple-element.195), channel_id=1, source_target_pairs={{0,8},{8,0},{16,24},{24,16},{1,9},{9,1},{17,25},{25,17},{2,10},{10... | collective-permute-start | bytes 1572872 | tf_op jit(solution)/shard_map/ppermute | solution.py:893
  325.5 22.6 %collective-permute-start.30 = (bf16[512,512]{1,0:T(8,128)(2,1)}, bf16[512,512]{1,0:T(8,128)(2,1)S(1)}, u32[]{:S(2)}, u32[]{:S(2)}) collective-permute-start(bf16[512,512]{1,0:T(8,128)(2,1)} %get-tuple-element.196), channel_id=1, source_target_pairs={{0,16},{8,24},{16,0},{24,8},{1,17},{9,25},{17,1},{25,9},{2,18},{10... | collective-permute-start | bytes 1572872 | tf_op jit(solution)/shard_map/ppermute | solution.py:893
  326.9 21.4 %collective-permute-start.31 = (bf16[512,512]{1,0:T(8,128)(2,1)}, bf16[512,512]{1,0:T(8,128)(2,1)S(1)}, u32[]{:S(2)}, u32[]{:S(2)}) collective-permute-start(bf16[512,512]{1,0:T(8,128)(2,1)} %get-tuple-element.197), channel_id=1, source_target_pairs={{0,24},{8,16},{16,8},{24,0},{1,25},{9,17},{17,9},{25,1},{2,26},{10... | collective-permute-start | bytes 1572872 | tf_op jit(solution)/shard_map/ppermute | solution.py:893
  339.1 16.0 %copy-start.28 = (bf16[512,512]{1,0:T(8,128)(2,1)}, bf16[512,512]{1,0:T(8,128)(2,1)S(1)}, u32[]{:S(2)}) copy-start(bf16[512,512]{1,0:T(8,128)(2,1)S(1)} %collective-permute-done.29.g1_ref) | copy-start | bytes 1572868
  348.0 7.0 %copy-start.29 = (bf16[512,512]{1,0:T(8,128)(2,1)}, bf16[512,512]{1,0:T(8,128)(2,1)S(1)}, u32[]{:S(2)}) copy-start(bf16[512,512]{1,0:T(8,128)(2,1)S(1)} %collective-permute-done.30.g2_ref) | copy-start | bytes 1572868
  348.3 6.8 %copy-start.30 = (bf16[512,512]{1,0:T(8,128)(2,1)}, bf16[512,512]{1,0:T(8,128)(2,1)S(1)}, u32[]{:S(2)}) copy-start(bf16[512,512]{1,0:T(8,128)(2,1)S(1)} %collective-permute-done.31.g3_ref) | copy-start | bytes 1572868
  348.3 22.9 %collective-permute-start.35 = (bf16[128,3456]{1,0:T(8,128)(2,1)}, bf16[128,3456]{1,0:T(8,128)(2,1)}, u32[]{:S(2)}, u32[]{:S(2)}) collective-permute-start(bf16[128,3456]{1,0:T(8,128)(2,1)} %reduce-scatter.3.cloned.1.call-done.p0_ref), channel_id=1, source_target_pairs={{0,8},{8,0},{16,24},{24,16},{1,9},{9,1},{17,25},{25,17},{2,10},{10... | collective-permute-start | bytes 2654216 | tf_op jit(solution)/shard_map/ppermute | solution.py:893
  349.7 41.9 %collective-permute-start.36 = (bf16[128,3456]{1,0:T(8,128)(2,1)}, bf16[128,3456]{1,0:T(8,128)(2,1)}, u32[]{:S(2)}, u32[]{:S(2)}) collective-permute-start(bf16[128,3456]{1,0:T(8,128)(2,1)} %reduce-scatter.3.cloned.1.call-done.p0_ref), channel_id=1, source_target_pairs={{0,16},{8,24},{16,0},{24,8},{1,17},{9,25},{17,1},{25,9},{2,18},{10... | collective-permute-start | bytes 2654216 | tf_op jit(solution)/shard_map/ppermute | solution.py:893
  350.3 41.2 %collective-permute-start.37 = (bf16[128,3456]{1,0:T(8,128)(2,1)}, bf16[128,3456]{1,0:T(8,128)(2,1)}, u32[]{:S(2)}, u32[]{:S(2)}) collective-permute-start(bf16[128,3456]{1,0:T(8,128)(2,1)} %reduce-scatter.3.cloned.1.call-done.p0_ref), channel_id=1, source_target_pairs={{0,24},{8,16},{16,8},{24,0},{1,25},{9,17},{17,9},{25,1},{2,26},{10... | collective-permute-start | bytes 2654216 | tf_op jit(solution)/shard_map/ppermute | solution.py:893
  355.1 52.1 %copy-start.1 = (bf16[576,1024]{1,0:T(8,128)(2,1)S(1)}, bf16[576,1024]{1,0:T(8,128)(2,1)}, u32[]{:S(2)}) copy-start(bf16[576,1024]{1,0:T(8,128)(2,1)} %param.28) | copy-start | bytes 3538948
  362.4 37.2 %copy-start.37 = (bf16[128]{0:T(256)(128)(2,1)S(1)}, bf16[128]{0:T(256)(128)(2,1)}, u32[]{:S(2)}) copy-start(bf16[128]{0:T(256)(128)(2,1)} %param.25) | copy-start | bytes 772
  362.4 44.2 %copy-start.38 = (bf16[128]{0:T(256)(128)(2,1)S(1)}, bf16[128]{0:T(256)(128)(2,1)}, u32[]{:S(2)}) copy-start(bf16[128]{0:T(256)(128)(2,1)} %param.18) | copy-start | bytes 772
  362.5 37.7 %collective-permute-start.32 = (bf16[128,896]{1,0:T(8,128)(2,1)}, bf16[128,896]{1,0:T(8,128)(2,1)S(1)}, u32[]{:S(2)}, u32[]{:S(2)}) collective-permute-start(bf16[128,896]{1,0:T(8,128)(2,1)} %reduce-scatter.5.cloned.1.call-done.p0_ref), channel_id=1, source_target_pairs={{0,8},{8,0},{16,24},{24,16},{1,9},{9,1},{17,25},{25,17},{2,10},{10... | collective-permute-start | bytes 688136 | tf_op jit(solution)/shard_map/ppermute | solution.py:893
  363.9 36.3 %collective-permute-start.33 = (bf16[128,896]{1,0:T(8,128)(2,1)}, bf16[128,896]{1,0:T(8,128)(2,1)S(1)}, u32[]{:S(2)}, u32[]{:S(2)}) collective-permute-start(bf16[128,896]{1,0:T(8,128)(2,1)} %reduce-scatter.5.cloned.1.call-done.p0_ref), channel_id=1, source_target_pairs={{0,16},{8,24},{16,0},{24,8},{1,17},{9,25},{17,1},{25,9},{2,18},{10... | collective-permute-start | bytes 688136 | tf_op jit(solution)/shard_map/ppermute | solution.py:893
  371.2 29.0 %collective-permute-start.34 = (bf16[128,896]{1,0:T(8,128)(2,1)}, bf16[128,896]{1,0:T(8,128)(2,1)S(1)}, u32[]{:S(2)}, u32[]{:S(2)}) collective-permute-start(bf16[128,896]{1,0:T(8,128)(2,1)} %reduce-scatter.5.cloned.1.call-done.p0_ref), channel_id=1, source_target_pairs={{0,24},{8,16},{16,8},{24,0},{1,25},{9,17},{17,9},{25,1},{2,26},{10... | collective-permute-start | bytes 688136 | tf_op jit(solution)/shard_map/ppermute | solution.py:893
  (19 other events, 29.6 us)
Sparse Core Ops, SparseCore 0:
  10.2 26.1 all-gather.3
  38.6 90.2 all-gather.5
  130.5 45.5 all-gather.7
  239.8 84.0 reduce-scatter.2
  326.6 35.3 reduce-scatter.4

commit v5 on v4

--- a/solution.py
+++ b/solution.py
@@ -144,7 +144,12 @@
     )(me, w_gate, w_up, w_down, w_out)
 
 
-def join_kernel(shards, me_ref, p0_ref, p1_ref, p2_ref, p3_ref, gate_ref, up_ref, dgate_ref, dup_ref, ddown_ref, dot_ref, st_ref):
+def divided_row(column, gain_ref):
+    across = jnp.transpose(jnp.broadcast_to(column, (column.shape[0], LANES)))
+    return across[0:1, :] / gain_ref[...].astype(F32)
+
+
+def join_kernel(shards, me_ref, p0_ref, p1_ref, p2_ref, p3_ref, gate_ref, up_ref, gain_ref, dgate_ref, dup_ref, ddown_ref, dot_ref, st_ref):
     for d, ref in enumerate((p0_ref, p1_ref, p2_ref, p3_ref)):
         st_ref[d] = ref[...]
     units = p0_ref.shape[1] // 3
@@ -157,32 +162,32 @@
         joined = jnp.concatenate(parts, axis=1)
         out_ref[...] = joined
         total = total + jnp.sum(joined * w_ref[...].astype(F32), axis=1, keepdims=True)
-    dot_ref[...] = total
+    dot_ref[...] = divided_row(total, gain_ref)
     for q, quarter in enumerate(quarters):
         block = unpack_rows(quarter[:, 2 * units:].astype(F32), ddown_ref.shape[1])
         ddown_ref[q * piece:(q + 1) * piece, :] = block
 
 
-def join_weights(me, parts, w_gate, w_up, down_shape, shards):
+def join_weights(me, parts, w_gate, w_up, gain, down_shape, shards):
     depth, whole = w_gate.shape
     return pl.pallas_call(
         functools.partial(join_kernel, shards),
         out_shape=(jax.ShapeDtypeStruct((depth, whole), F32),) * 2
-        + (jax.ShapeDtypeStruct(down_shape, F32), jax.ShapeDtypeStruct((depth, 1), F32)),
-        in_specs=[smem()] + [vmem()] * 6,
+        + (jax.ShapeDtypeStruct(down_shape, F32), jax.ShapeDtypeStruct((1, depth), F32)),
+        in_specs=[smem()] + [vmem()] * 7,
         out_specs=(vmem(),) * 4,
         scratch_shapes=[pltpu.VMEM((4,) + parts[0].shape, BF16)],
         compiler_params=params(),
         cost_estimate=COST,
         name="join_weights",
-    )(me, *parts, w_gate, w_up)
-
-
-def join_last_kernel(me_ref, p0_ref, p1_ref, p2_ref, p3_ref, q_ref, k_ref, v_ref,
-                     dq_ref, dk_ref, dv_ref, do_ref, dot_ref, gain_ref):
+    )(me, *parts, w_gate, w_up, gain[None])
+
+
+def join_last_kernel(me_ref, p0_ref, p1_ref, p2_ref, p3_ref, q_ref, k_ref, v_ref, gain_ref,
+                     dq_ref, dk_ref, dv_ref, do_ref, dot_ref, qgain_ref, kgain_ref):
     at = 0
     parts = (p0_ref, p1_ref, p2_ref, p3_ref)
-    total = jnp.zeros(dot_ref.shape, F32)
+    total = jnp.zeros((dq_ref.shape[0], 1), F32)
     for out_ref, w_ref in ((dq_ref, q_ref), (dk_ref, k_ref), (dv_ref, v_ref), (do_ref, None)):
         size = out_ref.shape[1] // 4
         for d, ref in enumerate(parts):
@@ -192,28 +197,31 @@
             if w_ref is not None:
                 total = total + jnp.sum(part * w_ref[:, there].astype(F32), axis=1, keepdims=True)
         at += size
-    dot_ref[...] = total
-    gains = jnp.zeros(gain_ref.shape, F32)
+    dot_ref[...] = divided_row(total, gain_ref)
+    gains = jnp.zeros((8, LANES), F32)
     for ref in parts:
         gains = gains + ref[0:16, at:].astype(F32)[:8]
-    gain_ref[...] = gains
-
-
-def join_last(me, parts, w_query, w_key, w_value, out_width):
+    head_dim = qgain_ref.shape[1]
+    gains = gains[:, :head_dim] + gains[:, head_dim:]
+    qgain_ref[...] = gains[0:1]
+    kgain_ref[...] = gains[1:2]
+
+
+def join_last(me, parts, w_query, w_key, w_value, gain, out_width, head_dim):
     depth = w_query.shape[0]
     out = lambda c: jax.ShapeDtypeStruct((depth, c), F32)
     return pl.pallas_call(
         join_last_kernel,
         out_shape=(
-            out(w_query.shape[1]), out(w_key.shape[1]), out(w_value.shape[1]), out(out_width), out(1),
-            jax.ShapeDtypeStruct((8, LANES), F32),
-        ),
-        in_specs=[smem()] + [vmem()] * 7,
-        out_specs=(vmem(),) * 6,
+            out(w_query.shape[1]), out(w_key.shape[1]), out(w_value.shape[1]), out(out_width),
+            jax.ShapeDtypeStruct((1, depth), F32),
+        ) + (jax.ShapeDtypeStruct((1, head_dim), F32),) * 2,
+        in_specs=[smem()] + [vmem()] * 8,
+        out_specs=(vmem(),) * 7,
         compiler_params=params(),
         cost_estimate=COST,
         name="join_last",
-    )(me, *parts, w_query, w_key, w_value)
+    )(me, *parts, w_query, w_key, w_value, gain[None])
 
 
 def table_kernel(half, me_ref, lens_ref, order_ref, freq_ref, cos_ref, up_ref, down_ref, ocol_ref, orow_ref):
@@ -532,31 +540,31 @@
     lax.fori_loop(0, all_rows // tok, key_block, 0)
 
 
-def rows_back_kernel(period, orow_ref, draw_ref, normed_ref, o0_ref, o1_ref, o2_ref, o3_ref, gain_ref, *refs):
-    d_refs, out_ref, grad_ref = refs[-6:-2], refs[-2], refs[-1]
+def rows_back_kernel(orow_ref, draw_ref, *refs):
+    grad_ref, d_refs = refs[-5], refs[-4:]
     i = pl.program_id(0)
-    all_rows, width = draw_ref.shape
-    rows = all_rows // 4
+    all_rows = draw_ref.shape[0]
+    rows = grad_ref.shape[0]
+    pick = (orow_ref[...] == i * rows + row_iota(rows, all_rows)).astype(F32).astype(BF16)
+    grads = dot_nn(pick, draw_ref[...]).astype(BF16)
+    grad_ref[...] = grads
     for d, ref in enumerate(d_refs):
 
         @pl.when(i == d)
-        def _(d=d, ref=ref):
-            pick = (orow_ref[...] == d * rows + row_iota(rows, all_rows)).astype(F32).astype(BF16)
-            grads = dot_nn(pick, draw_ref[...]).astype(BF16)
-            grad_ref[d * rows:(d + 1) * rows, :] = grads
+        def _(ref=ref):
             ref[...] = grads
 
-    @pl.when(i >= 4)
-    def _():
-        extra = o0_ref.shape[1]
-        out_ref[:, :width] = dot_tn(normed_ref[...], grad_ref[...]).astype(BF16)
-        total = o0_ref[...].astype(F32)
-        for ref in (o1_ref, o2_ref, o3_ref):
-            total = total + ref[...].astype(F32)
-        out_ref[:, width:width + extra] = total.astype(BF16)
-        place = row_iota(out_ref.shape[0], LANES) % period
-        gains = jnp.where(place == 0, gain_ref[0:1, :], jnp.where(place == 1, gain_ref[1:2, :], 0.0))
-        out_ref[:, width + extra:] = gains.astype(BF16)
+
+def last_kernel(period, normed_ref, grads_ref, o0_ref, o1_ref, o2_ref, o3_ref, gain_ref, out_ref):
+    width, extra = grads_ref.shape[1], o0_ref.shape[1]
+    out_ref[:, :width] = dot_tn(normed_ref[...], grads_ref[...]).astype(BF16)
+    total = o0_ref[...].astype(F32)
+    for ref in (o1_ref, o2_ref, o3_ref):
+        total = total + ref[...].astype(F32)
+    out_ref[:, width:width + extra] = total.astype(BF16)
+    place = row_iota(out_ref.shape[0], LANES) % period
+    gains = jnp.where(place == 0, gain_ref[0:1, :], jnp.where(place == 1, gain_ref[1:2, :], 0.0))
+    out_ref[:, width + extra:] = gains.astype(BF16)
 
 
 def norm_back(pair, raw, gain, cosine, su, sd, ones, head_dim):
@@ -597,24 +605,38 @@
     )(lens, ocol, *lses, *dealts, *grads, qg, kg, *late)
 
 
-def rows_back(orow, draw, normed, parts, gains, shards, after):
+def rows_back(orow, draw, after):
     all_rows, width = draw.shape
+    tok = all_rows // 4
+    return pl.pallas_call(
+        rows_back_kernel,
+        grid=(4,),
+        out_shape=(jax.ShapeDtypeStruct((all_rows, width), BF16),) + (jax.ShapeDtypeStruct((tok, width), BF16),) * 4,
+        in_specs=[fixed(orow), fixed(draw)] + anywhere(after),
+        out_specs=(pl.BlockSpec((tok, width), lambda i: (i, 0)),)
+        + (pl.BlockSpec((tok, width), lambda i: (0, 0)),) * 4,
+        compiler_params=params(),
+        cost_estimate=COST,
+        name="rows_back",
+    )(orow, draw, *after)
+
+
+def last_weights(normed, grads, parts, gains, shards):
+    all_rows, width = grads.shape
     depth, extra = normed.shape[1], parts[0].shape[1]
-    tok = all_rows // 4
-    late = lambda c: pl.BlockSpec((depth // 4, c), lambda i: (jnp.maximum(i - 4, 0), 0))
     wide = width + extra + LANES
-    return pl.pallas_call(
-        functools.partial(rows_back_kernel, depth // shards),
-        grid=(8,),
-        out_shape=(jax.ShapeDtypeStruct((tok, width), BF16),) * 4 + (jax.ShapeDtypeStruct((depth, wide), BF16),),
-        in_specs=[fixed(orow), fixed(draw), pl.BlockSpec((all_rows, depth // 4), lambda i: (0, jnp.maximum(i - 4, 0)))]
-        + [late(extra)] * 4 + [fixed(gains)] + anywhere(after),
-        out_specs=(pl.BlockSpec((tok, width), lambda i: (0, 0)),) * 4 + (late(wide),),
-        scratch_shapes=[pltpu.VMEM((all_rows, width), BF16)],
-        compiler_params=params(),
-        cost_estimate=COST,
-        name="rows_back",
-    )(orow, draw, normed, *parts, gains, *after)
+    block = lambda c: pl.BlockSpec((depth // 4, c), lambda i: (i, 0))
+    return pl.pallas_call(
+        functools.partial(last_kernel, depth // shards),
+        grid=(4,),
+        out_shape=jax.ShapeDtypeStruct((depth, wide), BF16),
+        in_specs=[pl.BlockSpec((all_rows, depth // 4), lambda i: (0, i)), fixed(grads)]
+        + [block(extra)] * 4 + [fixed(gains)],
+        out_specs=block(wide),
+        compiler_params=params(),
+        cost_estimate=COST,
+        name="last_weights",
+    )(normed, grads, *parts, gains)
 
 
 def tokens_kernel(me_ref, g0_ref, g1_ref, g2_ref, g3_ref, w_ref, x_ref, mid_ref, gain_ref, *refs):
@@ -778,14 +800,26 @@
     )(*operands)
 
 
-def weights_kernel(shards, nf_ref, dgu_ref, hid_ref, cot_ref, out_ref, down_ref):
+DOWN_STEPS = 3
+
+
+def weights_kernel(shards, nf_ref, dgu_from, hid_ref, cot_ref, out_ref, down_ref, dgu_ref, sem):
     i = pl.program_id(0)
+    copy = pltpu.make_async_copy(dgu_from, dgu_ref, sem)
 
     @pl.when(i == 0)
     def _():
-        down_ref[...] = dot_tn(hid_ref[...], cot_ref[...])
-
-    @pl.when(i > 0)
+        copy.start()
+
+    @pl.when(i < DOWN_STEPS)
+    def _():
+        down_ref[at_rows(i, hid_ref.shape[1]), :] = dot_tn(hid_ref[...], cot_ref[...])
+
+    @pl.when(i == DOWN_STEPS)
+    def _():
+        copy.wait()
+
+    @pl.when(i >= DOWN_STEPS)
     def _():
         out_ref[:, :dgu_ref.shape[1]] = dot_tn(nf_ref[...], dgu_ref[...]).astype(BF16)
 
@@ -793,7 +827,7 @@
     rows = out_ref.shape[0] // per
     for k in range(shards):
 
-        @pl.when(i == 1 + k // per)
+        @pl.when(i == DOWN_STEPS + k // per)
         def _(k=k):
             block = pack_rows(down_ref[k * piece:(k + 1) * piece, :], rows)
             at = k % per * rows
@@ -802,15 +836,21 @@
 
 def weights_back(nf, d_gu, hidden, cot, shards):
     rows, depth = nf.shape
-    late = lambda i: jnp.maximum(i - 1, 0)
-    wide = d_gu.shape[1] + hidden.shape[1]
+    late = lambda i: jnp.maximum(i - DOWN_STEPS, 0)
+    units = hidden.shape[1]
+    wide = d_gu.shape[1] + units
     return pl.pallas_call(
         functools.partial(weights_kernel, shards),
-        grid=(5,),
+        grid=(DOWN_STEPS + 4,),
         out_shape=jax.ShapeDtypeStruct((depth, wide), BF16),
-        in_specs=[pl.BlockSpec((rows, depth // 4), lambda i: (0, late(i))), fixed(d_gu), fixed(hidden), fixed(cot)],
+        in_specs=[
+            pl.BlockSpec((rows, depth // 4), lambda i: (0, late(i))), pl.BlockSpec(memory_space=pl.ANY),
+            pl.BlockSpec((rows, units // DOWN_STEPS), lambda i: (0, jnp.minimum(i, DOWN_STEPS - 1))), fixed(cot),
+        ],
         out_specs=pl.BlockSpec((depth // 4, wide), lambda i: (late(i), 0)),
-        scratch_shapes=[pltpu.VMEM((hidden.shape[1], cot.shape[1]), F32)],
+        scratch_shapes=[
+            pltpu.VMEM((units, cot.shape[1]), F32), pltpu.VMEM(d_gu.shape, BF16), pltpu.SemaphoreType.DMA,
+        ],
         compiler_params=params(),
         cost_estimate=COST,
         name="weights_back",
@@ -819,8 +859,11 @@
 
 def middle_kernel(*refs):
     me_ref, dn_refs = refs[0], refs[1:4]
-    cot_ref, mid_ref, gain_ref, wo_ref = refs[4:8]
-    dmid_ref, branch_ref, da_refs = refs[-6], refs[-5], refs[-4:]
+    cot_ref, mid_ref, gain_ref, wide_ref = refs[4:8]
+    dmid_ref, branch_ref, da_refs, wo_ref, sem = refs[-8], refs[-7], refs[-6:-2], refs[-2], refs[-1]
+    at = wide_ref.shape[1] // 4 * 3
+    copy = pltpu.make_async_copy(wide_ref.at[:, at:at + wo_ref.shape[1]], wo_ref, sem)
+    copy.start()
     me = me_ref[0]
     tok = mid_ref.shape[0]
 
@@ -839,6 +882,7 @@
         return carry
 
     lax.fori_loop(0, tok // ROWS, rows_of, 0)
+    copy.wait()
     span = 2 * LANES
     for d in range(4):
         there = pl.ds(pl.multiple_of(jnp.bitwise_xor(me, d) * span, span), span)
@@ -874,15 +918,15 @@
 
 def middle_back(me, parts, cot, middle, gain, wide, after):
     tok, width = middle.shape
-    wo = pl.BlockSpec((wide.shape[0], wide.shape[1] // 4), lambda i: (0, 3))
     whole = lambda r, c: pl.BlockSpec((r, c), lambda i: (0, 0))
     out = lambda r, c, t=BF16: jax.ShapeDtypeStruct((r, c), t)
     return pl.pallas_call(
         middle_kernel,
         grid=(1,),
         out_shape=(out(tok, width, F32), out(tok, width)) + (out(tok, 2 * LANES),) * 4,
-        in_specs=[smem()] + [whole(tok, width)] * 5 + [whole(1, width), wo] + anywhere(after),
+        in_specs=[smem()] + [whole(tok, width)] * 5 + [whole(1, width)] + anywhere((wide,) + tuple(after)),
         out_specs=(whole(tok, width),) * 2 + (whole(tok, 2 * LANES),) * 4,
+        scratch_shapes=[pltpu.VMEM((wide.shape[0], width), BF16), pltpu.SemaphoreType.DMA],
         compiler_params=params(),
         cost_estimate=COST,
         name="middle_back",
@@ -978,26 +1022,25 @@
     bo1, bo2, *p_wo = after([bo1, bo2] + list(p_wo), d_att)
     bo = [bo0, swap(bo1, 1), swap(bo2, 2)]
     p_wo = [p_wo[0]] + [swap(p_wo[d], d) for d in (1, 2, 3)]
-    *d_raw, p_last = rows_back(orow, draw, normed, p_wo, head_gains, shards, bo[1:3])
+    grads, *d_raw = rows_back(orow, draw, bo[1:3])
+    d_raw = [d_raw[0]] + [swap(d_raw[d], d) for d in (1, 2, 3)]
+    p_last = last_weights(normed, grads, p_wo, head_gains, shards)
     block_out = (middle + sum(b.astype(F32) for b in after(bo, p_last))).astype(BF16)
-    d_raw = [d_raw[0]] + [swap(d_raw[d], d) for d in (1, 2, 3)]
-    d_last = scatter(after(p_last, d_ffn))
+    d_last = scatter(after(p_last, d_ffn, d_raw))
     d_tokens = tokens_back(me_arr, d_raw, w_all, tokens[0], d_middle, gain_a, (p_last,))
     d_ffn = after(d_ffn, d_raw, p_last)
 
     def parts_of(part):
         return [part] + [swap(part, d) for d in (1, 2, 3)]
 
-    d_wg, d_wu, d_wd, ffn_dots = join_weights(me_arr, parts_of(d_ffn), w_gate, w_up, w_down.shape, shards)
-    d_wq, d_wk, d_wv, d_wo, attn_dots, head_gains = join_last(
-        me_arr, parts_of(after(d_last, d_ffn, d_tokens, block_out)), w_query, w_key, w_value, w_out.shape[1]
+    d_wg, d_wu, d_wd, d_ffn_gain = join_weights(me_arr, parts_of(d_ffn), w_gate, w_up, ffn_gain, w_down.shape, shards)
+    d_wq, d_wk, d_wv, d_wo, d_attn_gain, d_query_gain, d_key_gain = join_last(
+        me_arr, parts_of(after(d_last, d_ffn, d_tokens, block_out)), w_query, w_key, w_value, attn_gain,
+        w_out.shape[1], head_dim,
     )
-    d_attn_gain = attn_dots[:, 0] / attn_gain.astype(F32)
-    d_ffn_gain = ffn_dots[:, 0] / ffn_gain.astype(F32)
-    head_gains = head_gains[0:2, :head_dim] + head_gains[0:2, head_dim:]
     return (
-        block_out[None], d_tokens[None], d_attn_gain, d_wq, d_wk, d_wv, head_gains[0], head_gains[1],
-        d_wo, d_ffn_gain, d_wg, d_wu, d_wd,
+        block_out[None], d_tokens[None], d_attn_gain[0], d_wq, d_wk, d_wv, d_query_gain[0], d_key_gain[0],
+        d_wo, d_ffn_gain[0], d_wg, d_wu, d_wd,
     )
 
 

time: 420 us -> 402 us (0.957)
  waiting for transfers between devices: 107 us -> 93.2 us
    ppermute x38, waiting for transfers between devices: 102 us -> 66.5 us  [swap(): return lax.ppermute(array, 'seq', [(s, s ^ distance) for s in range(4)])]
    reduce_scatter x2, waiting for transfers between devices: 4.95 us -> 26.6 us  [body(): lax.psum_scatter(a, 'shard', scatter_dimension=0, tiled=True)]
    pallas_call x2 -> x3, Pallas kernels: 37.7 us -> 37.2 us  [the longest x1 21.5 us: weights_back(): pl.pallas_call(functools.partial(weights_kernel, shards), grid=(DOWN_STEP...]
  transfers between devices with their start and end apart: 43 -> 43, of which waited for: 17 -> 12; matrix products, arithmetic and copies ran while one was open for 3% -> 3% of each run, Pallas kernels for 53% -> 56%
where the time goes in v5:
time: 402 us; the launch traced here: 396 us
  Pallas kernels  226 us (56%)
  waiting for transfers between devices  93.2 us (23%)
  starting transfers between devices  43.1 us (11%)
  between operations  14.7 us (4%)
  local copies, waits for them, and re-layouts  14.6 us (4%)
  other arithmetic  5.14 us (1%)
    ppermute x38, waiting for transfers between devices, swap(): return lax.ppermute(array, 'seq', [(s, s ^ distance) for s in range(4)])  66.5 us
    pallas_call x3, Pallas kernels, ffn(): pl.pallas_call(functools.partial(ffn_kernel, per, shards, blocks, len(car...  66.2 us
    ppermute x38, starting transfers between devices, swap(): return lax.ppermute(array, 'seq', [(s, s ^ distance) for s in range(4)])  42.4 us
    pallas_call x1, Pallas kernels, attend_back(): pl.pallas_call(functools.partial(attend_back_kernel, head_dim, len(late))...  37.6 us
    pallas_call x2, Pallas kernels, attend(): pl.pallas_call(functools.partial(attend_kernel, head_dim, group, all_rows...  27.6 us
    reduce_scatter x2, waiting for transfers between devices, body(): lax.psum_scatter(a, 'shard', scatter_dimension=0, tiled=True)  26.6 us
    pallas_call x1, Pallas kernels, weights_back(): pl.pallas_call(functools.partial(weights_kernel, shards), grid=(DOWN_STEP...  21.5 us
    pallas_call x1, Pallas kernels, qkv(): pl.pallas_call(functools.partial(qkv_kernel, head_dim), grid=(8,), out_sh...  16.9 us
  transfers between devices with their start and end apart: 43, of which 12 were waited for; matrix products, arithmetic and copies ran while one was open for 3% of the time, Pallas kernels for 56%

profile of v5, /device:TPU:0, one launch (start us, length us, event | category | flops | bytes accessed | tf_op | source)
XLA Modules:
  0.0 396.3 jit_solution(12440123289852717665)
XLA Ops:
  7.2 1.9 first_weights.1
  9.2 3.0 collective-permute-start
  12.2 1.5 collective-permute-start.1
  16.9 5.5 %make_tables.1 = (f32[2048,128]{1,0:T(8,128)}, f32[2048,128]{1,0:T(8,128)}, f32[2048,128]{1,0:T(8,128)}, s32[2048,128]{1,0:T(8,128)}, s32[1,2048]{1,0:T(1,128)}) custom-call(s32[1]{0:T(128)} %bitcast.me_ref.refs_0_, s32[1,3]{1,0:T(1,128)} %refs_0_.1, s32[1,2048]{1,0:T(1,128)} %order_ref.1, f32[1,128]{1,0:T(1,128)} %broadcast_in_dim_tile.9.freq_ref), custom_call_target="tpu_custom_call" | custom-call | flops 1048576 | bytes 65536 | tf_op jit(solution)/shard_map/make_tables/pallas_call | solution.py:260
  23.1 4.7 %cut_weights.1 = bf16[128,4608]{1,0:T(8,128)(2,1)} custom-call(s32[1]{0:T(128)} %bitcast.me_ref.refs_0_, bf16[128,4608]{1,0:T(8,128)(2,1)} %gate_ref.3, bf16[128,4608]{1,0:T(8,128)(2,1)} %up_ref.3, bf16[144,1024]{1,0:T(8,128)(2,1)} %constant_dynamic-slice_fusion.down_ref, bf16[128,1024]{1,0:T(8,128)(2,1)} %wo_ref.1), custom_call_target="tpu_custom_call" | custom-call | flops 1048576 | bytes 65536 | tf_op jit(solution)/shard_map/cut_weights/pallas_call | solution.py:136
  27.8 7.8 %collective-permute-done.x1_ref.refs_11_ = bf16[512,1024]{1,0:T(8,128)(2,1)S(1)} collective-permute-done((bf16[512,1024]{1,0:T(8,128)(2,1)}, bf16[512,1024]{1,0:T(8,128)(2,1)S(1)}, u32[]{:S(2)}, u32[]{:S(2)}) %collective-permute-start) | collective-permute-done | bytes 1048608 | tf_op jit(solution)/shard_map/ppermute | solution.py:937
  35.6 1.5 collective-permute-done.1.x2_ref.refs_12_
  37.2 1.6 collective-permute-start.2
  39.4 10.3 %collective-permute-done.2.x3a_ref.refs_9_ = bf16[512,512]{1,0:T(8,128)(2,1)S(1)} collective-permute-done((bf16[512,512]{1,0:T(8,128)(2,1)S(1)}, bf16[512,512]{1,0:T(8,128)(2,1)S(1)}, u32[]{:S(2)}, u32[]{:S(2)}) %collective-permute-start.2) | collective-permute-done | bytes 524320 | tf_op jit(solution)/shard_map/ppermute | solution.py:937
  49.7 1.3 collective-permute-done.3.x3b_ref.refs_10_
  51.1 1.9 pad_maximum_fusion
  53.6 0.8 collective-permute-start.10
  55.0 16.9 %qkv.1 = (bf16[2048,1024]{1,0:T(8,128)(2,1)}, bf16[4,2048,128]{2,1,0:T(8,128)(2,1)}, bf16[2048,128]{1,0:T(8,128)(2,1)}, bf16[2048,128]{1,0:T(8,128)(2,1)}, bf16[...) custom-call(bf16[512,1024]{1,0:T(8,128)(2,1)} %bitcast.13, ...), custom_call_target="tpu_custom_call" | custom-call | flops 1048576 | bytes 65536 | tf_op jit(solution)/shard_map/qkv/pallas_call | solution.py:333
  71.9 13.7 %attend.3 = (bf16[2048,128]{1,0:T(8,128)(2,1)}, bf16[2048,128]{1,0:T(8,128)(2,1)}, f32[2,2048]{1,0:T(2,128)}) custom-call(s32[1,3]{1,0:T(1,128)} %refs_0_.1, s32[1,2048]{1,0:T(1,128)} %get-tuple-element.119.orow_ref, bf16[4,2048,128]{2,1,0:T(8,128)(2,1)} %get-tuple-element.128.qx_ref.refs_12_, bf16[2048,128]{1,0:T(8,128)(2,1)} %get-tuple-element.129.k_ref.refs_13_, ...), custom_call_target="tpu_custom_call" | custom-call | flops 1048576 | bytes 65536 | tf_op jit(solution)/shard_map/attend/pallas_call | solution.py:421
  85.6 1.2 collective-permute-start.5
  86.8 1.5 collective-permute-start.7
  88.3 13.9 %attend.2 = (bf16[2048,128]{1,0:T(8,128)(2,1)}, bf16[2048,128]{1,0:T(8,128)(2,1)}, f32[2,2048]{1,0:T(2,128)}) custom-call(s32[1,3]{1,0:T(1,128)} %refs_0_.1, s32[1,2048]{1,0:T(1,128)} %get-tuple-element.119.orow_ref, bf16[4,2048,128]{2,1,0:T(8,128)(2,1)} %get-tuple-element.128.qx_ref.refs_12_, bf16[2048,128]{1,0:T(8,128)(2,1)} %get-tuple-element.129.k_ref.refs_13_, ...), custom_call_target="tpu_custom_call" | custom-call | flops 1048576 | bytes 65536 | tf_op jit(solution)/shard_map/attend/pallas_call | solution.py:421
  103.6 2.1 collective-permute-start.8
  105.7 1.1 slice.29
  106.8 1.1 slice.30
  108.4 0.9 collective-permute-start.14
  109.4 7.9 %collective-permute-done.4.refs_3_.refs_2_ = bf16[2048,128]{1,0:T(8,128)(2,1)S(1)} collective-permute-done((bf16[2048,128]{1,0:T(8,128)(2,1)}, bf16[2048,128]{1,0:T(8,128)(2,1)S(1)}, u32[]{:S(2)}, u32[]{:S(2)}) %collective-permute-start.4) | collective-permute-done | bytes 524320 | tf_op jit(solution)/shard_map/ppermute | solution.py:937
  117.8 11.5 %collective-permute-done.6.refs_5_.refs_4_ = bf16[2048,128]{1,0:T(8,128)(2,1)S(1)} collective-permute-done((bf16[2048,128]{1,0:T(8,128)(2,1)}, bf16[2048,128]{1,0:T(8,128)(2,1)S(1)}, u32[]{:S(2)}, u32[]{:S(2)}) %collective-permute-start.6) | collective-permute-done | bytes 524320 | tf_op jit(solution)/shard_map/ppermute | solution.py:937
  129.2 1.3 collective-permute-start.9
  130.5 1.4 fusion
  132.0 9.4 %collective-permute-done.12.refs_8_.refs_10_ = bf16[1024,128]{1,0:T(8,128)(2,1)S(1)} collective-permute-done((bf16[1024,128]{1,0:T(8,128)(2,1)S(1)}, bf16[1024,128]{1,0:T(8,128)(2,1)S(1)}, u32[]{:S(2)}, u32[]{:S(2)}) %collective-permute-start.12) | collective-permute-done | bytes 262176 | tf_op jit(solution)/shard_map/ppermute | solution.py:937
  142.1 17.1 %ffn.3 = (bf16[2048,1024]{1,0:T(8,128)(2,1)}, bf16[2048,1152]{1,0:T(8,128)(2,1)}, bf16[2048,2304]{1,0:T(8,128)(2,1)}, bf16[2048,1024]{1,0:T(8,128)(2,1)}, bf16[5...) custom-call(s32[1]{0:T(128)} %bitcast.me_ref.refs_0_, ...), custom_call_target="tpu_custom_call" | custom-call | flops 1048576 | bytes 65536 | tf_op jit(solution)/shard_map/ffn/pallas_call | solution.py:788
  159.2 1.1 collective-permute-start.15
  160.8 1.3 collective-permute-start.17
  162.1 1.3 collective-permute-start.18
  163.3 17.3 %ffn.4 = (bf16[2048,1024]{1,0:T(8,128)(2,1)}, bf16[2048,1152]{1,0:T(8,128)(2,1)}, bf16[2048,2304]{1,0:T(8,128)(2,1)}, bf16[2048,1024]{1,0:T(8,128)(2,1)}, bf16[5...) custom-call(s32[1]{0:T(128)} %bitcast.me_ref.refs_0_, ...), custom_call_target="tpu_custom_call", output_to_operand_aliasing={{0}: (16, {}), {1}: (17, {}), {2}: (18, {}), {3}: (19, {})} | custom-call | flops 1048576 | bytes 65536 | tf_op jit(solution)/shard_map/ffn/pallas_call | solution.py:788
  182.0 31.8 %ffn.5 = (bf16[2048,1024]{1,0:T(8,128)(2,1)}, bf16[2048,1152]{1,0:T(8,128)(2,1)}, bf16[2048,2304]{1,0:T(8,128)(2,1)}, bf16[2048,1024]{1,0:T(8,128)(2,1)}, bf16[5...) custom-call(s32[1]{0:T(128)} %bitcast.me_ref.refs_0_, ...), custom_call_target="tpu_custom_call", output_to_operand_aliasing={{0}: (24, {}), {1}: (25, {}), {2}: (26, {}), {3}: (27, {})} | custom-call | flops 1048576 | bytes 65536 | tf_op jit(solution)/shard_map/ffn/pallas_call | solution.py:788
  213.8 1.1 collective-permute-start.19
  215.6 21.5 %weights_back.1.refs_8_ = bf16[1024,3456]{1,0:T(8,128)(2,1)} custom-call(bf16[2048,1024]{1,0:T(8,128)(2,1)} %get-tuple-element.158.nf_ref, bf16[2048,2304]{1,0:T(8,128)(2,1)} %get-tuple-element.159.dgu_from, bf16[2048,1152]{1,0:T(8,128)(2,1)} %get-tuple-element.160.hid_ref, bf16[2048,1024]{1,0:T(8,128)(2,1)} %get-tuple-element.161.cot_ref), custom_call_target="tpu_custom_call" | custom-call | flops 1048576 | bytes 65536 | tf_op jit(solution)/shard_map/weights_back/pallas_call | solution.py:842
  237.2 1.0 copy-done.19
  238.6 6.5 %middle_back.1 = (f32[512,1024]{1,0:T(8,128)}, bf16[512,1024]{1,0:T(8,128)(2,1)}, bf16[512,256]{1,0:T(8,128)(2,1)}, bf16[512,256]{1,0:T(8,128)(2,1)}, bf16[512,2...) custom-call(s32[1]{0:T(128)} %bitcast.me_ref.refs_0_, bf16[512,1024]{1,0:T(8,128)(2,1)} %get-tuple-element.155.refs_1_, ...), custom_call_target="tpu_custom_call" | custom-call | flops 1048576 | bytes 65536 | tf_op jit(solution)/shard_map/middle_back/pallas_call | solution.py:923
  245.1 1.1 collective-permute-start.21
  246.3 1.3 collective-permute-start.22
  247.5 1.2 collective-permute-start.23
  248.7 4.2 %out_weights.1 = (bf16[1024,256]{1,0:T(8,128)(2,1)}, bf16[1024,256]{1,0:T(8,128)(2,1)}, bf16[1024,256]{1,0:T(8,128)(2,1)}, bf16[1024,256]{1,0:T(8,128)(2,1)}) custom-call(s32[1]{0:T(128)} %bitcast.me_ref.refs_0_, bf16[2048,128]{1,0:T(8,128)(2,1)} %get-tuple-element.131.refs_1_.refs_0_, bf16[2048,128]{1,0:T(8,128)(2,1)} %get-tuple-element.132.refs_2_.refs_1_, ...), custom_call_target="tpu_custom_call" | custom-call | flops 1048576 | bytes 65536 | tf_op jit(solution)/shard_map/out_weights/pallas_call | solution.py:907
  252.9 1.3 collective-permute-done.22.refs_8_
  254.3 4.8 %collective-permute-done.23.refs_9_ = bf16[512,256]{1,0:T(8,128)(2,1)S(1)} collective-permute-done((bf16[512,256]{1,0:T(8,128)(2,1)}, bf16[512,256]{1,0:T(8,128)(2,1)S(1)}, u32[]{:S(2)}, u32[]{:S(2)}) %collective-permute-start.23) | collective-permute-done | bytes 262176 | tf_op jit(solution)/shard_map/ppermute | solution.py:937
  259.1 0.8 collective-permute-start.24
  260.5 0.8 collective-permute-start.26
  261.3 1.9 collective-permute-start.27
  263.2 0.8 collective-permute-start.28
  264.0 37.6 %attend_back.1 = (bf16[2048,512]{1,0:T(8,128)(2,1)}, f32[2,128]{1,0:T(2,128)}) custom-call(s32[1,3]{1,0:T(1,128)} %refs_0_.1, s32[2048,128]{1,0:T(8,128)} %get-tuple-element.122.ocol_ref.refs_1_, f32[2,2048]{1,0:T(2,128)} %get-tuple-element.177.refs_2_, f32[2,2048]{1,0:T(2,128)} %get-tuple-element.178.refs_3_, bf16[2048,128]{1,0:T(8,128)(2,1)} %get-tuple-element.179.refs_4_, ...), custom_call_target="tpu_custom_call" | custom-call | flops 1048576 | bytes 65536 | tf_op jit(solution)/shard_map/attend_back/pallas_call | solution.py:587
  301.7 0.9 copy-done.11
  303.0 8.3 %rows_back.1 = (bf16[2048,512]{1,0:T(8,128)(2,1)}, bf16[512,512]{1,0:T(8,128)(2,1)}, bf16[512,512]{1,0:T(8,128)(2,1)}, bf16[512,512]{1,0:T(8,128)(2,1)}, bf16[512,512]{1,0:T(8,128)(2,1)}) custom-call(s32[1,2048]{1,0:T(1,128)} %get-tuple-element.119.orow_ref, bf16[2048,512]{1,0:T(8,128)(2,1)} %get-tuple-element.185.draw_ref, bf16[512,1024]{1,0:T(8,128)(2,1)} %copy-done.11, ...), custom_call_target="tpu_custom_call" | custom-call | flops 1048576 | bytes 65536 | tf_op jit(solution)/shard_map/rows_back/pallas_call | solution.py:611
  311.3 0.8 collective-permute-start.29
  312.1 1.9 collective-permute-start.30
  314.0 0.8 collective-permute-start.31
  314.8 0.8 copy-done.26
  315.9 7.3 %last_weights.1.refs_0_ = bf16[1024,896]{1,0:T(8,128)(2,1)} custom-call(bf16[2048,1024]{1,0:T(8,128)(2,1)} %get-tuple-element.176.normed_ref, bf16[2048,512]{1,0:T(8,128)(2,1)} %get-tuple-element.186.grads_ref, bf16[1024,256]{1,0:T(8,128)(2,1)} %get-tuple-element.187.o0_ref, bf16[1024,256]{1,0:T(8,128)(2,1)} %copy-done.25, bf16[1024,256]{1,0:T(8,128)(2,1)} %copy-done.26, ...), custom_call_target="tpu_custom_call" | custom-call | flops 1048576 | bytes 65536 | tf_op jit(solution)/shard_map/last_weights/pallas_call | solution.py:629
  323.2 10.5 %collective-permute-done.31.g3_ref = bf16[512,512]{1,0:T(8,128)(2,1)} collective-permute-done((bf16[512,512]{1,0:T(8,128)(2,1)}, bf16[512,512]{1,0:T(8,128)(2,1)}, u32[]{:S(2)}, u32[]{:S(2)}) %collective-permute-start.31) | collective-permute-done | bytes 524320 | tf_op jit(solution)/shard_map/ppermute | solution.py:937
  333.7 1.1 collective-permute-start.35
  334.8 2.5 collective-permute-start.37
  337.2 3.2 add_convert_fusion
  340.5 7.4 %tokens_back.1 = bf16[512,1024]{1,0:T(8,128)(2,1)} custom-call(s32[1]{0:T(128)} %bitcast.me_ref.refs_0_, bf16[512,512]{1,0:T(8,128)(2,1)} %get-tuple-element.195.g0_ref, bf16[512,512]{1,0:T(8,128)(2,1)} %collective-permute-done.29.g1_ref, bf16[512,512]{1,0:T(8,128)(2,1)} %collective-permute-done.30.g2_ref, bf16[512,512]{1,0:T(8,128)(2,1)} %collective-permute-done.31.g3_ref, ...), custom_call_target="tpu_custom_call" | custom-call | flops 1048576 | bytes 65536 | tf_op jit(solution)/shard_map/tokens_back/pallas_call | solution.py:662
  347.8 26.6 %reduce-scatter.5.cloned.1.call-done.p0_ref = bf16[128,896]{1,0:T(8,128)(2,1)} async-done(((bf16[1024,896]{1,0:T(8,128)(2,1)}), bf16[128,896]{1,0:T(8,128)(2,1)}) %reduce-scatter.5.cloned.1.call-update) | async-done | bytes 229392 | tf_op jit(solution)/shard_map/reduce_scatter | solution.py:1011
  374.5 1.5 collective-permute-start.32
  376.0 1.6 collective-permute-start.33
  378.0 7.1 %join_weights.1 = (f32[128,4608]{1,0:T(8,128)}, f32[128,4608]{1,0:T(8,128)}, f32[576,1024]{1,0:T(8,128)}, f32[1,128]{1,0:T(1,128)}) custom-call(s32[1]{0:T(128)} %bitcast.me_ref.refs_0_, bf16[128,3456]{1,0:T(8,128)(2,1)} %reduce-scatter.3.cloned.1.call-done.p0_ref, bf16[128,3456]{1,0:T(8,128)(2,1)} %collective-permute-done.35.p1_ref, ...), custom_call_target="tpu_custom_call" | custom-call | flops 1048576 | bytes 65536 | tf_op jit(solution)/shard_map/join_weights/pallas_call | solution.py:173
  386.6 2.7 join_last.1
  (132 shorter events, 15.1 us)
Async XLA Ops:
  7.2 15.2 %copy-start = (bf16[576,1024]{1,0:T(8,128)(2,1)S(1)}, bf16[576,1024]{1,0:T(8,128)(2,1)}, u32[]{:S(2)}) copy-start(bf16[576,1024]{1,0:T(8,128)(2,1)} %param.28) | copy-start | bytes 3538948
  7.2 47.8 %all-gather.4.cloned.1.call-start = ((), (), s32[]{:S(2)}) async-start(), calls=%async_computation.2 | async-start | bytes 1474560 | tf_op jit(solution)/shard_map/all_gather | solution.py:975
  9.2 132.2 %all-gather.6.cloned.1.call-start = ((), (), s32[]{:S(2)}) async-start(), calls=%async_computation.3 | async-start | bytes 10616832 | tf_op jit(solution)/shard_map/all_gather | solution.py:977
  9.2 26.4 %collective-permute-start = (bf16[512,1024]{1,0:T(8,128)(2,1)}, bf16[512,1024]{1,0:T(8,128)(2,1)S(1)}, u32[]{:S(2)}, u32[]{:S(2)}) collective-permute-start(bf16[512,1024]{1,0:T(8,128)(2,1)} %bitcast.11), channel_id=1, source_target_pairs={{0,8},{8,0},{16,24},{24,16},{1,9},{9,1},{17,25},{25,17},{2,10},{10... | collective-permute-start | bytes 3145736 | tf_op jit(solution)/shard_map/ppermute | solution.py:937
  12.2 24.8 %collective-permute-start.1 = (bf16[512,1024]{1,0:T(8,128)(2,1)}, bf16[512,1024]{1,0:T(8,128)(2,1)S(1)}, u32[]{:S(2)}, u32[]{:S(2)}) collective-permute-start(bf16[512,1024]{1,0:T(8,128)(2,1)} %bitcast.12), channel_id=1, source_target_pairs={{0,16},{8,24},{16,0},{24,8},{1,17},{9,25},{17,1},{25,9},{2,18},{10... | collective-permute-start | bytes 3145736 | tf_op jit(solution)/shard_map/ppermute | solution.py:937
  27.8 23.3 %copy-start.14 = (bf16[128,1024]{1,0:T(8,128)(2,1)S(1)}, bf16[128,1024]{1,0:T(8,128)(2,1)}, u32[]{:S(2)}) copy-start(bf16[128,1024]{1,0:T(8,128)(2,1)} %q_ref.3) | copy-start | bytes 786436
  27.8 23.3 %copy-start.17 = (bf16[128,512]{1,0:T(8,128)(2,1)S(1)}, bf16[128,512]{1,0:T(8,128)(2,1)}, u32[]{:S(2)}) copy-start(bf16[128,512]{1,0:T(8,128)(2,1)} %k_ref.3) | copy-start | bytes 393220
  35.6 17.4 %copy-start.8 = (bf16[512,1024]{1,0:T(8,128)(2,1)}, bf16[512,1024]{1,0:T(8,128)(2,1)S(1)}, u32[]{:S(2)}) copy-start(bf16[512,1024]{1,0:T(8,128)(2,1)S(1)} %collective-permute-done.x1_ref.refs_11_) | copy-start | bytes 3145732
  37.1 15.9 %copy-start.9 = (bf16[512,1024]{1,0:T(8,128)(2,1)}, bf16[512,1024]{1,0:T(8,128)(2,1)S(1)}, u32[]{:S(2)}) copy-start(bf16[512,1024]{1,0:T(8,128)(2,1)S(1)} %collective-permute-done.1.x2_ref.refs_12_) | copy-start | bytes 3145732
  37.1 201.5 %all-gather.8.cloned.1.call-start = ((), (), s32[]{:S(2)}) async-start(), calls=%async_computation.4 | async-start | bytes 4718592 | tf_op jit(solution)/shard_map/all_gather | solution.py:989
  37.2 12.5 %collective-permute-start.2 = (bf16[512,512]{1,0:T(8,128)(2,1)S(1)}, bf16[512,512]{1,0:T(8,128)(2,1)S(1)}, u32[]{:S(2)}, u32[]{:S(2)}) collective-permute-start(bf16[512,512]{1,0:T(8,128)(2,1)S(1)} %slice.24), channel_id=1, source_target_pairs={{0,16},{8,24},{16,0},{24,8},{1,17},{9,25},{17,1},{25,9},{2,18},{10... | collective-permute-start | bytes 1572872 | tf_op jit(solution)/shard_map/ppermute | solution.py:937
  38.8 12.3 %collective-permute-start.3 = (bf16[512,512]{1,0:T(8,128)(2,1)S(1)}, bf16[512,512]{1,0:T(8,128)(2,1)S(1)}, u32[]{:S(2)}, u32[]{:S(2)}) collective-permute-start(bf16[512,512]{1,0:T(8,128)(2,1)S(1)} %slice.25), channel_id=1, source_target_pairs={{0,8},{8,0},{16,24},{24,16},{1,9},{9,1},{17,25},{25,17},{2,10},{10... | collective-permute-start | bytes 1572872 | tf_op jit(solution)/shard_map/ppermute | solution.py:937
  49.7 5.2 %copy-start.15 = (bf16[512,512]{1,0:T(8,128)(2,1)}, bf16[512,512]{1,0:T(8,128)(2,1)S(1)}, u32[]{:S(2)}) copy-start(bf16[512,512]{1,0:T(8,128)(2,1)S(1)} %collective-permute-done.2.x3a_ref.refs_9_) | copy-start | bytes 1572868
  51.1 3.9 copy-start.16
  53.0 280.6 %reduce-scatter.3.cloned.1.call-start = ((), (), s32[]{:S(2)}) async-start(), calls=%async_computation.5 | async-start | bytes 7962624 | tf_op jit(solution)/shard_map/reduce_scatter | solution.py:1011
  53.6 49.3 %collective-permute-start.10 = (bf16[512,1024]{1,0:T(8,128)(2,1)}, bf16[512,1024]{1,0:T(8,128)(2,1)}, u32[]{:S(2)}, u32[]{:S(2)}) collective-permute-start(bf16[512,1024]{1,0:T(8,128)(2,1)} %bitcast.4.refs_10_.refs_4_), channel_id=1, source_target_pairs={{0,8},{8,0},{16,24},{24,16},{1,9},{9,1},{17,25},{25,17},{2,10},{10... | collective-permute-start | bytes 3145736 | tf_op jit(solution)/shard_map/ppermute | solution.py:937
  54.4 49.2 %collective-permute-start.11 = (bf16[512,1024]{1,0:T(8,128)(2,1)}, bf16[512,1024]{1,0:T(8,128)(2,1)}, u32[]{:S(2)}, u32[]{:S(2)}) collective-permute-start(bf16[512,1024]{1,0:T(8,128)(2,1)} %bitcast.4.refs_10_.refs_4_), channel_id=1, source_target_pairs={{0,16},{8,24},{16,0},{24,8},{1,17},{9,25},{17,1},{25,9},{2,18},{10... | collective-permute-start | bytes 3145736 | tf_op jit(solution)/shard_map/ppermute | solution.py:937
  85.6 22.2 %collective-permute-start.5 = (bf16[2048,128]{1,0:T(8,128)(2,1)}, bf16[2048,128]{1,0:T(8,128)(2,1)S(1)}, u32[]{:S(2)}, u32[]{:S(2)}) collective-permute-start(bf16[2048,128]{1,0:T(8,128)(2,1)} %get-tuple-element.132.refs_2_.refs_1_), channel_id=1, source_target_pairs={{0,8},{8,0},{16,24},{24,16},{1,9},{9,1},{17,25},{25,17},{2,10},{10... | collective-permute-start | bytes 1572872 | tf_op jit(solution)/shard_map/ppermute | solution.py:937
  86.8 21.7 %collective-permute-start.7 = (bf16[2048,128]{1,0:T(8,128)(2,1)}, bf16[2048,128]{1,0:T(8,128)(2,1)S(1)}, u32[]{:S(2)}, u32[]{:S(2)}) collective-permute-start(bf16[2048,128]{1,0:T(8,128)(2,1)} %get-tuple-element.132.refs_2_.refs_1_), channel_id=1, source_target_pairs={{0,16},{8,24},{16,0},{24,8},{1,17},{9,25},{17,1},{25,9},{2,18},{10... | collective-permute-start | bytes 1572872 | tf_op jit(solution)/shard_map/ppermute | solution.py:937
  102.2 15.1 %collective-permute-start.4 = (bf16[2048,128]{1,0:T(8,128)(2,1)}, bf16[2048,128]{1,0:T(8,128)(2,1)S(1)}, u32[]{:S(2)}, u32[]{:S(2)}) collective-permute-start(bf16[2048,128]{1,0:T(8,128)(2,1)} %get-tuple-element.131.refs_1_.refs_0_), channel_id=1, source_target_pairs={{0,8},{8,0},{16,24},{24,16},{1,9},{9,1},{17,25},{25,17},{2,10},{10... | collective-permute-start | bytes 1572872 | tf_op jit(solution)/shard_map/ppermute | solution.py:937
  102.9 26.3 %collective-permute-start.6 = (bf16[2048,128]{1,0:T(8,128)(2,1)}, bf16[2048,128]{1,0:T(8,128)(2,1)S(1)}, u32[]{:S(2)}, u32[]{:S(2)}) collective-permute-start(bf16[2048,128]{1,0:T(8,128)(2,1)} %get-tuple-element.131.refs_1_.refs_0_), channel_id=1, source_target_pairs={{0,16},{8,24},{16,0},{24,8},{1,17},{9,25},{17,1},{25,9},{2,18},{10... | collective-permute-start | bytes 1572872 | tf_op jit(solution)/shard_map/ppermute | solution.py:937
  103.6 28.4 %collective-permute-start.8 = (bf16[2048,128]{1,0:T(8,128)(2,1)}, bf16[2048,128]{1,0:T(8,128)(2,1)S(1)}, u32[]{:S(2)}, u32[]{:S(2)}) collective-permute-start(bf16[2048,128]{1,0:T(8,128)(2,1)} %get-tuple-element.131.refs_1_.refs_0_), channel_id=1, source_target_pairs={{0,24},{8,16},{16,8},{24,0},{1,25},{9,17},{17,9},{25,1},{2,26},{10... | collective-permute-start | bytes 1572872 | tf_op jit(solution)/shard_map/ppermute | solution.py:937
  107.9 33.5 %copy-start.3 = (bf16[2048,128]{1,0:T(8,128)(2,1)}, bf16[2048,128]{1,0:T(8,128)(2,1)S(1)}, u32[]{:S(2)}) copy-start(bf16[2048,128]{1,0:T(8,128)(2,1)S(1)} %collective-permute-done.5.refs_4_.refs_3_) | copy-start | bytes 1572868
  107.9 33.5 %collective-permute-start.13 = (bf16[512,512]{1,0:T(8,128)(2,1)S(1)}, bf16[512,512]{1,0:T(8,128)(2,1)}, u32[]{:S(2)}, u32[]{:S(2)}) collective-permute-start(bf16[512,512]{1,0:T(8,128)(2,1)S(1)} %slice.29), channel_id=1, source_target_pairs={{0,16},{8,24},{16,0},{24,8},{1,17},{9,25},{17,1},{25,9},{2,18},{10... | collective-permute-start | bytes 1572872 | tf_op jit(solution)/shard_map/ppermute | solution.py:937
  108.4 33.0 %copy-start.4 = (bf16[2048,128]{1,0:T(8,128)(2,1)}, bf16[2048,128]{1,0:T(8,128)(2,1)S(1)}, u32[]{:S(2)}) copy-start(bf16[2048,128]{1,0:T(8,128)(2,1)S(1)} %collective-permute-done.7.refs_6_.refs_5_) | copy-start | bytes 1572868
  108.4 32.9 %collective-permute-start.14 = (bf16[512,512]{1,0:T(8,128)(2,1)S(1)}, bf16[512,512]{1,0:T(8,128)(2,1)}, u32[]{:S(2)}, u32[]{:S(2)}) collective-permute-start(bf16[512,512]{1,0:T(8,128)(2,1)S(1)} %slice.30), channel_id=1, source_target_pairs={{0,8},{8,0},{16,24},{24,16},{1,9},{9,1},{17,25},{25,17},{2,10},{10... | collective-permute-start | bytes 1572872 | tf_op jit(solution)/shard_map/ppermute | solution.py:937
  117.3 24.1 %copy-start.5 = (bf16[2048,128]{1,0:T(8,128)(2,1)}, bf16[2048,128]{1,0:T(8,128)(2,1)S(1)}, u32[]{:S(2)}) copy-start(bf16[2048,128]{1,0:T(8,128)(2,1)S(1)} %collective-permute-done.4.refs_3_.refs_2_) | copy-start | bytes 1572868
  117.3 24.1 %collective-permute-start.12 = (bf16[1024,128]{1,0:T(8,128)(2,1)S(1)}, bf16[1024,128]{1,0:T(8,128)(2,1)S(1)}, u32[]{:S(2)}, u32[]{:S(2)}) collective-permute-start(bf16[1024,128]{1,0:T(8,128)(2,1)S(1)} %slice.33), channel_id=1, source_target_pairs={{0,16},{8,24},{16,0},{24,8},{1,17},{9,25},{17,1},{25,9},{2,18},{10... | collective-permute-start | bytes 786440 | tf_op jit(solution)/shard_map/ppermute | solution.py:937
  129.2 12.2 %copy-start.6 = (bf16[2048,128]{1,0:T(8,128)(2,1)}, bf16[2048,128]{1,0:T(8,128)(2,1)S(1)}, u32[]{:S(2)}) copy-start(bf16[2048,128]{1,0:T(8,128)(2,1)S(1)} %collective-permute-done.6.refs_5_.refs_4_) | copy-start | bytes 1572868
  129.2 12.1 %collective-permute-start.9 = (bf16[1024,128]{1,0:T(8,128)(2,1)S(1)}, bf16[1024,128]{1,0:T(8,128)(2,1)S(1)}, u32[]{:S(2)}, u32[]{:S(2)}) collective-permute-start(bf16[1024,128]{1,0:T(8,128)(2,1)S(1)} %slice.32), channel_id=1, source_target_pairs={{0,8},{8,0},{16,24},{24,16},{1,9},{9,1},{17,25},{25,17},{2,10},{10... | collective-permute-start | bytes 786440 | tf_op jit(solution)/shard_map/ppermute | solution.py:937
  132.0 9.5 %copy-start.2 = (bf16[2048,128]{1,0:T(8,128)(2,1)}, bf16[2048,128]{1,0:T(8,128)(2,1)S(1)}, u32[]{:S(2)}) copy-start(bf16[2048,128]{1,0:T(8,128)(2,1)S(1)} %collective-permute-done.8.refs_7_.refs_9_.refs_6_) | copy-start | bytes 1572868
  159.2 21.4 %collective-permute-start.15 = (bf16[512,512]{1,0:T(8,128)(2,1)}, bf16[512,512]{1,0:T(8,128)(2,1)S(1)}, u32[]{:S(2)}, u32[]{:S(2)}) collective-permute-start(bf16[512,512]{1,0:T(8,128)(2,1)} %get-tuple-element.145), channel_id=1, source_target_pairs={{0,8},{8,0},{16,24},{24,16},{1,9},{9,1},{17,25},{25,17},{2,10},{10... | collective-permute-start | bytes 1572872 | tf_op jit(solution)/shard_map/ppermute | solution.py:937
  160.3 20.3 %collective-permute-start.16 = (bf16[512,512]{1,0:T(8,128)(2,1)}, bf16[512,512]{1,0:T(8,128)(2,1)S(1)}, u32[]{:S(2)}, u32[]{:S(2)}) collective-permute-start(bf16[512,512]{1,0:T(8,128)(2,1)} %get-tuple-element.146), channel_id=1, source_target_pairs={{0,16},{8,24},{16,0},{24,8},{1,17},{9,25},{17,1},{25,9},{2,18},{10... | collective-permute-start | bytes 1572872 | tf_op jit(solution)/shard_map/ppermute | solution.py:937
  160.8 19.9 %collective-permute-start.17 = (bf16[512,512]{1,0:T(8,128)(2,1)}, bf16[512,512]{1,0:T(8,128)(2,1)S(1)}, u32[]{:S(2)}, u32[]{:S(2)}) collective-permute-start(bf16[512,512]{1,0:T(8,128)(2,1)} %get-tuple-element.147), channel_id=1, source_target_pairs={{0,8},{8,0},{16,24},{24,16},{1,9},{9,1},{17,25},{25,17},{2,10},{10... | collective-permute-start | bytes 1572872 | tf_op jit(solution)/shard_map/ppermute | solution.py:937
  162.1 18.8 %collective-permute-start.18 = (bf16[512,512]{1,0:T(8,128)(2,1)}, bf16[512,512]{1,0:T(8,128)(2,1)S(1)}, u32[]{:S(2)}, u32[]{:S(2)}) collective-permute-start(bf16[512,512]{1,0:T(8,128)(2,1)} %get-tuple-element.148), channel_id=1, source_target_pairs={{0,16},{8,24},{16,0},{24,8},{1,17},{9,25},{17,1},{25,9},{2,18},{10... | collective-permute-start | bytes 1572872 | tf_op jit(solution)/shard_map/ppermute | solution.py:937
  213.8 23.3 %collective-permute-start.19 = (bf16[512,1024]{1,0:T(8,128)(2,1)}, bf16[512,1024]{1,0:T(8,128)(2,1)S(1)}, u32[]{:S(2)}, u32[]{:S(2)}) collective-permute-start(bf16[512,1024]{1,0:T(8,128)(2,1)} %get-tuple-element.156), channel_id=1, source_target_pairs={{0,8},{8,0},{16,24},{24,16},{1,9},{9,1},{17,25},{25,17},{2,10},{10... | collective-permute-start | bytes 3145736 | tf_op jit(solution)/shard_map/ppermute | solution.py:937
  214.9 22.2 %collective-permute-start.20 = (bf16[512,1024]{1,0:T(8,128)(2,1)}, bf16[512,1024]{1,0:T(8,128)(2,1)S(1)}, u32[]{:S(2)}, u32[]{:S(2)}) collective-permute-start(bf16[512,1024]{1,0:T(8,128)(2,1)} %get-tuple-element.157), channel_id=1, source_target_pairs={{0,16},{8,24},{16,0},{24,8},{1,17},{9,25},{17,1},{25,9},{2,18},{10... | collective-permute-start | bytes 3145736 | tf_op jit(solution)/shard_map/ppermute | solution.py:937
  237.2 1.4 copy-start.20
  238.6 135.9 %reduce-scatter.5.cloned.1.call-start = ((), (), s32[]{:S(2)}) async-start(), calls=%async_computation.6 | async-start | bytes 2064384 | tf_op jit(solution)/shard_map/reduce_scatter | solution.py:1011
  245.1 7.8 %collective-permute-start.21 = (bf16[512,256]{1,0:T(8,128)(2,1)}, bf16[512,256]{1,0:T(8,128)(2,1)S(1)}, u32[]{:S(2)}, u32[]{:S(2)}) collective-permute-start(bf16[512,256]{1,0:T(8,128)(2,1)} %get-tuple-element.171), channel_id=1, source_target_pairs={{0,8},{8,0},{16,24},{24,16},{1,9},{9,1},{17,25},{25,17},{2,10},{10... | collective-permute-start | bytes 786440 | tf_op jit(solution)/shard_map/ppermute | solution.py:937
  246.3 8.0 %collective-permute-start.22 = (bf16[512,256]{1,0:T(8,128)(2,1)}, bf16[512,256]{1,0:T(8,128)(2,1)S(1)}, u32[]{:S(2)}, u32[]{:S(2)}) collective-permute-start(bf16[512,256]{1,0:T(8,128)(2,1)} %get-tuple-element.172), channel_id=1, source_target_pairs={{0,16},{8,24},{16,0},{24,8},{1,17},{9,25},{17,1},{25,9},{2,18},{10... | collective-permute-start | bytes 786440 | tf_op jit(solution)/shard_map/ppermute | solution.py:937
  247.5 11.6 %collective-permute-start.23 = (bf16[512,256]{1,0:T(8,128)(2,1)}, bf16[512,256]{1,0:T(8,128)(2,1)S(1)}, u32[]{:S(2)}, u32[]{:S(2)}) collective-permute-start(bf16[512,256]{1,0:T(8,128)(2,1)} %get-tuple-element.173), channel_id=1, source_target_pairs={{0,24},{8,16},{16,8},{24,0},{1,25},{9,17},{17,9},{25,1},{2,26},{10... | collective-permute-start | bytes 786440 | tf_op jit(solution)/shard_map/ppermute | solution.py:937
  248.7 11.2 %copy-start.34 = (bf16[512,1024]{1,0:T(8,128)(2,1)S(1)}, bf16[512,1024]{1,0:T(8,128)(2,1)}, u32[]{:S(2)}) copy-start(bf16[512,1024]{1,0:T(8,128)(2,1)} %get-tuple-element.175) | copy-start | bytes 3145732
  252.9 11.0 %copy-start.28 = (bf16[512,256]{1,0:T(8,128)(2,1)}, bf16[512,256]{1,0:T(8,128)(2,1)S(1)}, u32[]{:S(2)}) copy-start(bf16[512,256]{1,0:T(8,128)(2,1)S(1)} %collective-permute-done.21.refs_7_) | copy-start | bytes 786436
  254.3 9.7 %copy-start.29 = (bf16[512,256]{1,0:T(8,128)(2,1)}, bf16[512,256]{1,0:T(8,128)(2,1)S(1)}, u32[]{:S(2)}) copy-start(bf16[512,256]{1,0:T(8,128)(2,1)S(1)} %collective-permute-done.22.refs_8_) | copy-start | bytes 786436
  259.1 4.9 %copy-start.30 = (bf16[512,256]{1,0:T(8,128)(2,1)}, bf16[512,256]{1,0:T(8,128)(2,1)S(1)}, u32[]{:S(2)}) copy-start(bf16[512,256]{1,0:T(8,128)(2,1)S(1)} %collective-permute-done.23.refs_9_) | copy-start | bytes 786436
  259.1 42.5 %collective-permute-start.24 = (bf16[512,1024]{1,0:T(8,128)(2,1)}, bf16[512,1024]{1,0:T(8,128)(2,1)S(1)}, u32[]{:S(2)}, u32[]{:S(2)}) collective-permute-start(bf16[512,1024]{1,0:T(8,128)(2,1)} %get-tuple-element.174), channel_id=1, source_target_pairs={{0,8},{8,0},{16,24},{24,16},{1,9},{9,1},{17,25},{25,17},{2,10},{10... | collective-permute-start | bytes 3145736 | tf_op jit(solution)/shard_map/ppermute | solution.py:937
  259.9 41.8 %collective-permute-start.25 = (bf16[512,1024]{1,0:T(8,128)(2,1)S(1)}, bf16[512,1024]{1,0:T(8,128)(2,1)S(1)}, u32[]{:S(2)}, u32[]{:S(2)}) collective-permute-start(bf16[512,1024]{1,0:T(8,128)(2,1)S(1)} %copy-done.34), channel_id=1, source_target_pairs={{0,16},{8,24},{16,0},{24,8},{1,17},{9,25},{17,1},{25,9},{2,18},{10... | collective-permute-start | bytes 3145736 | tf_op jit(solution)/shard_map/ppermute | solution.py:937
  260.5 53.5 %collective-permute-start.26 = (bf16[1024,256]{1,0:T(8,128)(2,1)}, bf16[1024,256]{1,0:T(8,128)(2,1)S(1)}, u32[]{:S(2)}, u32[]{:S(2)}) collective-permute-start(bf16[1024,256]{1,0:T(8,128)(2,1)} %get-tuple-element.188), channel_id=1, source_target_pairs={{0,8},{8,0},{16,24},{24,16},{1,9},{9,1},{17,25},{25,17},{2,10},{10... | collective-permute-start | bytes 1572872 | tf_op jit(solution)/shard_map/ppermute | solution.py:937
  261.3 53.5 %collective-permute-start.27 = (bf16[1024,256]{1,0:T(8,128)(2,1)}, bf16[1024,256]{1,0:T(8,128)(2,1)S(1)}, u32[]{:S(2)}, u32[]{:S(2)}) collective-permute-start(bf16[1024,256]{1,0:T(8,128)(2,1)} %get-tuple-element.189), channel_id=1, source_target_pairs={{0,16},{8,24},{16,0},{24,8},{1,17},{9,25},{17,1},{25,9},{2,18},{10... | collective-permute-start | bytes 1572872 | tf_op jit(solution)/shard_map/ppermute | solution.py:937
  263.2 51.6 %collective-permute-start.28 = (bf16[1024,256]{1,0:T(8,128)(2,1)}, bf16[1024,256]{1,0:T(8,128)(2,1)S(1)}, u32[]{:S(2)}, u32[]{:S(2)}) collective-permute-start(bf16[1024,256]{1,0:T(8,128)(2,1)} %get-tuple-element.190), channel_id=1, source_target_pairs={{0,24},{8,16},{16,8},{24,0},{1,25},{9,17},{17,9},{25,1},{2,26},{10... | collective-permute-start | bytes 1572872 | tf_op jit(solution)/shard_map/ppermute | solution.py:937
  301.7 1.3 copy-start.13
  311.3 11.8 %collective-permute-start.29 = (bf16[512,512]{1,0:T(8,128)(2,1)}, bf16[512,512]{1,0:T(8,128)(2,1)}, u32[]{:S(2)}, u32[]{:S(2)}) collective-permute-start(bf16[512,512]{1,0:T(8,128)(2,1)} %get-tuple-element.196), channel_id=1, source_target_pairs={{0,8},{8,0},{16,24},{24,16},{1,9},{9,1},{17,25},{25,17},{2,10},{10... | collective-permute-start | bytes 1572872 | tf_op jit(solution)/shard_map/ppermute | solution.py:937
  312.1 11.0 %collective-permute-start.30 = (bf16[512,512]{1,0:T(8,128)(2,1)}, bf16[512,512]{1,0:T(8,128)(2,1)}, u32[]{:S(2)}, u32[]{:S(2)}) collective-permute-start(bf16[512,512]{1,0:T(8,128)(2,1)} %get-tuple-element.197), channel_id=1, source_target_pairs={{0,16},{8,24},{16,0},{24,8},{1,17},{9,25},{17,1},{25,9},{2,18},{10... | collective-permute-start | bytes 1572872 | tf_op jit(solution)/shard_map/ppermute | solution.py:937
  314.0 19.7 %collective-permute-start.31 = (bf16[512,512]{1,0:T(8,128)(2,1)}, bf16[512,512]{1,0:T(8,128)(2,1)}, u32[]{:S(2)}, u32[]{:S(2)}) collective-permute-start(bf16[512,512]{1,0:T(8,128)(2,1)} %get-tuple-element.198), channel_id=1, source_target_pairs={{0,24},{8,16},{16,8},{24,0},{1,25},{9,17},{17,9},{25,1},{2,26},{10... | collective-permute-start | bytes 1572872 | tf_op jit(solution)/shard_map/ppermute | solution.py:937
  315.9 21.4 %copy-start.7 = (f32[512,1024]{1,0:T(8,128)S(1)}, f32[512,1024]{1,0:T(8,128)}, u32[]{:S(2)}) copy-start(f32[512,1024]{1,0:T(8,128)} %get-tuple-element.143.refs_5_) | copy-start | bytes 6291460
  323.1 14.1 %copy-start.12 = (bf16[512,1024]{1,0:T(8,128)(2,1)S(1)}, bf16[512,1024]{1,0:T(8,128)(2,1)}, u32[]{:S(2)}) copy-start(bf16[512,1024]{1,0:T(8,128)(2,1)} %copy-done.11) | copy-start | bytes 3145732
  333.7 43.9 %collective-permute-start.35 = (bf16[128,3456]{1,0:T(8,128)(2,1)}, bf16[128,3456]{1,0:T(8,128)(2,1)}, u32[]{:S(2)}, u32[]{:S(2)}) collective-permute-start(bf16[128,3456]{1,0:T(8,128)(2,1)} %reduce-scatter.3.cloned.1.call-done.p0_ref), channel_id=1, source_target_pairs={{0,8},{8,0},{16,24},{24,16},{1,9},{9,1},{17,25},{25,17},{2,10},{10... | collective-permute-start | bytes 2654216 | tf_op jit(solution)/shard_map/ppermute | solution.py:937
  334.7 43.2 %collective-permute-start.36 = (bf16[128,3456]{1,0:T(8,128)(2,1)}, bf16[128,3456]{1,0:T(8,128)(2,1)}, u32[]{:S(2)}, u32[]{:S(2)}) collective-permute-start(bf16[128,3456]{1,0:T(8,128)(2,1)} %reduce-scatter.3.cloned.1.call-done.p0_ref), channel_id=1, source_target_pairs={{0,16},{8,24},{16,0},{24,8},{1,17},{9,25},{17,1},{25,9},{2,18},{10... | collective-permute-start | bytes 2654216 | tf_op jit(solution)/shard_map/ppermute | solution.py:937
  334.8 43.2 %collective-permute-start.37 = (bf16[128,3456]{1,0:T(8,128)(2,1)}, bf16[128,3456]{1,0:T(8,128)(2,1)}, u32[]{:S(2)}, u32[]{:S(2)}) collective-permute-start(bf16[128,3456]{1,0:T(8,128)(2,1)} %reduce-scatter.3.cloned.1.call-done.p0_ref), channel_id=1, source_target_pairs={{0,24},{8,16},{16,8},{24,0},{1,25},{9,17},{17,9},{25,1},{2,26},{10... | collective-permute-start | bytes 2654216 | tf_op jit(solution)/shard_map/ppermute | solution.py:937
  340.5 48.8 %copy-start.1 = (bf16[576,1024]{1,0:T(8,128)(2,1)S(1)}, bf16[576,1024]{1,0:T(8,128)(2,1)}, u32[]{:S(2)}) copy-start(bf16[576,1024]{1,0:T(8,128)(2,1)} %param.28) | copy-start | bytes 3538948
  374.5 10.6 %collective-permute-start.32 = (bf16[128,896]{1,0:T(8,128)(2,1)}, bf16[128,896]{1,0:T(8,128)(2,1)S(1)}, u32[]{:S(2)}, u32[]{:S(2)}) collective-permute-start(bf16[128,896]{1,0:T(8,128)(2,1)} %reduce-scatter.5.cloned.1.call-done.p0_ref), channel_id=1, source_target_pairs={{0,8},{8,0},{16,24},{24,16},{1,9},{9,1},{17,25},{25,17},{2,10},{10... | collective-permute-start | bytes 688136 | tf_op jit(solution)/shard_map/ppermute | solution.py:937
  376.0 9.1 %collective-permute-start.33 = (bf16[128,896]{1,0:T(8,128)(2,1)}, bf16[128,896]{1,0:T(8,128)(2,1)S(1)}, u32[]{:S(2)}, u32[]{:S(2)}) collective-permute-start(bf16[128,896]{1,0:T(8,128)(2,1)} %reduce-scatter.5.cloned.1.call-done.p0_ref), channel_id=1, source_target_pairs={{0,16},{8,24},{16,0},{24,8},{1,17},{9,25},{17,1},{25,9},{2,18},{10... | collective-permute-start | bytes 688136 | tf_op jit(solution)/shard_map/ppermute | solution.py:937
  377.6 7.5 %collective-permute-start.34 = (bf16[128,896]{1,0:T(8,128)(2,1)}, bf16[128,896]{1,0:T(8,128)(2,1)S(1)}, u32[]{:S(2)}, u32[]{:S(2)}) collective-permute-start(bf16[128,896]{1,0:T(8,128)(2,1)} %reduce-scatter.5.cloned.1.call-done.p0_ref), channel_id=1, source_target_pairs={{0,24},{8,16},{16,8},{24,0},{1,25},{9,17},{17,9},{25,1},{2,26},{10... | collective-permute-start | bytes 688136 | tf_op jit(solution)/shard_map/ppermute | solution.py:937
  (14 other events, 12.4 us)
Sparse Core Ops, SparseCore 0:
  10.2 26.1 all-gather.3
  38.6 90.2 all-gather.5
  130.5 45.5 all-gather.7
  237.3 81.9 reduce-scatter.2
  333.8 40.6 reduce-scatter.4

commit v6 on v5

--- a/solution.py
+++ b/solution.py
@@ -149,9 +149,10 @@
     return across[0:1, :] / gain_ref[...].astype(F32)
 
 
-def join_kernel(shards, me_ref, p0_ref, p1_ref, p2_ref, p3_ref, gate_ref, up_ref, gain_ref, dgate_ref, dup_ref, ddown_ref, dot_ref, st_ref):
-    for d, ref in enumerate((p0_ref, p1_ref, p2_ref, p3_ref)):
+def join_kernel(shards, me_ref, p0_ref, p1_ref, p2_ref, p3a_ref, p3b_ref, gate_ref, up_ref, gain_ref, dgate_ref, dup_ref, ddown_ref, dot_ref, st_ref):
+    for d, ref in enumerate((p0_ref, p1_ref, p2_ref)):
         st_ref[d] = ref[...]
+    st_ref[3] = jnp.concatenate([p3a_ref[...], p3b_ref[...]], axis=1)
     units = p0_ref.shape[1] // 3
     piece = units // shards
     quarters = [st_ref[jnp.bitwise_xor(me_ref[0], q)] for q in range(4)]
@@ -174,7 +175,7 @@
         functools.partial(join_kernel, shards),
         out_shape=(jax.ShapeDtypeStruct((depth, whole), F32),) * 2
         + (jax.ShapeDtypeStruct(down_shape, F32), jax.ShapeDtypeStruct((1, depth), F32)),
-        in_specs=[smem()] + [vmem()] * 7,
+        in_specs=[smem()] + [vmem()] * 8,
         out_specs=(vmem(),) * 4,
         scratch_shapes=[pltpu.VMEM((4,) + parts[0].shape, BF16)],
         compiler_params=params(),
@@ -1030,10 +1031,15 @@
     d_tokens = tokens_back(me_arr, d_raw, w_all, tokens[0], d_middle, gain_a, (p_last,))
     d_ffn = after(d_ffn, d_raw, p_last)
 
+    def two_stages(part):
+        half = part.shape[1] // 2 // LANES * LANES
+        one, two = swap(part, 1), swap(part, 2)
+        return [part, one, two, swap(one[:, :half], 2), swap(two[:, half:], 1)]
+
     def parts_of(part):
         return [part] + [swap(part, d) for d in (1, 2, 3)]
 
-    d_wg, d_wu, d_wd, d_ffn_gain = join_weights(me_arr, parts_of(d_ffn), w_gate, w_up, ffn_gain, w_down.shape, shards)
+    d_wg, d_wu, d_wd, d_ffn_gain = join_weights(me_arr, two_stages(d_ffn), w_gate, w_up, ffn_gain, w_down.shape, shards)
     d_wq, d_wk, d_wv, d_wo, d_attn_gain, d_query_gain, d_key_gain = join_last(
         me_arr, parts_of(after(d_last, d_ffn, d_tokens, block_out)), w_query, w_key, w_value, attn_gain,
         w_out.shape[1], head_dim,

time: 402 us -> 402 us (level)
    reduce_scatter x2, waiting for transfers between devices: 26.6 us -> 14.1 us  [body(): lax.psum_scatter(a, 'shard', scatter_dimension=0, tiled=True)]
    ppermute x38 -> x39, waiting for transfers between devices: 66.5 us -> 78.1 us  [swap(): return lax.ppermute(array, 'seq', [(s, s ^ distance) for s in range(4)])]
    unnamed x70 -> x74, local copies, waits for them, and re-layouts: 7.08 us -> 8.78 us
    ppermute x38 -> x39, starting transfers between devices: 42.4 us -> 42.1 us  [swap(): return lax.ppermute(array, 'seq', [(s, s ^ distance) for s in range(4)])]
  transfers between devices with their start and end apart: 43 -> 44, of which waited for: 12 -> 14; matrix products, arithmetic and copies ran while one was open for 3% -> 4% of each run, Pallas kernels for 56% -> 55%
where the time goes in v6:
time: 402 us; the launch traced here: 397 us
  Pallas kernels  224 us (56%)
  waiting for transfers between devices  92.3 us (23%)
  starting transfers between devices  42.8 us (11%)
  local copies, waits for them, and re-layouts  17.9 us (4%)
  between operations  14.7 us (4%)
  other arithmetic  5.15 us (1%)
    ppermute x39, waiting for transfers between devices, swap(): return lax.ppermute(array, 'seq', [(s, s ^ distance) for s in range(4)])  78.1 us
    pallas_call x3, Pallas kernels, ffn(): pl.pallas_call(functools.partial(ffn_kernel, per, shards, blocks, len(car...  66.1 us
    ppermute x39, starting transfers between devices, swap(): return lax.ppermute(array, 'seq', [(s, s ^ distance) for s in range(4)])  42.1 us
    pallas_call x1, Pallas kernels, attend_back(): pl.pallas_call(functools.partial(attend_back_kernel, head_dim, len(late))...  36 us
    pallas_call x2, Pallas kernels, attend(): pl.pallas_call(functools.partial(attend_kernel, head_dim, group, all_rows...  27.5 us
    pallas_call x1, Pallas kernels, weights_back(): pl.pallas_call(functools.partial(weights_kernel, shards), grid=(DOWN_STEP...  21.5 us
    pallas_call x1, Pallas kernels, qkv(): pl.pallas_call(functools.partial(qkv_kernel, head_dim), grid=(8,), out_sh...  16.9 us
    reduce_scatter x2, waiting for transfers between devices, body(): lax.psum_scatter(a, 'shard', scatter_dimension=0, tiled=True)  14.1 us
  transfers between devices with their start and end apart: 44, of which 14 were waited for; matrix products, arithmetic and copies ran while one was open for 4% of the time, Pallas kernels for 55%

profile of v6, /device:TPU:0, one launch (start us, length us, event | category | flops | bytes accessed | tf_op | source)
XLA Modules:
  0.0 397.1 jit_solution(3625517465584269976)
XLA Ops:
  7.2 1.9 first_weights.1
  9.2 3.0 collective-permute-start
  12.2 1.5 collective-permute-start.1
  16.9 5.5 %make_tables.1 = (f32[2048,128]{1,0:T(8,128)}, f32[2048,128]{1,0:T(8,128)}, f32[2048,128]{1,0:T(8,128)}, s32[2048,128]{1,0:T(8,128)}, s32[1,2048]{1,0:T(1,128)}) custom-call(s32[1]{0:T(128)} %bitcast.me_ref.refs_0_, s32[1,3]{1,0:T(1,128)} %refs_0_.1, s32[1,2048]{1,0:T(1,128)} %order_ref.1, f32[1,128]{1,0:T(1,128)} %broadcast_in_dim_tile.9.freq_ref), custom_call_target="tpu_custom_call" | custom-call | flops 1048576 | bytes 65536 | tf_op jit(solution)/shard_map/make_tables/pallas_call | solution.py:261
  23.1 4.7 %cut_weights.1 = bf16[128,4608]{1,0:T(8,128)(2,1)} custom-call(s32[1]{0:T(128)} %bitcast.me_ref.refs_0_, bf16[128,4608]{1,0:T(8,128)(2,1)} %gate_ref.3, bf16[128,4608]{1,0:T(8,128)(2,1)} %up_ref.3, bf16[144,1024]{1,0:T(8,128)(2,1)} %constant_dynamic-slice_fusion.down_ref, bf16[128,1024]{1,0:T(8,128)(2,1)} %wo_ref.1), custom_call_target="tpu_custom_call" | custom-call | flops 1048576 | bytes 65536 | tf_op jit(solution)/shard_map/cut_weights/pallas_call | solution.py:136
  27.8 7.8 %collective-permute-done.x1_ref.refs_11_ = bf16[512,1024]{1,0:T(8,128)(2,1)S(1)} collective-permute-done((bf16[512,1024]{1,0:T(8,128)(2,1)}, bf16[512,1024]{1,0:T(8,128)(2,1)S(1)}, u32[]{:S(2)}, u32[]{:S(2)}) %collective-permute-start) | collective-permute-done | bytes 1048608 | tf_op jit(solution)/shard_map/ppermute | solution.py:938
  35.6 1.5 collective-permute-done.1.x2_ref.refs_12_
  37.2 1.6 collective-permute-start.2
  39.4 10.3 %collective-permute-done.2.x3a_ref.refs_9_ = bf16[512,512]{1,0:T(8,128)(2,1)S(1)} collective-permute-done((bf16[512,512]{1,0:T(8,128)(2,1)S(1)}, bf16[512,512]{1,0:T(8,128)(2,1)S(1)}, u32[]{:S(2)}, u32[]{:S(2)}) %collective-permute-start.2) | collective-permute-done | bytes 524320 | tf_op jit(solution)/shard_map/ppermute | solution.py:938
  49.7 1.3 collective-permute-done.3.x3b_ref.refs_10_
  51.1 1.9 pad_maximum_fusion
  55.0 16.9 %qkv.1 = (bf16[2048,1024]{1,0:T(8,128)(2,1)}, bf16[4,2048,128]{2,1,0:T(8,128)(2,1)}, bf16[2048,128]{1,0:T(8,128)(2,1)}, bf16[2048,128]{1,0:T(8,128)(2,1)}, bf16[...) custom-call(bf16[512,1024]{1,0:T(8,128)(2,1)} %bitcast.13, ...), custom_call_target="tpu_custom_call" | custom-call | flops 1048576 | bytes 65536 | tf_op jit(solution)/shard_map/qkv/pallas_call | solution.py:334
  71.9 13.7 %attend.3 = (bf16[2048,128]{1,0:T(8,128)(2,1)}, bf16[2048,128]{1,0:T(8,128)(2,1)}, f32[2,2048]{1,0:T(2,128)}) custom-call(s32[1,3]{1,0:T(1,128)} %refs_0_.1, s32[1,2048]{1,0:T(1,128)} %get-tuple-element.119.orow_ref, bf16[4,2048,128]{2,1,0:T(8,128)(2,1)} %get-tuple-element.128.qx_ref.refs_12_, bf16[2048,128]{1,0:T(8,128)(2,1)} %get-tuple-element.129.k_ref.refs_13_, ...), custom_call_target="tpu_custom_call" | custom-call | flops 1048576 | bytes 65536 | tf_op jit(solution)/shard_map/attend/pallas_call | solution.py:422
  85.6 1.2 collective-permute-start.5
  86.7 1.5 collective-permute-start.7
  88.3 13.8 %attend.2 = (bf16[2048,128]{1,0:T(8,128)(2,1)}, bf16[2048,128]{1,0:T(8,128)(2,1)}, f32[2,2048]{1,0:T(2,128)}) custom-call(s32[1,3]{1,0:T(1,128)} %refs_0_.1, s32[1,2048]{1,0:T(1,128)} %get-tuple-element.119.orow_ref, bf16[4,2048,128]{2,1,0:T(8,128)(2,1)} %get-tuple-element.128.qx_ref.refs_12_, bf16[2048,128]{1,0:T(8,128)(2,1)} %get-tuple-element.129.k_ref.refs_13_, ...), custom_call_target="tpu_custom_call" | custom-call | flops 1048576 | bytes 65536 | tf_op jit(solution)/shard_map/attend/pallas_call | solution.py:422
  103.5 2.1 collective-permute-start.8
  105.6 1.1 slice.35
  106.7 1.1 slice.36
  108.4 0.9 collective-permute-start.14
  109.3 7.9 %collective-permute-done.4.refs_3_.refs_2_ = bf16[2048,128]{1,0:T(8,128)(2,1)S(1)} collective-permute-done((bf16[2048,128]{1,0:T(8,128)(2,1)}, bf16[2048,128]{1,0:T(8,128)(2,1)S(1)}, u32[]{:S(2)}, u32[]{:S(2)}) %collective-permute-start.4) | collective-permute-done | bytes 524320 | tf_op jit(solution)/shard_map/ppermute | solution.py:938
  117.7 11.5 %collective-permute-done.6.refs_5_.refs_4_ = bf16[2048,128]{1,0:T(8,128)(2,1)S(1)} collective-permute-done((bf16[2048,128]{1,0:T(8,128)(2,1)}, bf16[2048,128]{1,0:T(8,128)(2,1)S(1)}, u32[]{:S(2)}, u32[]{:S(2)}) %collective-permute-start.6) | collective-permute-done | bytes 524320 | tf_op jit(solution)/shard_map/ppermute | solution.py:938
  129.2 1.3 collective-permute-start.9
  130.5 1.4 fusion
  131.9 9.6 %collective-permute-done.12.refs_8_.refs_10_ = bf16[1024,128]{1,0:T(8,128)(2,1)S(1)} collective-permute-done((bf16[1024,128]{1,0:T(8,128)(2,1)S(1)}, bf16[1024,128]{1,0:T(8,128)(2,1)S(1)}, u32[]{:S(2)}, u32[]{:S(2)}) %collective-permute-start.12) | collective-permute-done | bytes 262176 | tf_op jit(solution)/shard_map/ppermute | solution.py:938
  142.2 17.0 %ffn.3 = (bf16[2048,1024]{1,0:T(8,128)(2,1)}, bf16[2048,1152]{1,0:T(8,128)(2,1)}, bf16[2048,2304]{1,0:T(8,128)(2,1)}, bf16[2048,1024]{1,0:T(8,128)(2,1)}, bf16[5...) custom-call(s32[1]{0:T(128)} %bitcast.me_ref.refs_0_, ...), custom_call_target="tpu_custom_call" | custom-call | flops 1048576 | bytes 65536 | tf_op jit(solution)/shard_map/ffn/pallas_call | solution.py:789
  159.3 1.2 collective-permute-start.15
  160.9 1.3 collective-permute-start.17
  162.2 1.2 collective-permute-start.18
  163.4 17.3 %ffn.4 = (bf16[2048,1024]{1,0:T(8,128)(2,1)}, bf16[2048,1152]{1,0:T(8,128)(2,1)}, bf16[2048,2304]{1,0:T(8,128)(2,1)}, bf16[2048,1024]{1,0:T(8,128)(2,1)}, bf16[5...) custom-call(s32[1]{0:T(128)} %bitcast.me_ref.refs_0_, ...), custom_call_target="tpu_custom_call", output_to_operand_aliasing={{0}: (16, {}), {1}: (17, {}), {2}: (18, {}), {3}: (19, {})} | custom-call | flops 1048576 | bytes 65536 | tf_op jit(solution)/shard_map/ffn/pallas_call | solution.py:789
  182.0 31.8 %ffn.5 = (bf16[2048,1024]{1,0:T(8,128)(2,1)}, bf16[2048,1152]{1,0:T(8,128)(2,1)}, bf16[2048,2304]{1,0:T(8,128)(2,1)}, bf16[2048,1024]{1,0:T(8,128)(2,1)}, bf16[5...) custom-call(s32[1]{0:T(128)} %bitcast.me_ref.refs_0_, ...), custom_call_target="tpu_custom_call", output_to_operand_aliasing={{0}: (24, {}), {1}: (25, {}), {2}: (26, {}), {3}: (27, {})} | custom-call | flops 1048576 | bytes 65536 | tf_op jit(solution)/shard_map/ffn/pallas_call | solution.py:789
  213.8 1.1 collective-permute-start.19
  215.0 0.8 collective-permute-start.20
  215.8 21.5 %weights_back.1.refs_8_ = bf16[1024,3456]{1,0:T(8,128)(2,1)} custom-call(bf16[2048,1024]{1,0:T(8,128)(2,1)} %get-tuple-element.158.nf_ref, bf16[2048,2304]{1,0:T(8,128)(2,1)} %get-tuple-element.159.dgu_from, bf16[2048,1152]{1,0:T(8,128)(2,1)} %get-tuple-element.160.hid_ref, bf16[2048,1024]{1,0:T(8,128)(2,1)} %get-tuple-element.161.cot_ref), custom_call_target="tpu_custom_call" | custom-call | flops 1048576 | bytes 65536 | tf_op jit(solution)/shard_map/weights_back/pallas_call | solution.py:843
  237.4 1.0 copy-done.21
  238.8 6.5 %middle_back.1 = (f32[512,1024]{1,0:T(8,128)}, bf16[512,1024]{1,0:T(8,128)(2,1)}, bf16[512,256]{1,0:T(8,128)(2,1)}, bf16[512,256]{1,0:T(8,128)(2,1)}, bf16[512,2...) custom-call(s32[1]{0:T(128)} %bitcast.me_ref.refs_0_, bf16[512,1024]{1,0:T(8,128)(2,1)} %get-tuple-element.155.refs_1_, ...), custom_call_target="tpu_custom_call" | custom-call | flops 1048576 | bytes 65536 | tf_op jit(solution)/shard_map/middle_back/pallas_call | solution.py:924
  245.3 1.0 collective-permute-start.21
  246.3 1.2 collective-permute-start.22
  247.6 1.3 collective-permute-start.23
  248.9 4.8 %out_weights.1 = (bf16[1024,256]{1,0:T(8,128)(2,1)}, bf16[1024,256]{1,0:T(8,128)(2,1)}, bf16[1024,256]{1,0:T(8,128)(2,1)}, bf16[1024,256]{1,0:T(8,128)(2,1)}) custom-call(s32[1]{0:T(128)} %bitcast.me_ref.refs_0_, bf16[2048,128]{1,0:T(8,128)(2,1)} %get-tuple-element.131.refs_1_.refs_0_, bf16[2048,128]{1,0:T(8,128)(2,1)} %get-tuple-element.132.refs_2_.refs_1_, ...), custom_call_target="tpu_custom_call" | custom-call | flops 1048576 | bytes 65536 | tf_op jit(solution)/shard_map/out_weights/pallas_call | solution.py:908
  254.1 4.9 %collective-permute-done.23.refs_9_ = bf16[512,256]{1,0:T(8,128)(2,1)S(1)} collective-permute-done((bf16[512,256]{1,0:T(8,128)(2,1)}, bf16[512,256]{1,0:T(8,128)(2,1)S(1)}, u32[]{:S(2)}, u32[]{:S(2)}) %collective-permute-start.23) | collective-permute-done | bytes 262176 | tf_op jit(solution)/shard_map/ppermute | solution.py:938
  260.3 1.1 collective-permute-start.26
  261.5 1.6 collective-permute-start.27
  263.8 36.0 %attend_back.1 = (bf16[2048,512]{1,0:T(8,128)(2,1)}, f32[2,128]{1,0:T(2,128)}) custom-call(s32[1,3]{1,0:T(1,128)} %refs_0_.1, s32[2048,128]{1,0:T(8,128)} %get-tuple-element.122.ocol_ref.refs_1_, f32[2,2048]{1,0:T(2,128)} %get-tuple-element.177.refs_2_, f32[2,2048]{1,0:T(2,128)} %get-tuple-element.178.refs_3_, bf16[2048,128]{1,0:T(8,128)(2,1)} %get-tuple-element.179.refs_4_, ...), custom_call_target="tpu_custom_call" | custom-call | flops 1048576 | bytes 65536 | tf_op jit(solution)/shard_map/attend_back/pallas_call | solution.py:588
  299.9 0.9 copy-done.11
  301.2 8.4 %rows_back.1 = (bf16[2048,512]{1,0:T(8,128)(2,1)}, bf16[512,512]{1,0:T(8,128)(2,1)}, bf16[512,512]{1,0:T(8,128)(2,1)}, bf16[512,512]{1,0:T(8,128)(2,1)}, bf16[512,512]{1,0:T(8,128)(2,1)}) custom-call(s32[1,2048]{1,0:T(1,128)} %get-tuple-element.119.orow_ref, bf16[2048,512]{1,0:T(8,128)(2,1)} %get-tuple-element.185.draw_ref, bf16[512,1024]{1,0:T(8,128)(2,1)} %copy-done.11, ...), custom_call_target="tpu_custom_call" | custom-call | flops 1048576 | bytes 65536 | tf_op jit(solution)/shard_map/rows_back/pallas_call | solution.py:612
  309.6 1.2 collective-permute-start.29
  310.7 1.6 collective-permute-start.30
  314.1 7.1 %last_weights.1.refs_0_ = bf16[1024,896]{1,0:T(8,128)(2,1)} custom-call(bf16[2048,1024]{1,0:T(8,128)(2,1)} %get-tuple-element.176.normed_ref, bf16[2048,512]{1,0:T(8,128)(2,1)} %get-tuple-element.186.grads_ref, bf16[1024,256]{1,0:T(8,128)(2,1)} %get-tuple-element.187.o0_ref, bf16[1024,256]{1,0:T(8,128)(2,1)} %copy-done.27, bf16[1024,256]{1,0:T(8,128)(2,1)} %copy-done.28, ...), custom_call_target="tpu_custom_call" | custom-call | flops 1048576 | bytes 65536 | tf_op jit(solution)/shard_map/last_weights/pallas_call | solution.py:630
  321.2 2.6 collective-permute-done.30.g2_ref
  323.8 4.8 %collective-permute-done.31.g3_ref = bf16[512,512]{1,0:T(8,128)(2,1)} collective-permute-done((bf16[512,512]{1,0:T(8,128)(2,1)}, bf16[512,512]{1,0:T(8,128)(2,1)}, u32[]{:S(2)}, u32[]{:S(2)}) %collective-permute-start.31) | collective-permute-done | bytes 524320 | tf_op jit(solution)/shard_map/ppermute | solution.py:938
  329.6 15.3 %collective-permute-done.36.p2_ref = bf16[128,3456]{1,0:T(8,128)(2,1)S(1)} collective-permute-done((bf16[128,3456]{1,0:T(8,128)(2,1)}, bf16[128,3456]{1,0:T(8,128)(2,1)S(1)}, u32[]{:S(2)}, u32[]{:S(2)}) %collective-permute-start.36) | collective-permute-done | bytes 884768 | tf_op jit(solution)/shard_map/ppermute | solution.py:938
  344.9 0.9 copy-done.17
  345.8 0.8 slice.43
  346.6 1.1 collective-permute-start.38
  347.7 1.0 copy-done.18
  349.5 1.1 collective-permute-start.37
  350.5 3.3 add_convert_fusion
  353.8 7.4 %tokens_back.1 = bf16[512,1024]{1,0:T(8,128)(2,1)} custom-call(s32[1]{0:T(128)} %bitcast.me_ref.refs_0_, bf16[512,512]{1,0:T(8,128)(2,1)} %get-tuple-element.195.g0_ref, bf16[512,512]{1,0:T(8,128)(2,1)} %collective-permute-done.29.g1_ref, bf16[512,512]{1,0:T(8,128)(2,1)} %collective-permute-done.30.g2_ref, bf16[512,512]{1,0:T(8,128)(2,1)} %collective-permute-done.31.g3_ref, ...), custom_call_target="tpu_custom_call" | custom-call | flops 1048576 | bytes 65536 | tf_op jit(solution)/shard_map/tokens_back/pallas_call | solution.py:663
  361.2 14.1 %reduce-scatter.5.cloned.1.call-done.p0_ref = bf16[128,896]{1,0:T(8,128)(2,1)} async-done(((bf16[1024,896]{1,0:T(8,128)(2,1)}), bf16[128,896]{1,0:T(8,128)(2,1)}) %reduce-scatter.5.cloned.1.call-update) | async-done | bytes 229392 | tf_op jit(solution)/shard_map/reduce_scatter | solution.py:1012
  375.3 1.5 collective-permute-start.32
  376.9 1.5 collective-permute-start.33
  378.8 7.1 %join_weights.1 = (f32[128,4608]{1,0:T(8,128)}, f32[128,4608]{1,0:T(8,128)}, f32[576,1024]{1,0:T(8,128)}, f32[1,128]{1,0:T(1,128)}) custom-call(s32[1]{0:T(128)} %bitcast.me_ref.refs_0_, bf16[128,3456]{1,0:T(8,128)(2,1)} %reduce-scatter.3.cloned.1.call-done.p0_ref, bf16[128,3456]{1,0:T(8,128)(2,1)} %copy-done.18, bf16[128,3456]{1,0:T(8,128)(2,1)} %copy-done.17, ...), custom_call_target="tpu_custom_call" | custom-call | flops 1048576 | bytes 65536 | tf_op jit(solution)/shard_map/join_weights/pallas_call | solution.py:174
  387.4 2.7 join_last.1
  (140 shorter events, 20.2 us)
Async XLA Ops:
  7.2 15.2 %copy-start = (bf16[576,1024]{1,0:T(8,128)(2,1)S(1)}, bf16[576,1024]{1,0:T(8,128)(2,1)}, u32[]{:S(2)}) copy-start(bf16[576,1024]{1,0:T(8,128)(2,1)} %param.28) | copy-start | bytes 3538948
  7.2 47.8 %all-gather.4.cloned.1.call-start = ((), (), s32[]{:S(2)}) async-start(), calls=%async_computation.2 | async-start | bytes 1474560 | tf_op jit(solution)/shard_map/all_gather | solution.py:976
  9.2 132.3 %all-gather.6.cloned.1.call-start = ((), (), s32[]{:S(2)}) async-start(), calls=%async_computation.3 | async-start | bytes 10616832 | tf_op jit(solution)/shard_map/all_gather | solution.py:978
  9.2 26.4 %collective-permute-start = (bf16[512,1024]{1,0:T(8,128)(2,1)}, bf16[512,1024]{1,0:T(8,128)(2,1)S(1)}, u32[]{:S(2)}, u32[]{:S(2)}) collective-permute-start(bf16[512,1024]{1,0:T(8,128)(2,1)} %bitcast.11), channel_id=1, source_target_pairs={{0,8},{8,0},{16,24},{24,16},{1,9},{9,1},{17,25},{25,17},{2,10},{10... | collective-permute-start | bytes 3145736 | tf_op jit(solution)/shard_map/ppermute | solution.py:938
  12.2 24.8 %collective-permute-start.1 = (bf16[512,1024]{1,0:T(8,128)(2,1)}, bf16[512,1024]{1,0:T(8,128)(2,1)S(1)}, u32[]{:S(2)}, u32[]{:S(2)}) collective-permute-start(bf16[512,1024]{1,0:T(8,128)(2,1)} %bitcast.12), channel_id=1, source_target_pairs={{0,16},{8,24},{16,0},{24,8},{1,17},{9,25},{17,1},{25,9},{2,18},{10... | collective-permute-start | bytes 3145736 | tf_op jit(solution)/shard_map/ppermute | solution.py:938
  27.8 23.3 %copy-start.14 = (bf16[128,1024]{1,0:T(8,128)(2,1)S(1)}, bf16[128,1024]{1,0:T(8,128)(2,1)}, u32[]{:S(2)}) copy-start(bf16[128,1024]{1,0:T(8,128)(2,1)} %q_ref.3) | copy-start | bytes 786436
  27.8 23.3 %copy-start.19 = (bf16[128,512]{1,0:T(8,128)(2,1)S(1)}, bf16[128,512]{1,0:T(8,128)(2,1)}, u32[]{:S(2)}) copy-start(bf16[128,512]{1,0:T(8,128)(2,1)} %k_ref.3) | copy-start | bytes 393220
  35.6 17.4 %copy-start.8 = (bf16[512,1024]{1,0:T(8,128)(2,1)}, bf16[512,1024]{1,0:T(8,128)(2,1)S(1)}, u32[]{:S(2)}) copy-start(bf16[512,1024]{1,0:T(8,128)(2,1)S(1)} %collective-permute-done.x1_ref.refs_11_) | copy-start | bytes 3145732
  37.1 15.9 %copy-start.9 = (bf16[512,1024]{1,0:T(8,128)(2,1)}, bf16[512,1024]{1,0:T(8,128)(2,1)S(1)}, u32[]{:S(2)}) copy-start(bf16[512,1024]{1,0:T(8,128)(2,1)S(1)} %collective-permute-done.1.x2_ref.refs_12_) | copy-start | bytes 3145732
  37.1 201.7 %all-gather.8.cloned.1.call-start = ((), (), s32[]{:S(2)}) async-start(), calls=%async_computation.4 | async-start | bytes 4718592 | tf_op jit(solution)/shard_map/all_gather | solution.py:990
  37.2 12.5 %collective-permute-start.2 = (bf16[512,512]{1,0:T(8,128)(2,1)S(1)}, bf16[512,512]{1,0:T(8,128)(2,1)S(1)}, u32[]{:S(2)}, u32[]{:S(2)}) collective-permute-start(bf16[512,512]{1,0:T(8,128)(2,1)S(1)} %slice.30), channel_id=1, source_target_pairs={{0,16},{8,24},{16,0},{24,8},{1,17},{9,25},{17,1},{25,9},{2,18},{10... | collective-permute-start | bytes 1572872 | tf_op jit(solution)/shard_map/ppermute | solution.py:938
  38.8 12.3 %collective-permute-start.3 = (bf16[512,512]{1,0:T(8,128)(2,1)S(1)}, bf16[512,512]{1,0:T(8,128)(2,1)S(1)}, u32[]{:S(2)}, u32[]{:S(2)}) collective-permute-start(bf16[512,512]{1,0:T(8,128)(2,1)S(1)} %slice.31), channel_id=1, source_target_pairs={{0,8},{8,0},{16,24},{24,16},{1,9},{9,1},{17,25},{25,17},{2,10},{10... | collective-permute-start | bytes 1572872 | tf_op jit(solution)/shard_map/ppermute | solution.py:938
  49.7 5.2 %copy-start.15 = (bf16[512,512]{1,0:T(8,128)(2,1)}, bf16[512,512]{1,0:T(8,128)(2,1)S(1)}, u32[]{:S(2)}) copy-start(bf16[512,512]{1,0:T(8,128)(2,1)S(1)} %collective-permute-done.2.x3a_ref.refs_9_) | copy-start | bytes 1572868
  51.1 3.9 copy-start.16
  53.0 275.6 %reduce-scatter.3.cloned.1.call-start = ((), (), s32[]{:S(2)}) async-start(), calls=%async_computation.5 | async-start | bytes 7962624 | tf_op jit(solution)/shard_map/reduce_scatter | solution.py:1012
  53.6 49.3 %collective-permute-start.10 = (bf16[512,1024]{1,0:T(8,128)(2,1)}, bf16[512,1024]{1,0:T(8,128)(2,1)}, u32[]{:S(2)}, u32[]{:S(2)}) collective-permute-start(bf16[512,1024]{1,0:T(8,128)(2,1)} %bitcast.4.refs_10_.refs_4_), channel_id=1, source_target_pairs={{0,8},{8,0},{16,24},{24,16},{1,9},{9,1},{17,25},{25,17},{2,10},{10... | collective-permute-start | bytes 3145736 | tf_op jit(solution)/shard_map/ppermute | solution.py:938
  54.4 49.1 %collective-permute-start.11 = (bf16[512,1024]{1,0:T(8,128)(2,1)}, bf16[512,1024]{1,0:T(8,128)(2,1)}, u32[]{:S(2)}, u32[]{:S(2)}) collective-permute-start(bf16[512,1024]{1,0:T(8,128)(2,1)} %bitcast.4.refs_10_.refs_4_), channel_id=1, source_target_pairs={{0,16},{8,24},{16,0},{24,8},{1,17},{9,25},{17,1},{25,9},{2,18},{10... | collective-permute-start | bytes 3145736 | tf_op jit(solution)/shard_map/ppermute | solution.py:938
  85.6 22.2 %collective-permute-start.5 = (bf16[2048,128]{1,0:T(8,128)(2,1)}, bf16[2048,128]{1,0:T(8,128)(2,1)S(1)}, u32[]{:S(2)}, u32[]{:S(2)}) collective-permute-start(bf16[2048,128]{1,0:T(8,128)(2,1)} %get-tuple-element.132.refs_2_.refs_1_), channel_id=1, source_target_pairs={{0,8},{8,0},{16,24},{24,16},{1,9},{9,1},{17,25},{25,17},{2,10},{10... | collective-permute-start | bytes 1572872 | tf_op jit(solution)/shard_map/ppermute | solution.py:938
  86.7 21.6 %collective-permute-start.7 = (bf16[2048,128]{1,0:T(8,128)(2,1)}, bf16[2048,128]{1,0:T(8,128)(2,1)S(1)}, u32[]{:S(2)}, u32[]{:S(2)}) collective-permute-start(bf16[2048,128]{1,0:T(8,128)(2,1)} %get-tuple-element.132.refs_2_.refs_1_), channel_id=1, source_target_pairs={{0,16},{8,24},{16,0},{24,8},{1,17},{9,25},{17,1},{25,9},{2,18},{10... | collective-permute-start | bytes 1572872 | tf_op jit(solution)/shard_map/ppermute | solution.py:938
  102.1 15.1 %collective-permute-start.4 = (bf16[2048,128]{1,0:T(8,128)(2,1)}, bf16[2048,128]{1,0:T(8,128)(2,1)S(1)}, u32[]{:S(2)}, u32[]{:S(2)}) collective-permute-start(bf16[2048,128]{1,0:T(8,128)(2,1)} %get-tuple-element.131.refs_1_.refs_0_), channel_id=1, source_target_pairs={{0,8},{8,0},{16,24},{24,16},{1,9},{9,1},{17,25},{25,17},{2,10},{10... | collective-permute-start | bytes 1572872 | tf_op jit(solution)/shard_map/ppermute | solution.py:938
  102.9 26.3 %collective-permute-start.6 = (bf16[2048,128]{1,0:T(8,128)(2,1)}, bf16[2048,128]{1,0:T(8,128)(2,1)S(1)}, u32[]{:S(2)}, u32[]{:S(2)}) collective-permute-start(bf16[2048,128]{1,0:T(8,128)(2,1)} %get-tuple-element.131.refs_1_.refs_0_), channel_id=1, source_target_pairs={{0,16},{8,24},{16,0},{24,8},{1,17},{9,25},{17,1},{25,9},{2,18},{10... | collective-permute-start | bytes 1572872 | tf_op jit(solution)/shard_map/ppermute | solution.py:938
  103.5 28.4 %collective-permute-start.8 = (bf16[2048,128]{1,0:T(8,128)(2,1)}, bf16[2048,128]{1,0:T(8,128)(2,1)S(1)}, u32[]{:S(2)}, u32[]{:S(2)}) collective-permute-start(bf16[2048,128]{1,0:T(8,128)(2,1)} %get-tuple-element.131.refs_1_.refs_0_), channel_id=1, source_target_pairs={{0,24},{8,16},{16,8},{24,0},{1,25},{9,17},{17,9},{25,1},{2,26},{10... | collective-permute-start | bytes 1572872 | tf_op jit(solution)/shard_map/ppermute | solution.py:938
  107.8 33.7 %copy-start.3 = (bf16[2048,128]{1,0:T(8,128)(2,1)}, bf16[2048,128]{1,0:T(8,128)(2,1)S(1)}, u32[]{:S(2)}) copy-start(bf16[2048,128]{1,0:T(8,128)(2,1)S(1)} %collective-permute-done.5.refs_4_.refs_3_) | copy-start | bytes 1572868
  107.8 33.7 %collective-permute-start.13 = (bf16[512,512]{1,0:T(8,128)(2,1)S(1)}, bf16[512,512]{1,0:T(8,128)(2,1)}, u32[]{:S(2)}, u32[]{:S(2)}) collective-permute-start(bf16[512,512]{1,0:T(8,128)(2,1)S(1)} %slice.35), channel_id=1, source_target_pairs={{0,16},{8,24},{16,0},{24,8},{1,17},{9,25},{17,1},{25,9},{2,18},{10... | collective-permute-start | bytes 1572872 | tf_op jit(solution)/shard_map/ppermute | solution.py:938
  108.4 33.2 %copy-start.4 = (bf16[2048,128]{1,0:T(8,128)(2,1)}, bf16[2048,128]{1,0:T(8,128)(2,1)S(1)}, u32[]{:S(2)}) copy-start(bf16[2048,128]{1,0:T(8,128)(2,1)S(1)} %collective-permute-done.7.refs_6_.refs_5_) | copy-start | bytes 1572868
  108.4 33.1 %collective-permute-start.14 = (bf16[512,512]{1,0:T(8,128)(2,1)S(1)}, bf16[512,512]{1,0:T(8,128)(2,1)}, u32[]{:S(2)}, u32[]{:S(2)}) collective-permute-start(bf16[512,512]{1,0:T(8,128)(2,1)S(1)} %slice.36), channel_id=1, source_target_pairs={{0,8},{8,0},{16,24},{24,16},{1,9},{9,1},{17,25},{25,17},{2,10},{10... | collective-permute-start | bytes 1572872 | tf_op jit(solution)/shard_map/ppermute | solution.py:938
  117.2 24.3 %copy-start.5 = (bf16[2048,128]{1,0:T(8,128)(2,1)}, bf16[2048,128]{1,0:T(8,128)(2,1)S(1)}, u32[]{:S(2)}) copy-start(bf16[2048,128]{1,0:T(8,128)(2,1)S(1)} %collective-permute-done.4.refs_3_.refs_2_) | copy-start | bytes 1572868
  117.2 24.3 %collective-permute-start.12 = (bf16[1024,128]{1,0:T(8,128)(2,1)S(1)}, bf16[1024,128]{1,0:T(8,128)(2,1)S(1)}, u32[]{:S(2)}, u32[]{:S(2)}) collective-permute-start(bf16[1024,128]{1,0:T(8,128)(2,1)S(1)} %slice.41), channel_id=1, source_target_pairs={{0,16},{8,24},{16,0},{24,8},{1,17},{9,25},{17,1},{25,9},{2,18},{10... | collective-permute-start | bytes 786440 | tf_op jit(solution)/shard_map/ppermute | solution.py:938
  129.2 12.4 %copy-start.6 = (bf16[2048,128]{1,0:T(8,128)(2,1)}, bf16[2048,128]{1,0:T(8,128)(2,1)S(1)}, u32[]{:S(2)}) copy-start(bf16[2048,128]{1,0:T(8,128)(2,1)S(1)} %collective-permute-done.6.refs_5_.refs_4_) | copy-start | bytes 1572868
  129.2 12.3 %collective-permute-start.9 = (bf16[1024,128]{1,0:T(8,128)(2,1)S(1)}, bf16[1024,128]{1,0:T(8,128)(2,1)S(1)}, u32[]{:S(2)}, u32[]{:S(2)}) collective-permute-start(bf16[1024,128]{1,0:T(8,128)(2,1)S(1)} %slice.40), channel_id=1, source_target_pairs={{0,8},{8,0},{16,24},{24,16},{1,9},{9,1},{17,25},{25,17},{2,10},{10... | collective-permute-start | bytes 786440 | tf_op jit(solution)/shard_map/ppermute | solution.py:938
  131.9 9.7 %copy-start.2 = (bf16[2048,128]{1,0:T(8,128)(2,1)}, bf16[2048,128]{1,0:T(8,128)(2,1)S(1)}, u32[]{:S(2)}) copy-start(bf16[2048,128]{1,0:T(8,128)(2,1)S(1)} %collective-permute-done.8.refs_7_.refs_9_.refs_6_) | copy-start | bytes 1572868
  159.3 21.4 %collective-permute-start.15 = (bf16[512,512]{1,0:T(8,128)(2,1)}, bf16[512,512]{1,0:T(8,128)(2,1)S(1)}, u32[]{:S(2)}, u32[]{:S(2)}) collective-permute-start(bf16[512,512]{1,0:T(8,128)(2,1)} %get-tuple-element.145), channel_id=1, source_target_pairs={{0,8},{8,0},{16,24},{24,16},{1,9},{9,1},{17,25},{25,17},{2,10},{10... | collective-permute-start | bytes 1572872 | tf_op jit(solution)/shard_map/ppermute | solution.py:938
  160.4 20.3 %collective-permute-start.16 = (bf16[512,512]{1,0:T(8,128)(2,1)}, bf16[512,512]{1,0:T(8,128)(2,1)S(1)}, u32[]{:S(2)}, u32[]{:S(2)}) collective-permute-start(bf16[512,512]{1,0:T(8,128)(2,1)} %get-tuple-element.146), channel_id=1, source_target_pairs={{0,16},{8,24},{16,0},{24,8},{1,17},{9,25},{17,1},{25,9},{2,18},{10... | collective-permute-start | bytes 1572872 | tf_op jit(solution)/shard_map/ppermute | solution.py:938
  160.9 19.9 %collective-permute-start.17 = (bf16[512,512]{1,0:T(8,128)(2,1)}, bf16[512,512]{1,0:T(8,128)(2,1)S(1)}, u32[]{:S(2)}, u32[]{:S(2)}) collective-permute-start(bf16[512,512]{1,0:T(8,128)(2,1)} %get-tuple-element.147), channel_id=1, source_target_pairs={{0,8},{8,0},{16,24},{24,16},{1,9},{9,1},{17,25},{25,17},{2,10},{10... | collective-permute-start | bytes 1572872 | tf_op jit(solution)/shard_map/ppermute | solution.py:938
  162.2 18.9 %collective-permute-start.18 = (bf16[512,512]{1,0:T(8,128)(2,1)}, bf16[512,512]{1,0:T(8,128)(2,1)S(1)}, u32[]{:S(2)}, u32[]{:S(2)}) collective-permute-start(bf16[512,512]{1,0:T(8,128)(2,1)} %get-tuple-element.148), channel_id=1, source_target_pairs={{0,16},{8,24},{16,0},{24,8},{1,17},{9,25},{17,1},{25,9},{2,18},{10... | collective-permute-start | bytes 1572872 | tf_op jit(solution)/shard_map/ppermute | solution.py:938
  213.8 23.5 %collective-permute-start.19 = (bf16[512,1024]{1,0:T(8,128)(2,1)}, bf16[512,1024]{1,0:T(8,128)(2,1)S(1)}, u32[]{:S(2)}, u32[]{:S(2)}) collective-permute-start(bf16[512,1024]{1,0:T(8,128)(2,1)} %get-tuple-element.156), channel_id=1, source_target_pairs={{0,8},{8,0},{16,24},{24,16},{1,9},{9,1},{17,25},{25,17},{2,10},{10... | collective-permute-start | bytes 3145736 | tf_op jit(solution)/shard_map/ppermute | solution.py:938
  215.0 22.4 %collective-permute-start.20 = (bf16[512,1024]{1,0:T(8,128)(2,1)}, bf16[512,1024]{1,0:T(8,128)(2,1)S(1)}, u32[]{:S(2)}, u32[]{:S(2)}) collective-permute-start(bf16[512,1024]{1,0:T(8,128)(2,1)} %get-tuple-element.157), channel_id=1, source_target_pairs={{0,16},{8,24},{16,0},{24,8},{1,17},{9,25},{17,1},{25,9},{2,18},{10... | collective-permute-start | bytes 3145736 | tf_op jit(solution)/shard_map/ppermute | solution.py:938
  237.4 1.4 copy-start.22
  238.8 136.5 %reduce-scatter.5.cloned.1.call-start = ((), (), s32[]{:S(2)}) async-start(), calls=%async_computation.6 | async-start | bytes 2064384 | tf_op jit(solution)/shard_map/reduce_scatter | solution.py:1012
  245.3 8.4 %collective-permute-start.21 = (bf16[512,256]{1,0:T(8,128)(2,1)}, bf16[512,256]{1,0:T(8,128)(2,1)S(1)}, u32[]{:S(2)}, u32[]{:S(2)}) collective-permute-start(bf16[512,256]{1,0:T(8,128)(2,1)} %get-tuple-element.171), channel_id=1, source_target_pairs={{0,8},{8,0},{16,24},{24,16},{1,9},{9,1},{17,25},{25,17},{2,10},{10... | collective-permute-start | bytes 786440 | tf_op jit(solution)/shard_map/ppermute | solution.py:938
  246.3 7.8 %collective-permute-start.22 = (bf16[512,256]{1,0:T(8,128)(2,1)}, bf16[512,256]{1,0:T(8,128)(2,1)S(1)}, u32[]{:S(2)}, u32[]{:S(2)}) collective-permute-start(bf16[512,256]{1,0:T(8,128)(2,1)} %get-tuple-element.172), channel_id=1, source_target_pairs={{0,16},{8,24},{16,0},{24,8},{1,17},{9,25},{17,1},{25,9},{2,18},{10... | collective-permute-start | bytes 786440 | tf_op jit(solution)/shard_map/ppermute | solution.py:938
  247.6 11.5 %collective-permute-start.23 = (bf16[512,256]{1,0:T(8,128)(2,1)}, bf16[512,256]{1,0:T(8,128)(2,1)S(1)}, u32[]{:S(2)}, u32[]{:S(2)}) collective-permute-start(bf16[512,256]{1,0:T(8,128)(2,1)} %get-tuple-element.173), channel_id=1, source_target_pairs={{0,24},{8,16},{16,8},{24,0},{1,25},{9,17},{17,9},{25,1},{2,26},{10... | collective-permute-start | bytes 786440 | tf_op jit(solution)/shard_map/ppermute | solution.py:938
  248.9 10.9 %copy-start.36 = (bf16[512,1024]{1,0:T(8,128)(2,1)S(1)}, bf16[512,1024]{1,0:T(8,128)(2,1)}, u32[]{:S(2)}) copy-start(bf16[512,1024]{1,0:T(8,128)(2,1)} %get-tuple-element.175) | copy-start | bytes 3145732
  253.7 10.1 %copy-start.30 = (bf16[512,256]{1,0:T(8,128)(2,1)}, bf16[512,256]{1,0:T(8,128)(2,1)S(1)}, u32[]{:S(2)}) copy-start(bf16[512,256]{1,0:T(8,128)(2,1)S(1)} %collective-permute-done.21.refs_7_) | copy-start | bytes 786436
  254.1 9.8 %copy-start.31 = (bf16[512,256]{1,0:T(8,128)(2,1)}, bf16[512,256]{1,0:T(8,128)(2,1)S(1)}, u32[]{:S(2)}) copy-start(bf16[512,256]{1,0:T(8,128)(2,1)S(1)} %collective-permute-done.22.refs_8_) | copy-start | bytes 786436
  259.0 4.8 %copy-start.32 = (bf16[512,256]{1,0:T(8,128)(2,1)}, bf16[512,256]{1,0:T(8,128)(2,1)S(1)}, u32[]{:S(2)}) copy-start(bf16[512,256]{1,0:T(8,128)(2,1)S(1)} %collective-permute-done.23.refs_9_) | copy-start | bytes 786436
  259.0 40.9 %collective-permute-start.24 = (bf16[512,1024]{1,0:T(8,128)(2,1)}, bf16[512,1024]{1,0:T(8,128)(2,1)S(1)}, u32[]{:S(2)}, u32[]{:S(2)}) collective-permute-start(bf16[512,1024]{1,0:T(8,128)(2,1)} %get-tuple-element.174), channel_id=1, source_target_pairs={{0,8},{8,0},{16,24},{24,16},{1,9},{9,1},{17,25},{25,17},{2,10},{10... | collective-permute-start | bytes 3145736 | tf_op jit(solution)/shard_map/ppermute | solution.py:938
  259.8 40.1 %collective-permute-start.25 = (bf16[512,1024]{1,0:T(8,128)(2,1)S(1)}, bf16[512,1024]{1,0:T(8,128)(2,1)S(1)}, u32[]{:S(2)}, u32[]{:S(2)}) collective-permute-start(bf16[512,1024]{1,0:T(8,128)(2,1)S(1)} %copy-done.36), channel_id=1, source_target_pairs={{0,16},{8,24},{16,0},{24,8},{1,17},{9,25},{17,1},{25,9},{2,18},{10... | collective-permute-start | bytes 3145736 | tf_op jit(solution)/shard_map/ppermute | solution.py:938
  260.3 52.0 %collective-permute-start.26 = (bf16[1024,256]{1,0:T(8,128)(2,1)}, bf16[1024,256]{1,0:T(8,128)(2,1)S(1)}, u32[]{:S(2)}, u32[]{:S(2)}) collective-permute-start(bf16[1024,256]{1,0:T(8,128)(2,1)} %get-tuple-element.188), channel_id=1, source_target_pairs={{0,8},{8,0},{16,24},{24,16},{1,9},{9,1},{17,25},{25,17},{2,10},{10... | collective-permute-start | bytes 1572872 | tf_op jit(solution)/shard_map/ppermute | solution.py:938
  261.5 51.6 %collective-permute-start.27 = (bf16[1024,256]{1,0:T(8,128)(2,1)}, bf16[1024,256]{1,0:T(8,128)(2,1)S(1)}, u32[]{:S(2)}, u32[]{:S(2)}) collective-permute-start(bf16[1024,256]{1,0:T(8,128)(2,1)} %get-tuple-element.189), channel_id=1, source_target_pairs={{0,16},{8,24},{16,0},{24,8},{1,17},{9,25},{17,1},{25,9},{2,18},{10... | collective-permute-start | bytes 1572872 | tf_op jit(solution)/shard_map/ppermute | solution.py:938
  263.1 50.0 %collective-permute-start.28 = (bf16[1024,256]{1,0:T(8,128)(2,1)}, bf16[1024,256]{1,0:T(8,128)(2,1)S(1)}, u32[]{:S(2)}, u32[]{:S(2)}) collective-permute-start(bf16[1024,256]{1,0:T(8,128)(2,1)} %get-tuple-element.190), channel_id=1, source_target_pairs={{0,24},{8,16},{16,8},{24,0},{1,25},{9,17},{17,9},{25,1},{2,26},{10... | collective-permute-start | bytes 1572872 | tf_op jit(solution)/shard_map/ppermute | solution.py:938
  309.6 11.6 %collective-permute-start.29 = (bf16[512,512]{1,0:T(8,128)(2,1)}, bf16[512,512]{1,0:T(8,128)(2,1)}, u32[]{:S(2)}, u32[]{:S(2)}) collective-permute-start(bf16[512,512]{1,0:T(8,128)(2,1)} %get-tuple-element.196), channel_id=1, source_target_pairs={{0,8},{8,0},{16,24},{24,16},{1,9},{9,1},{17,25},{25,17},{2,10},{10... | collective-permute-start | bytes 1572872 | tf_op jit(solution)/shard_map/ppermute | solution.py:938
  310.7 13.1 %collective-permute-start.30 = (bf16[512,512]{1,0:T(8,128)(2,1)}, bf16[512,512]{1,0:T(8,128)(2,1)}, u32[]{:S(2)}, u32[]{:S(2)}) collective-permute-start(bf16[512,512]{1,0:T(8,128)(2,1)} %get-tuple-element.197), channel_id=1, source_target_pairs={{0,16},{8,24},{16,0},{24,8},{1,17},{9,25},{17,1},{25,9},{2,18},{10... | collective-permute-start | bytes 1572872 | tf_op jit(solution)/shard_map/ppermute | solution.py:938
  312.3 16.3 %collective-permute-start.31 = (bf16[512,512]{1,0:T(8,128)(2,1)}, bf16[512,512]{1,0:T(8,128)(2,1)}, u32[]{:S(2)}, u32[]{:S(2)}) collective-permute-start(bf16[512,512]{1,0:T(8,128)(2,1)} %get-tuple-element.198), channel_id=1, source_target_pairs={{0,24},{8,16},{16,8},{24,0},{1,25},{9,17},{17,9},{25,1},{2,26},{10... | collective-permute-start | bytes 1572872 | tf_op jit(solution)/shard_map/ppermute | solution.py:938
  321.2 29.4 %copy-start.7 = (f32[512,1024]{1,0:T(8,128)S(1)}, f32[512,1024]{1,0:T(8,128)}, u32[]{:S(2)}) copy-start(f32[512,1024]{1,0:T(8,128)} %get-tuple-element.143.refs_5_) | copy-start | bytes 6291460
  321.2 29.4 %copy-start.12 = (bf16[512,1024]{1,0:T(8,128)(2,1)S(1)}, bf16[512,1024]{1,0:T(8,128)(2,1)}, u32[]{:S(2)}) copy-start(bf16[512,1024]{1,0:T(8,128)(2,1)} %copy-done.11) | copy-start | bytes 3145732
  328.6 16.2 %collective-permute-start.36 = (bf16[128,3456]{1,0:T(8,128)(2,1)}, bf16[128,3456]{1,0:T(8,128)(2,1)S(1)}, u32[]{:S(2)}, u32[]{:S(2)}) collective-permute-start(bf16[128,3456]{1,0:T(8,128)(2,1)} %reduce-scatter.3.cloned.1.call-done.p0_ref), channel_id=1, source_target_pairs={{0,16},{8,24},{16,0},{24,8},{1,17},{9,25},{17,1},{25,9},{2,18},{10... | collective-permute-start | bytes 2654216 | tf_op jit(solution)/shard_map/ppermute | solution.py:938
  329.2 18.5 %collective-permute-start.35 = (bf16[128,3456]{1,0:T(8,128)(2,1)}, bf16[128,3456]{1,0:T(8,128)(2,1)S(1)}, u32[]{:S(2)}, u32[]{:S(2)}) collective-permute-start(bf16[128,3456]{1,0:T(8,128)(2,1)} %reduce-scatter.3.cloned.1.call-done.p0_ref), channel_id=1, source_target_pairs={{0,8},{8,0},{16,24},{24,16},{1,9},{9,1},{17,25},{25,17},{2,10},{10... | collective-permute-start | bytes 2654216 | tf_op jit(solution)/shard_map/ppermute | solution.py:938
  346.6 32.2 %collective-permute-start.38 = (bf16[128,1792]{1,0:T(8,128)(2,1)}, bf16[128,1792]{1,0:T(8,128)(2,1)}, u32[]{:S(2)}, u32[]{:S(2)}) collective-permute-start(bf16[128,1792]{1,0:T(8,128)(2,1)} %slice.43), channel_id=1, source_target_pairs={{0,8},{8,0},{16,24},{24,16},{1,9},{9,1},{17,25},{25,17},{2,10},{10... | collective-permute-start | bytes 1376264 | tf_op jit(solution)/shard_map/ppermute | solution.py:938
  349.5 29.3 %collective-permute-start.37 = (bf16[128,1664]{1,0:T(8,128)(2,1)}, bf16[128,1664]{1,0:T(8,128)(2,1)}, u32[]{:S(2)}, u32[]{:S(2)}) collective-permute-start(bf16[128,1664]{1,0:T(8,128)(2,1)} %slice.42), channel_id=1, source_target_pairs={{0,16},{8,24},{16,0},{24,8},{1,17},{9,25},{17,1},{25,9},{2,18},{10... | collective-permute-start | bytes 1277960 | tf_op jit(solution)/shard_map/ppermute | solution.py:938
  353.8 36.3 %copy-start.1 = (bf16[576,1024]{1,0:T(8,128)(2,1)S(1)}, bf16[576,1024]{1,0:T(8,128)(2,1)}, u32[]{:S(2)}) copy-start(bf16[576,1024]{1,0:T(8,128)(2,1)} %param.28) | copy-start | bytes 3538948
  375.3 10.6 %collective-permute-start.32 = (bf16[128,896]{1,0:T(8,128)(2,1)}, bf16[128,896]{1,0:T(8,128)(2,1)S(1)}, u32[]{:S(2)}, u32[]{:S(2)}) collective-permute-start(bf16[128,896]{1,0:T(8,128)(2,1)} %reduce-scatter.5.cloned.1.call-done.p0_ref), channel_id=1, source_target_pairs={{0,8},{8,0},{16,24},{24,16},{1,9},{9,1},{17,25},{25,17},{2,10},{10... | collective-permute-start | bytes 688136 | tf_op jit(solution)/shard_map/ppermute | solution.py:938
  376.9 9.1 %collective-permute-start.33 = (bf16[128,896]{1,0:T(8,128)(2,1)}, bf16[128,896]{1,0:T(8,128)(2,1)S(1)}, u32[]{:S(2)}, u32[]{:S(2)}) collective-permute-start(bf16[128,896]{1,0:T(8,128)(2,1)} %reduce-scatter.5.cloned.1.call-done.p0_ref), channel_id=1, source_target_pairs={{0,16},{8,24},{16,0},{24,8},{1,17},{9,25},{17,1},{25,9},{2,18},{10... | collective-permute-start | bytes 688136 | tf_op jit(solution)/shard_map/ppermute | solution.py:938
  378.4 7.6 %collective-permute-start.34 = (bf16[128,896]{1,0:T(8,128)(2,1)}, bf16[128,896]{1,0:T(8,128)(2,1)S(1)}, u32[]{:S(2)}, u32[]{:S(2)}) collective-permute-start(bf16[128,896]{1,0:T(8,128)(2,1)} %reduce-scatter.5.cloned.1.call-done.p0_ref), channel_id=1, source_target_pairs={{0,24},{8,16},{16,8},{24,0},{1,25},{9,17},{17,9},{25,1},{2,26},{10... | collective-permute-start | bytes 688136 | tf_op jit(solution)/shard_map/ppermute | solution.py:938
  (17 other events, 15.3 us)
Sparse Core Ops, SparseCore 0:
  10.2 26.1 all-gather.3
  38.6 90.2 all-gather.5
  130.5 45.5 all-gather.7
  237.5 83.7 reduce-scatter.2
  328.8 46.5 reduce-scatter.4
